TPU v7x, 256 devices: a whole 4x4x8 slice. The times are simulated.
256 devices in a mesh: grp: 4 (over y), own: 64 (over x, z, core).
Axes of the slice: x: 4, y: 4, z: 8, core: 2. Of those that a mesh axis runs over, the one named last changes fastest.
Arguments:
- grad_parts: bfloat16 [4, 64, 1024, 1024], P('grp', None, 'own'), may hold values from -6 to 6
- assign: int32 [64], replicated, may hold values from 0 to 63, each once
- block_bounds: int32 [64, 4], replicated, may hold values from 0 to 22016, as said below
- left_root: float32 [64, 1024, 1024], P('own', 'grp'), may hold values from -0.1875 to 0.1875
- right_root: float32 [64, 1024, 1024], P('own', 'grp'), may hold values from -0.1875 to 0.1875
- left_stat: float32 [64, 1024, 1024], P('own', 'grp'), may hold values from -6 to 6
- right_stat: float32 [64, 1024, 1024], P('own', 'grp'), may hold values from -6 to 6
- first_moment: float32 [64, 1024, 1024], P(None, 'own', 'grp'), may hold values from -3 to 3
- second_moment: float32 [64, 1024, 1024], P(None, 'own', 'grp'), may hold values from 1 to 8
Outputs:
- update: bfloat16 [64, 1024, 1024], P(None, 'own', 'grp')
- first_next: float32 [64, 1024, 1024], P(None, 'own', 'grp')
- second_next: float32 [64, 1024, 1024], P(None, 'own', 'grp')
- left_next: float32 [64, 1024, 1024], P('own', 'grp')
- right_next: float32 [64, 1024, 1024], P('own', 'grp')
Inputs may be any that keep to these rules, and one draw needn't show every extreme that they name: `assign`: a permutation of 0 to 63. `block_bounds`: offsets are multiples of 1024 inside the matrix; the matrix is 8192 x 22016 or 22016 x 8192; block 0 sits at offsets 0, block 1 at the last column block of a 8192 x 22016 matrix.
All inputs are finite; a program needn't handle non-finite values.
Results may differ from a plain program's by a relative error of at most 0.015.
Values may be sent and summed in bfloat16 or wider, within the bound.
No kernel may reach another device: no remote copies, remote signals or barrier semaphores. Data moves between devices by JAX's collectives and lax.ppermute only.
A program may use at most 128 MiB of HBM per device.

v0:
```python
import jax
import jax.numpy as jnp
from jax import lax
from jax.sharding import PartitionSpec as P

BETA_FIRST = 0.9
BETA_SECOND = 0.95
BIAS_FIRST = 1.0 - 0.9**10
BIAS_SECOND = 1.0 - 0.95**10
ADAM_EPS = 1e-08
STAT_DECAY = 0.95
NORM_EPS = 1e-06
HIGH = lax.Precision.HIGHEST


def block_mask(bounds, row_ids, col_ids):
    row_ok = bounds[:, 0:1] + row_ids[None, :] < bounds[:, 2:3]
    col_ok = bounds[:, 1:2] + col_ids[None, :] < bounds[:, 3:4]
    return (row_ok[:, :, None] & col_ok[:, None, :]).astype(jnp.float32)


def on_device(
    grad_parts,
    assign,
    block_bounds,
    left_root,
    right_root,
    left_stat,
    right_stat,
    first_moment,
    second_moment,
):
    n_own = lax.axis_size("own")
    n_grp = lax.axis_size("grp")
    own_index = lax.axis_index("own")
    grp_index = lax.axis_index("grp")
    total_blocks = assign.shape[0]
    per_owner = total_blocks // n_own
    shard_rows = grad_parts.shape[2]
    width = grad_parts.shape[3]
    quarter = width // n_grp
    summed = lax.psum_scatter(
        grad_parts[0].astype(jnp.float32).astype(jnp.bfloat16),
        "grp",
        scatter_dimension=2,
        tiled=True,
    ).astype(jnp.float32)
    row_ids = own_index * shard_rows + jnp.arange(shard_rows, dtype=jnp.int32)
    col_ids = grp_index * quarter + jnp.arange(quarter, dtype=jnp.int32)
    mask = block_mask(block_bounds, row_ids, col_ids)
    gradient = summed * mask
    first_next = BETA_FIRST * first_moment + (1.0 - BETA_FIRST) * gradient
    second_next = BETA_SECOND * second_moment + (1.0 - BETA_SECOND) * gradient * gradient
    adam = mask * (first_next / BIAS_FIRST) / (jnp.sqrt(second_next / BIAS_SECOND) + ADAM_EPS)
    adam_sq = jnp.sum(adam * adam, axis=(1, 2))
    key = assign % n_own * per_owner + assign // n_own
    order = jnp.argsort(key)
    sorted_grad = gradient[order]
    column_part = lax.all_to_all(
        sorted_grad.reshape(n_own, per_owner, shard_rows, quarter),
        "own",
        split_axis=0,
        concat_axis=2,
        tiled=True,
    )[0]
    piece = lax.all_gather(column_part, "grp", axis=2, tiled=True)
    left_acc = STAT_DECAY * left_stat
    right_acc = STAT_DECAY * right_stat
    absorb_mixed = jnp.einsum("bik,bkj->bij", left_root, piece, precision=HIGH)
    left_acc = left_acc + jnp.einsum(
        "bik,bjk->bij",
        lax.dynamic_slice_in_dim(piece, grp_index * quarter, quarter, 1),
        piece,
        precision=HIGH,
    )
    current = right_acc
    right_acc = current + jnp.einsum("bki,bkj->bij", column_part, piece, precision=HIGH)
    precond = jnp.einsum(
        "bik,bkj->bij",
        absorb_mixed,
        lax.all_gather(right_root, "grp", axis=1, tiled=True),
        precision=HIGH,
    )
    pre_sq = jnp.sum(precond * precond, axis=(1, 2))
    adam_total = lax.psum(adam_sq, ("grp", "own"))
    pre_total = lax.psum(pre_sq, "grp")
    adam_owned = lax.dynamic_slice_in_dim(adam_total[order], own_index * per_owner, per_owner, 0)
    cells = float(width * width)
    scale = jnp.sqrt(adam_owned / cells) / jnp.sqrt(pre_total / cells + NORM_EPS)
    owned_ids = lax.dynamic_slice_in_dim(order, own_index * per_owner, per_owner, 0)
    owner_rows = grp_index * quarter + jnp.arange(quarter, dtype=jnp.int32)
    owner_mask = block_mask(block_bounds[owned_ids], owner_rows, jnp.arange(width, dtype=jnp.int32))
    grafted = (-scale[:, None, None] * precond * owner_mask).astype(jnp.bfloat16)
    back = lax.all_to_all(
        lax.all_to_all(grafted[None], "grp", split_axis=3, concat_axis=2, tiled=True),
        "own",
        split_axis=2,
        concat_axis=0,
        tiled=True,
    )
    update = back.reshape(total_blocks, shard_rows, quarter)[key]
    return (update, first_next, second_next, left_acc, right_acc)


def solution(mesh):
    placed = (
        P("grp", None, "own", None),
        P(),
        P(),
        P("own", "grp", None),
        P("own", "grp", None),
        P("own", "grp", None),
        P("own", "grp", None),
        P(None, "own", "grp"),
        P(None, "own", "grp"),
    )
    return jax.shard_map(
        on_device,
        mesh=mesh,
        in_specs=placed,
        out_specs=(
            P(None, "own", "grp"),
            P(None, "own", "grp"),
            P(None, "own", "grp"),
            P("own", "grp", None),
            P("own", "grp", None),
        ),
        check_vma=False,
    )
```

profile of v0, /device:TPU:1, one launch (start us, length us, event | category | flops | bytes accessed | tf_op | source)
XLA Modules:
  0.0 266.5 jit_solution(15899246843637876010)
XLA Ops:
  7.2 0.7 reduce-scatter.2.cloned.1.call-update
  8.0 0.8 slice_bitcast_fusion.3
  9.0 0.7 compare_select_fusion
  9.7 2.0 sort.17
  11.8 34.9 %reduce-scatter.2.cloned.1.call-done = bf16[64,16,256]{2,1,0:T(8,128)(2,1)} async-done(((bf16[64,16,1024]{2,1,0:T(8,128)(2,1)}), bf16[64,16,256]{2,1,0:T(8,128)(2,1)}) %reduce-scatter.2.cloned.1.call-update) | async-done | bytes 524304 | tf_op jit(solution)/shard_map/reduce_scatter | solution.py:42
  46.7 4.1 %fusion.26 = (f32[64]{0:T(128)S(1)}, f32[64,16,256]{2,1,0:T(8,128)}, f32[64,16,256]{2,1,0:T(8,128)}, f32[64,16,256]{2,1,0:T(8,128)S(1)}) fusion(pred[64,256]{1,0:T(8,128)(4,1)S(1)} %add_compare_fusion, pred[64,16]{1,0:T(8,128)(4,1)S(1)} %copy.20, bf16[64,16,256]{2,1,0:T(8,128)(2,1)} %reduce-scatter.2.cloned.1.call-done, f32[64,16,256]{2,1,0:T(8,128)} %param.16, ...), kind=kLoop, calls=%fused_computation.27 | loop fusion | flops 4456384 | bytes 5784832 | tf_op jit(solution)/shard_map/reduce_sum | solution.py:55
  50.8 0.6 gather_fusion.1
  51.4 39.1 %all_to_all.36 = f32[64,1,16,256]{3,2,1,0:T(8,128)} all-to-all(f32[64,1,16,256]{3,2,1,0:T(8,128)S(1)} %bitcast.70), channel_id=1, replica_groups=mesh['grp'=4,'own'=64] {'own'}, dimensions={0} | all-to-all | bytes 2097152 | tf_op jit(solution)/shard_map/all_to_all | solution.py:59
  90.6 0.7 all-gather.5.cloned.1.call-update
  91.3 0.6 dynamic_slice.9
  93.9 0.6 fusion.32
  94.5 1.3 add_compare_fusion.3
  95.8 1.3 add_compare_fusion.2
  97.1 75.5 %psum.14 = f32[64]{0:T(128)S(1)} all-reduce(f32[64]{0:T(128)S(1)} %get-tuple-element.20), channel_id=1, replica_groups=mesh['grp'=4,'own'=64] {'grp','own'}, use_global_device_ids=true, to_apply=%region_3.4 | all-reduce | flops 64 | bytes 512 | tf_op jit(solution)/shard_map/psum | solution.py:85
  172.6 0.8 gather_fusion
  173.4 0.6 dynamic_slice.10
  174.7 8.5 %fusion.6 = f32[1024,256]{1,0:T(8,128)S(1)} fusion(f32[1,1024,1024]{2,1,0:T(8,128)} %all-gather.3.cloned.1.call-done, f32[1,256,1024]{2,1,0:T(8,128)S(1)} %copy-done), kind=kOutput, calls=%fused_computation.9 | convolution fusion | flops 3221225472 | bytes 6291456 | tf_op jit(solution)/shard_map/bik,bkj->bij/dot_general | solution.py:69
  183.2 8.0 %all-gather.5.cloned.1.call-done = f32[1,1024,1024]{2,1,0:T(8,128)} async-done(((f32[1,256,1024]{2,1,0:T(8,128)}), f32[1,1024,1024]{2,1,0:T(8,128)}) %all-gather.5.cloned.1.call-update) | async-done | bytes 4194320 | tf_op jit(solution)/shard_map/all_gather | solution.py:81
  191.2 6.3 %multiply_reduce_fusion = (f32[]{:T(128)}, f32[256,1024]{1,0:T(8,128)S(1)}) fusion(f32[1024,256]{1,0:T(8,128)S(1)} %fusion.6, f32[1,1024,1024]{2,1,0:T(8,128)} %all-gather.5.cloned.1.call-done), kind=kOutput, calls=%fused_computation.25 | convolution fusion | flops 3221749760 | bytes 6291460 | tf_op jit(solution)/shard_map/bik,bkj->bij/dot_general | solution.py:78
  197.5 7.4 %psum.15 = f32[1]{0:T(128)} all-reduce(f32[1]{0:T(128)} %bitcast.15), channel_id=1, replica_groups=mesh['grp'=4,'own'=64] {'grp'}, use_global_device_ids=true, to_apply=%region_5.6 | all-reduce | flops 1 | bytes 8 | tf_op jit(solution)/shard_map/psum | solution.py:86
  205.8 0.9 copy.21
  207.2 3.8 %reduce.2 = bf16[1024,256]{1,0:T(8,128)(2,1)S(1)} reduce(bf16[1024,1,1,256]{3,2,1,0:T(2,128)(2,1)S(1)} %bitcast.73, bf16[]{:T(256)} %broadcast.168), dimensions={1,2}, to_apply=%bitcast.58.reduce_sub_computation | reduce | bytes 1048578
  211.1 9.3 %all_to_all.37 = bf16[4,2,32768]{2,1,0:T(2,128)(2,1)S(1)} all-to-all(bf16[4,2,32768]{2,1,0:T(2,128)(2,1)S(1)} %reshape.233), channel_id=1, replica_groups=mesh['grp'=4,'own'=64] {'grp'}, dimensions={0} | all-to-all | bytes 1048576 | tf_op jit(solution)/shard_map/all_to_all | solution.py:95
  221.3 0.8 copy.27
  222.1 3.8 %reduce.3 = bf16[1024,256]{1,0:T(8,128)(2,1)S(1)} reduce(bf16[1024,1,1,256]{3,2,1,0:T(2,128)(2,1)S(1)} %bitcast.74, bf16[]{:T(256)} %broadcast.168), dimensions={1,2}, to_apply=%bitcast.67.reduce_sub_computation | reduce | bytes 1048578
  226.0 0.9 reshape.235
  226.9 13.8 %all-to-all-start.2 = ((bf16[64,2,2048]{2,1,0:T(2,128)(2,1)}), bf16[64,2,2048]{2,1,0:T(2,128)(2,1)S(1)}, u32[]{:S(2)}, u32[]{:S(2)}) async-start(bf16[64,2,2048]{2,1,0:T(2,128)(2,1)} %reshape.235), calls=%async_computation.3 | async-start | bytes 1048576 | tf_op jit(solution)/shard_map/all_to_all | solution.py:94
  240.7 7.6 %fusion.17 = f32[1,256,1024]{2,1,0:T(8,128)} fusion(f32[1,1024,1024]{2,1,0:T(8,128)} %all-gather.3.cloned.1.call-done, s32[]{:T(128)S(6)} %select_n.35, f32[1,256,1024]{2,1,0:T(8,128)} %param.14), kind=kOutput, calls=%fused_computation.17 | convolution fusion | flops 3221749760 | bytes 7340036 | tf_op jit(solution)/shard_map/bik,bjk->bij/dot_general | solution.py:70
  248.3 4.7 %fusion.14 = f32[1,256,1024]{2,1,0:T(8,128)} fusion(f32[1024,256]{1,0:T(8,128)S(1)} %bitcast.69, f32[1,1024,1024]{2,1,0:T(8,128)S(1)} %copy-done.1, f32[1,256,1024]{2,1,0:T(8,128)S(1)} %copy-done.3), kind=kOutput, calls=%fused_computation.16 | convolution fusion | flops 3221749760 | bytes 7340032 | tf_op jit(solution)/shard_map/bki,bkj->bij/dot_general | solution.py:77
  253.0 4.9 %all-to-all-done.2 = bf16[64,2,2048]{2,1,0:T(2,128)(2,1)S(1)} async-done(((bf16[64,2,2048]{2,1,0:T(2,128)(2,1)}), bf16[64,2,2048]{2,1,0:T(2,128)(2,1)S(1)}, u32[]{:S(2)}, u32[]{:S(2)}) %all-to-all-start.2) | async-done | bytes 524320 | tf_op jit(solution)/shard_map/all_to_all | solution.py:94
  258.0 0.5 reshape.236
  258.6 1.4 gather_fusion.2
  (32 shorter events, 2.3 us)
Async XLA Ops:
  7.2 167.5 %copy-start = (f32[1,256,1024]{2,1,0:T(8,128)S(1)}, f32[1,256,1024]{2,1,0:T(8,128)}, u32[]{:S(2)}) copy-start(f32[1,256,1024]{2,1,0:T(8,128)} %param.12) | copy-start | bytes 3145732
  7.2 39.5 %reduce-scatter.2.cloned.1.call-start = ((), (), s32[]{:S(2)}) async-start(), calls=%async_computation.4 | async-start | bytes 2621440 | tf_op jit(solution)/shard_map/reduce_scatter | solution.py:42
  7.9 166.8 %all-gather.3.cloned.1.call-start = ((), (), s32[]{:S(2)}) async-start(), calls=%async_computation.5 | async-start | bytes 5242880 | tf_op jit(solution)/shard_map/all_gather | solution.py:66
  50.8 43.0 %copy-start.4 = (s32[64,4]{0,1:T(4,128)S(1)}, s32[64,4]{0,1:T(4,128)}, u32[]{:S(2)}) copy-start(s32[64,4]{0,1:T(4,128)} %param.11) | copy-start | bytes 3076
  90.5 100.6 %all-gather.5.cloned.1.call-start = ((), (), s32[]{:S(2)}) async-start(), calls=%async_computation.6 | async-start | bytes 5242880 | tf_op jit(solution)/shard_map/all_gather | solution.py:81
  225.9 22.4 %copy-start.2 = (f32[64,1,16,256]{3,2,1,0:T(8,128)S(1)}, f32[64,1,16,256]{3,2,1,0:T(8,128)}, u32[]{:S(2)}) copy-start(f32[64,1,16,256]{3,2,1,0:T(8,128)} %all_to_all.36) | copy-start | bytes 3145732
  226.9 31.1 %all-to-all-start.2 = ((bf16[64,2,2048]{2,1,0:T(2,128)(2,1)}), bf16[64,2,2048]{2,1,0:T(2,128)(2,1)S(1)}, u32[]{:S(2)}, u32[]{:S(2)}) async-start(bf16[64,2,2048]{2,1,0:T(2,128)(2,1)} %reshape.235), calls=%async_computation.3 | async-start | bytes 1048576 | tf_op jit(solution)/shard_map/all_to_all | solution.py:94
  240.7 7.7 %copy-start.1 = (f32[1,1024,1024]{2,1,0:T(8,128)S(1)}, f32[1,1024,1024]{2,1,0:T(8,128)}, u32[]{:S(2)}) copy-start(f32[1,1024,1024]{2,1,0:T(8,128)} %all-gather.3.cloned.1.call-done) | copy-start | bytes 12582916
  240.7 7.7 %copy-start.3 = (f32[1,256,1024]{2,1,0:T(8,128)S(1)}, f32[1,256,1024]{2,1,0:T(8,128)}, u32[]{:S(2)}) copy-start(f32[1,256,1024]{2,1,0:T(8,128)} %param.15) | copy-start | bytes 3145732
Sparse Core Ops, SparseCore 0:
  10.6 36.0 reduce-scatter.1
  90.7 46.9 all-gather.2
  139.6 51.5 all-gather.4
where the time goes:
time: 267 us
  blocking collectives  131 us (49%)
  waiting for transfers between devices  49.2 us (18%)
  matrix products  27.2 us (10%)
  other arithmetic  17.4 us (7%)
  between operations  17.3 us (6%)
  starting transfers between devices  13.9 us (5%)
  local copies, waits for them, and re-layouts  10.2 us (4%)
    psum x1, blocking collectives, on_device(): adam_total = lax.psum(adam_sq, ('grp', 'own'))  75.5 us
    all_to_all x1, blocking collectives, on_device(): lax.all_to_all(sorted_grad.reshape(n_own, per_owner, shard_rows, quarter)...  39.1 us
    reduce_scatter x1, waiting for transfers between devices, on_device(): lax.psum_scatter(grad_parts[0].astype(jnp.float32).astype(jnp.bfloat16),...  34.9 us
    all_to_all x1, starting transfers between devices, on_device(): lax.all_to_all(lax.all_to_all(grafted[None], 'grp', split_axis=3, concat_...  13.8 us
    all_to_all x1, blocking collectives, on_device(): lax.all_to_all(grafted[None], 'grp', split_axis=3, concat_axis=2, tiled=T...  9.33 us
    dot_general x1, matrix products, on_device(): absorb_mixed = jnp.einsum('bik,bkj->bij', left_root, piece, precision=HIGH)  8.51 us
    all_gather x1, waiting for transfers between devices, on_device(): lax.all_gather(right_root, 'grp', axis=1, tiled=True)  7.96 us
    unnamed x2, other arithmetic  7.65 us
  transfers between devices with their start and end apart: 4, of which 3 were waited for; matrix products, arithmetic and copies ran while one was open for 11% of the time, Pallas kernels for 0%

commit v1 on v0

v1 whole, which is shorter than its diff:
```python
import jax
import jax.numpy as jnp
from jax import lax
from jax.sharding import PartitionSpec as P

BETA_FIRST = 0.9
BETA_SECOND = 0.95
BIAS_FIRST = 1.0 - 0.9**10
BIAS_SECOND = 1.0 - 0.95**10
ADAM_EPS = 1e-08
STAT_DECAY = 0.95
NORM_EPS = 1e-06
F32 = jnp.float32
BF16 = jnp.bfloat16


def block_mask(bounds, row_ids, col_ids):
    row_ok = bounds[:, 0:1] + row_ids[None, :] < bounds[:, 2:3]
    col_ok = bounds[:, 1:2] + col_ids[None, :] < bounds[:, 3:4]
    return (row_ok[:, :, None] & col_ok[:, None, :]).astype(F32)


def shift(array, step):
    n = lax.axis_size("grp")
    return lax.ppermute(array, "grp", [(i, (i + step) % n) for i in range(n)])


def grp_sum(array):
    return array + shift(array, 1) + shift(array, 2) + shift(array, 3)


def dot(a, b, dims):
    return lax.dot_general(a, b, (dims, ((), ())), preferred_element_type=F32)


def on_device(
    grad_parts,
    assign,
    block_bounds,
    left_root,
    right_root,
    left_stat,
    right_stat,
    first_moment,
    second_moment,
):
    n_own = lax.axis_size("own")
    n_grp = lax.axis_size("grp")
    own_index = lax.axis_index("own")
    grp_index = lax.axis_index("grp")
    total_blocks = assign.shape[0]
    per_owner = total_blocks // n_own
    shard_rows = grad_parts.shape[2]
    width = grad_parts.shape[3]
    quarter = width // n_grp
    half = total_blocks // 2
    part = grad_parts[0]

    def columns(array, step):
        start = (grp_index + step) % n_grp * quarter
        return lax.dynamic_slice_in_dim(array, start, quarter, array.ndim - 1)

    far = columns(part, 2)
    far_up = shift(far[:half], 1)
    far_down = shift(far[half:], -1)
    up = columns(part, 1)
    down = columns(part, 3)
    up_direct = shift(up[half:], 1)
    down_direct = shift(down[:half], -1)
    up_sum = shift((up[:half].astype(F32) + far_up.astype(F32)).astype(BF16), 1)
    down_sum = shift((down[half:].astype(F32) + far_down.astype(F32)).astype(BF16), -1)
    parts = (columns(part, 0), up_sum, up_direct, down_direct, down_sum)

    def total(parts):
        own, up_sum, up_direct, down_direct, down_sum = parts
        from_up = jnp.concatenate([up_sum, up_direct]).astype(F32)
        from_down = jnp.concatenate([down_direct, down_sum]).astype(F32)
        return own.astype(F32) + from_up + from_down

    row_ids = own_index * shard_rows + jnp.arange(shard_rows, dtype=jnp.int32)
    col_ids = grp_index * quarter + jnp.arange(quarter, dtype=jnp.int32)
    mask = block_mask(block_bounds, row_ids, col_ids)
    key = assign % n_own * per_owner + assign // n_own
    slots = jnp.arange(total_blocks, dtype=jnp.int32)
    order = jnp.sum(jnp.where(key[None, :] == slots[:, None], slots[None, :], 0), axis=1)
    sorted_grad = (total(parts) * mask).astype(BF16)[order]

    left_bf, right_bf = lax.optimization_barrier(
        (left_root[0].astype(BF16), right_root[0].astype(BF16))
    )
    left_bf, right_bf, _, _ = lax.optimization_barrier((left_bf, right_bf, up_sum, down_sum))
    sorted_grad, left_bf, right_bf = lax.optimization_barrier((sorted_grad, left_bf, right_bf))
    left_full = lax.all_gather(left_bf, "grp", axis=0, tiled=True)
    roots = [columns(right_bf, 0)] + [
        shift(columns(right_bf, step), step) for step in (3, 2, 1)
    ]
    right_cols = jnp.concatenate(roots, axis=0)

    own_cols = lax.all_to_all(sorted_grad, "own", split_axis=0, concat_axis=0, tiled=True)

    parts, _ = lax.optimization_barrier((parts, sorted_grad))
    gradient = total(parts) * mask
    first_next = BETA_FIRST * first_moment + (1.0 - BETA_FIRST) * gradient
    second_next = BETA_SECOND * second_moment + (1.0 - BETA_SECOND) * gradient * gradient
    adam = mask * (first_next / BIAS_FIRST) / (jnp.sqrt(second_next / BIAS_SECOND) + ADAM_EPS)
    adam_sq = jnp.sum(adam * adam, axis=(1, 2))
    adam_total = lax.psum(adam_sq, ("grp", "own"))

    low, high = own_cols[:half], own_cols[half:]
    prev_low = shift(low, 1)
    next_high = shift(high, -1)
    prev_high = shift(high, 1)
    next_low = shift(low, -1)
    far_low = shift(prev_low, 1)
    far_high = shift(next_high, -1)
    piece = jnp.concatenate(
        [
            own_cols,
            jnp.concatenate([next_low, next_high]),
            jnp.concatenate([far_low, far_high]),
            jnp.concatenate([prev_low, prev_high]),
        ],
        axis=2,
    ).reshape(width, width)

    mixed = dot(piece, right_cols, ((1,), (0,))).astype(BF16)
    precond = dot(left_full, mixed, ((1,), (0,)))
    pre_sq = jnp.sum(precond * precond).reshape(1)
    pre_total = grp_sum(pre_sq)
    adam_owned = lax.dynamic_slice_in_dim(adam_total[order], own_index * per_owner, per_owner, 0)
    cells = float(width * width)
    scale = jnp.sqrt(adam_owned / cells) / jnp.sqrt(pre_total / cells + NORM_EPS)
    grafted = (-scale * precond).astype(BF16).reshape(n_own, shard_rows, quarter)
    piece, own_cols, grafted = lax.optimization_barrier((piece, own_cols, grafted))
    back = lax.all_to_all(grafted, "own", split_axis=0, concat_axis=0, tiled=True)

    rows = lax.dynamic_slice_in_dim(piece, grp_index * quarter, quarter, 0)
    left_acc = STAT_DECAY * left_stat + dot(rows, piece, ((1,), (1,)))[None]
    cross = dot(own_cols.reshape(width, quarter), piece, ((0,), (0,)))
    cross = jnp.concatenate([cross, cross], axis=1)
    cross = lax.dynamic_slice_in_dim(cross, (n_grp - grp_index) % n_grp * quarter, width, 1)
    right_acc = STAT_DECAY * right_stat + cross[None]

    update = back[key] * mask.astype(BF16)
    return (update, first_next, second_next, left_acc, right_acc)


def solution(mesh):
    placed = (
        P("grp", None, "own", None),
        P(),
        P(),
        P("own", "grp", None),
        P("own", "grp", None),
        P("own", "grp", None),
        P("own", "grp", None),
        P(None, "own", "grp"),
        P(None, "own", "grp"),
    )
    return jax.shard_map(
        on_device,
        mesh=mesh,
        in_specs=placed,
        out_specs=(
            P(None, "own", "grp"),
            P(None, "own", "grp"),
            P(None, "own", "grp"),
            P("own", "grp", None),
            P("own", "grp", None),
        ),
        check_vma=False,
    )
```

time: 267 us -> 221 us (0.83)
  waiting for transfers between devices: 49.2 us -> 25.6 us
  blocking collectives: 131 us -> 110 us
  matrix products: 27.2 us -> 7.86 us
  starting transfers between devices: 13.9 us -> 32.5 us
    reduce_scatter x1 -> x0, waiting for transfers between devices: 34.9 us -> none  [on_device(): lax.psum_scatter(grad_parts[0].astype(jnp.float32).astype(jnp.bfloat16),...]
    ppermute x0 -> x18, starting transfers between devices: none -> 23.9 us  [shift(): return lax.ppermute(array, 'grp', [(i, (i + step) % n) for i in range(n)])]
    dot_general x4 -> x3, matrix products: 27.2 us -> 7.86 us  [dot(): return lax.dot_general(a, b, (dims, ((), ())), preferred_element_type=F32)]
    all_to_all x2 -> x1, blocking collectives: 48.4 us -> 32.4 us  [on_device(): lax.all_to_all(sorted_grad, 'own', split_axis=0, concat_axis=0, tiled=True)]
    ppermute x0 -> x18, waiting for transfers between devices: none -> 12.5 us  [shift(): return lax.ppermute(array, 'grp', [(i, (i + step) % n) for i in range(n)])]
    convert_element_type x0 -> x4, other arithmetic: none -> 8.82 us  [the longest x1 2.5 us: on_device(): right_root[0].astype(BF16)]
    all_to_all x1, waiting for transfers between devices: 4.94 us -> 13 us  [on_device(): lax.all_to_all(grafted, 'own', split_axis=0, concat_axis=0, tiled=True)]
    all_gather x2 -> x1, waiting for transfers between devices: 7.98 us -> 0.01 us  [on_device(): left_full = lax.all_gather(left_bf, 'grp', axis=0, tiled=True)]
  transfers between devices with their start and end apart: 4 -> 20, of which waited for: 3 -> 6; matrix products, arithmetic and copies ran while one was open for 11% -> 8% of each run, Pallas kernels for 0% -> 0%
where the time goes in v1:
time: 221 us; the launch traced here: 220 us
  blocking collectives  110 us (50%)
  starting transfers between devices  32.5 us (15%)
  waiting for transfers between devices  25.6 us (12%)
  between operations  17.5 us (8%)
  other arithmetic  17.1 us (8%)
  local copies, waits for them, and re-layouts  9.45 us (4%)
  matrix products  7.86 us (4%)
    psum x1, blocking collectives, on_device(): adam_total = lax.psum(adam_sq, ('grp', 'own'))  77.9 us
    all_to_all x1, blocking collectives, on_device(): lax.all_to_all(sorted_grad, 'own', split_axis=0, concat_axis=0, tiled=True)  32.4 us
    ppermute x18, starting transfers between devices, shift(): return lax.ppermute(array, 'grp', [(i, (i + step) % n) for i in range(n)])  23.9 us
    all_to_all x1, waiting for transfers between devices, on_device(): lax.all_to_all(grafted, 'own', split_axis=0, concat_axis=0, tiled=True)  13 us
    ppermute x18, waiting for transfers between devices, shift(): return lax.ppermute(array, 'grp', [(i, (i + step) % n) for i in range(n)])  12.5 us
    all_to_all x1, starting transfers between devices, on_device(): lax.all_to_all(grafted, 'own', split_axis=0, concat_axis=0, tiled=True)  8.59 us
    dot_general x3, matrix products, dot(): return lax.dot_general(a, b, (dims, ((), ())), preferred_element_type=F32)  7.86 us
  transfers between devices with their start and end apart: 20, of which 6 were waited for; matrix products, arithmetic and copies ran while one was open for 8% of the time, Pallas kernels for 0%

profile of v1, /device:TPU:1, one launch (start us, length us, event | category | flops | bytes accessed | tf_op | source)
XLA Modules:
  0.0 220.3 jit_solution(12587267942712281334)
XLA Ops:
  7.3 2.1 dynamic-slice_bitcast_fusion.3
  9.4 2.1 collective-permute-start
  11.5 1.5 collective-permute-start.4
  13.0 2.7 %collective-permute-start.3 = (bf16[32,16,256]{2,1,0:T(8,128)(2,1)}, bf16[32,16,256]{2,1,0:T(8,128)(2,1)}, u32[]{:S(2)}, u32[]{:S(2)}) collective-permute-start(bf16[32,16,256]{2,1,0:T(8,128)(2,1)} %get-tuple-element.42), channel_id=1, source_target_pairs={{0,192},{64,0},{128,64},{192,128},{1,193},{65,1},{129,65},{193,129... | collective-permute-start | bytes 786440 | tf_op jit(solution)/shard_map/ppermute | solution.py:25
  15.8 2.5 %convert_bitcast_fusion = (bf16[256,1024]{1,0:T(8,128)(2,1)S(1)}, bf16[256,1024]{1,0:T(8,128)(2,1)}) fusion(f32[1,256,1024]{2,1,0:T(8,128)} %param.13, f32[1,256,1024]{2,1,0:T(8,128)} %param.12), kind=kLoop, calls=%fused_computation.42 | loop fusion | flops 524288 | bytes 3145728 | tf_op jit(solution)/shard_map/convert_element_type | solution.py:89
  18.4 2.0 fusion.26
  20.4 1.3 collective-permute-start.1
  21.7 1.4 collective-permute-start.5
  23.3 4.9 %collective-permute-done.1 = bf16[32,16,256]{2,1,0:T(8,128)(2,1)S(1)} collective-permute-done((bf16[32,16,256]{2,1,0:T(8,128)(2,1)}, bf16[32,16,256]{2,1,0:T(8,128)(2,1)S(1)}, u32[]{:S(2)}, u32[]{:S(2)}) %collective-permute-start.1) | collective-permute-done | bytes 262176 | tf_op jit(solution)/shard_map/ppermute | solution.py:25
  28.9 2.3 %fusion.3 = (bf16[64,16,256]{2,1,0:T(8,128)(2,1)}, bf16[64,16,256]{2,1,0:T(8,128)(2,1)S(1)}) fusion(bf16[32,16,256]{2,1,0:T(8,128)(2,1)S(1)} %collective-permute-done.2, bf16[32,16,256]{2,1,0:T(8,128)(2,1)} %copy-done.2, bf16[32,16,256]{2,1,0:T(8,128)(2,1)} %copy-done.4, bf16[32,16,256]{2,1,0:T(8,128)(2,1)} %collective-permute-done.3, ...), kind=kLoop, calls=%fused_computation.16 | loop fusion | flops 3670016 | bytes 2638852 | tf_op jit(solution)/shard_map/convert_element_type | solution.py:86
  31.2 1.6 gather_fusion
  32.9 32.4 %all_to_all.10 = bf16[64,16,256]{2,1,0:T(8,128)(2,1)S(1)} all-to-all(bf16[64,16,256]{2,1,0:T(8,128)(2,1)S(1)} %gather_fusion), channel_id=1, replica_groups=mesh['grp'=4,'own'=64] {'own'}, dimensions={0} | all-to-all | bytes 1048576 | tf_op jit(solution)/shard_map/all_to_all | solution.py:99
  66.1 2.6 %collective-permute-start.7 = (bf16[32,16,256]{2,1,0:T(8,128)(2,1)}, bf16[32,16,256]{2,1,0:T(8,128)(2,1)S(1)}, u32[]{:S(2)}, u32[]{:S(2)}) collective-permute-start(bf16[32,16,256]{2,1,0:T(8,128)(2,1)} %get-tuple-element.53), channel_id=1, source_target_pairs={{0,192},{64,0},{128,64},{192,128},{1,193},{65,1},{129,65},{193,129... | collective-permute-start | bytes 786440 | tf_op jit(solution)/shard_map/ppermute | solution.py:25
  69.6 2.7 %collective-permute-start.12 = (bf16[256,256]{1,0:T(8,128)(2,1)}, bf16[256,256]{1,0:T(8,128)(2,1)}, u32[]{:S(2)}, u32[]{:S(2)}) collective-permute-start(bf16[256,256]{1,0:T(8,128)(2,1)} %get-tuple-element.51), channel_id=1, source_target_pairs={{0,192},{64,0},{128,64},{192,128},{1,193},{65,1},{129,65},{193,129... | collective-permute-start | bytes 393224 | tf_op jit(solution)/shard_map/ppermute | solution.py:25
  72.2 2.7 %collective-permute-start.6 = (bf16[32,16,256]{2,1,0:T(8,128)(2,1)}, bf16[32,16,256]{2,1,0:T(8,128)(2,1)S(1)}, u32[]{:S(2)}, u32[]{:S(2)}) collective-permute-start(bf16[32,16,256]{2,1,0:T(8,128)(2,1)} %get-tuple-element.52), channel_id=1, source_target_pairs={{0,192},{64,0},{128,64},{192,128},{1,193},{65,1},{129,65},{193,129... | collective-permute-start | bytes 786440 | tf_op jit(solution)/shard_map/ppermute | solution.py:25
  74.9 1.5 collective-permute-done.7
  76.4 1.3 collective-permute-start.10
  77.9 4.1 %fusion.10 = (f32[64]{0:T(128)S(1)}, f32[64,16,256]{2,1,0:T(8,128)}, f32[64,16,256]{2,1,0:T(8,128)}) fusion(pred[64,256]{1,0:T(8,128)(4,1)S(1)} %add_compare_fusion, pred[64,16]{1,0:T(8,128)(4,1)S(1)} %copy.14, bf16[32,16,256]{2,1,0:T(8,128)(2,1)S(1)} %copy-done.5, bf16[32,16,256]{2,1,0:T(8,128)(2,1)} %collective-permute-done.3, ...), kind=kLoop, calls=%fused_computation.26 | loop fusion | flops 7077824 | bytes 5784832 | tf_op jit(solution)/shard_map/reduce_sum | solution.py:106
  82.0 77.9 %psum.7 = f32[64]{0:T(128)S(1)} all-reduce(f32[64]{0:T(128)S(1)} %get-tuple-element.37), channel_id=1, replica_groups=mesh['grp'=4,'own'=64] {'grp','own'}, use_global_device_ids=true, to_apply=%region_2.3 | all-reduce | flops 64 | bytes 512 | tf_op jit(solution)/shard_map/psum | solution.py:107
  162.0 1.2 collective-permute-start.13
  164.8 1.5 maximum_maximum_fusion
  166.3 1.9 collective-permute-done.13
  168.2 3.8 %collective-permute-done.14 = bf16[256,256]{1,0:T(8,128)(2,1)} collective-permute-done((bf16[256,256]{1,0:T(8,128)(2,1)}, bf16[256,256]{1,0:T(8,128)(2,1)}, u32[]{:S(2)}, u32[]{:S(2)}) %collective-permute-start.14) | collective-permute-done | bytes 131104 | tf_op jit(solution)/shard_map/ppermute | solution.py:25
  171.9 5.4 %multiply_reduce_fusion = (f32[]{:T(128)}, f32[1024,256]{1,0:T(8,128)}) fusion(bf16[1024,1024]{1,0:T(8,128)(2,1)} %all-gather.2.cloned.1.call-done, bf16[1024,1024]{1,0:T(8,128)(2,1)S(1)} %bitcast.55, bf16[256,256]{1,0:T(8,128)(2,1)} %collective-permute-done.14, bf16[256,256]{1,0:T(8,128)(2,1)S(1)} %collective-permute-done.13, ...), kind=kOutput, calls=%fused_computation.24 | convolution fusion | flops 1076625408 | bytes 5767172 | tf_op jit(solution)/shard_map/dot_general | solution.py:33
  177.3 1.3 collective-permute-start.16
  178.6 2.1 collective-permute-start.17
  183.7 2.1 multiply_convert_fusion
  185.8 8.6 %all-to-all-start.1 = ((bf16[64,16,256]{2,1,0:T(8,128)(2,1)}), bf16[64,16,256]{2,1,0:T(8,128)(2,1)S(1)}, u32[]{:S(2)}, u32[]{:S(2)}) async-start(bf16[64,16,256]{2,1,0:T(8,128)(2,1)} %bitcast.59), calls=%async_computation.1 | async-start | bytes 1048576 | tf_op jit(solution)/shard_map/all_to_all | solution.py:135
  195.7 1.3 fusion.9
  197.0 1.7 fusion
  198.7 13.0 %all-to-all-done.1 = bf16[64,16,256]{2,1,0:T(8,128)(2,1)S(1)} async-done(((bf16[64,16,256]{2,1,0:T(8,128)(2,1)}), bf16[64,16,256]{2,1,0:T(8,128)(2,1)S(1)}, u32[]{:S(2)}, u32[]{:S(2)}) %all-to-all-start.1) | async-done | bytes 524320 | tf_op jit(solution)/shard_map/all_to_all | solution.py:135
  212.4 1.1 fusion.11
  (66 shorter events, 8.4 us)
Async XLA Ops:
  7.2 8.5 %copy-start.11 = (s32[64,4]{0,1:T(4,128)S(1)}, s32[64,4]{0,1:T(4,128)}, u32[]{:S(2)}) copy-start(s32[64,4]{0,1:T(4,128)} %param.11) | copy-start | bytes 3076
  7.2 8.5 %copy-start.12 = (s32[64]{0:T(128)S(1)}, s32[64]{0:T(128)}, u32[]{:S(2)}) copy-start(s32[64]{0:T(128)} %param.10) | copy-start | bytes 772
  7.2 164.8 %all-gather.2.cloned.1.call-start = ((), (), s32[]{:S(2)}) async-start(), calls=%async_computation.2 | async-start | bytes 2621440 | tf_op jit(solution)/shard_map/all_gather | solution.py:93
  9.4 9.1 %copy-start = (bf16[1,64,16,1024]{3,2,1,0:T(8,128)(2,1)S(1)}, bf16[1,64,16,1024]{3,2,1,0:T(8,128)(2,1)}, u32[]{:S(2)}) copy-start(bf16[1,64,16,1024]{3,2,1,0:T(8,128)(2,1)} %param.9) | copy-start | bytes 6291460
  9.4 9.0 %collective-permute-start = (bf16[32,16,256]{2,1,0:T(8,128)(2,1)}, bf16[32,16,256]{2,1,0:T(8,128)(2,1)S(1)}, u32[]{:S(2)}, u32[]{:S(2)}) collective-permute-start(bf16[32,16,256]{2,1,0:T(8,128)(2,1)} %get-tuple-element.43), channel_id=1, source_target_pairs={{0,64},{64,128},{128,192},{192,0},{1,65},{65,129},{129,193},{193,1... | collective-permute-start | bytes 786440 | tf_op jit(solution)/shard_map/ppermute | solution.py:25
  11.5 6.9 %collective-permute-start.4 = (bf16[32,16,256]{2,1,0:T(8,128)(2,1)S(1)}, bf16[32,16,256]{2,1,0:T(8,128)(2,1)}, u32[]{:S(2)}, u32[]{:S(2)}) collective-permute-start(bf16[32,16,256]{2,1,0:T(8,128)(2,1)S(1)} %get-tuple-element.45), channel_id=1, source_target_pairs={{0,192},{64,0},{128,64},{192,128},{1,193},{65,1},{129,65},{193,129... | collective-permute-start | bytes 786440 | tf_op jit(solution)/shard_map/ppermute | solution.py:25
  13.0 15.2 %collective-permute-start.2 = (bf16[32,16,256]{2,1,0:T(8,128)(2,1)}, bf16[32,16,256]{2,1,0:T(8,128)(2,1)S(1)}, u32[]{:S(2)}, u32[]{:S(2)}) collective-permute-start(bf16[32,16,256]{2,1,0:T(8,128)(2,1)} %get-tuple-element.44), channel_id=1, source_target_pairs={{0,64},{64,128},{128,192},{192,0},{1,65},{65,129},{129,193},{193,1... | collective-permute-start | bytes 786440 | tf_op jit(solution)/shard_map/ppermute | solution.py:25
  13.0 15.9 %collective-permute-start.3 = (bf16[32,16,256]{2,1,0:T(8,128)(2,1)}, bf16[32,16,256]{2,1,0:T(8,128)(2,1)}, u32[]{:S(2)}, u32[]{:S(2)}) collective-permute-start(bf16[32,16,256]{2,1,0:T(8,128)(2,1)} %get-tuple-element.42), channel_id=1, source_target_pairs={{0,192},{64,0},{128,64},{192,128},{1,193},{65,1},{129,65},{193,129... | collective-permute-start | bytes 786440 | tf_op jit(solution)/shard_map/ppermute | solution.py:25
  20.4 7.8 %collective-permute-start.1 = (bf16[32,16,256]{2,1,0:T(8,128)(2,1)}, bf16[32,16,256]{2,1,0:T(8,128)(2,1)S(1)}, u32[]{:S(2)}, u32[]{:S(2)}) collective-permute-start(bf16[32,16,256]{2,1,0:T(8,128)(2,1)} %get-tuple-element.47), channel_id=1, source_target_pairs={{0,64},{64,128},{128,192},{192,0},{1,65},{65,129},{129,193},{193,1... | collective-permute-start | bytes 786440 | tf_op jit(solution)/shard_map/ppermute | solution.py:25
  21.7 6.5 %collective-permute-start.5 = (bf16[32,16,256]{2,1,0:T(8,128)(2,1)}, bf16[32,16,256]{2,1,0:T(8,128)(2,1)S(1)}, u32[]{:S(2)}, u32[]{:S(2)}) collective-permute-start(bf16[32,16,256]{2,1,0:T(8,128)(2,1)} %get-tuple-element.46), channel_id=1, source_target_pairs={{0,192},{64,0},{128,64},{192,128},{1,193},{65,1},{129,65},{193,129... | collective-permute-start | bytes 786440 | tf_op jit(solution)/shard_map/ppermute | solution.py:25
  28.2 0.8 copy-start.4
  32.9 45.0 %copy-start.3 = (bf16[32,16,256]{2,1,0:T(8,128)(2,1)S(1)}, bf16[32,16,256]{2,1,0:T(8,128)(2,1)}, u32[]{:S(2)}) copy-start(bf16[32,16,256]{2,1,0:T(8,128)(2,1)} %copy-done.2) | copy-start | bytes 786436
  32.9 45.0 %copy-start.5 = (bf16[32,16,256]{2,1,0:T(8,128)(2,1)S(1)}, bf16[32,16,256]{2,1,0:T(8,128)(2,1)}, u32[]{:S(2)}) copy-start(bf16[32,16,256]{2,1,0:T(8,128)(2,1)} %copy-done.4) | copy-start | bytes 786436
  66.1 10.3 %collective-permute-start.7 = (bf16[32,16,256]{2,1,0:T(8,128)(2,1)}, bf16[32,16,256]{2,1,0:T(8,128)(2,1)S(1)}, u32[]{:S(2)}, u32[]{:S(2)}) collective-permute-start(bf16[32,16,256]{2,1,0:T(8,128)(2,1)} %get-tuple-element.53), channel_id=1, source_target_pairs={{0,192},{64,0},{128,64},{192,128},{1,193},{65,1},{129,65},{193,129... | collective-permute-start | bytes 786440 | tf_op jit(solution)/shard_map/ppermute | solution.py:25
  68.8 9.0 %collective-permute-start.8 = (bf16[32,16,256]{2,1,0:T(8,128)(2,1)}, bf16[32,16,256]{2,1,0:T(8,128)(2,1)S(1)}, u32[]{:S(2)}, u32[]{:S(2)}) collective-permute-start(bf16[32,16,256]{2,1,0:T(8,128)(2,1)} %get-tuple-element.52), channel_id=1, source_target_pairs={{0,64},{64,128},{128,192},{192,0},{1,65},{65,129},{129,193},{193,1... | collective-permute-start | bytes 786440 | tf_op jit(solution)/shard_map/ppermute | solution.py:25
  69.6 96.7 %collective-permute-start.12 = (bf16[256,256]{1,0:T(8,128)(2,1)}, bf16[256,256]{1,0:T(8,128)(2,1)}, u32[]{:S(2)}, u32[]{:S(2)}) collective-permute-start(bf16[256,256]{1,0:T(8,128)(2,1)} %get-tuple-element.51), channel_id=1, source_target_pairs={{0,192},{64,0},{128,64},{192,128},{1,193},{65,1},{129,65},{193,129... | collective-permute-start | bytes 393224 | tf_op jit(solution)/shard_map/ppermute | solution.py:25
  72.2 89.7 %collective-permute-start.11 = (bf16[32,16,256]{2,1,0:T(8,128)(2,1)}, bf16[32,16,256]{2,1,0:T(8,128)(2,1)S(1)}, u32[]{:S(2)}, u32[]{:S(2)}) collective-permute-start(bf16[32,16,256]{2,1,0:T(8,128)(2,1)} %get-tuple-element.53), channel_id=1, source_target_pairs={{0,64},{64,128},{128,192},{192,0},{1,65},{65,129},{129,193},{193,1... | collective-permute-start | bytes 786440 | tf_op jit(solution)/shard_map/ppermute | solution.py:25
  72.2 91.0 %collective-permute-start.6 = (bf16[32,16,256]{2,1,0:T(8,128)(2,1)}, bf16[32,16,256]{2,1,0:T(8,128)(2,1)S(1)}, u32[]{:S(2)}, u32[]{:S(2)}) collective-permute-start(bf16[32,16,256]{2,1,0:T(8,128)(2,1)} %get-tuple-element.52), channel_id=1, source_target_pairs={{0,192},{64,0},{128,64},{192,128},{1,193},{65,1},{129,65},{193,129... | collective-permute-start | bytes 786440 | tf_op jit(solution)/shard_map/ppermute | solution.py:25
  76.4 5.6 %copy-start.7 = (bf16[32,16,256]{2,1,0:T(8,128)(2,1)}, bf16[32,16,256]{2,1,0:T(8,128)(2,1)S(1)}, u32[]{:S(2)}) copy-start(bf16[32,16,256]{2,1,0:T(8,128)(2,1)S(1)} %collective-permute-done.7) | copy-start | bytes 786436
  76.4 87.7 %collective-permute-start.10 = (bf16[32,16,256]{2,1,0:T(8,128)(2,1)S(1)}, bf16[32,16,256]{2,1,0:T(8,128)(2,1)S(1)}, u32[]{:S(2)}, u32[]{:S(2)}) collective-permute-start(bf16[32,16,256]{2,1,0:T(8,128)(2,1)S(1)} %collective-permute-done.7), channel_id=1, source_target_pairs={{0,192},{64,0},{128,64},{192,128},{1,193},{65,1},{129,65},{193,129... | collective-permute-start | bytes 786440 | tf_op jit(solution)/shard_map/ppermute | solution.py:25
  77.8 4.3 %copy-start.8 = (bf16[32,16,256]{2,1,0:T(8,128)(2,1)}, bf16[32,16,256]{2,1,0:T(8,128)(2,1)S(1)}, u32[]{:S(2)}) copy-start(bf16[32,16,256]{2,1,0:T(8,128)(2,1)S(1)} %collective-permute-done.8) | copy-start | bytes 786436
  77.8 87.1 %collective-permute-start.9 = (bf16[32,16,256]{2,1,0:T(8,128)(2,1)S(1)}, bf16[32,16,256]{2,1,0:T(8,128)(2,1)}, u32[]{:S(2)}, u32[]{:S(2)}) collective-permute-start(bf16[32,16,256]{2,1,0:T(8,128)(2,1)S(1)} %collective-permute-done.8), channel_id=1, source_target_pairs={{0,64},{64,128},{128,192},{192,0},{1,65},{65,129},{129,193},{193,1... | collective-permute-start | bytes 786440 | tf_op jit(solution)/shard_map/ppermute | solution.py:25
  162.0 6.2 %collective-permute-start.13 = (bf16[256,256]{1,0:T(8,128)(2,1)}, bf16[256,256]{1,0:T(8,128)(2,1)S(1)}, u32[]{:S(2)}, u32[]{:S(2)}) collective-permute-start(bf16[256,256]{1,0:T(8,128)(2,1)} %get-tuple-element.50), channel_id=1, source_target_pairs={{0,128},{64,192},{128,0},{192,64},{1,129},{65,193},{129,1},{193,65... | collective-permute-start | bytes 393224 | tf_op jit(solution)/shard_map/ppermute | solution.py:25
  163.2 8.7 %copy-start.10 = (bf16[256,256]{1,0:T(8,128)(2,1)S(1)}, bf16[256,256]{1,0:T(8,128)(2,1)}, u32[]{:S(2)}) copy-start(bf16[256,256]{1,0:T(8,128)(2,1)} %get-tuple-element.48) | copy-start | bytes 393220
  163.2 8.7 %collective-permute-start.14 = (bf16[256,256]{1,0:T(8,128)(2,1)}, bf16[256,256]{1,0:T(8,128)(2,1)}, u32[]{:S(2)}, u32[]{:S(2)}) collective-permute-start(bf16[256,256]{1,0:T(8,128)(2,1)} %get-tuple-element.49), channel_id=1, source_target_pairs={{0,64},{64,128},{128,192},{192,0},{1,65},{65,129},{129,193},{193,1... | collective-permute-start | bytes 393224 | tf_op jit(solution)/shard_map/ppermute | solution.py:25
  164.1 0.7 copy-start.9
  177.3 3.8 %collective-permute-start.15 = (f32[1]{0:T(128)}, f32[1]{0:T(128)}, u32[]{:S(2)}, u32[]{:S(2)}) collective-permute-start(f32[1]{0:T(128)} %bitcast.16), channel_id=1, source_target_pairs={{0,64},{64,128},{128,192},{192,0},{1,65},{65,129},{129,193},{193,1... | collective-permute-start | bytes 20 | tf_op jit(solution)/shard_map/ppermute | solution.py:25
  177.3 5.1 %collective-permute-start.16 = (f32[1]{0:T(128)}, f32[1]{0:T(128)}, u32[]{:S(2)}, u32[]{:S(2)}) collective-permute-start(f32[1]{0:T(128)} %bitcast.16), channel_id=1, source_target_pairs={{0,128},{64,192},{128,0},{192,64},{1,129},{65,193},{129,1},{193,65... | collective-permute-start | bytes 20 | tf_op jit(solution)/shard_map/ppermute | solution.py:25
  178.6 4.4 %collective-permute-start.17 = (f32[1]{0:T(128)}, f32[1]{0:T(128)}, u32[]{:S(2)}, u32[]{:S(2)}) collective-permute-start(f32[1]{0:T(128)} %bitcast.16), channel_id=1, source_target_pairs={{0,192},{64,0},{128,64},{192,128},{1,193},{65,1},{129,65},{193,129... | collective-permute-start | bytes 20 | tf_op jit(solution)/shard_map/ppermute | solution.py:25
  185.8 25.9 %all-to-all-start.1 = ((bf16[64,16,256]{2,1,0:T(8,128)(2,1)}), bf16[64,16,256]{2,1,0:T(8,128)(2,1)S(1)}, u32[]{:S(2)}, u32[]{:S(2)}) async-start(bf16[64,16,256]{2,1,0:T(8,128)(2,1)} %bitcast.59), calls=%async_computation.1 | async-start | bytes 1048576 | tf_op jit(solution)/shard_map/all_to_all | solution.py:135
  194.4 1.2 copy-start.6
  195.7 1.3 copy-start.1
  (1 other events, 0.7 us)
Sparse Core Ops, SparseCore 0:
  33.0 39.6 all-gather.1

commit v2 on v1

v2 whole, which is shorter than its diff:
```python
import functools

import jax
import jax.numpy as jnp
from jax import lax
from jax.experimental import pallas as pl
from jax.experimental.pallas import tpu as pltpu
from jax.sharding import PartitionSpec as P

BETA_FIRST = 0.9
BETA_SECOND = 0.95
BIAS_FIRST = 1.0 - 0.9**10
BIAS_SECOND = 1.0 - 0.95**10
ADAM_EPS = 1e-08
STAT_DECAY = 0.95
NORM_EPS = 1e-06
F32 = jnp.float32
BF16 = jnp.bfloat16
VMEM_LIMIT = 40 * 1024 * 1024
SMEM = pltpu.SMEM
VMEM = pltpu.VMEM


def block_mask(bounds, row_ids, col_ids):
    row_ok = bounds[:, 0:1] + row_ids[None, :] < bounds[:, 2:3]
    col_ok = bounds[:, 1:2] + col_ids[None, :] < bounds[:, 3:4]
    return (row_ok[:, :, None] & col_ok[:, None, :]).astype(F32)


def shift(array, step):
    n = lax.axis_size("grp")
    return lax.ppermute(array, "grp", [(i, (i + step) % n) for i in range(n)])


def dot(a, b, dims):
    return lax.dot_general(a, b, (dims, ((), ())), preferred_element_type=F32)


def pack_kernel(
    place, key, bounds, own, up_sum, up_direct, down_direct, down_sum, out
):
    blocks, rows, cols = out.shape
    half = blocks // 2
    row = lax.broadcasted_iota(jnp.int32, (rows, cols), 0) + place[1] * rows
    col = lax.broadcasted_iota(jnp.int32, (rows, cols), 1) + place[0] * cols

    def one(block, value):
        ok = (row < bounds[block, 2] - bounds[block, 0]) & (
            col < bounds[block, 3] - bounds[block, 1]
        )
        out[key[block]] = jnp.where(ok, value, 0.0).astype(BF16)

    def step(i, carry):
        low = own[0, i].astype(F32) + up_sum[i].astype(F32) + down_direct[i].astype(F32)
        one(i, low)
        j = i + half
        high = own[0, j].astype(F32) + up_direct[i].astype(F32) + down_sum[i].astype(F32)
        one(j, high)
        return carry

    lax.fori_loop(0, half, step, 0, unroll=4)


def pack(place, key, bounds, part, up_sum, up_direct, down_direct, down_sum):
    _, blocks, rows, width = part.shape
    cols = up_sum.shape[2]

    def whole(array):
        return pl.BlockSpec(array.shape, lambda i, *_: (0,) * array.ndim)

    return pl.pallas_call(
        pack_kernel,
        out_shape=jax.ShapeDtypeStruct((blocks, rows, cols), BF16),
        grid_spec=pltpu.PrefetchScalarGridSpec(
            num_scalar_prefetch=3,
            grid=(1,),
            in_specs=[
                pl.BlockSpec((1, blocks, rows, cols), lambda i, place, *_: (0, 0, 0, place[0])),
                whole(up_sum),
                whole(up_direct),
                whole(down_direct),
                whole(down_sum),
            ],
            out_specs=pl.BlockSpec((blocks, rows, cols), lambda i, *_: (0, 0, 0)),
        ),
        compiler_params=pltpu.CompilerParams(vmem_limit_bytes=VMEM_LIMIT),
    )(place, key, bounds, part, up_sum, up_direct, down_direct, down_sum)


def precond_kernel(
    place,
    own,
    next_low,
    next_high,
    far_low,
    far_high,
    prev_low,
    prev_high,
    root_own,
    root_next,
    root_far,
    root_prev,
    left_own,
    left_next,
    left_far_low,
    left_far_high,
    left_prev,
    adam,
    out,
    norms,
    mixed,
):
    width, quarter = out.shape
    half = width // 2
    me = place[0]
    n = width // quarter
    for top, parts in (
        (0, (own.at[pl.ds(0, half)], next_low, far_low, prev_low)),
        (half, (own.at[pl.ds(half, half)], next_high, far_high, prev_high)),
    ):
        for row in range(0, half, quarter):
            total = jnp.zeros((quarter, quarter), F32)
            for piece, root in zip(parts, (root_own, root_next, root_far, root_prev)):
                total += dot(piece[pl.ds(row, quarter), :], root[...], ((1,), (0,)))
            mixed[pl.ds(top + row, quarter), :] = total.astype(BF16)
    square = jnp.zeros((8, quarter), F32)
    eighth = quarter // 2
    for step, left, extra in (
        (0, left_own, 0),
        (1, left_next, 0),
        (2, left_far_low, 0),
        (2, left_far_high, eighth),
        (3, left_prev, 0),
    ):
        base = lax.rem(me + step, n) * quarter + extra
        rows = left.shape[0]
        value = dot(left[...], mixed[...], ((1,), (0,)))
        out[pl.ds(pl.multiple_of(base, eighth), rows), :] = value
        square += jnp.sum((value * value).reshape(rows // 8, 8, quarter), axis=0)
    norms[...] = jnp.zeros_like(norms)
    norms[0:1, :] = jnp.broadcast_to(jnp.sum(square), (1, 128))
    norms[1:2, :] = jnp.sum(adam[...], axis=0, keepdims=True)


def precondition(place, own, pieces, roots, lefts, adam):
    width, quarter = own.shape
    operands = (own, *pieces, *roots, *lefts, adam)
    return pl.pallas_call(
        precond_kernel,
        out_shape=(
            jax.ShapeDtypeStruct((width, quarter), F32),
            jax.ShapeDtypeStruct((8, 128), F32),
        ),
        in_specs=[pl.BlockSpec(memory_space=SMEM)]
        + [pl.BlockSpec(memory_space=VMEM)] * len(operands),
        out_specs=(pl.BlockSpec(memory_space=VMEM),) * 2,
        scratch_shapes=[VMEM((width, quarter), BF16)],
        compiler_params=pltpu.CompilerParams(vmem_limit_bytes=VMEM_LIMIT),
    )(place, *operands)


def graft_kernel(cells, precond, first, second, third, fourth, out):
    sums = first[...] + second[...] + third[...] + fourth[...]
    pre, adam = sums[0:1, :], sums[1:2, :]
    scale = -jnp.sqrt(adam / cells) / jnp.sqrt(pre / cells + NORM_EPS)
    width, quarter = out.shape
    scale = jnp.concatenate([scale] * (quarter // 128), axis=1)
    out[...] = (scale * precond[...]).astype(BF16)


def graft(precond, norms):
    width, quarter = precond.shape
    tiles = 4
    rows = width // tiles
    small = pl.BlockSpec((8, 128), lambda i: (0, 0))
    return pl.pallas_call(
        functools.partial(graft_kernel, float(width * width)),
        out_shape=jax.ShapeDtypeStruct((width, quarter), BF16),
        grid=(tiles,),
        in_specs=[pl.BlockSpec((rows, quarter), lambda i: (i, 0))] + [small] * 4,
        out_specs=pl.BlockSpec((rows, quarter), lambda i: (i, 0)),
        compiler_params=pltpu.CompilerParams(vmem_limit_bytes=VMEM_LIMIT),
    )(precond, *norms)


def on_device(
    grad_parts,
    assign,
    block_bounds,
    left_root,
    right_root,
    left_stat,
    right_stat,
    first_moment,
    second_moment,
):
    n_own = lax.axis_size("own")
    n_grp = lax.axis_size("grp")
    own_index = lax.axis_index("own")
    grp_index = lax.axis_index("grp")
    total_blocks = assign.shape[0]
    per_owner = total_blocks // n_own
    shard_rows = grad_parts.shape[2]
    width = grad_parts.shape[3]
    quarter = width // n_grp
    half = total_blocks // 2
    part = grad_parts[0]
    place = jnp.stack([grp_index, own_index]).astype(jnp.int32)

    def columns(array, step):
        start = (grp_index + step) % n_grp * quarter
        return lax.dynamic_slice_in_dim(array, start, quarter, array.ndim - 1)

    far = columns(part, 2)
    far_up = shift(far[:half], 1)
    far_down = shift(far[half:], -1)
    later, far_up, far_down = lax.optimization_barrier((part, far_up, far_down))
    up = columns(later, 1)
    down = columns(later, 3)
    up_direct = shift(up[half:], 1)
    down_direct = shift(down[:half], -1)
    up_sum = shift((up[:half].astype(F32) + far_up.astype(F32)).astype(BF16), 1)
    down_sum = shift((down[half:].astype(F32) + far_down.astype(F32)).astype(BF16), -1)

    key = (assign % n_own * per_owner + assign // n_own).astype(jnp.int32)
    slots = jnp.arange(total_blocks, dtype=jnp.int32)
    order = jnp.sum(jnp.where(key[None, :] == slots[:, None], slots[None, :], 0), axis=1)
    left_bf, right_bf = left_root[0].astype(BF16), right_root[0].astype(BF16)
    right_parts = [columns(right_bf, step) for step in range(4)]
    up_sum, up_direct, down_direct, down_sum, left_bf, right_parts = lax.optimization_barrier(
        (up_sum, up_direct, down_direct, down_sum, left_bf, right_parts)
    )

    sorted_grad = pack(
        place, key, block_bounds, grad_parts, up_sum, up_direct, down_direct, down_sum
    )
    own_cols = lax.all_to_all(sorted_grad, "own", split_axis=0, concat_axis=0, tiled=True)
    left_half = quarter // 2
    left_prev = shift(left_bf, 1)
    left_next = shift(left_bf, -1)
    left_far_low = shift(left_prev[:left_half], 1)
    left_far_high = shift(left_next[left_half:], -1)
    roots = [right_parts[0]] + [shift(right_parts[step], step) for step in (3, 2, 1)]
    lefts = [left_bf, left_next, left_far_low, left_far_high, left_prev]

    row_ids = own_index * shard_rows + jnp.arange(shard_rows, dtype=jnp.int32)
    col_ids = grp_index * quarter + jnp.arange(quarter, dtype=jnp.int32)
    mask = block_mask(block_bounds, row_ids, col_ids)
    up_sum, up_direct, down_direct, down_sum, later, _ = lax.optimization_barrier(
        (up_sum, up_direct, down_direct, down_sum, part, sorted_grad)
    )
    from_up = jnp.concatenate([up_sum, up_direct]).astype(F32)
    from_down = jnp.concatenate([down_direct, down_sum]).astype(F32)
    gradient = (columns(later, 0).astype(F32) + from_up + from_down) * mask
    first_next = BETA_FIRST * first_moment + (1.0 - BETA_FIRST) * gradient
    second_next = BETA_SECOND * second_moment + (1.0 - BETA_SECOND) * gradient * gradient
    adam = mask * (first_next / BIAS_FIRST) / (jnp.sqrt(second_next / BIAS_SECOND) + ADAM_EPS)
    adam_sq = jnp.sum(adam * adam, axis=(1, 2))

    own_cols, adam_sq, lefts, roots = lax.optimization_barrier((own_cols, adam_sq, lefts, roots))
    low, high = own_cols[:half], own_cols[half:]
    prev_low = shift(low, 1)
    next_high = shift(high, -1)
    prev_high = shift(high, 1)
    next_low = shift(low, -1)
    far_low = shift(prev_low, 1)
    far_high = shift(next_high, -1)
    pieces = [next_low, next_high, far_low, far_high, prev_low, prev_high]

    shares = jnp.broadcast_to(adam_sq[order][:, None, None], (n_own, 1, 128))
    shares = lax.all_to_all(shares, "own", split_axis=0, concat_axis=0, tiled=True)

    flat = [piece.reshape(width // 2, quarter) for piece in pieces]
    precond, norms = precondition(
        place, own_cols.reshape(width, quarter), flat, roots, lefts, shares.reshape(n_own, 128)
    )
    norms = [norms] + [shift(norms, step) for step in (1, 2, 3)]
    grafted = graft(precond, norms).reshape(n_own, shard_rows, quarter)
    pieces, own_cols, grafted = lax.optimization_barrier((pieces, own_cols, grafted))
    back = lax.all_to_all(grafted, "own", split_axis=0, concat_axis=0, tiled=True)

    whole = jnp.concatenate(
        [own_cols] + [jnp.concatenate(pieces[i : i + 2]) for i in (0, 2, 4)], axis=2
    ).reshape(width, width)
    rows = lax.dynamic_slice_in_dim(whole, grp_index * quarter, quarter, 0)
    left_acc = STAT_DECAY * left_stat + dot(rows, whole, ((1,), (1,)))[None]
    cross = dot(own_cols.reshape(width, quarter), whole, ((0,), (0,)))
    cross = jnp.concatenate([cross, cross], axis=1)
    cross = lax.dynamic_slice_in_dim(cross, (n_grp - grp_index) % n_grp * quarter, width, 1)
    right_acc = STAT_DECAY * right_stat + cross[None]

    update = back[key] * mask.astype(BF16)
    return (update, first_next, second_next, left_acc, right_acc)


def solution(mesh):
    placed = (
        P("grp", None, "own", None),
        P(),
        P(),
        P("own", "grp", None),
        P("own", "grp", None),
        P("own", "grp", None),
        P("own", "grp", None),
        P(None, "own", "grp"),
        P(None, "own", "grp"),
    )
    return jax.shard_map(
        on_device,
        mesh=mesh,
        in_specs=placed,
        out_specs=(
            P(None, "own", "grp"),
            P(None, "own", "grp"),
            P(None, "own", "grp"),
            P("own", "grp", None),
            P("own", "grp", None),
        ),
        check_vma=False,
    )
```

time: 221 us -> 156 us (0.71)
  blocking collectives: 110 us -> 26.7 us
  local copies, waits for them, and re-layouts: 9.45 us -> 27.1 us
  between operations: 17.5 us -> 1 us
  starting transfers between devices: 32.5 us -> 47.6 us
  waiting for transfers between devices: 25.6 us -> 32.8 us
  other arithmetic: 17.1 us -> 11.4 us
  Pallas kernels: 0 us -> 5.7 us
  matrix products: 7.86 us -> 2.48 us
    psum x1 -> x0, blocking collectives: 77.9 us -> none  [on_device(): adam_total = lax.psum(adam_sq, ('grp', 'own'))]
    unnamed x26 -> x77, local copies, waits for them, and re-layouts: 2 us -> 19.6 us
    all_to_all x0 -> x1, starting transfers between devices: none -> 15.1 us  [on_device(): lax.all_to_all(sorted_grad, 'own', split_axis=0, concat_axis=0, tiled=True)]
    ppermute x18 -> x22, waiting for transfers between devices: 12.5 us -> 20.1 us  [shift(): return lax.ppermute(array, 'grp', [(i, (i + step) % n) for i in range(n)])]
    all_to_all x1, blocking collectives: 32.4 us -> 26.7 us  [on_device(): lax.all_to_all(shares, 'own', split_axis=0, concat_axis=0, tiled=True)]
    pallas_call x0 -> x3, Pallas kernels: none -> 5.7 us  [the longest x1 2.77 us: precondition(): pl.pallas_call(precond_kernel, out_shape=(jax.ShapeDtypeStruct((width, qu...]
    convert_element_type x3 -> x2, other arithmetic: 6.87 us -> 1.36 us  [on_device(): left_bf, right_bf = (left_root[0].astype(BF16), right_root[0].astype(BF16))]
    dot_general x3 -> x2, matrix products: 7.86 us -> 2.48 us  [dot(): return lax.dot_general(a, b, (dims, ((), ())), preferred_element_type=F32)]
  transfers between devices with their start and end apart: 20 -> 24, of which waited for: 6 -> 12; matrix products, arithmetic and copies ran while one was open for 8% -> 11% of each run, Pallas kernels for 0% -> 0%
where the time goes in v2:
time: 156 us; the launch traced here: 155 us
  starting transfers between devices  47.6 us (31%)
  waiting for transfers between devices  32.8 us (21%)
  local copies, waits for them, and re-layouts  27.1 us (17%)
  blocking collectives  26.7 us (17%)
  other arithmetic  11.4 us (7%)
  Pallas kernels  5.7 us (4%)
  matrix products  2.48 us (2%)
    ppermute x22, starting transfers between devices, shift(): return lax.ppermute(array, 'grp', [(i, (i + step) % n) for i in range(n)])  26.7 us
    all_to_all x1, blocking collectives, on_device(): lax.all_to_all(shares, 'own', split_axis=0, concat_axis=0, tiled=True)  26.7 us
    ppermute x22, waiting for transfers between devices, shift(): return lax.ppermute(array, 'grp', [(i, (i + step) % n) for i in range(n)])  20.1 us
    unnamed x77, local copies, waits for them, and re-layouts  19.6 us
    all_to_all x1, starting transfers between devices, on_device(): lax.all_to_all(sorted_grad, 'own', split_axis=0, concat_axis=0, tiled=True)  15.1 us
    all_to_all x1, waiting for transfers between devices, on_device(): lax.all_to_all(grafted, 'own', split_axis=0, concat_axis=0, tiled=True)  12.7 us
    all_to_all x1, starting transfers between devices, on_device(): lax.all_to_all(grafted, 'own', split_axis=0, concat_axis=0, tiled=True)  5.87 us
    reduce_sum x1, other arithmetic, on_device(): adam_sq = jnp.sum(adam * adam, axis=(1, 2))  4.32 us
  transfers between devices with their start and end apart: 24, of which 12 were waited for; matrix products, arithmetic and copies ran while one was open for 11% of the time, Pallas kernels for 0%

profile of v2, /device:TPU:1, one launch (start us, length us, event | category | flops | bytes accessed | tf_op | source)
XLA Modules:
  0.0 154.7 jit_solution(3360332804390644077)
XLA Ops:
  0.7 1.9 %dynamic-slice_bitcast_fusion = (bf16[32,16,256]{2,1,0:T(8,128)(2,1)S(1)}, bf16[32,16,256]{2,1,0:T(8,128)(2,1)}) fusion(bf16[1,64,16,1024]{3,2,1,0:T(8,128)(2,1)} %own.1, s32[]{:T(128)S(6)} %add.203, s32[]{:T(128)S(6)} %select_n.84), kind=kLoop, calls=%fused_computation.28 | loop fusion | bytes 1048584 | tf_op jit(solution)/shard_map/slice | solution.py:216
  2.6 2.1 %collective-permute-start = (bf16[32,16,256]{2,1,0:T(8,128)(2,1)}, bf16[32,16,256]{2,1,0:T(8,128)(2,1)S(1)}, u32[]{:S(2)}, u32[]{:S(2)}) collective-permute-start(bf16[32,16,256]{2,1,0:T(8,128)(2,1)} %get-tuple-element.91), channel_id=1, source_target_pairs={{0,64},{64,128},{128,192},{192,0},{1,65},{65,129},{129,193},{193,1... | collective-permute-start | bytes 786440 | tf_op jit(solution)/shard_map/ppermute | solution.py:32
  4.7 1.4 collective-permute-start.1
  6.2 1.3 convert_element_type.51
  10.1 1.3 collective-permute-done.1
  11.5 1.5 %collective-permute-start.3 = (bf16[32,16,256]{2,1,0:T(8,128)(2,1)S(1)}, bf16[32,16,256]{2,1,0:T(8,128)(2,1)S(1)}, u32[]{:S(2)}, u32[]{:S(2)}) collective-permute-start(bf16[32,16,256]{2,1,0:T(8,128)(2,1)S(1)} %get-tuple-element.89), channel_id=1, source_target_pairs={{0,64},{64,128},{128,192},{192,0},{1,65},{65,129},{129,193},{193,1... | collective-permute-start | bytes 786440 | tf_op jit(solution)/shard_map/ppermute | solution.py:32
  13.0 1.2 collective-permute-start.4
  14.8 2.4 %collective-permute-start.5 = (bf16[32,16,256]{2,1,0:T(8,128)(2,1)S(1)}, bf16[32,16,256]{2,1,0:T(8,128)(2,1)S(1)}, u32[]{:S(2)}, u32[]{:S(2)}) collective-permute-start(bf16[32,16,256]{2,1,0:T(8,128)(2,1)S(1)} %get-tuple-element.86), channel_id=1, source_target_pairs={{0,192},{64,0},{128,64},{192,128},{1,193},{65,1},{129,65},{193,129... | collective-permute-start | bytes 786440 | tf_op jit(solution)/shard_map/ppermute | solution.py:32
  17.3 1.1 collective-permute-done.3.up_direct
  18.7 5.4 %collective-permute-done.2.up_sum = bf16[32,16,256]{2,1,0:T(8,128)(2,1)S(1)} collective-permute-done((bf16[32,16,256]{2,1,0:T(8,128)(2,1)S(1)}, bf16[32,16,256]{2,1,0:T(8,128)(2,1)S(1)}, u32[]{:S(2)}, u32[]{:S(2)}) %collective-permute-start.2) | collective-permute-done | bytes 262176 | tf_op jit(solution)/shard_map/ppermute | solution.py:32
  24.3 1.5 shard_map.128
  28.7 15.1 %all-to-all-start = ((bf16[64,16,256]{2,1,0:T(8,128)(2,1)}), bf16[64,16,256]{2,1,0:T(8,128)(2,1)S(1)}, u32[]{:S(2)}, u32[]{:S(2)}) async-start(bf16[64,16,256]{2,1,0:T(8,128)(2,1)} %copy-done.1), calls=%async_computation | async-start | bytes 1048576 | tf_op jit(solution)/shard_map/all_to_all | solution.py:237
  44.8 2.2 %collective-permute-start.6 = (bf16[256,1024]{1,0:T(8,128)(2,1)S(1)}, bf16[256,1024]{1,0:T(8,128)(2,1)}, u32[]{:S(2)}, u32[]{:S(2)}) collective-permute-start(bf16[256,1024]{1,0:T(8,128)(2,1)S(1)} %convert_bitcast_fusion.left_own), channel_id=1, source_target_pairs={{0,192},{64,0},{128,64},{192,128},{1,193},{65,1},{129,65},{193,129... | collective-permute-start | bytes 1572872 | tf_op jit(solution)/shard_map/ppermute | solution.py:32
  49.1 1.5 collective-permute-start.10
  51.4 7.3 %collective-permute-done.7.left_prev = bf16[256,1024]{1,0:T(8,128)(2,1)} collective-permute-done((bf16[256,1024]{1,0:T(8,128)(2,1)S(1)}, bf16[256,1024]{1,0:T(8,128)(2,1)}, u32[]{:S(2)}, u32[]{:S(2)}) %collective-permute-start.7) | collective-permute-done | bytes 524320 | tf_op jit(solution)/shard_map/ppermute | solution.py:32
  59.7 1.0 slice.75
  60.7 2.9 %collective-permute-start.9 = (bf16[128,1024]{1,0:T(8,128)(2,1)S(1)}, bf16[128,1024]{1,0:T(8,128)(2,1)S(1)}, u32[]{:S(2)}, u32[]{:S(2)}) collective-permute-start(bf16[128,1024]{1,0:T(8,128)(2,1)S(1)} %slice.75), channel_id=1, source_target_pairs={{0,192},{64,0},{128,64},{192,128},{1,193},{65,1},{129,65},{193,129... | collective-permute-start | bytes 786440 | tf_op jit(solution)/shard_map/ppermute | solution.py:32
  63.6 4.3 %fusion.8 = (f32[64]{0:T(128)S(1)}, f32[64,16,256]{2,1,0:T(8,128)}, f32[64,16,256]{2,1,0:T(8,128)}) fusion(pred[64,256]{1,0:T(8,128)(4,1)S(1)} %add_compare_fusion, pred[64,16]{1,0:T(8,128)(4,1)} %copy.23, bf16[32,16,256]{2,1,0:T(8,128)(2,1)} %copy-done.16, bf16[32,16,256]{2,1,0:T(8,128)(2,1)} %copy-done.14, ...), kind=kLoop, calls=%fused_computation.20 | loop fusion | flops 7077824 | bytes 5784836 | tf_op jit(solution)/shard_map/reduce_sum | solution.py:258
  71.4 2.7 %collective-permute-start.14 = (bf16[32,16,256]{2,1,0:T(8,128)(2,1)S(1)}, bf16[32,16,256]{2,1,0:T(8,128)(2,1)S(1)}, u32[]{:S(2)}, u32[]{:S(2)}) collective-permute-start(bf16[32,16,256]{2,1,0:T(8,128)(2,1)S(1)} %get-tuple-element.92), channel_id=1, source_target_pairs={{0,192},{64,0},{128,64},{192,128},{1,193},{65,1},{129,65},{193,129... | collective-permute-start | bytes 786440 | tf_op jit(solution)/shard_map/ppermute | solution.py:32
  74.5 1.3 collective-permute-start.18
  75.8 2.1 %collective-permute-done.15 = bf16[32,16,256]{2,1,0:T(8,128)(2,1)S(1)} collective-permute-done((bf16[32,16,256]{2,1,0:T(8,128)(2,1)S(1)}, bf16[32,16,256]{2,1,0:T(8,128)(2,1)S(1)}, u32[]{:S(2)}, u32[]{:S(2)}) %collective-permute-start.15) | collective-permute-done | bytes 262176 | tf_op jit(solution)/shard_map/ppermute | solution.py:32
  77.9 2.7 %collective-permute-start.17 = (bf16[32,16,256]{2,1,0:T(8,128)(2,1)S(1)}, bf16[32,16,256]{2,1,0:T(8,128)(2,1)S(1)}, u32[]{:S(2)}, u32[]{:S(2)}) collective-permute-start(bf16[32,16,256]{2,1,0:T(8,128)(2,1)S(1)} %collective-permute-done.14), channel_id=1, source_target_pairs={{0,192},{64,0},{128,64},{192,128},{1,193},{65,1},{129,65},{193,129... | collective-permute-start | bytes 786440 | tf_op jit(solution)/shard_map/ppermute | solution.py:32
  81.5 26.7 %all_to_all.15 = f32[64,1,128]{2,1,0:T(1,128)S(1)} all-to-all(f32[64,1,128]{2,1,0:T(1,128)S(1)} %broadcast_in_dim.22), channel_id=1, replica_groups=mesh['grp'=4,'own'=64] {'own'}, dimensions={0} | all-to-all | bytes 65536 | tf_op jit(solution)/shard_map/all_to_all | solution.py:271
  118.7 2.8 %shard_map.129 = (f32[1024,256]{1,0:T(8,128)S(1)}, f32[8,128]{1,0:T(8,128)S(1)}) custom-call(s32[2]{0:T(128)S(1)} %pad_add_fusion.place, bf16[1024,256]{1,0:T(8,128)(2,1)S(1)} %bitcast.52, bf16[512,256]{1,0:T(8,128)(2,1)S(1)} %bitcast.58, bf16[512,256]{1,0:T(8,128)(2,1)S(1)} %bitcast.57, bf16[512,256]{1,0:T(8,128)(2,1)S(1)} %bitcast.60, ...), custom_call_target="tpu_custom_call" | custom-call | tf_op jit(solution)/shard_map/pallas_call | solution.py:148
  123.4 1.8 %collective-permute-start.21 = (f32[8,128]{1,0:T(8,128)S(1)}, f32[8,128]{1,0:T(8,128)S(1)}, u32[]{:S(2)}, u32[]{:S(2)}) collective-permute-start(f32[8,128]{1,0:T(8,128)S(1)} %get-tuple-element.72.first), channel_id=1, source_target_pairs={{0,192},{64,0},{128,64},{192,128},{1,193},{65,1},{129,65},{193,129... | collective-permute-start | bytes 12296 | tf_op jit(solution)/shard_map/ppermute | solution.py:32
  127.1 1.2 copy-done.18
  128.3 1.4 shard_map.130
  129.8 5.9 %all-to-all-start.2 = ((bf16[64,16,256]{2,1,0:T(8,128)(2,1)}), bf16[64,16,256]{2,1,0:T(8,128)(2,1)S(1)}, u32[]{:S(2)}, u32[]{:S(2)}) async-start(bf16[64,16,256]{2,1,0:T(8,128)(2,1)} %bitcast.24), calls=%async_computation.2 | async-start | bytes 1048576 | tf_op jit(solution)/shard_map/all_to_all | solution.py:280
  137.2 1.3 fusion.7
  138.5 1.7 %fusion = f32[1,256,1024]{2,1,0:T(8,128)} fusion(bf16[1024,1024]{1,0:T(8,128)(2,1)S(1)} %bitcast.63, f32[1,256,1024]{2,1,0:T(8,128)S(1)} %copy-done.29, s32[]{:T(128)S(6)} %select_n.94), kind=kOutput, calls=%fused_computation.11 | convolution fusion | flops 537395200 | bytes 4718596 | tf_op jit(solution)/shard_map/dot_general | solution.py:36
  140.3 12.7 %all-to-all-done.2 = bf16[64,16,256]{2,1,0:T(8,128)(2,1)S(1)} async-done(((bf16[64,16,256]{2,1,0:T(8,128)(2,1)}), bf16[64,16,256]{2,1,0:T(8,128)(2,1)S(1)}, u32[]{:S(2)}, u32[]{:S(2)}) %all-to-all-start.2) | async-done | bytes 524320 | tf_op jit(solution)/shard_map/all_to_all | solution.py:280
  153.6 1.1 fusion.9
  (127 shorter events, 33.0 us)
Async XLA Ops:
  2.6 7.5 %collective-permute-start = (bf16[32,16,256]{2,1,0:T(8,128)(2,1)}, bf16[32,16,256]{2,1,0:T(8,128)(2,1)S(1)}, u32[]{:S(2)}, u32[]{:S(2)}) collective-permute-start(bf16[32,16,256]{2,1,0:T(8,128)(2,1)} %get-tuple-element.91), channel_id=1, source_target_pairs={{0,64},{64,128},{128,192},{192,0},{1,65},{65,129},{129,193},{193,1... | collective-permute-start | bytes 786440 | tf_op jit(solution)/shard_map/ppermute | solution.py:32
  4.7 6.7 %collective-permute-start.1 = (bf16[32,16,256]{2,1,0:T(8,128)(2,1)S(1)}, bf16[32,16,256]{2,1,0:T(8,128)(2,1)S(1)}, u32[]{:S(2)}, u32[]{:S(2)}) collective-permute-start(bf16[32,16,256]{2,1,0:T(8,128)(2,1)S(1)} %get-tuple-element.90), channel_id=1, source_target_pairs={{0,192},{64,0},{128,64},{192,128},{1,193},{65,1},{129,65},{193,129... | collective-permute-start | bytes 786440 | tf_op jit(solution)/shard_map/ppermute | solution.py:32
  11.5 6.9 %collective-permute-start.3 = (bf16[32,16,256]{2,1,0:T(8,128)(2,1)S(1)}, bf16[32,16,256]{2,1,0:T(8,128)(2,1)S(1)}, u32[]{:S(2)}, u32[]{:S(2)}) collective-permute-start(bf16[32,16,256]{2,1,0:T(8,128)(2,1)S(1)} %get-tuple-element.89), channel_id=1, source_target_pairs={{0,64},{64,128},{128,192},{192,0},{1,65},{65,129},{129,193},{193,1... | collective-permute-start | bytes 786440 | tf_op jit(solution)/shard_map/ppermute | solution.py:32
  13.0 5.6 %collective-permute-start.4 = (bf16[32,16,256]{2,1,0:T(8,128)(2,1)S(1)}, bf16[32,16,256]{2,1,0:T(8,128)(2,1)S(1)}, u32[]{:S(2)}, u32[]{:S(2)}) collective-permute-start(bf16[32,16,256]{2,1,0:T(8,128)(2,1)S(1)} %get-tuple-element.88), channel_id=1, source_target_pairs={{0,192},{64,0},{128,64},{192,128},{1,193},{65,1},{129,65},{193,129... | collective-permute-start | bytes 786440 | tf_op jit(solution)/shard_map/ppermute | solution.py:32
  14.4 9.6 %collective-permute-start.2 = (bf16[32,16,256]{2,1,0:T(8,128)(2,1)S(1)}, bf16[32,16,256]{2,1,0:T(8,128)(2,1)S(1)}, u32[]{:S(2)}, u32[]{:S(2)}) collective-permute-start(bf16[32,16,256]{2,1,0:T(8,128)(2,1)S(1)} %get-tuple-element.87), channel_id=1, source_target_pairs={{0,64},{64,128},{128,192},{192,0},{1,65},{65,129},{129,193},{193,1... | collective-permute-start | bytes 786440 | tf_op jit(solution)/shard_map/ppermute | solution.py:32
  14.8 9.5 %collective-permute-start.5 = (bf16[32,16,256]{2,1,0:T(8,128)(2,1)S(1)}, bf16[32,16,256]{2,1,0:T(8,128)(2,1)S(1)}, u32[]{:S(2)}, u32[]{:S(2)}) collective-permute-start(bf16[32,16,256]{2,1,0:T(8,128)(2,1)S(1)} %get-tuple-element.86), channel_id=1, source_target_pairs={{0,192},{64,0},{128,64},{192,128},{1,193},{65,1},{129,65},{193,129... | collective-permute-start | bytes 786440 | tf_op jit(solution)/shard_map/ppermute | solution.py:32
  28.7 42.6 %all-to-all-start = ((bf16[64,16,256]{2,1,0:T(8,128)(2,1)}), bf16[64,16,256]{2,1,0:T(8,128)(2,1)S(1)}, u32[]{:S(2)}, u32[]{:S(2)}) async-start(bf16[64,16,256]{2,1,0:T(8,128)(2,1)} %copy-done.1), calls=%async_computation | async-start | bytes 1048576 | tf_op jit(solution)/shard_map/all_to_all | solution.py:237
  44.3 14.4 %collective-permute-start.7 = (bf16[256,1024]{1,0:T(8,128)(2,1)S(1)}, bf16[256,1024]{1,0:T(8,128)(2,1)}, u32[]{:S(2)}, u32[]{:S(2)}) collective-permute-start(bf16[256,1024]{1,0:T(8,128)(2,1)S(1)} %convert_bitcast_fusion.left_own), channel_id=1, source_target_pairs={{0,64},{64,128},{128,192},{192,0},{1,65},{65,129},{129,193},{193,1... | collective-permute-start | bytes 1572872 | tf_op jit(solution)/shard_map/ppermute | solution.py:32
  44.8 14.9 %collective-permute-start.6 = (bf16[256,1024]{1,0:T(8,128)(2,1)S(1)}, bf16[256,1024]{1,0:T(8,128)(2,1)}, u32[]{:S(2)}, u32[]{:S(2)}) collective-permute-start(bf16[256,1024]{1,0:T(8,128)(2,1)S(1)} %convert_bitcast_fusion.left_own), channel_id=1, source_target_pairs={{0,192},{64,0},{128,64},{192,128},{1,193},{65,1},{129,65},{193,129... | collective-permute-start | bytes 1572872 | tf_op jit(solution)/shard_map/ppermute | solution.py:32
  49.1 18.8 %copy-start.32 = (pred[64,256]{1,0:T(8,128)(4,1)}, pred[64,256]{1,0:T(8,128)(4,1)S(1)}, u32[]{:S(2)}) copy-start(pred[64,256]{1,0:T(8,128)(4,1)S(1)} %add_compare_fusion) | copy-start | bytes 49156
  49.1 18.8 %collective-permute-start.10 = (bf16[256,256]{1,0:T(8,128)(2,1)}, bf16[256,256]{1,0:T(8,128)(2,1)S(1)}, u32[]{:S(2)}, u32[]{:S(2)}) collective-permute-start(bf16[256,256]{1,0:T(8,128)(2,1)} %get-tuple-element.57), channel_id=1, source_target_pairs={{0,192},{64,0},{128,64},{192,128},{1,193},{65,1},{129,65},{193,129... | collective-permute-start | bytes 393224 | tf_op jit(solution)/shard_map/ppermute | solution.py:32
  50.7 17.9 %collective-permute-start.11 = (bf16[256,256]{1,0:T(8,128)(2,1)}, bf16[256,256]{1,0:T(8,128)(2,1)S(1)}, u32[]{:S(2)}, u32[]{:S(2)}) collective-permute-start(bf16[256,256]{1,0:T(8,128)(2,1)} %get-tuple-element.58), channel_id=1, source_target_pairs={{0,128},{64,192},{128,0},{192,64},{1,129},{65,193},{129,1},{193,65... | collective-permute-start | bytes 393224 | tf_op jit(solution)/shard_map/ppermute | solution.py:32
  50.7 18.5 %collective-permute-start.12 = (bf16[256,256]{1,0:T(8,128)(2,1)}, bf16[256,256]{1,0:T(8,128)(2,1)S(1)}, u32[]{:S(2)}, u32[]{:S(2)}) collective-permute-start(bf16[256,256]{1,0:T(8,128)(2,1)} %get-tuple-element.59), channel_id=1, source_target_pairs={{0,64},{64,128},{128,192},{192,0},{1,65},{65,129},{129,193},{193,1... | collective-permute-start | bytes 393224 | tf_op jit(solution)/shard_map/ppermute | solution.py:32
  59.6 10.3 %collective-permute-start.8 = (bf16[128,1024]{1,0:T(8,128)(2,1)S(1)}, bf16[128,1024]{1,0:T(8,128)(2,1)S(1)}, u32[]{:S(2)}, u32[]{:S(2)}) collective-permute-start(bf16[128,1024]{1,0:T(8,128)(2,1)S(1)} %slice.74), channel_id=1, source_target_pairs={{0,64},{64,128},{128,192},{192,0},{1,65},{65,129},{129,193},{193,1... | collective-permute-start | bytes 786440 | tf_op jit(solution)/shard_map/ppermute | solution.py:32
  60.7 9.9 %collective-permute-start.9 = (bf16[128,1024]{1,0:T(8,128)(2,1)S(1)}, bf16[128,1024]{1,0:T(8,128)(2,1)S(1)}, u32[]{:S(2)}, u32[]{:S(2)}) collective-permute-start(bf16[128,1024]{1,0:T(8,128)(2,1)S(1)} %slice.75), channel_id=1, source_target_pairs={{0,192},{64,0},{128,64},{192,128},{1,193},{65,1},{129,65},{193,129... | collective-permute-start | bytes 786440 | tf_op jit(solution)/shard_map/ppermute | solution.py:32
  71.4 6.5 %collective-permute-start.15 = (bf16[32,16,256]{2,1,0:T(8,128)(2,1)S(1)}, bf16[32,16,256]{2,1,0:T(8,128)(2,1)S(1)}, u32[]{:S(2)}, u32[]{:S(2)}) collective-permute-start(bf16[32,16,256]{2,1,0:T(8,128)(2,1)S(1)} %get-tuple-element.93), channel_id=1, source_target_pairs={{0,64},{64,128},{128,192},{192,0},{1,65},{65,129},{129,193},{193,1... | collective-permute-start | bytes 786440 | tf_op jit(solution)/shard_map/ppermute | solution.py:32
  71.4 6.4 %collective-permute-start.14 = (bf16[32,16,256]{2,1,0:T(8,128)(2,1)S(1)}, bf16[32,16,256]{2,1,0:T(8,128)(2,1)S(1)}, u32[]{:S(2)}, u32[]{:S(2)}) collective-permute-start(bf16[32,16,256]{2,1,0:T(8,128)(2,1)S(1)} %get-tuple-element.92), channel_id=1, source_target_pairs={{0,192},{64,0},{128,64},{192,128},{1,193},{65,1},{129,65},{193,129... | collective-permute-start | bytes 786440 | tf_op jit(solution)/shard_map/ppermute | solution.py:32
  74.2 33.9 %collective-permute-start.13 = (bf16[32,16,256]{2,1,0:T(8,128)(2,1)S(1)}, bf16[32,16,256]{2,1,0:T(8,128)(2,1)S(1)}, u32[]{:S(2)}, u32[]{:S(2)}) collective-permute-start(bf16[32,16,256]{2,1,0:T(8,128)(2,1)S(1)} %get-tuple-element.93), channel_id=1, source_target_pairs={{0,192},{64,0},{128,64},{192,128},{1,193},{65,1},{129,65},{193,129... | collective-permute-start | bytes 786440 | tf_op jit(solution)/shard_map/ppermute | solution.py:32
  74.5 34.4 %collective-permute-start.18 = (bf16[32,16,256]{2,1,0:T(8,128)(2,1)S(1)}, bf16[32,16,256]{2,1,0:T(8,128)(2,1)S(1)}, u32[]{:S(2)}, u32[]{:S(2)}) collective-permute-start(bf16[32,16,256]{2,1,0:T(8,128)(2,1)S(1)} %get-tuple-element.92), channel_id=1, source_target_pairs={{0,64},{64,128},{128,192},{192,0},{1,65},{65,129},{129,193},{193,1... | collective-permute-start | bytes 786440 | tf_op jit(solution)/shard_map/ppermute | solution.py:32
  77.9 31.7 %collective-permute-start.16 = (bf16[32,16,256]{2,1,0:T(8,128)(2,1)S(1)}, bf16[32,16,256]{2,1,0:T(8,128)(2,1)S(1)}, u32[]{:S(2)}, u32[]{:S(2)}) collective-permute-start(bf16[32,16,256]{2,1,0:T(8,128)(2,1)S(1)} %collective-permute-done.15), channel_id=1, source_target_pairs={{0,64},{64,128},{128,192},{192,0},{1,65},{65,129},{129,193},{193,1... | collective-permute-start | bytes 786440 | tf_op jit(solution)/shard_map/ppermute | solution.py:32
  77.9 31.7 %copy-start.2 = (bf16[32,16,256]{2,1,0:T(8,128)(2,1)}, bf16[32,16,256]{2,1,0:T(8,128)(2,1)S(1)}, u32[]{:S(2)}) copy-start(bf16[32,16,256]{2,1,0:T(8,128)(2,1)S(1)} %collective-permute-done.14) | copy-start | bytes 786436
  77.9 31.7 %collective-permute-start.17 = (bf16[32,16,256]{2,1,0:T(8,128)(2,1)S(1)}, bf16[32,16,256]{2,1,0:T(8,128)(2,1)S(1)}, u32[]{:S(2)}, u32[]{:S(2)}) collective-permute-start(bf16[32,16,256]{2,1,0:T(8,128)(2,1)S(1)} %collective-permute-done.14), channel_id=1, source_target_pairs={{0,192},{64,0},{128,64},{192,128},{1,193},{65,1},{129,65},{193,129... | collective-permute-start | bytes 786440 | tf_op jit(solution)/shard_map/ppermute | solution.py:32
  122.4 13.2 %copy-start.4 = (bf16[32,16,256]{2,1,0:T(8,128)(2,1)S(1)}, bf16[32,16,256]{2,1,0:T(8,128)(2,1)}, u32[]{:S(2)}) copy-start(bf16[32,16,256]{2,1,0:T(8,128)(2,1)} %copy-done.2) | copy-start | bytes 786436
  122.4 13.2 %copy-start.7 = (bf16[32,16,256]{2,1,0:T(8,128)(2,1)S(1)}, bf16[32,16,256]{2,1,0:T(8,128)(2,1)}, u32[]{:S(2)}) copy-start(bf16[32,16,256]{2,1,0:T(8,128)(2,1)} %copy-done.5) | copy-start | bytes 786436
  122.4 13.2 %copy-start.10 = (bf16[32,16,256]{2,1,0:T(8,128)(2,1)S(1)}, bf16[32,16,256]{2,1,0:T(8,128)(2,1)}, u32[]{:S(2)}) copy-start(bf16[32,16,256]{2,1,0:T(8,128)(2,1)} %copy-done.8) | copy-start | bytes 786436
  122.4 13.2 %copy-start.13 = (bf16[32,16,256]{2,1,0:T(8,128)(2,1)S(1)}, bf16[32,16,256]{2,1,0:T(8,128)(2,1)}, u32[]{:S(2)}) copy-start(bf16[32,16,256]{2,1,0:T(8,128)(2,1)} %copy-done.11) | copy-start | bytes 786436
  122.4 3.7 %collective-permute-start.19 = (f32[8,128]{1,0:T(8,128)S(1)}, f32[8,128]{1,0:T(8,128)S(1)}, u32[]{:S(2)}, u32[]{:S(2)}) collective-permute-start(f32[8,128]{1,0:T(8,128)S(1)} %get-tuple-element.72.first), channel_id=1, source_target_pairs={{0,64},{64,128},{128,192},{192,0},{1,65},{65,129},{129,193},{193,1... | collective-permute-start | bytes 12296 | tf_op jit(solution)/shard_map/ppermute | solution.py:32
  122.5 4.0 %collective-permute-start.20 = (f32[8,128]{1,0:T(8,128)S(1)}, f32[8,128]{1,0:T(8,128)S(1)}, u32[]{:S(2)}, u32[]{:S(2)}) collective-permute-start(f32[8,128]{1,0:T(8,128)S(1)} %get-tuple-element.72.first), channel_id=1, source_target_pairs={{0,128},{64,192},{128,0},{192,64},{1,129},{65,193},{129,1},{193,65... | collective-permute-start | bytes 12296 | tf_op jit(solution)/shard_map/ppermute | solution.py:32
  123.4 3.7 %collective-permute-start.21 = (f32[8,128]{1,0:T(8,128)S(1)}, f32[8,128]{1,0:T(8,128)S(1)}, u32[]{:S(2)}, u32[]{:S(2)}) collective-permute-start(f32[8,128]{1,0:T(8,128)S(1)} %get-tuple-element.72.first), channel_id=1, source_target_pairs={{0,192},{64,0},{128,64},{192,128},{1,193},{65,1},{129,65},{193,129... | collective-permute-start | bytes 12296 | tf_op jit(solution)/shard_map/ppermute | solution.py:32
  129.8 23.2 %all-to-all-start.2 = ((bf16[64,16,256]{2,1,0:T(8,128)(2,1)}), bf16[64,16,256]{2,1,0:T(8,128)(2,1)S(1)}, u32[]{:S(2)}, u32[]{:S(2)}) async-start(bf16[64,16,256]{2,1,0:T(8,128)(2,1)} %bitcast.24), calls=%async_computation.2 | async-start | bytes 1048576 | tf_op jit(solution)/shard_map/all_to_all | solution.py:280
  138.5 15.1 %copy-start.33 = (pred[64,256]{1,0:T(8,128)(4,1)S(1)}, pred[64,256]{1,0:T(8,128)(4,1)}, u32[]{:S(2)}) copy-start(pred[64,256]{1,0:T(8,128)(4,1)} %copy-done.32) | copy-start | bytes 49156
  138.5 15.1 %copy-start.34 = (pred[64,16]{1,0:T(8,128)(4,1)S(1)}, pred[64,16]{1,0:T(8,128)(4,1)}, u32[]{:S(2)}) copy-start(pred[64,16]{1,0:T(8,128)(4,1)} %copy.23) | copy-start | bytes 3076
  (30 other events, 62.1 us)

commit v3 on v2

v3 whole, which is shorter than its diff:
```python
import functools

import jax
import jax.numpy as jnp
from jax import lax
from jax.experimental import pallas as pl
from jax.experimental.pallas import tpu as pltpu
from jax.sharding import PartitionSpec as P

BETA_FIRST = 0.9
BETA_SECOND = 0.95
BIAS_FIRST = 1.0 - 0.9**10
BIAS_SECOND = 1.0 - 0.95**10
ADAM_EPS = 1e-08
STAT_DECAY = 0.95
NORM_EPS = 1e-06
F32 = jnp.float32
BF16 = jnp.bfloat16
MIB = 1024 * 1024
SMEM = pltpu.SMEM
VMEM = pltpu.VMEM


def shift(array, step):
    n = lax.axis_size("grp")
    return lax.ppermute(array, "grp", [(i, (i + step) % n) for i in range(n)])


def in_hbm(array):
    return pltpu.with_memory_space_constraint(array, pltpu.HBM)


def slice_at(array, start, size, axis):
    starts = [start if i == axis else 0 for i in range(array.ndim)]
    sizes = [size if i == axis else n for i, n in enumerate(array.shape)]
    return lax.dynamic_slice(array, starts, sizes, allow_negative_indices=False)


def dot(a, b, dims):
    return lax.dot_general(a, b, (dims, ((), ())), preferred_element_type=F32)


def inside(place, bounds, block, rows, cols):
    row = lax.broadcasted_iota(jnp.int32, (rows, cols), 0) + place[1] * rows
    col = lax.broadcasted_iota(jnp.int32, (rows, cols), 1) + place[0] * cols
    return (row < bounds[block, 2] - bounds[block, 0]) & (
        col < bounds[block, 3] - bounds[block, 1]
    )


def pack_kernel(
    place,
    key,
    bounds,
    own,
    up_sum,
    up_direct,
    down_direct,
    down_sum,
    first,
    second,
    out,
    first_out,
    second_out,
):
    _, count, rows, cols = own.shape
    half = out.shape[0] // 2
    begin = pl.program_id(0) * count
    lanes = 128

    def one(side, i, value):
        block = side * half + begin + i
        ok = inside(place, bounds, block, rows, cols)
        grad = jnp.where(ok, value, 0.0)
        first_next = BETA_FIRST * first[side, i] + (1.0 - BETA_FIRST) * grad
        second_next = BETA_SECOND * second[side, i] + (1.0 - BETA_SECOND) * grad * grad
        first_out[side, i] = first_next
        second_out[side, i] = second_next
        adam = (first_next / BIAS_FIRST) / (jnp.sqrt(second_next / BIAS_SECOND) + ADAM_EPS)
        square = jnp.where(ok, adam * adam, 0.0)
        square = square[:, :lanes] + square[:, lanes:]
        square = square[: rows // 2] + square[rows // 2 :]
        piece = jnp.concatenate([grad[:, :lanes], grad[:, lanes:], square], axis=0)
        out[key[block]] = piece.astype(BF16)

    def step(i, carry):
        low = own[0, i].astype(F32) + up_sum[i].astype(F32) + down_direct[i].astype(F32)
        one(0, i, low)
        high = own[1, i].astype(F32) + up_direct[i].astype(F32) + down_sum[i].astype(F32)
        one(1, i, high)
        return carry

    lax.fori_loop(0, count, step, 0, unroll=4)


def pack(place, key, bounds, part, sums, first, second):
    blocks, rows, width = part.shape
    cols = first.shape[2]
    half, steps = blocks // 2, 4 if blocks >= 32 else 1
    count = half // steps
    piece = 2 * rows + rows // 2
    moment = pl.BlockSpec((2, count, rows, cols), lambda i, *_: (0, i, 0, 0))
    halves = jax.ShapeDtypeStruct((2, half, rows, cols), F32)
    out, first_next, second_next = pl.pallas_call(
        pack_kernel,
        out_shape=(pltpu.HBM((blocks, piece, 128), BF16), halves, halves),
        grid_spec=pltpu.PrefetchScalarGridSpec(
            num_scalar_prefetch=3,
            grid=(steps,),
            in_specs=[
                pl.BlockSpec((2, count, rows, cols), lambda i, place, *_: (0, i, 0, place[0]))
            ]
            + [pl.BlockSpec((count, rows, cols), lambda i, *_: (i, 0, 0))] * 4
            + [moment] * 2,
            out_specs=[
                pl.BlockSpec((blocks, piece, 128), lambda i, *_: (0, 0, 0)),
                moment,
                moment,
            ],
        ),
        compiler_params=pltpu.CompilerParams(vmem_limit_bytes=10 * MIB),
    )(
        place,
        key,
        bounds,
        part.reshape(2, half, rows, width),
        *sums,
        in_hbm(first.reshape(halves.shape)),
        in_hbm(second.reshape(halves.shape)),
    )
    return out, first_next.reshape(first.shape), second_next.reshape(second.shape)


def finish_kernel(place, key, bounds, back, out):
    blocks, rows, cols = out.shape

    def step(block, carry):
        ok = inside(place, bounds, block, rows, cols)
        out[block] = jnp.where(ok, back[key[block]].astype(F32), 0.0).astype(BF16)
        return carry

    lax.fori_loop(0, blocks, step, 0, unroll=4)


def finish(place, key, bounds, back):
    whole = pl.BlockSpec(back.shape, lambda i, *_: (0, 0, 0))
    return pl.pallas_call(
        finish_kernel,
        out_shape=jax.ShapeDtypeStruct(back.shape, BF16),
        grid_spec=pltpu.PrefetchScalarGridSpec(
            num_scalar_prefetch=3, grid=(1,), in_specs=[whole], out_specs=whole
        ),
        compiler_params=pltpu.CompilerParams(vmem_limit_bytes=6 * MIB),
    )(place, key, bounds, back)


def precond_kernel(*refs):
    place, own_low, own_high, next_low, next_high, far_low, far_high, prev_low, prev_high = refs[:9]
    roots, lefts, (adam, out, norms, mixed) = refs[9:13], refs[13:20], refs[20:]
    width, quarter = out.shape
    half = width // 2
    me = place[0]
    n = width // quarter
    for top, parts in (
        (0, (own_low, next_low, far_low, prev_low)),
        (half, (own_high, next_high, far_high, prev_high)),
    ):
        for row in range(0, half, quarter):
            total = jnp.zeros((quarter, quarter), F32)
            for piece, root in zip(parts, roots):
                total += dot(piece[pl.ds(row, quarter), :], root[...], ((1,), (0,)))
            mixed[pl.ds(top + row, quarter), :] = total.astype(BF16)
    square = jnp.zeros((8, quarter), F32)
    eighth = quarter // 2
    places = ((0, 0), (1, 0), (1, eighth), (2, 0), (2, eighth), (3, 0), (3, eighth))
    for (step, extra), left in zip(places, lefts):
        base = lax.rem(me + step, n) * quarter + extra
        rows = left.shape[0]
        value = dot(left[...], mixed[...], ((1,), (0,)))
        out[pl.ds(pl.multiple_of(base, eighth), rows), :] = value
        square += jnp.sum((value * value).reshape(rows // 8, 8, quarter), axis=0)
    norms[...] = jnp.zeros_like(norms)
    norms[0:1, :] = jnp.broadcast_to(jnp.sum(square), (1, 128))
    norms[1:2, :] = jnp.broadcast_to(jnp.sum(adam[...].astype(F32)), (1, 128))


def precondition(place, pieces, roots, lefts, adam):
    rows, quarter = pieces[0].shape
    operands = (*pieces, *map(in_hbm, roots), *map(in_hbm, lefts), adam)
    return pl.pallas_call(
        precond_kernel,
        out_shape=(
            jax.ShapeDtypeStruct((2 * rows, quarter), F32),
            jax.ShapeDtypeStruct((8, 128), F32),
        ),
        in_specs=[pl.BlockSpec(memory_space=SMEM)]
        + [pl.BlockSpec(memory_space=VMEM)] * len(operands),
        out_specs=(pl.BlockSpec(memory_space=VMEM),) * 2,
        scratch_shapes=[VMEM((2 * rows, quarter), BF16)],
        compiler_params=pltpu.CompilerParams(vmem_limit_bytes=12 * MIB),
    )(place, *operands)


def graft_kernel(cells, precond, first, second, third, fourth, out):
    sums = first[...] + second[...] + third[...] + fourth[...]
    pre, adam = sums[0:1, :], sums[1:2, :]
    scale = -jnp.sqrt(adam / cells) / jnp.sqrt(pre / cells + NORM_EPS)
    width, quarter = out.shape
    scale = jnp.concatenate([scale] * (quarter // 128), axis=1)
    out[...] = (scale * precond[...]).astype(BF16)


def graft(precond, norms):
    width, quarter = precond.shape
    tiles = 4
    rows = width // tiles
    small = pl.BlockSpec((8, 128), lambda i: (0, 0))
    return pl.pallas_call(
        functools.partial(graft_kernel, float(width * width)),
        out_shape=jax.ShapeDtypeStruct((width, quarter), BF16),
        grid=(tiles,),
        in_specs=[pl.BlockSpec((rows, quarter), lambda i: (i, 0))] + [small] * 4,
        out_specs=pl.BlockSpec((rows, quarter), lambda i: (i, 0)),
        compiler_params=pltpu.CompilerParams(vmem_limit_bytes=6 * MIB),
    )(precond, *norms)


def on_device(
    grad_parts,
    assign,
    block_bounds,
    left_root,
    right_root,
    left_stat,
    right_stat,
    first_moment,
    second_moment,
):
    n_own = lax.axis_size("own")
    n_grp = lax.axis_size("grp")
    own_index = lax.axis_index("own")
    grp_index = lax.axis_index("grp")
    total_blocks = assign.shape[0]
    per_owner = total_blocks // n_own
    shard_rows = grad_parts.shape[2]
    width = grad_parts.shape[3]
    quarter = width // n_grp
    half = total_blocks // 2
    part = grad_parts[0]
    place = jnp.stack([grp_index, own_index]).astype(jnp.int32)
    starts = [((grp_index + step) & (n_grp - 1)) * quarter for step in range(4)]
    turn = ((n_grp - grp_index) & (n_grp - 1)) * quarter
    part, place, starts, turn = lax.optimization_barrier((part, place, starts, turn))

    def columns(array, step):
        return slice_at(array, starts[step], quarter, array.ndim - 1)

    far = columns(part, 2)
    far_up = shift(far[:half], 1)
    far_down = shift(far[half:], -1)
    left_bf, right_bf = left_root[0].astype(BF16), right_root[0].astype(BF16)
    left_low, left_high = left_bf[: quarter // 2], left_bf[quarter // 2 :]
    later, left_low, left_high, far_up, far_down = lax.optimization_barrier(
        (part, left_low, left_high, far_up, far_down)
    )
    up = columns(later, 1)
    down = columns(later, 3)
    up_direct = shift(up[half:], 1)
    down_direct = shift(down[:half], -1)
    up_sum = shift((up[:half].astype(F32) + far_up.astype(F32)).astype(BF16), 1)
    down_sum = shift((down[half:].astype(F32) + far_down.astype(F32)).astype(BF16), -1)
    left_prev_low = shift(left_low, 1)
    left_next_high = shift(left_high, -1)

    key = (assign % n_own * per_owner + assign // n_own).astype(jnp.int32)
    right_parts = [columns(right_bf, step) for step in range(4)]
    sums, left_prev_low, left_next_high, right_parts = lax.optimization_barrier(
        ((up_sum, up_direct, down_direct, down_sum), left_prev_low, left_next_high, right_parts)
    )

    sorted_grad, first_next, second_next = pack(
        place, key, block_bounds, part, sums, first_moment, second_moment
    )
    owned = lax.all_to_all(sorted_grad, "own", split_axis=0, concat_axis=0, tiled=True)
    left_far_low = shift(left_prev_low, 1)
    left_far_high = shift(left_next_high, -1)
    left_prev_high = shift(left_high, 1)
    left_next_low = shift(left_low, -1)
    roots = [right_parts[0]] + [shift(right_parts[step], step) for step in (3, 2, 1)]
    lefts = [
        left_bf,
        left_next_low,
        left_next_high,
        left_far_low,
        left_far_high,
        left_prev_low,
        left_prev_high,
    ]

    owned, lefts, roots = lax.optimization_barrier((owned, lefts, roots))
    own_cols = jnp.concatenate(
        [owned[:, :shard_rows], owned[:, shard_rows : 2 * shard_rows]], axis=2
    )
    adam = owned[:, 2 * shard_rows :].reshape(n_own * shard_rows // 2, 128)
    low, high = own_cols[:half], own_cols[half:]
    prev_low = shift(low, 1)
    next_high = shift(high, -1)
    prev_high = shift(high, 1)
    next_low = shift(low, -1)
    far_low = shift(prev_low, 1)
    far_high = shift(next_high, -1)
    pieces = [low, high, next_low, next_high, far_low, far_high, prev_low, prev_high]
    pieces = [piece.reshape(width // 2, quarter) for piece in pieces]

    precond, norms = precondition(place, pieces, roots, lefts, adam)
    norms = [norms] + [shift(norms, step) for step in (1, 2, 3)]
    grafted = graft(precond, norms).reshape(n_own, shard_rows, quarter)
    pieces, grafted = lax.optimization_barrier((pieces, grafted))
    back = lax.all_to_all(grafted, "own", split_axis=0, concat_axis=0, tiled=True)

    whole = jnp.concatenate([jnp.concatenate(pieces[i::2], axis=1) for i in (0, 1)], axis=0)
    rows = slice_at(whole, starts[0], quarter, 0)
    left_acc = STAT_DECAY * left_stat + dot(rows, whole, ((1,), (1,)))[None]
    cross = dot(whole[:, :quarter], whole, ((0,), (0,)))
    cross = jnp.concatenate([cross, cross], axis=1)
    cross = slice_at(cross, turn, width, 1)
    right_acc = STAT_DECAY * right_stat + cross[None]

    update = finish(place, key, block_bounds, back)
    return (update, first_next, second_next, left_acc, right_acc)


def solution(mesh):
    placed = (
        P("grp", None, "own", None),
        P(),
        P(),
        P("own", "grp", None),
        P("own", "grp", None),
        P("own", "grp", None),
        P("own", "grp", None),
        P(None, "own", "grp"),
        P(None, "own", "grp"),
    )
    return jax.shard_map(
        on_device,
        mesh=mesh,
        in_specs=placed,
        out_specs=(
            P(None, "own", "grp"),
            P(None, "own", "grp"),
            P(None, "own", "grp"),
            P("own", "grp", None),
            P("own", "grp", None),
        ),
        check_vma=False,
    )
```

time: 156 us -> 138 us (0.88)
  blocking collectives: 26.7 us -> 0 us
  local copies, waits for them, and re-layouts: 27.1 us -> 5.79 us
  waiting for transfers between devices: 32.8 us -> 45.4 us
  other arithmetic: 11.4 us -> 19.2 us
  Pallas kernels: 5.7 us -> 12.5 us
  starting transfers between devices: 47.6 us -> 51.5 us
    all_to_all x1 -> x0, blocking collectives: 26.7 us -> none  [on_device(): lax.all_to_all(shares, 'own', split_axis=0, concat_axis=0, tiled=True)]
    ppermute x22 -> x24, waiting for transfers between devices: 20.1 us -> 45 us  [shift(): return lax.ppermute(array, 'grp', [(i, (i + step) % n) for i in range(n)])]
    unnamed x77 -> x29, local copies, waits for them, and re-layouts: 19.6 us -> 1.37 us
    all_to_all x1, waiting for transfers between devices: 12.7 us -> 0.01 us  [on_device(): lax.all_to_all(grafted, 'own', split_axis=0, concat_axis=0, tiled=True)]
    concatenate x1 -> x2, other arithmetic: 0.31 us -> 12.9 us  [the longest x1 12.8 us: on_device(): jnp.concatenate([jnp.concatenate(pieces[i::2], axis=1) for i in (0, 1)],...]
    all_to_all x1, starting transfers between devices: 5.87 us -> 14 us  [on_device(): lax.all_to_all(grafted, 'own', split_axis=0, concat_axis=0, tiled=True)]
    pallas_call x2 -> x3, Pallas kernels: 4.26 us -> 11.1 us  [the longest x1 5.66 us: pack(): pl.pallas_call(pack_kernel, out_shape=(pltpu.HBM((blocks, piece, 128), BF...]
    reduce_sum x2 -> x0, other arithmetic: 4.43 us -> none  [the longest x1 4.32 us: on_device(): adam_sq = jnp.sum(adam * adam, axis=(1, 2))]
  transfers between devices with their start and end apart: 24 -> 26, of which waited for: 12 -> 18; matrix products, arithmetic and copies ran while one was open for 11% -> 17% of each run, Pallas kernels for 0% -> 0%
where the time goes in v3:
time: 138 us
  starting transfers between devices  51.5 us (37%)
  waiting for transfers between devices  45.4 us (33%)
  other arithmetic  19.2 us (14%)
  Pallas kernels  12.5 us (9%)
  local copies, waits for them, and re-layouts  5.79 us (4%)
  matrix products  2.47 us (2%)
    ppermute x24, waiting for transfers between devices, shift(): return lax.ppermute(array, 'grp', [(i, (i + step) % n) for i in range(n)])  45 us
    ppermute x24, starting transfers between devices, shift(): return lax.ppermute(array, 'grp', [(i, (i + step) % n) for i in range(n)])  23.2 us
    all_to_all x1, starting transfers between devices, on_device(): lax.all_to_all(sorted_grad, 'own', split_axis=0, concat_axis=0, tiled=True)  14.2 us
    all_to_all x1, starting transfers between devices, on_device(): lax.all_to_all(grafted, 'own', split_axis=0, concat_axis=0, tiled=True)  14 us
    concatenate x1, other arithmetic, on_device(): jnp.concatenate([jnp.concatenate(pieces[i::2], axis=1) for i in (0, 1)],...  12.8 us
    pallas_call x1, Pallas kernels, pack(): pl.pallas_call(pack_kernel, out_shape=(pltpu.HBM((blocks, piece, 128), BF...  5.66 us
    convert_element_type x3, other arithmetic, on_device(): left_bf, right_bf = (left_root[0].astype(BF16), right_root[0].astype(BF16))  3.64 us
    pallas_call x1, Pallas kernels, precondition(): pl.pallas_call(precond_kernel, out_shape=(jax.ShapeDtypeStruct((2 * rows,...  3.16 us
  transfers between devices with their start and end apart: 26, of which 18 were waited for; matrix products, arithmetic and copies ran while one was open for 17% of the time, Pallas kernels for 0%

profile of v3, /device:TPU:1, one launch (start us, length us, event | category | flops | bytes accessed | tf_op | source)
XLA Modules:
  0.0 137.6 jit_solution(11474770687850848469)
XLA Ops:
  0.7 1.5 %constant_dynamic-slice_fusion.3 = (bf16[32,16,256]{2,1,0:T(8,128)(2,1)S(1)}, bf16[32,16,256]{2,1,0:T(8,128)(2,1)S(1)}) fusion(bf16[64,16,1024]{2,1,0:T(8,128)(2,1)} %bitcast.43, s32[]{:T(128)S(6)} %add.41, s32[]{:T(128)S(6)} %mul.23), kind=kLoop, calls=%fused_computation.28 | loop fusion | bytes 1048584 | tf_op jit(solution)/shard_map/slice | solution.py:260
  2.2 3.6 %collective-permute-start.1 = (bf16[32,16,256]{2,1,0:T(8,128)(2,1)S(1)}, bf16[32,16,256]{2,1,0:T(8,128)(2,1)S(1)}, u32[]{:S(2)}, u32[]{:S(2)}) collective-permute-start(bf16[32,16,256]{2,1,0:T(8,128)(2,1)S(1)} %get-tuple-element.105), channel_id=1, source_target_pairs={{0,192},{64,0},{128,64},{192,128},{1,193},{65,1},{129,65},{193,129... | collective-permute-start | bytes 786440 | tf_op jit(solution)/shard_map/ppermute | solution.py:26
  8.1 2.7 %collective-permute-done.1 = bf16[32,16,256]{2,1,0:T(8,128)(2,1)S(1)} collective-permute-done((bf16[32,16,256]{2,1,0:T(8,128)(2,1)S(1)}, bf16[32,16,256]{2,1,0:T(8,128)(2,1)S(1)}, u32[]{:S(2)}, u32[]{:S(2)}) %collective-permute-start.1) | collective-permute-done | bytes 262176 | tf_op jit(solution)/shard_map/ppermute | solution.py:26
  10.8 3.1 %collective-permute-done = bf16[32,16,256]{2,1,0:T(8,128)(2,1)S(1)} collective-permute-done((bf16[32,16,256]{2,1,0:T(8,128)(2,1)S(1)}, bf16[32,16,256]{2,1,0:T(8,128)(2,1)S(1)}, u32[]{:S(2)}, u32[]{:S(2)}) %collective-permute-start) | collective-permute-done | bytes 262176 | tf_op jit(solution)/shard_map/ppermute | solution.py:26
  16.6 2.6 %collective-permute-start.7 = (bf16[128,1024]{1,0:T(8,128)(2,1)}, bf16[128,1024]{1,0:T(8,128)(2,1)}, u32[]{:S(2)}, u32[]{:S(2)}) collective-permute-start(bf16[128,1024]{1,0:T(8,128)(2,1)} %get-tuple-element.62), channel_id=1, source_target_pairs={{0,192},{64,0},{128,64},{192,128},{1,193},{65,1},{129,65},{193,129... | collective-permute-start | bytes 786440 | tf_op jit(solution)/shard_map/ppermute | solution.py:26
  22.9 5.5 %collective-permute-done.6.refs_18_ = bf16[128,1024]{1,0:T(8,128)(2,1)S(1)} collective-permute-done((bf16[128,1024]{1,0:T(8,128)(2,1)}, bf16[128,1024]{1,0:T(8,128)(2,1)S(1)}, u32[]{:S(2)}, u32[]{:S(2)}) %collective-permute-start.6) | collective-permute-done | bytes 262176 | tf_op jit(solution)/shard_map/ppermute | solution.py:26
  28.4 3.7 %collective-permute-done.4.down_direct = bf16[32,16,256]{2,1,0:T(8,128)(2,1)S(1)} collective-permute-done((bf16[32,16,256]{2,1,0:T(8,128)(2,1)}, bf16[32,16,256]{2,1,0:T(8,128)(2,1)S(1)}, u32[]{:S(2)}, u32[]{:S(2)}) %collective-permute-start.4) | collective-permute-done | bytes 262176 | tf_op jit(solution)/shard_map/ppermute | solution.py:26
  32.1 1.9 %collective-permute-done.3.up_direct = bf16[32,16,256]{2,1,0:T(8,128)(2,1)S(1)} collective-permute-done((bf16[32,16,256]{2,1,0:T(8,128)(2,1)}, bf16[32,16,256]{2,1,0:T(8,128)(2,1)S(1)}, u32[]{:S(2)}, u32[]{:S(2)}) %collective-permute-start.3) | collective-permute-done | bytes 262176 | tf_op jit(solution)/shard_map/ppermute | solution.py:26
  34.0 5.7 %shard_map.128 = (bf16[64,40,128]{2,1,0:T(8,128)(2,1)}, f32[2,32,16,256]{3,2,1,0:T(8,128)}, f32[2,32,16,256]{3,2,1,0:T(8,128)}) custom-call(s32[2]{0:T(128)S(1)} %pad_add_fusion.place.refs_0_, s32[64]{0:T(128)S(1)} %fusion.9.key, s32[64,4]{1,0:T(8,128)S(1)} %copy.15.bounds, bf16[2,32,16,1024]{3,2,1,0:T(8,128)(2,1)S(1)} %bitcast.46, ...), custom_call_target="tpu_custom_call" | custom-call | tf_op jit(solution)/shard_map/pallas_call | solution.py:104
  39.7 14.2 %all-to-all-start = ((bf16[64,40,128]{2,1,0:T(8,128)(2,1)}), bf16[64,40,128]{2,1,0:T(8,128)(2,1)S(1)}, u32[]{:S(2)}, u32[]{:S(2)}) async-start(bf16[64,40,128]{2,1,0:T(8,128)(2,1)} %get-tuple-element.68), calls=%async_computation | async-start | bytes 1310720 | tf_op jit(solution)/shard_map/all_to_all | solution.py:284
  54.0 1.5 %collective-permute-start.11 = (bf16[128,1024]{1,0:T(8,128)(2,1)}, bf16[128,1024]{1,0:T(8,128)(2,1)S(1)}, u32[]{:S(2)}, u32[]{:S(2)}) collective-permute-start(bf16[128,1024]{1,0:T(8,128)(2,1)} %get-tuple-element.62), channel_id=1, source_target_pairs={{0,64},{64,128},{128,192},{192,0},{1,65},{65,129},{129,193},{193,1... | collective-permute-start | bytes 786440 | tf_op jit(solution)/shard_map/ppermute | solution.py:26
  57.3 4.3 %collective-permute-done.8.refs_14_ = bf16[128,1024]{1,0:T(8,128)(2,1)S(1)} collective-permute-done((bf16[128,1024]{1,0:T(8,128)(2,1)}, bf16[128,1024]{1,0:T(8,128)(2,1)S(1)}, u32[]{:S(2)}, u32[]{:S(2)}) %collective-permute-start.8) | collective-permute-done | bytes 262176 | tf_op jit(solution)/shard_map/ppermute | solution.py:26
  61.6 1.5 %collective-permute-start.10 = (bf16[128,1024]{1,0:T(8,128)(2,1)}, bf16[128,1024]{1,0:T(8,128)(2,1)S(1)}, u32[]{:S(2)}, u32[]{:S(2)}) collective-permute-start(bf16[128,1024]{1,0:T(8,128)(2,1)} %collective-permute-done.7.refs_15_), channel_id=1, source_target_pairs={{0,192},{64,0},{128,64},{192,128},{1,193},{65,1},{129,65},{193,129... | collective-permute-start | bytes 786440 | tf_op jit(solution)/shard_map/ppermute | solution.py:26
  63.2 1.5 %collective-permute-done.11.refs_19_ = bf16[128,1024]{1,0:T(8,128)(2,1)S(1)} collective-permute-done((bf16[128,1024]{1,0:T(8,128)(2,1)}, bf16[128,1024]{1,0:T(8,128)(2,1)S(1)}, u32[]{:S(2)}, u32[]{:S(2)}) %collective-permute-start.11) | collective-permute-done | bytes 262176 | tf_op jit(solution)/shard_map/ppermute | solution.py:26
  64.7 2.2 %convert_bitcast_fusion.refs_13_ = bf16[256,1024]{1,0:T(8,128)(2,1)} fusion(f32[1,256,1024]{2,1,0:T(8,128)} %param.12), kind=kLoop, calls=%fused_computation.37 | loop fusion | flops 262144 | bytes 1572864 | tf_op jit(solution)/shard_map/convert_element_type | solution.py:261
  66.9 1.7 %collective-permute-done.14.refs_12_ = bf16[256,256]{1,0:T(8,128)(2,1)S(1)} collective-permute-done((bf16[256,256]{1,0:T(8,128)(2,1)}, bf16[256,256]{1,0:T(8,128)(2,1)S(1)}, u32[]{:S(2)}, u32[]{:S(2)}) %collective-permute-start.14) | collective-permute-done | bytes 131104 | tf_op jit(solution)/shard_map/ppermute | solution.py:26
  68.5 4.4 %collective-permute-done.10.refs_17_ = bf16[128,1024]{1,0:T(8,128)(2,1)S(1)} collective-permute-done((bf16[128,1024]{1,0:T(8,128)(2,1)}, bf16[128,1024]{1,0:T(8,128)(2,1)S(1)}, u32[]{:S(2)}, u32[]{:S(2)}) %collective-permute-start.10) | collective-permute-done | bytes 262176 | tf_op jit(solution)/shard_map/ppermute | solution.py:26
  74.2 1.5 %collective-permute-start.16 = (bf16[32,16,256]{2,1,0:T(8,128)(2,1)S(1)}, bf16[32,16,256]{2,1,0:T(8,128)(2,1)S(1)}, u32[]{:S(2)}, u32[]{:S(2)}) collective-permute-start(bf16[32,16,256]{2,1,0:T(8,128)(2,1)S(1)} %get-tuple-element.109), channel_id=1, source_target_pairs={{0,192},{64,0},{128,64},{192,128},{1,193},{65,1},{129,65},{193,129... | collective-permute-start | bytes 786440 | tf_op jit(solution)/shard_map/ppermute | solution.py:26
  76.4 2.0 %collective-permute-start.15 = (bf16[32,16,256]{2,1,0:T(8,128)(2,1)S(1)}, bf16[32,16,256]{2,1,0:T(8,128)(2,1)S(1)}, u32[]{:S(2)}, u32[]{:S(2)}) collective-permute-start(bf16[32,16,256]{2,1,0:T(8,128)(2,1)S(1)} %get-tuple-element.110), channel_id=1, source_target_pairs={{0,192},{64,0},{128,64},{192,128},{1,193},{65,1},{129,65},{193,129... | collective-permute-start | bytes 786440 | tf_op jit(solution)/shard_map/ppermute | solution.py:26
  78.4 1.6 %collective-permute-done.16 = bf16[32,16,256]{2,1,0:T(8,128)(2,1)S(1)} collective-permute-done((bf16[32,16,256]{2,1,0:T(8,128)(2,1)S(1)}, bf16[32,16,256]{2,1,0:T(8,128)(2,1)S(1)}, u32[]{:S(2)}, u32[]{:S(2)}) %collective-permute-start.16) | collective-permute-done | bytes 262176 | tf_op jit(solution)/shard_map/ppermute | solution.py:26
  80.0 3.4 %collective-permute-start.19 = (bf16[32,16,256]{2,1,0:T(8,128)(2,1)S(1)}, bf16[32,16,256]{2,1,0:T(8,128)(2,1)S(1)}, u32[]{:S(2)}, u32[]{:S(2)}) collective-permute-start(bf16[32,16,256]{2,1,0:T(8,128)(2,1)S(1)} %collective-permute-done.16), channel_id=1, source_target_pairs={{0,192},{64,0},{128,64},{192,128},{1,193},{65,1},{129,65},{193,129... | collective-permute-start | bytes 786440 | tf_op jit(solution)/shard_map/ppermute | solution.py:26
  83.4 5.3 %collective-permute-done.20 = bf16[32,16,256]{2,1,0:T(8,128)(2,1)S(1)} collective-permute-done((bf16[32,16,256]{2,1,0:T(8,128)(2,1)S(1)}, bf16[32,16,256]{2,1,0:T(8,128)(2,1)S(1)}, u32[]{:S(2)}, u32[]{:S(2)}) %collective-permute-start.20) | collective-permute-done | bytes 262176 | tf_op jit(solution)/shard_map/ppermute | solution.py:26
  88.8 2.5 %collective-permute-done.19 = bf16[32,16,256]{2,1,0:T(8,128)(2,1)S(1)} collective-permute-done((bf16[32,16,256]{2,1,0:T(8,128)(2,1)S(1)}, bf16[32,16,256]{2,1,0:T(8,128)(2,1)S(1)}, u32[]{:S(2)}, u32[]{:S(2)}) %collective-permute-start.19) | collective-permute-done | bytes 262176 | tf_op jit(solution)/shard_map/ppermute | solution.py:26
  91.2 3.1 %collective-permute-done.18 = bf16[32,16,256]{2,1,0:T(8,128)(2,1)S(1)} collective-permute-done((bf16[32,16,256]{2,1,0:T(8,128)(2,1)S(1)}, bf16[32,16,256]{2,1,0:T(8,128)(2,1)S(1)}, u32[]{:S(2)}, u32[]{:S(2)}) %collective-permute-start.18) | collective-permute-done | bytes 262176 | tf_op jit(solution)/shard_map/ppermute | solution.py:26
  94.4 3.2 %shard_map.129 = (f32[1024,256]{1,0:T(8,128)S(1)}, f32[8,128]{1,0:T(8,128)S(1)}) custom-call(s32[2]{0:T(128)S(1)} %pad_add_fusion.place.refs_0_, bf16[512,256]{1,0:T(8,128)(2,1)S(1)} %bitcast.49, bf16[512,256]{1,0:T(8,128)(2,1)S(1)} %bitcast.47, bf16[512,256]{1,0:T(8,128)(2,1)S(1)} %bitcast.57, bf16[512,256]{1,0:T(8,128)(2,1)S(1)} %bitcast.51, ...), custom_call_target="tpu_custom_call" | custom-call | tf_op jit(solution)/shard_map/pallas_call | solution.py:190
  100.1 1.8 %collective-permute-done.22.third = f32[8,128]{1,0:T(8,128)S(1)} collective-permute-done((f32[8,128]{1,0:T(8,128)S(1)}, f32[8,128]{1,0:T(8,128)S(1)}, u32[]{:S(2)}, u32[]{:S(2)}) %collective-permute-start.22) | collective-permute-done | bytes 4128 | tf_op jit(solution)/shard_map/ppermute | solution.py:26
  102.5 1.4 %shard_map.130 = bf16[1024,256]{1,0:T(8,128)(2,1)} custom-call(f32[1024,256]{1,0:T(8,128)S(1)} %get-tuple-element.87.precond, f32[8,128]{1,0:T(8,128)S(1)} %get-tuple-element.88.first, f32[8,128]{1,0:T(8,128)S(1)} %collective-permute-done.21.second, f32[8,128]{1,0:T(8,128)S(1)} %collective-permute-done.22.third, f32[8,128]{1,0:T(8,128)S(1)} %collective-permute-done.23.fourth), custom_call_target="tpu_custom_call" | custom-call | tf_op jit(solution)/shard_map/pallas_call | solution.py:218
  103.9 14.0 %all-to-all-start.1 = ((bf16[64,16,256]{2,1,0:T(8,128)(2,1)}), bf16[64,16,256]{2,1,0:T(8,128)(2,1)S(1)}, u32[]{:S(2)}, u32[]{:S(2)}) async-start(bf16[64,16,256]{2,1,0:T(8,128)(2,1)} %bitcast.22), calls=%async_computation.1 | async-start | bytes 1048576 | tf_op jit(solution)/shard_map/all_to_all | solution.py:319
  118.0 12.8 %maximum_maximum_fusion = bf16[1024,1024]{1,0:T(8,128)(2,1)S(1)} fusion(bf16[512,256]{1,0:T(8,128)(2,1)S(1)} %bitcast.56, bf16[512,256]{1,0:T(8,128)(2,1)S(1)} %bitcast.60, bf16[512,256]{1,0:T(8,128)(2,1)S(1)} %bitcast.52, bf16[512,256]{1,0:T(8,128)(2,1)S(1)} %bitcast.48, bf16[512,256]{1,0:T(8,128)(2,1)S(1)} %bitcast.54, bf16[512,256]{1,0:T(8,128)(2,1)S(1)} %bitcast.62, ...), kind=kLoop, calls=%fused_computation | loop fusion | flops 16777216 | bytes 4194304 | tf_op jit(solution)/shard_map/concatenate | solution.py:321
  132.0 1.6 %fusion.3 = f32[1,256,1024]{2,1,0:T(8,128)} fusion(s32[]{:T(128)S(6)} %mul.25, f32[256,1024]{1,0:T(8,128)S(1)} %fusion.4, f32[1,256,1024]{2,1,0:T(8,128)S(1)} %copy-done.3), kind=kLoop, calls=%fused_computation.7 | loop fusion | flops 786432 | bytes 3145732 | tf_op jit(solution)/shard_map/add | solution.py:327
  133.6 1.7 %fusion = f32[1,256,1024]{2,1,0:T(8,128)} fusion(bf16[1024,1024]{1,0:T(8,128)(2,1)S(1)} %maximum_maximum_fusion, f32[1,256,1024]{2,1,0:T(8,128)S(1)} %copy-done.1, s32[]{:T(128)S(6)} %mul.21), kind=kOutput, calls=%fused_computation.4 | convolution fusion | flops 537395200 | bytes 4718596 | tf_op jit(solution)/shard_map/dot_general | solution.py:40
  135.3 2.3 %shard_map.131 = bf16[64,16,256]{2,1,0:T(8,128)(2,1)} custom-call(s32[2]{0:T(128)S(1)} %pad_add_fusion.place.refs_0_, s32[64]{0:T(128)S(1)} %fusion.9.key, s32[64,4]{1,0:T(8,128)S(1)} %copy.15.bounds, bf16[64,16,256]{2,1,0:T(8,128)(2,1)S(1)} %all-to-all-done.1.back), custom_call_target="tpu_custom_call" | custom-call | tf_op jit(solution)/shard_map/pallas_call | solution.py:147
  (70 shorter events, 17.0 us)
Async XLA Ops:
  0.6 13.3 %copy-start = (bf16[1,64,16,1024]{3,2,1,0:T(8,128)(2,1)S(1)}, bf16[1,64,16,1024]{3,2,1,0:T(8,128)(2,1)}, u32[]{:S(2)}) copy-start(bf16[1,64,16,1024]{3,2,1,0:T(8,128)(2,1)} %param.9) | copy-start | bytes 6291460
  2.2 8.6 %collective-permute-start.1 = (bf16[32,16,256]{2,1,0:T(8,128)(2,1)S(1)}, bf16[32,16,256]{2,1,0:T(8,128)(2,1)S(1)}, u32[]{:S(2)}, u32[]{:S(2)}) collective-permute-start(bf16[32,16,256]{2,1,0:T(8,128)(2,1)S(1)} %get-tuple-element.105), channel_id=1, source_target_pairs={{0,192},{64,0},{128,64},{192,128},{1,193},{65,1},{129,65},{193,129... | collective-permute-start | bytes 786440 | tf_op jit(solution)/shard_map/ppermute | solution.py:26
  5.8 9.4 %copy-start.2 = (f32[1,256,1024]{2,1,0:T(8,128)S(1)}, f32[1,256,1024]{2,1,0:T(8,128)}, u32[]{:S(2)}) copy-start(f32[1,256,1024]{2,1,0:T(8,128)} %param.13) | copy-start | bytes 3145732
  5.9 8.1 %collective-permute-start = (bf16[32,16,256]{2,1,0:T(8,128)(2,1)S(1)}, bf16[32,16,256]{2,1,0:T(8,128)(2,1)S(1)}, u32[]{:S(2)}, u32[]{:S(2)}) collective-permute-start(bf16[32,16,256]{2,1,0:T(8,128)(2,1)S(1)} %get-tuple-element.106), channel_id=1, source_target_pairs={{0,64},{64,128},{128,192},{192,0},{1,65},{65,129},{129,193},{193,1... | collective-permute-start | bytes 786440 | tf_op jit(solution)/shard_map/ppermute | solution.py:26
  14.9 5.9 %collective-permute-start.5 = (bf16[32,16,256]{2,1,0:T(8,128)(2,1)S(1)}, bf16[32,16,256]{2,1,0:T(8,128)(2,1)S(1)}, u32[]{:S(2)}, u32[]{:S(2)}) collective-permute-start(bf16[32,16,256]{2,1,0:T(8,128)(2,1)S(1)} %get-tuple-element.101), channel_id=1, source_target_pairs={{0,192},{64,0},{128,64},{192,128},{1,193},{65,1},{129,65},{193,129... | collective-permute-start | bytes 786440 | tf_op jit(solution)/shard_map/ppermute | solution.py:26
  15.3 7.6 %collective-permute-start.2 = (bf16[32,16,256]{2,1,0:T(8,128)(2,1)}, bf16[32,16,256]{2,1,0:T(8,128)(2,1)S(1)}, u32[]{:S(2)}, u32[]{:S(2)}) collective-permute-start(bf16[32,16,256]{2,1,0:T(8,128)(2,1)} %get-tuple-element.102), channel_id=1, source_target_pairs={{0,64},{64,128},{128,192},{192,0},{1,65},{65,129},{129,193},{193,1... | collective-permute-start | bytes 786440 | tf_op jit(solution)/shard_map/ppermute | solution.py:26
  16.5 11.9 %collective-permute-start.6 = (bf16[128,1024]{1,0:T(8,128)(2,1)}, bf16[128,1024]{1,0:T(8,128)(2,1)S(1)}, u32[]{:S(2)}, u32[]{:S(2)}) collective-permute-start(bf16[128,1024]{1,0:T(8,128)(2,1)} %get-tuple-element.61), channel_id=1, source_target_pairs={{0,64},{64,128},{128,192},{192,0},{1,65},{65,129},{129,193},{193,1... | collective-permute-start | bytes 786440 | tf_op jit(solution)/shard_map/ppermute | solution.py:26
  16.6 11.8 %collective-permute-start.7 = (bf16[128,1024]{1,0:T(8,128)(2,1)}, bf16[128,1024]{1,0:T(8,128)(2,1)}, u32[]{:S(2)}, u32[]{:S(2)}) collective-permute-start(bf16[128,1024]{1,0:T(8,128)(2,1)} %get-tuple-element.62), channel_id=1, source_target_pairs={{0,192},{64,0},{128,64},{192,128},{1,193},{65,1},{129,65},{193,129... | collective-permute-start | bytes 786440 | tf_op jit(solution)/shard_map/ppermute | solution.py:26
  20.2 11.8 %collective-permute-start.4 = (bf16[32,16,256]{2,1,0:T(8,128)(2,1)}, bf16[32,16,256]{2,1,0:T(8,128)(2,1)S(1)}, u32[]{:S(2)}, u32[]{:S(2)}) collective-permute-start(bf16[32,16,256]{2,1,0:T(8,128)(2,1)} %get-tuple-element.103), channel_id=1, source_target_pairs={{0,192},{64,0},{128,64},{192,128},{1,193},{65,1},{129,65},{193,129... | collective-permute-start | bytes 786440 | tf_op jit(solution)/shard_map/ppermute | solution.py:26
  20.8 13.2 %collective-permute-start.3 = (bf16[32,16,256]{2,1,0:T(8,128)(2,1)}, bf16[32,16,256]{2,1,0:T(8,128)(2,1)S(1)}, u32[]{:S(2)}, u32[]{:S(2)}) collective-permute-start(bf16[32,16,256]{2,1,0:T(8,128)(2,1)} %get-tuple-element.104), channel_id=1, source_target_pairs={{0,64},{64,128},{128,192},{192,0},{1,65},{65,129},{129,193},{193,1... | collective-permute-start | bytes 786440 | tf_op jit(solution)/shard_map/ppermute | solution.py:26
  28.4 36.2 %copy-start.4 = (bf16[128,1024]{1,0:T(8,128)(2,1)}, bf16[128,1024]{1,0:T(8,128)(2,1)S(1)}, u32[]{:S(2)}) copy-start(bf16[128,1024]{1,0:T(8,128)(2,1)S(1)} %collective-permute-done.6.refs_18_) | copy-start | bytes 786436
  39.7 34.4 %all-to-all-start = ((bf16[64,40,128]{2,1,0:T(8,128)(2,1)}), bf16[64,40,128]{2,1,0:T(8,128)(2,1)S(1)}, u32[]{:S(2)}, u32[]{:S(2)}) async-start(bf16[64,40,128]{2,1,0:T(8,128)(2,1)} %get-tuple-element.68), calls=%async_computation | async-start | bytes 1310720 | tf_op jit(solution)/shard_map/all_to_all | solution.py:284
  53.9 7.7 %collective-permute-start.8 = (bf16[128,1024]{1,0:T(8,128)(2,1)}, bf16[128,1024]{1,0:T(8,128)(2,1)S(1)}, u32[]{:S(2)}, u32[]{:S(2)}) collective-permute-start(bf16[128,1024]{1,0:T(8,128)(2,1)} %get-tuple-element.61), channel_id=1, source_target_pairs={{0,192},{64,0},{128,64},{192,128},{1,193},{65,1},{129,65},{193,129... | collective-permute-start | bytes 786440 | tf_op jit(solution)/shard_map/ppermute | solution.py:26
  54.0 10.6 %collective-permute-start.11 = (bf16[128,1024]{1,0:T(8,128)(2,1)}, bf16[128,1024]{1,0:T(8,128)(2,1)S(1)}, u32[]{:S(2)}, u32[]{:S(2)}) collective-permute-start(bf16[128,1024]{1,0:T(8,128)(2,1)} %get-tuple-element.62), channel_id=1, source_target_pairs={{0,64},{64,128},{128,192},{192,0},{1,65},{65,129},{129,193},{193,1... | collective-permute-start | bytes 786440 | tf_op jit(solution)/shard_map/ppermute | solution.py:26
  55.5 11.4 %collective-permute-start.12 = (bf16[256,256]{1,0:T(8,128)(2,1)}, bf16[256,256]{1,0:T(8,128)(2,1)S(1)}, u32[]{:S(2)}, u32[]{:S(2)}) collective-permute-start(bf16[256,256]{1,0:T(8,128)(2,1)} %get-tuple-element.72), channel_id=1, source_target_pairs={{0,192},{64,0},{128,64},{192,128},{1,193},{65,1},{129,65},{193,129... | collective-permute-start | bytes 393224 | tf_op jit(solution)/shard_map/ppermute | solution.py:26
  56.8 10.1 %collective-permute-start.13 = (bf16[256,256]{1,0:T(8,128)(2,1)}, bf16[256,256]{1,0:T(8,128)(2,1)S(1)}, u32[]{:S(2)}, u32[]{:S(2)}) collective-permute-start(bf16[256,256]{1,0:T(8,128)(2,1)} %get-tuple-element.73), channel_id=1, source_target_pairs={{0,128},{64,192},{128,0},{192,64},{1,129},{65,193},{129,1},{193,65... | collective-permute-start | bytes 393224 | tf_op jit(solution)/shard_map/ppermute | solution.py:26
  57.2 11.3 %collective-permute-start.14 = (bf16[256,256]{1,0:T(8,128)(2,1)}, bf16[256,256]{1,0:T(8,128)(2,1)S(1)}, u32[]{:S(2)}, u32[]{:S(2)}) collective-permute-start(bf16[256,256]{1,0:T(8,128)(2,1)} %get-tuple-element.74), channel_id=1, source_target_pairs={{0,64},{64,128},{128,192},{192,0},{1,65},{65,129},{129,193},{193,1... | collective-permute-start | bytes 393224 | tf_op jit(solution)/shard_map/ppermute | solution.py:26
  61.6 32.7 %copy-start.5 = (bf16[128,1024]{1,0:T(8,128)(2,1)}, bf16[128,1024]{1,0:T(8,128)(2,1)S(1)}, u32[]{:S(2)}) copy-start(bf16[128,1024]{1,0:T(8,128)(2,1)S(1)} %collective-permute-done.8.refs_14_) | copy-start | bytes 786436
  61.6 11.3 %collective-permute-start.10 = (bf16[128,1024]{1,0:T(8,128)(2,1)}, bf16[128,1024]{1,0:T(8,128)(2,1)S(1)}, u32[]{:S(2)}, u32[]{:S(2)}) collective-permute-start(bf16[128,1024]{1,0:T(8,128)(2,1)} %collective-permute-done.7.refs_15_), channel_id=1, source_target_pairs={{0,192},{64,0},{128,64},{192,128},{1,193},{65,1},{129,65},{193,129... | collective-permute-start | bytes 786440 | tf_op jit(solution)/shard_map/ppermute | solution.py:26
  64.6 9.4 %copy-start.6 = (bf16[128,1024]{1,0:T(8,128)(2,1)}, bf16[128,1024]{1,0:T(8,128)(2,1)S(1)}, u32[]{:S(2)}) copy-start(bf16[128,1024]{1,0:T(8,128)(2,1)S(1)} %collective-permute-done.11.refs_19_) | copy-start | bytes 786436
  64.6 8.3 %collective-permute-start.9 = (bf16[128,1024]{1,0:T(8,128)(2,1)S(1)}, bf16[128,1024]{1,0:T(8,128)(2,1)S(1)}, u32[]{:S(2)}, u32[]{:S(2)}) collective-permute-start(bf16[128,1024]{1,0:T(8,128)(2,1)S(1)} %collective-permute-done.6.refs_18_), channel_id=1, source_target_pairs={{0,64},{64,128},{128,192},{192,0},{1,65},{65,129},{129,193},{193,1... | collective-permute-start | bytes 786440 | tf_op jit(solution)/shard_map/ppermute | solution.py:26
  66.8 27.5 %copy-start.9 = (bf16[256,256]{1,0:T(8,128)(2,1)}, bf16[256,256]{1,0:T(8,128)(2,1)S(1)}, u32[]{:S(2)}) copy-start(bf16[256,256]{1,0:T(8,128)(2,1)S(1)} %collective-permute-done.12.refs_10_) | copy-start | bytes 393220
  74.2 5.8 %collective-permute-start.16 = (bf16[32,16,256]{2,1,0:T(8,128)(2,1)S(1)}, bf16[32,16,256]{2,1,0:T(8,128)(2,1)S(1)}, u32[]{:S(2)}, u32[]{:S(2)}) collective-permute-start(bf16[32,16,256]{2,1,0:T(8,128)(2,1)S(1)} %get-tuple-element.109), channel_id=1, source_target_pairs={{0,192},{64,0},{128,64},{192,128},{1,193},{65,1},{129,65},{193,129... | collective-permute-start | bytes 786440 | tf_op jit(solution)/shard_map/ppermute | solution.py:26
  75.6 7.8 %collective-permute-start.17 = (bf16[32,16,256]{2,1,0:T(8,128)(2,1)S(1)}, bf16[32,16,256]{2,1,0:T(8,128)(2,1)S(1)}, u32[]{:S(2)}, u32[]{:S(2)}) collective-permute-start(bf16[32,16,256]{2,1,0:T(8,128)(2,1)S(1)} %get-tuple-element.110), channel_id=1, source_target_pairs={{0,64},{64,128},{128,192},{192,0},{1,65},{65,129},{129,193},{193,1... | collective-permute-start | bytes 786440 | tf_op jit(solution)/shard_map/ppermute | solution.py:26
  75.7 13.0 %collective-permute-start.20 = (bf16[32,16,256]{2,1,0:T(8,128)(2,1)S(1)}, bf16[32,16,256]{2,1,0:T(8,128)(2,1)S(1)}, u32[]{:S(2)}, u32[]{:S(2)}) collective-permute-start(bf16[32,16,256]{2,1,0:T(8,128)(2,1)S(1)} %get-tuple-element.109), channel_id=1, source_target_pairs={{0,64},{64,128},{128,192},{192,0},{1,65},{65,129},{129,193},{193,1... | collective-permute-start | bytes 786440 | tf_op jit(solution)/shard_map/ppermute | solution.py:26
  76.4 12.4 %collective-permute-start.15 = (bf16[32,16,256]{2,1,0:T(8,128)(2,1)S(1)}, bf16[32,16,256]{2,1,0:T(8,128)(2,1)S(1)}, u32[]{:S(2)}, u32[]{:S(2)}) collective-permute-start(bf16[32,16,256]{2,1,0:T(8,128)(2,1)S(1)} %get-tuple-element.110), channel_id=1, source_target_pairs={{0,192},{64,0},{128,64},{192,128},{1,193},{65,1},{129,65},{193,129... | collective-permute-start | bytes 786440 | tf_op jit(solution)/shard_map/ppermute | solution.py:26
  80.0 11.2 %collective-permute-start.19 = (bf16[32,16,256]{2,1,0:T(8,128)(2,1)S(1)}, bf16[32,16,256]{2,1,0:T(8,128)(2,1)S(1)}, u32[]{:S(2)}, u32[]{:S(2)}) collective-permute-start(bf16[32,16,256]{2,1,0:T(8,128)(2,1)S(1)} %collective-permute-done.16), channel_id=1, source_target_pairs={{0,192},{64,0},{128,64},{192,128},{1,193},{65,1},{129,65},{193,129... | collective-permute-start | bytes 786440 | tf_op jit(solution)/shard_map/ppermute | solution.py:26
  83.4 11.0 %collective-permute-start.18 = (bf16[32,16,256]{2,1,0:T(8,128)(2,1)S(1)}, bf16[32,16,256]{2,1,0:T(8,128)(2,1)S(1)}, u32[]{:S(2)}, u32[]{:S(2)}) collective-permute-start(bf16[32,16,256]{2,1,0:T(8,128)(2,1)S(1)} %collective-permute-done.17), channel_id=1, source_target_pairs={{0,64},{64,128},{128,192},{192,0},{1,65},{65,129},{129,193},{193,1... | collective-permute-start | bytes 786440 | tf_op jit(solution)/shard_map/ppermute | solution.py:26
  97.5 2.5 %collective-permute-start.23 = (f32[8,128]{1,0:T(8,128)S(1)}, f32[8,128]{1,0:T(8,128)S(1)}, u32[]{:S(2)}, u32[]{:S(2)}) collective-permute-start(f32[8,128]{1,0:T(8,128)S(1)} %get-tuple-element.88.first), channel_id=1, source_target_pairs={{0,192},{64,0},{128,64},{192,128},{1,193},{65,1},{129,65},{193,129... | collective-permute-start | bytes 12296 | tf_op jit(solution)/shard_map/ppermute | solution.py:26
  97.9 4.0 %collective-permute-start.22 = (f32[8,128]{1,0:T(8,128)S(1)}, f32[8,128]{1,0:T(8,128)S(1)}, u32[]{:S(2)}, u32[]{:S(2)}) collective-permute-start(f32[8,128]{1,0:T(8,128)S(1)} %get-tuple-element.88.first), channel_id=1, source_target_pairs={{0,128},{64,192},{128,0},{192,64},{1,129},{65,193},{129,1},{193,65... | collective-permute-start | bytes 12296 | tf_op jit(solution)/shard_map/ppermute | solution.py:26
  97.9 4.6 %collective-permute-start.21 = (f32[8,128]{1,0:T(8,128)S(1)}, f32[8,128]{1,0:T(8,128)S(1)}, u32[]{:S(2)}, u32[]{:S(2)}) collective-permute-start(f32[8,128]{1,0:T(8,128)S(1)} %get-tuple-element.88.first), channel_id=1, source_target_pairs={{0,64},{64,128},{128,192},{192,0},{1,65},{65,129},{129,193},{193,1... | collective-permute-start | bytes 12296 | tf_op jit(solution)/shard_map/ppermute | solution.py:26
  103.9 31.4 %all-to-all-start.1 = ((bf16[64,16,256]{2,1,0:T(8,128)(2,1)}), bf16[64,16,256]{2,1,0:T(8,128)(2,1)S(1)}, u32[]{:S(2)}, u32[]{:S(2)}) async-start(bf16[64,16,256]{2,1,0:T(8,128)(2,1)} %bitcast.22), calls=%async_computation.1 | async-start | bytes 1048576 | tf_op jit(solution)/shard_map/all_to_all | solution.py:319
  (8 other events, 31.0 us)

commit v4 on v3

v4 whole, which is shorter than its diff:
```python
import functools

import jax
import jax.numpy as jnp
from jax import lax
from jax.experimental import pallas as pl
from jax.experimental.pallas import tpu as pltpu
from jax.sharding import PartitionSpec as P

BETA_FIRST = 0.9
BETA_SECOND = 0.95
BIAS_FIRST = 1.0 - 0.9**10
BIAS_SECOND = 1.0 - 0.95**10
ADAM_EPS = 1e-08
STAT_DECAY = 0.95
NORM_EPS = 1e-06
F32 = jnp.float32
BF16 = jnp.bfloat16
MIB = 1024 * 1024
VMEM = pltpu.VMEM
LONG = pl.CostEstimate(flops=2 * 10**11, bytes_accessed=10**9, transcendentals=0)


def shift(array, step):
    n = lax.axis_size("grp")
    return lax.ppermute(array, "grp", [(i, (i + step) % n) for i in range(n)])


def slots_of(assign, n_own, per_owner):
    return (assign % n_own * per_owner + assign // n_own).astype(jnp.int32)


def in_hbm(array):
    return pltpu.with_memory_space_constraint(array, pltpu.HBM)


def slice_at(array, start, size, axis):
    starts = [start if i == axis else 0 for i in range(array.ndim)]
    sizes = [size if i == axis else n for i, n in enumerate(array.shape)]
    return lax.dynamic_slice(array, starts, sizes, allow_negative_indices=False)


def dot(a, b, dims):
    return lax.dot_general(a, b, (dims, ((), ())), preferred_element_type=F32)


def inside(bounds, block, rows, cols):
    row = lax.broadcasted_iota(jnp.int32, (rows, cols), 0) + lax.axis_index("own") * rows
    col = lax.broadcasted_iota(jnp.int32, (rows, cols), 1) + lax.axis_index("grp") * cols
    row_off, col_off, n_rows, n_cols = [bounds[4 * block + i] for i in range(4)]
    return (row < n_rows - row_off) & (col < n_cols - col_off)


def gather_kernel(place, own, up_direct, down_direct, out):
    half = own.shape[1]

    def step(i, carry):
        out[0, i] = own[0, i].astype(F32) + down_direct[i].astype(F32)
        out[1, i] = own[1, i].astype(F32) + up_direct[i].astype(F32)
        return carry

    lax.fori_loop(0, half, step, 0, unroll=4)


def gather(place, part, up_direct, down_direct):
    blocks, rows, width = part.shape
    half, cols = blocks // 2, up_direct.shape[2]
    whole = pl.BlockSpec(up_direct.shape, lambda i, *_: (0, 0, 0))
    return pl.pallas_call(
        gather_kernel,
        out_shape=jax.ShapeDtypeStruct((2, half, rows, cols), F32),
        grid_spec=pltpu.PrefetchScalarGridSpec(
            num_scalar_prefetch=1,
            grid=(1,),
            in_specs=[
                pl.BlockSpec((2, half, rows, cols), lambda i, place: (0, 0, 0, place[0])),
                whole,
                whole,
            ],
            out_specs=pl.BlockSpec((2, half, rows, cols), lambda i, *_: (0, 0, 0, 0)),
        ),
        compiler_params=pltpu.CompilerParams(vmem_limit_bytes=8 * MIB),
        cost_estimate=LONG,
    )(place, part.reshape(2, half, rows, width), up_direct, down_direct)


def pack_kernel(
    key, bounds, partial, up_sum, down_sum, first, second, out, first_out, second_out
):
    _, count, rows, cols = partial.shape
    half = out.shape[0] // 2
    begin = pl.program_id(0) * count
    lanes = 128

    def one(side, i, value):
        block = side * half + begin + i
        ok = inside(bounds, block, rows, cols)
        grad = jnp.where(ok, value, 0.0)
        first_next = BETA_FIRST * first[side, i] + (1.0 - BETA_FIRST) * grad
        second_next = BETA_SECOND * second[side, i] + (1.0 - BETA_SECOND) * grad * grad
        first_out[side, i] = first_next
        second_out[side, i] = second_next
        adam = first_next / (jnp.sqrt(second_next) + ADAM_EPS * BIAS_SECOND**0.5)
        square = jnp.where(ok, adam * adam, 0.0)
        square = square[:, :lanes] + square[:, lanes:]
        square = square[: rows // 2] + square[rows // 2 :]
        piece = jnp.concatenate([grad[:, :lanes], grad[:, lanes:], square], axis=0)
        out[key[block]] = piece.astype(BF16)

    def step(i, carry):
        one(0, i, partial[0, i] + up_sum[i].astype(F32))
        one(1, i, partial[1, i] + down_sum[i].astype(F32))
        return carry

    lax.fori_loop(0, count, step, 0, unroll=4)


def pack(key, bounds, partial, up_sum, down_sum, first, second):
    _, half, rows, cols = partial.shape
    blocks = 2 * half
    steps = 4 if half >= 16 else 1
    count = half // steps
    piece = 2 * rows + rows // 2
    moment = pl.BlockSpec((2, count, rows, cols), lambda i, *_: (0, i, 0, 0))
    halves = jax.ShapeDtypeStruct((2, half, rows, cols), F32)
    out, first_next, second_next = pl.pallas_call(
        pack_kernel,
        out_shape=(pltpu.HBM((blocks, piece, 128), BF16), halves, halves),
        grid_spec=pltpu.PrefetchScalarGridSpec(
            num_scalar_prefetch=2,
            grid=(steps,),
            in_specs=[
                moment,
                pl.BlockSpec((count, rows, cols), lambda i, *_: (i, 0, 0)),
                pl.BlockSpec((count, rows, cols), lambda i, *_: (i, 0, 0)),
                moment,
                moment,
            ],
            out_specs=[
                pl.BlockSpec((blocks, piece, 128), lambda i, *_: (0, 0, 0)),
                moment,
                moment,
            ],
        ),
        compiler_params=pltpu.CompilerParams(vmem_limit_bytes=10 * MIB),
    )(
        key,
        bounds,
        partial,
        up_sum,
        down_sum,
        in_hbm(first.reshape(halves.shape)),
        in_hbm(second.reshape(halves.shape)),
    )
    return out, first_next.reshape(first.shape), second_next.reshape(second.shape)


def relay_kernel(prev, following, low, high):
    rows = low.shape[0]
    low[...] = prev[pl.ds(0, rows), :]
    high[...] = following[pl.ds(rows, rows), :]


def relay(prev, following):
    rows, width = prev.shape
    half = jax.ShapeDtypeStruct((rows // 2, width), BF16)
    return pl.pallas_call(
        relay_kernel,
        out_shape=(half, half),
        in_specs=[pl.BlockSpec(memory_space=VMEM)] * 2,
        out_specs=(pl.BlockSpec(memory_space=VMEM),) * 2,
        compiler_params=pltpu.CompilerParams(vmem_limit_bytes=6 * MIB),
        cost_estimate=LONG,
    )(prev, following)


def finish_kernel(key, bounds, back, out):
    blocks, rows, cols = out.shape

    def step(block, carry):
        ok = inside(bounds, block, rows, cols)
        out[block] = jnp.where(ok, back[key[block]].astype(F32), 0.0).astype(BF16)
        return carry

    lax.fori_loop(0, blocks, step, 0, unroll=4)


def finish(key, bounds, back):
    whole = pl.BlockSpec(back.shape, lambda i, *_: (0, 0, 0))
    return pl.pallas_call(
        finish_kernel,
        out_shape=jax.ShapeDtypeStruct(back.shape, BF16),
        grid_spec=pltpu.PrefetchScalarGridSpec(
            num_scalar_prefetch=2, grid=(1,), in_specs=[whole], out_specs=whole
        ),
        compiler_params=pltpu.CompilerParams(vmem_limit_bytes=6 * MIB),
    )(key, bounds, back)


def precond_kernel(*refs):
    own_low, own_high, next_low, next_high, far_low, far_high, prev_low, prev_high = refs[:8]
    roots, lefts, (adam, out, norms, mixed) = refs[8:12], refs[12:17], refs[17:]
    width, quarter = out.shape
    half = width // 2
    me = lax.axis_index("grp")
    n = width // quarter
    for top, parts in (
        (0, (own_low, next_low, far_low, prev_low)),
        (half, (own_high, next_high, far_high, prev_high)),
    ):
        for row in range(0, half, quarter):
            total = jnp.zeros((quarter, quarter), F32)
            for piece, root in zip(parts, roots):
                total += dot(piece[pl.ds(row, quarter), :], root[...], ((1,), (0,)))
            mixed[pl.ds(top + row, quarter), :] = total.astype(BF16)
    square = jnp.zeros((8, quarter), F32)
    eighth = quarter // 2
    places = ((0, 0), (1, 0), (2, 0), (2, eighth), (3, 0))
    for (step, extra), left in zip(places, lefts):
        base = lax.rem(me + step, n) * quarter + extra
        rows = left.shape[0]
        value = dot(left[...], mixed[...], ((1,), (0,)))
        out[pl.ds(pl.multiple_of(base, eighth), rows), :] = value
        square += jnp.sum((value * value).reshape(rows // 8, 8, quarter), axis=0)
    norms[...] = jnp.zeros_like(norms)
    norms[0:1, :] = jnp.broadcast_to(jnp.sum(square), (1, 128))
    norms[1:2, :] = jnp.broadcast_to(jnp.sum(adam[...].astype(F32)), (1, 128))


def precondition(pieces, roots, lefts, adam):
    rows, quarter = pieces[0].shape
    operands = (*pieces, *map(in_hbm, roots), *map(in_hbm, lefts), adam)
    return pl.pallas_call(
        precond_kernel,
        out_shape=(
            jax.ShapeDtypeStruct((2 * rows, quarter), F32),
            jax.ShapeDtypeStruct((8, 128), F32),
        ),
        in_specs=[pl.BlockSpec(memory_space=VMEM)] * len(operands),
        out_specs=(pl.BlockSpec(memory_space=VMEM),) * 2,
        scratch_shapes=[VMEM((2 * rows, quarter), BF16)],
        compiler_params=pltpu.CompilerParams(vmem_limit_bytes=12 * MIB),
    )(*operands)


def graft_kernel(cells, precond, first, second, third, fourth, out):
    sums = first[...] + second[...] + third[...] + fourth[...]
    pre, adam = sums[0:1, :], sums[1:2, :]
    adam = adam * (BIAS_SECOND / (BIAS_FIRST * BIAS_FIRST))
    scale = -jnp.sqrt(adam / cells) / jnp.sqrt(pre / cells + NORM_EPS)
    width, quarter = out.shape
    scale = jnp.concatenate([scale] * (quarter // 128), axis=1)
    out[...] = (scale * precond[...]).astype(BF16)


def graft(precond, norms):
    width, quarter = precond.shape
    tiles = 4
    rows = width // tiles
    small = pl.BlockSpec((8, 128), lambda i: (0, 0))
    return pl.pallas_call(
        functools.partial(graft_kernel, float(width * width)),
        out_shape=jax.ShapeDtypeStruct((width, quarter), BF16),
        grid=(tiles,),
        in_specs=[pl.BlockSpec((rows, quarter), lambda i: (i, 0))] + [small] * 4,
        out_specs=pl.BlockSpec((rows, quarter), lambda i: (i, 0)),
        compiler_params=pltpu.CompilerParams(vmem_limit_bytes=6 * MIB),
    )(precond, *norms)


def on_device(
    grad_parts,
    assign,
    block_bounds,
    left_root,
    right_root,
    left_stat,
    right_stat,
    first_moment,
    second_moment,
):
    n_own = lax.axis_size("own")
    n_grp = lax.axis_size("grp")
    grp_index = lax.axis_index("grp")
    total_blocks = assign.shape[0]
    per_owner = total_blocks // n_own
    shard_rows = grad_parts.shape[2]
    width = grad_parts.shape[3]
    quarter = width // n_grp
    half = total_blocks // 2
    part = grad_parts[0]
    place = grp_index.reshape(1).astype(jnp.int32)
    starts = [((grp_index + step) & (n_grp - 1)) * quarter for step in range(4)]
    turn = ((n_grp - grp_index) & (n_grp - 1)) * quarter
    part, place, starts, turn = lax.optimization_barrier((part, place, starts, turn))

    def columns(array, step):
        return slice_at(array, starts[step], quarter, array.ndim - 1)

    far = columns(part, 2)
    up = columns(part, 1)
    down = columns(part, 3)
    far_up = shift(far[:half], 1)
    far_down = shift(far[half:], -1)
    up_direct = shift(up[half:], 1)
    down_direct = shift(down[:half], -1)
    up_sum = shift((up[:half].astype(F32) + far_up.astype(F32)).astype(BF16), 1)
    down_sum = shift((down[half:].astype(F32) + far_down.astype(F32)).astype(BF16), -1)
    key, bounds = slots_of(assign, n_own, per_owner), block_bounds.reshape(-1)
    up_direct, down_direct, key, bounds = lax.optimization_barrier(
        (up_direct, down_direct, key, bounds)
    )
    partial = gather(place, part, up_direct, down_direct)

    left_bf, right_bf = left_root[0].astype(BF16), right_root[0].astype(BF16)
    right_parts = [columns(right_bf, step) for step in range(4)]
    left_bf, right_parts, up_sum, down_sum, partial = lax.optimization_barrier(
        (left_bf, right_parts, up_sum, down_sum, partial)
    )
    sorted_grad, first_next, second_next = pack(
        key, bounds, partial, up_sum, down_sum, first_moment, second_moment
    )
    owned = lax.all_to_all(sorted_grad, "own", split_axis=0, concat_axis=0, tiled=True)
    left_prev = shift(left_bf, 1)
    left_next = shift(left_bf, -1)
    far_halves = relay(left_prev, left_next)
    left_far_low = shift(far_halves[0], 1)
    left_far_high = shift(far_halves[1], -1)
    right_parts, far_halves = lax.optimization_barrier((right_parts, far_halves))
    roots = [right_parts[0]] + [shift(right_parts[step], step) for step in (3, 2, 1)]
    lefts = [left_bf, left_next, left_far_low, left_far_high, left_prev]

    owned, lefts, roots = lax.optimization_barrier((owned, lefts, roots))
    own_cols = jnp.concatenate(
        [owned[:, :shard_rows], owned[:, shard_rows : 2 * shard_rows]], axis=2
    )
    adam = owned[:, 2 * shard_rows :].reshape(n_own * shard_rows // 2, 128)
    low, high = own_cols[:half], own_cols[half:]
    prev_low = shift(low, 1)
    next_high = shift(high, -1)
    prev_high = shift(high, 1)
    next_low = shift(low, -1)
    far_low = shift(prev_low, 1)
    far_high = shift(next_high, -1)
    pieces = [low, high, next_low, next_high, far_low, far_high, prev_low, prev_high]
    flat = [piece.reshape(width // 2, quarter) for piece in pieces]
    precond, norms = precondition(flat, roots, lefts, adam)
    norms = [norms] + [shift(norms, step) for step in (1, 2, 3)]
    grafted = graft(precond, norms).reshape(n_own, shard_rows, quarter)
    pieces, grafted, assign, bounds = lax.optimization_barrier(
        (pieces, grafted, assign, block_bounds)
    )
    key, bounds = slots_of(assign, n_own, per_owner), bounds.reshape(-1)
    back = lax.all_to_all(grafted, "own", split_axis=0, concat_axis=0, tiled=True)

    whole = jnp.concatenate(
        [jnp.concatenate(pieces[i : i + 2], axis=0) for i in (0, 2, 4, 6)], axis=2
    ).reshape(width, width)
    rows = slice_at(whole, starts[0], quarter, 0)
    left_acc = STAT_DECAY * left_stat + dot(rows, whole, ((1,), (1,)))[None]
    cross = dot(whole[:, :quarter], whole, ((0,), (0,)))
    cross = jnp.concatenate([cross, cross], axis=1)
    cross = slice_at(cross, turn, width, 1)
    right_acc = STAT_DECAY * right_stat + cross[None]

    update = finish(key, bounds, back)
    return (update, first_next, second_next, left_acc, right_acc)


def solution(mesh):
    placed = (
        P("grp", None, "own", None),
        P(),
        P(),
        P("own", "grp", None),
        P("own", "grp", None),
        P("own", "grp", None),
        P("own", "grp", None),
        P(None, "own", "grp"),
        P(None, "own", "grp"),
    )
    return jax.shard_map(
        on_device,
        mesh=mesh,
        in_specs=placed,
        out_specs=(
            P(None, "own", "grp"),
            P(None, "own", "grp"),
            P(None, "own", "grp"),
            P("own", "grp", None),
            P("own", "grp", None),
        ),
        check_vma=False,
    )
```

time: 138 us -> 129 us (0.935)
  other arithmetic: 19.2 us -> 7.73 us
  starting transfers between devices: 51.5 us -> 46.7 us
  waiting for transfers between devices: 45.4 us -> 49.6 us
  matrix products: 2.47 us -> 4.23 us
    concatenate x1, other arithmetic: 12.8 us -> 1.52 us  [on_device(): jnp.concatenate([jnp.concatenate(pieces[i:i + 2], axis=0) for i in (0, 2,...]
    ppermute x24 -> x22, waiting for transfers between devices: 45 us -> 36.6 us  [shift(): return lax.ppermute(array, 'grp', [(i, (i + step) % n) for i in range(n)])]
    all_to_all x1, waiting for transfers between devices: 0.01 us -> 8.24 us  [on_device(): lax.all_to_all(grafted, 'own', split_axis=0, concat_axis=0, tiled=True)]
    all_to_all x1, starting transfers between devices: 14 us -> 8.47 us  [on_device(): lax.all_to_all(grafted, 'own', split_axis=0, concat_axis=0, tiled=True)]
    all_to_all x1, waiting for transfers between devices: 0.37 us -> 4.78 us  [on_device(): lax.all_to_all(sorted_grad, 'own', split_axis=0, concat_axis=0, tiled=True)]
    convert_element_type x3 -> x2, other arithmetic: 3.64 us -> 0.94 us  [on_device(): left_bf, right_bf = (left_root[0].astype(BF16), right_root[0].astype(BF16))]
    slice x2 -> x0, local copies, waits for them, and re-layouts: 1.88 us -> none  [the longest x1 1.02 us: on_device(): down_direct = shift(down[:half], -1)]
    dot_general x2, matrix products: 2.47 us -> 4.23 us  [dot(): return lax.dot_general(a, b, (dims, ((), ())), preferred_element_type=F32)]
  transfers between devices with their start and end apart: 26 -> 24, of which waited for: 18 -> 16; matrix products, arithmetic and copies ran while one was open for 17% -> 11% of each run, Pallas kernels for 0% -> 4%
where the time goes in v4:
time: 129 us; the launch traced here: 128 us
  waiting for transfers between devices  49.6 us (38%)
  starting transfers between devices  46.7 us (36%)
  Pallas kernels  11.9 us (9%)
  other arithmetic  7.73 us (6%)
  local copies, waits for them, and re-layouts  7.16 us (6%)
  matrix products  4.23 us (3%)
    ppermute x22, waiting for transfers between devices, shift(): return lax.ppermute(array, 'grp', [(i, (i + step) % n) for i in range(n)])  36.6 us
    ppermute x22, starting transfers between devices, shift(): return lax.ppermute(array, 'grp', [(i, (i + step) % n) for i in range(n)])  22.3 us
    all_to_all x1, starting transfers between devices, on_device(): lax.all_to_all(sorted_grad, 'own', split_axis=0, concat_axis=0, tiled=True)  16 us
    all_to_all x1, starting transfers between devices, on_device(): lax.all_to_all(grafted, 'own', split_axis=0, concat_axis=0, tiled=True)  8.47 us
    all_to_all x1, waiting for transfers between devices, on_device(): lax.all_to_all(grafted, 'own', split_axis=0, concat_axis=0, tiled=True)  8.24 us
    pallas_call x1, Pallas kernels, pack(): pl.pallas_call(pack_kernel, out_shape=(pltpu.HBM((blocks, piece, 128), BF...  5.17 us
    all_to_all x1, waiting for transfers between devices, on_device(): lax.all_to_all(sorted_grad, 'own', split_axis=0, concat_axis=0, tiled=True)  4.78 us
    dot_general x2, matrix products, dot(): return lax.dot_general(a, b, (dims, ((), ())), preferred_element_type=F32)  4.23 us
  transfers between devices with their start and end apart: 24, of which 16 were waited for; matrix products, arithmetic and copies ran while one was open for 11% of the time, Pallas kernels for 4%

profile of v4, /device:TPU:1, one launch (start us, length us, event | category | flops | bytes accessed | tf_op | source)
XLA Modules:
  0.0 128.3 jit_solution(15111421484186457564)
XLA Ops:
  0.7 2.8 %constant_dynamic-slice_fusion.3 = (bf16[32,16,256]{2,1,0:T(8,128)(2,1)}, bf16[32,16,256]{2,1,0:T(8,128)(2,1)}, bf16[32,16,256]{2,1,0:T(8,128)(2,1)}, bf16[32,16,256]{2,1,0:T(8,128)(2,1)S(1)}) fusion(bf16[64,16,1024]{2,1,0:T(8,128)(2,1)} %bitcast.41, s32[]{:T(128)S(6)} %add.50, s32[]{:T(128)S(6)} %mul.23, s32[]{:T(128)S(6)} %mul.24, s32[]{:T(128)S(6)} %mul.22), kind=kLoop, calls=%fused_computation.27 | loop fusion | bytes 2097168 | tf_op jit(solution)/shard_map/slice | solution.py:304
  3.4 3.6 %collective-permute-start.4 = (bf16[32,16,256]{2,1,0:T(8,128)(2,1)}, bf16[32,16,256]{2,1,0:T(8,128)(2,1)}, u32[]{:S(2)}, u32[]{:S(2)}) collective-permute-start(bf16[32,16,256]{2,1,0:T(8,128)(2,1)} %get-tuple-element.109), channel_id=1, source_target_pairs={{0,192},{64,0},{128,64},{192,128},{1,193},{65,1},{129,65},{193,129... | collective-permute-start | bytes 786440 | tf_op jit(solution)/shard_map/ppermute | solution.py:26
  7.0 2.7 %collective-permute-start.1 = (bf16[32,16,256]{2,1,0:T(8,128)(2,1)}, bf16[32,16,256]{2,1,0:T(8,128)(2,1)S(1)}, u32[]{:S(2)}, u32[]{:S(2)}) collective-permute-start(bf16[32,16,256]{2,1,0:T(8,128)(2,1)} %get-tuple-element.111), channel_id=1, source_target_pairs={{0,192},{64,0},{128,64},{192,128},{1,193},{65,1},{129,65},{193,129... | collective-permute-start | bytes 786440 | tf_op jit(solution)/shard_map/ppermute | solution.py:26
  12.3 3.1 %collective-permute-done.2 = bf16[32,16,256]{2,1,0:T(8,128)(2,1)} collective-permute-done((bf16[32,16,256]{2,1,0:T(8,128)(2,1)}, bf16[32,16,256]{2,1,0:T(8,128)(2,1)}, u32[]{:S(2)}, u32[]{:S(2)}) %collective-permute-start.2) | collective-permute-done | bytes 262176 | tf_op jit(solution)/shard_map/ppermute | solution.py:26
  15.4 2.1 %add_convert_fusion = (bf16[32,16,256]{2,1,0:T(8,128)(2,1)}, bf16[32,16,256]{2,1,0:T(8,128)(2,1)}) fusion(bf16[32,16,256]{2,1,0:T(8,128)(2,1)} %collective-permute-done.4, bf16[64,16,1024]{2,1,0:T(8,128)(2,1)S(1)} %bitcast.42, s32[]{:T(128)S(6)} %add.50, s32[]{:T(128)S(6)} %mul.24, bf16[32,16,256]{2,1,0:T(8,128)(2,1)} %collective-permute-done.2, s32[]{:T(128)S(6)} %mul.22), kind=kLoop, calls=%fused_computation.13 | loop fusion | flops 1048576 | bytes 1572876 | tf_op jit(solution)/shard_map/convert_element_type | solution.py:308
  19.0 1.9 %collective-permute-done.up_direct = bf16[32,16,256]{2,1,0:T(8,128)(2,1)S(1)} collective-permute-done((bf16[32,16,256]{2,1,0:T(8,128)(2,1)S(1)}, bf16[32,16,256]{2,1,0:T(8,128)(2,1)S(1)}, u32[]{:S(2)}, u32[]{:S(2)}) %collective-permute-start) | collective-permute-done | bytes 262176 | tf_op jit(solution)/shard_map/ppermute | solution.py:26
  21.1 2.0 %collective-permute-done.5.down_sum = bf16[32,16,256]{2,1,0:T(8,128)(2,1)} collective-permute-done((bf16[32,16,256]{2,1,0:T(8,128)(2,1)}, bf16[32,16,256]{2,1,0:T(8,128)(2,1)}, u32[]{:S(2)}, u32[]{:S(2)}) %collective-permute-start.5) | collective-permute-done | bytes 262176 | tf_op jit(solution)/shard_map/ppermute | solution.py:26
  23.1 1.9 %collective-permute-done.3.up_sum = bf16[32,16,256]{2,1,0:T(8,128)(2,1)} collective-permute-done((bf16[32,16,256]{2,1,0:T(8,128)(2,1)}, bf16[32,16,256]{2,1,0:T(8,128)(2,1)}, u32[]{:S(2)}, u32[]{:S(2)}) %collective-permute-start.3) | collective-permute-done | bytes 262176 | tf_op jit(solution)/shard_map/ppermute | solution.py:26
  25.0 2.7 %collective-permute-start.6 = (bf16[256,1024]{1,0:T(8,128)(2,1)S(1)}, bf16[256,1024]{1,0:T(8,128)(2,1)S(1)}, u32[]{:S(2)}, u32[]{:S(2)}) collective-permute-start(bf16[256,1024]{1,0:T(8,128)(2,1)S(1)} %copy-done.4), channel_id=1, source_target_pairs={{0,192},{64,0},{128,64},{192,128},{1,193},{65,1},{129,65},{193,129... | collective-permute-start | bytes 1572872 | tf_op jit(solution)/shard_map/ppermute | solution.py:26
  27.7 5.2 %shard_map.129 = (bf16[64,40,128]{2,1,0:T(8,128)(2,1)}, f32[2,32,16,256]{3,2,1,0:T(8,128)}, f32[2,32,16,256]{3,2,1,0:T(8,128)}) custom-call(s32[64]{0:T(128)S(1)} %fusion.9.key, s32[256]{0:T(256)S(1)} %reshape.74.bounds, f32[2,32,16,256]{3,2,1,0:T(8,128)S(1)} %shard_map.128.partial, bf16[32,16,256]{2,1,0:T(8,128)(2,1)} %collective-permute-done.3.up_sum, ...), custom_call_target="tpu_custom_call" | custom-call | tf_op jit(solution)/shard_map/pallas_call | solution.py:126
  32.9 16.0 %all-to-all-start = ((bf16[64,40,128]{2,1,0:T(8,128)(2,1)}), bf16[64,40,128]{2,1,0:T(8,128)(2,1)}, u32[]{:S(2)}, u32[]{:S(2)}) async-start(bf16[64,40,128]{2,1,0:T(8,128)(2,1)} %get-tuple-element.69), calls=%async_computation | async-start | bytes 1310720 | tf_op jit(solution)/shard_map/all_to_all | solution.py:323
  50.2 2.3 %collective-permute-start.9 = (bf16[128,1024]{1,0:T(8,128)(2,1)S(1)}, bf16[128,1024]{1,0:T(8,128)(2,1)S(1)}, u32[]{:S(2)}, u32[]{:S(2)}) collective-permute-start(bf16[128,1024]{1,0:T(8,128)(2,1)S(1)} %get-tuple-element.72), channel_id=1, source_target_pairs={{0,192},{64,0},{128,64},{192,128},{1,193},{65,1},{129,65},{193,129... | collective-permute-start | bytes 786440 | tf_op jit(solution)/shard_map/ppermute | solution.py:26
  54.3 6.5 %collective-permute-done.10.refs_9_ = bf16[256,256]{1,0:T(8,128)(2,1)S(1)} collective-permute-done((bf16[256,256]{1,0:T(8,128)(2,1)S(1)}, bf16[256,256]{1,0:T(8,128)(2,1)S(1)}, u32[]{:S(2)}, u32[]{:S(2)}) %collective-permute-start.10) | collective-permute-done | bytes 131104 | tf_op jit(solution)/shard_map/ppermute | solution.py:26
  60.8 3.3 %collective-permute-done.12.refs_11_ = bf16[256,256]{1,0:T(8,128)(2,1)S(1)} collective-permute-done((bf16[256,256]{1,0:T(8,128)(2,1)S(1)}, bf16[256,256]{1,0:T(8,128)(2,1)S(1)}, u32[]{:S(2)}, u32[]{:S(2)}) %collective-permute-start.12) | collective-permute-done | bytes 131104 | tf_op jit(solution)/shard_map/ppermute | solution.py:26
  64.2 4.8 %all-to-all-done = bf16[64,40,128]{2,1,0:T(8,128)(2,1)} async-done(((bf16[64,40,128]{2,1,0:T(8,128)(2,1)}), bf16[64,40,128]{2,1,0:T(8,128)(2,1)}, u32[]{:S(2)}, u32[]{:S(2)}) %all-to-all-start) | async-done | bytes 655392 | tf_op jit(solution)/shard_map/all_to_all | solution.py:323
  70.2 1.5 %collective-permute-start.15 = (bf16[32,16,256]{2,1,0:T(8,128)(2,1)S(1)}, bf16[32,16,256]{2,1,0:T(8,128)(2,1)S(1)}, u32[]{:S(2)}, u32[]{:S(2)}) collective-permute-start(bf16[32,16,256]{2,1,0:T(8,128)(2,1)S(1)} %get-tuple-element.98), channel_id=1, source_target_pairs={{0,64},{64,128},{128,192},{192,0},{1,65},{65,129},{129,193},{193,1... | collective-permute-start | bytes 786440 | tf_op jit(solution)/shard_map/ppermute | solution.py:26
  72.0 2.3 %collective-permute-start.13 = (bf16[32,16,256]{2,1,0:T(8,128)(2,1)S(1)}, bf16[32,16,256]{2,1,0:T(8,128)(2,1)S(1)}, u32[]{:S(2)}, u32[]{:S(2)}) collective-permute-start(bf16[32,16,256]{2,1,0:T(8,128)(2,1)S(1)} %get-tuple-element.98), channel_id=1, source_target_pairs={{0,192},{64,0},{128,64},{192,128},{1,193},{65,1},{129,65},{193,129... | collective-permute-start | bytes 786440 | tf_op jit(solution)/shard_map/ppermute | solution.py:26
  74.3 3.5 %collective-permute-done.14 = bf16[32,16,256]{2,1,0:T(8,128)(2,1)S(1)} collective-permute-done((bf16[32,16,256]{2,1,0:T(8,128)(2,1)S(1)}, bf16[32,16,256]{2,1,0:T(8,128)(2,1)S(1)}, u32[]{:S(2)}, u32[]{:S(2)}) %collective-permute-start.14) | collective-permute-done | bytes 262176 | tf_op jit(solution)/shard_map/ppermute | solution.py:26
  77.8 1.5 %collective-permute-start.17 = (bf16[32,16,256]{2,1,0:T(8,128)(2,1)S(1)}, bf16[32,16,256]{2,1,0:T(8,128)(2,1)S(1)}, u32[]{:S(2)}, u32[]{:S(2)}) collective-permute-start(bf16[32,16,256]{2,1,0:T(8,128)(2,1)S(1)} %collective-permute-done.14), channel_id=1, source_target_pairs={{0,192},{64,0},{128,64},{192,128},{1,193},{65,1},{129,65},{193,129... | collective-permute-start | bytes 786440 | tf_op jit(solution)/shard_map/ppermute | solution.py:26
  80.2 4.5 %collective-permute-done.18 = bf16[32,16,256]{2,1,0:T(8,128)(2,1)S(1)} collective-permute-done((bf16[32,16,256]{2,1,0:T(8,128)(2,1)S(1)}, bf16[32,16,256]{2,1,0:T(8,128)(2,1)S(1)}, u32[]{:S(2)}, u32[]{:S(2)}) %collective-permute-start.18) | collective-permute-done | bytes 262176 | tf_op jit(solution)/shard_map/ppermute | solution.py:26
  84.7 4.3 %collective-permute-done.17 = bf16[32,16,256]{2,1,0:T(8,128)(2,1)S(1)} collective-permute-done((bf16[32,16,256]{2,1,0:T(8,128)(2,1)S(1)}, bf16[32,16,256]{2,1,0:T(8,128)(2,1)S(1)}, u32[]{:S(2)}, u32[]{:S(2)}) %collective-permute-start.17) | collective-permute-done | bytes 262176 | tf_op jit(solution)/shard_map/ppermute | solution.py:26
  90.3 3.3 %shard_map.131 = (f32[1024,256]{1,0:T(8,128)S(1)}, f32[8,128]{1,0:T(8,128)S(1)}) custom-call(bf16[512,256]{1,0:T(8,128)(2,1)S(1)} %bitcast.40, bf16[512,256]{1,0:T(8,128)(2,1)S(1)} %bitcast.39, bf16[512,256]{1,0:T(8,128)(2,1)S(1)} %bitcast.47, bf16[512,256]{1,0:T(8,128)(2,1)S(1)} %bitcast.44, bf16[512,256]{1,0:T(8,128)(2,1)S(1)} %bitcast.49, ...), custom_call_target="tpu_custom_call" | custom-call | tf_op jit(solution)/shard_map/pallas_call | solution.py:233
  96.2 1.7 %collective-permute-done.20.third = f32[8,128]{1,0:T(8,128)S(1)} collective-permute-done((f32[8,128]{1,0:T(8,128)S(1)}, f32[8,128]{1,0:T(8,128)S(1)}, u32[]{:S(2)}, u32[]{:S(2)}) %collective-permute-start.20) | collective-permute-done | bytes 4128 | tf_op jit(solution)/shard_map/ppermute | solution.py:26
  97.9 1.4 %collective-permute-done.19.second = f32[8,128]{1,0:T(8,128)S(1)} collective-permute-done((f32[8,128]{1,0:T(8,128)S(1)}, f32[8,128]{1,0:T(8,128)S(1)}, u32[]{:S(2)}, u32[]{:S(2)}) %collective-permute-start.19) | collective-permute-done | bytes 4128 | tf_op jit(solution)/shard_map/ppermute | solution.py:26
  99.3 1.4 %shard_map.132 = bf16[1024,256]{1,0:T(8,128)(2,1)} custom-call(f32[1024,256]{1,0:T(8,128)S(1)} %get-tuple-element.91.precond, f32[8,128]{1,0:T(8,128)S(1)} %get-tuple-element.92.first, f32[8,128]{1,0:T(8,128)S(1)} %collective-permute-done.19.second, f32[8,128]{1,0:T(8,128)S(1)} %collective-permute-done.20.third, f32[8,128]{1,0:T(8,128)S(1)} %collective-permute-done.21.fourth), custom_call_target="tpu_custom_call" | custom-call | tf_op jit(solution)/shard_map/pallas_call | solution.py:261
  100.8 8.5 %all-to-all-start.1 = ((bf16[64,16,256]{2,1,0:T(8,128)(2,1)}), bf16[64,16,256]{2,1,0:T(8,128)(2,1)S(1)}, u32[]{:S(2)}, u32[]{:S(2)}) async-start(bf16[64,16,256]{2,1,0:T(8,128)(2,1)} %bitcast.19), calls=%async_computation.1 | async-start | bytes 1048576 | tf_op jit(solution)/shard_map/all_to_all | solution.py:354
  109.3 1.5 %maximum_maximum_fusion = bf16[64,16,1024]{2,1,0:T(8,128)(2,1)} fusion(bf16[32,16,256]{2,1,0:T(8,128)(2,1)S(1)} %collective-permute-done.18, bf16[32,16,256]{2,1,0:T(8,128)(2,1)S(1)} %collective-permute-done.15, bf16[32,16,256]{2,1,0:T(8,128)(2,1)S(1)} %collective-permute-done.17, bf16[32,16,256]{2,1,0:T(8,128)(2,1)S(1)} %collective-permute-done.16, ...), kind=kLoop, calls=%fused_computation | loop fusion | flops 16777216 | bytes 4194304 | tf_op jit(solution)/shard_map/concatenate | solution.py:356
  111.0 2.5 %fusion.4 = f32[256,1024]{1,0:T(8,128)S(1)} fusion(bf16[1024,1024]{1,0:T(8,128)(2,1)} %bitcast.50), kind=kOutput, calls=%fused_computation.8 | convolution fusion | flops 536870912 | bytes 3670016 | tf_op jit(solution)/shard_map/dot_general | solution.py:44
  113.5 3.0 %fusion.3 = f32[1,256,1024]{2,1,0:T(8,128)} fusion(s32[]{:T(128)S(6)} %mul.25, f32[256,1024]{1,0:T(8,128)S(1)} %fusion.4, f32[1,256,1024]{2,1,0:T(8,128)} %param.15), kind=kLoop, calls=%fused_computation.7 | loop fusion | flops 786432 | bytes 3145732 | tf_op jit(solution)/shard_map/add | solution.py:364
  116.6 1.7 %fusion = f32[1,256,1024]{2,1,0:T(8,128)} fusion(bf16[1024,1024]{1,0:T(8,128)(2,1)S(1)} %bitcast.51, f32[1,256,1024]{2,1,0:T(8,128)S(1)} %copy-done.5, s32[]{:T(128)S(6)} %mul.21), kind=kOutput, calls=%fused_computation.4 | convolution fusion | flops 537395200 | bytes 4718596 | tf_op jit(solution)/shard_map/dot_general | solution.py:44
  118.3 8.2 %all-to-all-done.1.back = bf16[64,16,256]{2,1,0:T(8,128)(2,1)S(1)} async-done(((bf16[64,16,256]{2,1,0:T(8,128)(2,1)}), bf16[64,16,256]{2,1,0:T(8,128)(2,1)S(1)}, u32[]{:S(2)}, u32[]{:S(2)}) %all-to-all-start.1) | async-done | bytes 524320 | tf_op jit(solution)/shard_map/all_to_all | solution.py:354
  126.6 1.8 %shard_map.133 = bf16[64,16,256]{2,1,0:T(8,128)(2,1)} custom-call(s32[64]{0:T(128)S(1)} %fusion.10.key, s32[256]{0:T(256)S(1)} %reshape.88.bounds, bf16[64,16,256]{2,1,0:T(8,128)(2,1)S(1)} %all-to-all-done.1.back), custom_call_target="tpu_custom_call" | custom-call | tf_op jit(solution)/shard_map/pallas_call | solution.py:190
  (80 shorter events, 13.8 us)
Async XLA Ops:
  0.6 9.1 %copy-start.6 = (f32[1,256,1024]{2,1,0:T(8,128)S(1)}, f32[1,256,1024]{2,1,0:T(8,128)}, u32[]{:S(2)}) copy-start(f32[1,256,1024]{2,1,0:T(8,128)} %param.12) | copy-start | bytes 3145732
  0.7 10.0 %copy-start.7 = (f32[1,256,1024]{2,1,0:T(8,128)S(1)}, f32[1,256,1024]{2,1,0:T(8,128)}, u32[]{:S(2)}) copy-start(f32[1,256,1024]{2,1,0:T(8,128)} %param.13) | copy-start | bytes 3145732
  3.4 7.2 %copy-start.18 = (s32[64]{0:T(128)S(1)}, s32[64]{0:T(128)}, u32[]{:S(2)}) copy-start(s32[64]{0:T(128)} %param.10) | copy-start | bytes 772
  3.4 8.9 %collective-permute-start.4 = (bf16[32,16,256]{2,1,0:T(8,128)(2,1)}, bf16[32,16,256]{2,1,0:T(8,128)(2,1)}, u32[]{:S(2)}, u32[]{:S(2)}) collective-permute-start(bf16[32,16,256]{2,1,0:T(8,128)(2,1)} %get-tuple-element.109), channel_id=1, source_target_pairs={{0,192},{64,0},{128,64},{192,128},{1,193},{65,1},{129,65},{193,129... | collective-permute-start | bytes 786440 | tf_op jit(solution)/shard_map/ppermute | solution.py:26
  7.0 8.4 %collective-permute-start.2 = (bf16[32,16,256]{2,1,0:T(8,128)(2,1)}, bf16[32,16,256]{2,1,0:T(8,128)(2,1)}, u32[]{:S(2)}, u32[]{:S(2)}) collective-permute-start(bf16[32,16,256]{2,1,0:T(8,128)(2,1)} %get-tuple-element.110), channel_id=1, source_target_pairs={{0,64},{64,128},{128,192},{192,0},{1,65},{65,129},{129,193},{193,1... | collective-permute-start | bytes 786440 | tf_op jit(solution)/shard_map/ppermute | solution.py:26
  7.0 12.0 %collective-permute-start.1 = (bf16[32,16,256]{2,1,0:T(8,128)(2,1)}, bf16[32,16,256]{2,1,0:T(8,128)(2,1)S(1)}, u32[]{:S(2)}, u32[]{:S(2)}) collective-permute-start(bf16[32,16,256]{2,1,0:T(8,128)(2,1)} %get-tuple-element.111), channel_id=1, source_target_pairs={{0,192},{64,0},{128,64},{192,128},{1,193},{65,1},{129,65},{193,129... | collective-permute-start | bytes 786440 | tf_op jit(solution)/shard_map/ppermute | solution.py:26
  9.7 11.2 %collective-permute-start = (bf16[32,16,256]{2,1,0:T(8,128)(2,1)S(1)}, bf16[32,16,256]{2,1,0:T(8,128)(2,1)S(1)}, u32[]{:S(2)}, u32[]{:S(2)}) collective-permute-start(bf16[32,16,256]{2,1,0:T(8,128)(2,1)S(1)} %get-tuple-element.112), channel_id=1, source_target_pairs={{0,64},{64,128},{128,192},{192,0},{1,65},{65,129},{129,193},{193,1... | collective-permute-start | bytes 786440 | tf_op jit(solution)/shard_map/ppermute | solution.py:26
  17.6 5.5 %collective-permute-start.5 = (bf16[32,16,256]{2,1,0:T(8,128)(2,1)}, bf16[32,16,256]{2,1,0:T(8,128)(2,1)}, u32[]{:S(2)}, u32[]{:S(2)}) collective-permute-start(bf16[32,16,256]{2,1,0:T(8,128)(2,1)} %get-tuple-element.107), channel_id=1, source_target_pairs={{0,192},{64,0},{128,64},{192,128},{1,193},{65,1},{129,65},{193,129... | collective-permute-start | bytes 786440 | tf_op jit(solution)/shard_map/ppermute | solution.py:26
  17.9 7.1 %collective-permute-start.3 = (bf16[32,16,256]{2,1,0:T(8,128)(2,1)}, bf16[32,16,256]{2,1,0:T(8,128)(2,1)}, u32[]{:S(2)}, u32[]{:S(2)}) collective-permute-start(bf16[32,16,256]{2,1,0:T(8,128)(2,1)} %get-tuple-element.108), channel_id=1, source_target_pairs={{0,64},{64,128},{128,192},{192,0},{1,65},{65,129},{129,193},{193,1... | collective-permute-start | bytes 786440 | tf_op jit(solution)/shard_map/ppermute | solution.py:26
  25.0 23.8 %collective-permute-start.7 = (bf16[256,1024]{1,0:T(8,128)(2,1)S(1)}, bf16[256,1024]{1,0:T(8,128)(2,1)S(1)}, u32[]{:S(2)}, u32[]{:S(2)}) collective-permute-start(bf16[256,1024]{1,0:T(8,128)(2,1)S(1)} %copy-done.4), channel_id=1, source_target_pairs={{0,64},{64,128},{128,192},{192,0},{1,65},{65,129},{129,193},{193,1... | collective-permute-start | bytes 1572872 | tf_op jit(solution)/shard_map/ppermute | solution.py:26
  25.0 23.9 %collective-permute-start.6 = (bf16[256,1024]{1,0:T(8,128)(2,1)S(1)}, bf16[256,1024]{1,0:T(8,128)(2,1)S(1)}, u32[]{:S(2)}, u32[]{:S(2)}) collective-permute-start(bf16[256,1024]{1,0:T(8,128)(2,1)S(1)} %copy-done.4), channel_id=1, source_target_pairs={{0,192},{64,0},{128,64},{192,128},{1,193},{65,1},{129,65},{193,129... | collective-permute-start | bytes 1572872 | tf_op jit(solution)/shard_map/ppermute | solution.py:26
  32.9 36.1 %all-to-all-start = ((bf16[64,40,128]{2,1,0:T(8,128)(2,1)}), bf16[64,40,128]{2,1,0:T(8,128)(2,1)}, u32[]{:S(2)}, u32[]{:S(2)}) async-start(bf16[64,40,128]{2,1,0:T(8,128)(2,1)} %get-tuple-element.69), calls=%async_computation | async-start | bytes 1310720 | tf_op jit(solution)/shard_map/all_to_all | solution.py:323
  49.8 14.3 %collective-permute-start.8 = (bf16[128,1024]{1,0:T(8,128)(2,1)S(1)}, bf16[128,1024]{1,0:T(8,128)(2,1)S(1)}, u32[]{:S(2)}, u32[]{:S(2)}) collective-permute-start(bf16[128,1024]{1,0:T(8,128)(2,1)S(1)} %get-tuple-element.71), channel_id=1, source_target_pairs={{0,64},{64,128},{128,192},{192,0},{1,65},{65,129},{129,193},{193,1... | collective-permute-start | bytes 786440 | tf_op jit(solution)/shard_map/ppermute | solution.py:26
  50.2 13.9 %collective-permute-start.9 = (bf16[128,1024]{1,0:T(8,128)(2,1)S(1)}, bf16[128,1024]{1,0:T(8,128)(2,1)S(1)}, u32[]{:S(2)}, u32[]{:S(2)}) collective-permute-start(bf16[128,1024]{1,0:T(8,128)(2,1)S(1)} %get-tuple-element.72), channel_id=1, source_target_pairs={{0,192},{64,0},{128,64},{192,128},{1,193},{65,1},{129,65},{193,129... | collective-permute-start | bytes 786440 | tf_op jit(solution)/shard_map/ppermute | solution.py:26
  52.5 8.3 %collective-permute-start.10 = (bf16[256,256]{1,0:T(8,128)(2,1)S(1)}, bf16[256,256]{1,0:T(8,128)(2,1)S(1)}, u32[]{:S(2)}, u32[]{:S(2)}) collective-permute-start(bf16[256,256]{1,0:T(8,128)(2,1)S(1)} %copy-done.15), channel_id=1, source_target_pairs={{0,192},{64,0},{128,64},{192,128},{1,193},{65,1},{129,65},{193,129... | collective-permute-start | bytes 393224 | tf_op jit(solution)/shard_map/ppermute | solution.py:26
  52.6 8.3 %collective-permute-start.11 = (bf16[256,256]{1,0:T(8,128)(2,1)S(1)}, bf16[256,256]{1,0:T(8,128)(2,1)S(1)}, u32[]{:S(2)}, u32[]{:S(2)}) collective-permute-start(bf16[256,256]{1,0:T(8,128)(2,1)S(1)} %copy-done.14), channel_id=1, source_target_pairs={{0,128},{64,192},{128,0},{192,64},{1,129},{65,193},{129,1},{193,65... | collective-permute-start | bytes 393224 | tf_op jit(solution)/shard_map/ppermute | solution.py:26
  53.5 10.7 %collective-permute-start.12 = (bf16[256,256]{1,0:T(8,128)(2,1)S(1)}, bf16[256,256]{1,0:T(8,128)(2,1)S(1)}, u32[]{:S(2)}, u32[]{:S(2)}) collective-permute-start(bf16[256,256]{1,0:T(8,128)(2,1)S(1)} %copy-done.13), channel_id=1, source_target_pairs={{0,64},{64,128},{128,192},{192,0},{1,65},{65,129},{129,193},{193,1... | collective-permute-start | bytes 393224 | tf_op jit(solution)/shard_map/ppermute | solution.py:26
  60.8 29.5 %copy-start.10 = (bf16[256,256]{1,0:T(8,128)(2,1)}, bf16[256,256]{1,0:T(8,128)(2,1)S(1)}, u32[]{:S(2)}) copy-start(bf16[256,256]{1,0:T(8,128)(2,1)S(1)} %collective-permute-done.10.refs_9_) | copy-start | bytes 393220
  60.8 29.5 %copy-start.11 = (bf16[256,256]{1,0:T(8,128)(2,1)}, bf16[256,256]{1,0:T(8,128)(2,1)S(1)}, u32[]{:S(2)}) copy-start(bf16[256,256]{1,0:T(8,128)(2,1)S(1)} %collective-permute-done.11.refs_10_) | copy-start | bytes 393220
  64.1 26.2 %copy-start.12 = (bf16[256,256]{1,0:T(8,128)(2,1)}, bf16[256,256]{1,0:T(8,128)(2,1)S(1)}, u32[]{:S(2)}) copy-start(bf16[256,256]{1,0:T(8,128)(2,1)S(1)} %collective-permute-done.12.refs_11_) | copy-start | bytes 393220
  64.1 26.2 %copy-start.8 = (bf16[128,1024]{1,0:T(8,128)(2,1)}, bf16[128,1024]{1,0:T(8,128)(2,1)S(1)}, u32[]{:S(2)}) copy-start(bf16[128,1024]{1,0:T(8,128)(2,1)S(1)} %collective-permute-done.8.refs_14_) | copy-start | bytes 786436
  64.1 26.2 %copy-start.9 = (bf16[128,1024]{1,0:T(8,128)(2,1)}, bf16[128,1024]{1,0:T(8,128)(2,1)S(1)}, u32[]{:S(2)}) copy-start(bf16[128,1024]{1,0:T(8,128)(2,1)S(1)} %collective-permute-done.9.refs_15_) | copy-start | bytes 786436
  70.1 7.7 %collective-permute-start.14 = (bf16[32,16,256]{2,1,0:T(8,128)(2,1)S(1)}, bf16[32,16,256]{2,1,0:T(8,128)(2,1)S(1)}, u32[]{:S(2)}, u32[]{:S(2)}) collective-permute-start(bf16[32,16,256]{2,1,0:T(8,128)(2,1)S(1)} %get-tuple-element.99), channel_id=1, source_target_pairs={{0,192},{64,0},{128,64},{192,128},{1,193},{65,1},{129,65},{193,129... | collective-permute-start | bytes 786440 | tf_op jit(solution)/shard_map/ppermute | solution.py:26
  70.2 9.1 %collective-permute-start.15 = (bf16[32,16,256]{2,1,0:T(8,128)(2,1)S(1)}, bf16[32,16,256]{2,1,0:T(8,128)(2,1)S(1)}, u32[]{:S(2)}, u32[]{:S(2)}) collective-permute-start(bf16[32,16,256]{2,1,0:T(8,128)(2,1)S(1)} %get-tuple-element.98), channel_id=1, source_target_pairs={{0,64},{64,128},{128,192},{192,0},{1,65},{65,129},{129,193},{193,1... | collective-permute-start | bytes 786440 | tf_op jit(solution)/shard_map/ppermute | solution.py:26
  71.6 13.1 %collective-permute-start.18 = (bf16[32,16,256]{2,1,0:T(8,128)(2,1)S(1)}, bf16[32,16,256]{2,1,0:T(8,128)(2,1)S(1)}, u32[]{:S(2)}, u32[]{:S(2)}) collective-permute-start(bf16[32,16,256]{2,1,0:T(8,128)(2,1)S(1)} %get-tuple-element.99), channel_id=1, source_target_pairs={{0,64},{64,128},{128,192},{192,0},{1,65},{65,129},{129,193},{193,1... | collective-permute-start | bytes 786440 | tf_op jit(solution)/shard_map/ppermute | solution.py:26
  72.0 12.7 %collective-permute-start.13 = (bf16[32,16,256]{2,1,0:T(8,128)(2,1)S(1)}, bf16[32,16,256]{2,1,0:T(8,128)(2,1)S(1)}, u32[]{:S(2)}, u32[]{:S(2)}) collective-permute-start(bf16[32,16,256]{2,1,0:T(8,128)(2,1)S(1)} %get-tuple-element.98), channel_id=1, source_target_pairs={{0,192},{64,0},{128,64},{192,128},{1,193},{65,1},{129,65},{193,129... | collective-permute-start | bytes 786440 | tf_op jit(solution)/shard_map/ppermute | solution.py:26
  77.8 11.2 %collective-permute-start.17 = (bf16[32,16,256]{2,1,0:T(8,128)(2,1)S(1)}, bf16[32,16,256]{2,1,0:T(8,128)(2,1)S(1)}, u32[]{:S(2)}, u32[]{:S(2)}) collective-permute-start(bf16[32,16,256]{2,1,0:T(8,128)(2,1)S(1)} %collective-permute-done.14), channel_id=1, source_target_pairs={{0,192},{64,0},{128,64},{192,128},{1,193},{65,1},{129,65},{193,129... | collective-permute-start | bytes 786440 | tf_op jit(solution)/shard_map/ppermute | solution.py:26
  79.3 11.0 %collective-permute-start.16 = (bf16[32,16,256]{2,1,0:T(8,128)(2,1)S(1)}, bf16[32,16,256]{2,1,0:T(8,128)(2,1)S(1)}, u32[]{:S(2)}, u32[]{:S(2)}) collective-permute-start(bf16[32,16,256]{2,1,0:T(8,128)(2,1)S(1)} %collective-permute-done.15), channel_id=1, source_target_pairs={{0,64},{64,128},{128,192},{192,0},{1,65},{65,129},{129,193},{193,1... | collective-permute-start | bytes 786440 | tf_op jit(solution)/shard_map/ppermute | solution.py:26
  93.6 2.5 %collective-permute-start.21 = (f32[8,128]{1,0:T(8,128)S(1)}, f32[8,128]{1,0:T(8,128)S(1)}, u32[]{:S(2)}, u32[]{:S(2)}) collective-permute-start(f32[8,128]{1,0:T(8,128)S(1)} %get-tuple-element.92.first), channel_id=1, source_target_pairs={{0,192},{64,0},{128,64},{192,128},{1,193},{65,1},{129,65},{193,129... | collective-permute-start | bytes 12296 | tf_op jit(solution)/shard_map/ppermute | solution.py:26
  94.0 4.0 %collective-permute-start.20 = (f32[8,128]{1,0:T(8,128)S(1)}, f32[8,128]{1,0:T(8,128)S(1)}, u32[]{:S(2)}, u32[]{:S(2)}) collective-permute-start(f32[8,128]{1,0:T(8,128)S(1)} %get-tuple-element.92.first), channel_id=1, source_target_pairs={{0,128},{64,192},{128,0},{192,64},{1,129},{65,193},{129,1},{193,65... | collective-permute-start | bytes 12296 | tf_op jit(solution)/shard_map/ppermute | solution.py:26
  95.4 4.0 %collective-permute-start.19 = (f32[8,128]{1,0:T(8,128)S(1)}, f32[8,128]{1,0:T(8,128)S(1)}, u32[]{:S(2)}, u32[]{:S(2)}) collective-permute-start(f32[8,128]{1,0:T(8,128)S(1)} %get-tuple-element.92.first), channel_id=1, source_target_pairs={{0,64},{64,128},{128,192},{192,0},{1,65},{65,129},{129,193},{193,1... | collective-permute-start | bytes 12296 | tf_op jit(solution)/shard_map/ppermute | solution.py:26
  100.8 25.8 %all-to-all-start.1 = ((bf16[64,16,256]{2,1,0:T(8,128)(2,1)}), bf16[64,16,256]{2,1,0:T(8,128)(2,1)S(1)}, u32[]{:S(2)}, u32[]{:S(2)}) async-start(bf16[64,16,256]{2,1,0:T(8,128)(2,1)} %bitcast.19), calls=%async_computation.1 | async-start | bytes 1048576 | tf_op jit(solution)/shard_map/all_to_all | solution.py:354
  (12 other events, 34.6 us)

commit v5 on v4

--- a/solution.py
+++ b/solution.py
@@ -45,43 +45,113 @@
 
 
 def inside(bounds, block, rows, cols):
-    row = lax.broadcasted_iota(jnp.int32, (rows, cols), 0) + lax.axis_index("own") * rows
-    col = lax.broadcasted_iota(jnp.int32, (rows, cols), 1) + lax.axis_index("grp") * cols
     row_off, col_off, n_rows, n_cols = [bounds[4 * block + i] for i in range(4)]
+    row, col = lax.axis_index("own") * rows, lax.axis_index("grp") * cols
     return (row < n_rows - row_off) & (col < n_cols - col_off)
 
 
-def gather_kernel(place, own, up_direct, down_direct, out):
-    half = own.shape[1]
+def split_kernel(cuts, part, *refs):
+    outs, sems = refs[: len(cuts)], refs[len(cuts)]
+    quarter = outs[0].shape[2]
+    copies = []
+    for i, ((first, step), out) in enumerate(zip(cuts, outs)):
+        col = ((lax.axis_index("grp") + step) & 3) * quarter
+        source = part.at[0, pl.ds(first, out.shape[0]), :, pl.ds(pl.multiple_of(col, quarter), quarter)]
+        copies.append(pltpu.make_async_copy(source, out, sems.at[i]))
+    for copy in copies:
+        copy.start()
+    for copy in copies:
+        copy.wait()
+
+
+def split(part, cuts, quarter):
+    rows = part.shape[2]
+    return pl.pallas_call(
+        functools.partial(split_kernel, tuple((first, step) for first, _, step in cuts)),
+        out_shape=tuple(
+            pltpu.HBM((count, rows, quarter), BF16) for _, count, _ in cuts
+        ),
+        in_specs=[pl.BlockSpec(memory_space=pl.ANY)],
+        out_specs=(pl.BlockSpec(memory_space=pl.ANY),) * len(cuts),
+        scratch_shapes=[pltpu.SemaphoreType.DMA((len(cuts),))],
+        compiler_params=pltpu.CompilerParams(vmem_limit_bytes=2 * MIB),
+    )(in_hbm(part))
+
+
+def add_kernel(up, far_up, down, far_down, up_out, down_out):
+    up_out[...] = (up[...].astype(F32) + far_up[...].astype(F32)).astype(BF16)
+    down_out[...] = (down[...].astype(F32) + far_down[...].astype(F32)).astype(BF16)
+
+
+def add(*arrays):
+    shape = jax.ShapeDtypeStruct(arrays[0].shape, BF16)
+    return pl.pallas_call(
+        add_kernel,
+        out_shape=(shape, shape),
+        in_specs=[pl.BlockSpec(memory_space=VMEM)] * 4,
+        out_specs=(pl.BlockSpec(memory_space=VMEM),) * 2,
+        compiler_params=pltpu.CompilerParams(vmem_limit_bytes=4 * MIB),
+    )(*arrays)
+
+
+def roots_kernel(left, right, up, down, own):
+    _, units, _, cols = (1, *up.shape)
+    rows = up.shape[1]
+
+    def root(half, step):
+        col = ((lax.axis_index("grp") + step) & 3) * cols
+        col = pl.ds(pl.multiple_of(col, cols), cols)
+        return right[0, pl.ds(half * rows, rows), col].astype(BF16)
+
+    for half in range(2):
+        own[half] = root(half, 0)
+        up[9 + half] = root(half, 1)
+        down[9 + half] = root(half, 3)
+        for c in range(4):
+            unit = left[0, pl.ds(half * rows, rows), pl.ds(c * cols, cols)].astype(BF16)
+            up[5 * half + c] = unit
+            down[5 - 5 * half + c] = unit
+    up[4] = root(0, 2)
+    down[4] = root(1, 2)
+
+
+def root_pieces(left, right):
+    _, rows, width = left.shape
+    unit = (rows // 2, width // 4)
+    return pl.pallas_call(
+        roots_kernel,
+        out_shape=(
+            pltpu.HBM((11, *unit), BF16),
+            pltpu.HBM((11, *unit), BF16),
+            pltpu.HBM((2, *unit), BF16),
+        ),
+        grid=(1,),
+        in_specs=[pl.BlockSpec(left.shape, lambda i: (0, 0, 0))] * 2,
+        out_specs=tuple(pl.BlockSpec((n, *unit), lambda i: (0, 0, 0)) for n in (11, 11, 2)),
+        compiler_params=pltpu.CompilerParams(vmem_limit_bytes=8 * MIB),
+    )(in_hbm(left), in_hbm(right))
+
+
+def gather_kernel(own, up_direct, down_direct, out):
+    half = up_direct.shape[0]
 
     def step(i, carry):
-        out[0, i] = own[0, i].astype(F32) + down_direct[i].astype(F32)
-        out[1, i] = own[1, i].astype(F32) + up_direct[i].astype(F32)
+        out[0, i] = own[i].astype(F32) + down_direct[i].astype(F32)
+        out[1, i] = own[i + half].astype(F32) + up_direct[i].astype(F32)
         return carry
 
     lax.fori_loop(0, half, step, 0, unroll=4)
 
 
-def gather(place, part, up_direct, down_direct):
-    blocks, rows, width = part.shape
-    half, cols = blocks // 2, up_direct.shape[2]
-    whole = pl.BlockSpec(up_direct.shape, lambda i, *_: (0, 0, 0))
+def gather(own, up_direct, down_direct):
     return pl.pallas_call(
         gather_kernel,
-        out_shape=jax.ShapeDtypeStruct((2, half, rows, cols), F32),
-        grid_spec=pltpu.PrefetchScalarGridSpec(
-            num_scalar_prefetch=1,
-            grid=(1,),
-            in_specs=[
-                pl.BlockSpec((2, half, rows, cols), lambda i, place: (0, 0, 0, place[0])),
-                whole,
-                whole,
-            ],
-            out_specs=pl.BlockSpec((2, half, rows, cols), lambda i, *_: (0, 0, 0, 0)),
-        ),
-        compiler_params=pltpu.CompilerParams(vmem_limit_bytes=8 * MIB),
+        out_shape=jax.ShapeDtypeStruct((2, *up_direct.shape), F32),
+        in_specs=[pl.BlockSpec(memory_space=VMEM)] * 3,
+        out_specs=pl.BlockSpec(memory_space=VMEM),
+        compiler_params=pltpu.CompilerParams(vmem_limit_bytes=6 * MIB),
         cost_estimate=LONG,
-    )(place, part.reshape(2, half, rows, width), up_direct, down_direct)
+    )(own, up_direct, down_direct)
 
 
 def pack_kernel(
@@ -94,16 +164,17 @@
 
     def one(side, i, value):
         block = side * half + begin + i
-        ok = inside(bounds, block, rows, cols)
-        grad = jnp.where(ok, value, 0.0)
+        keep = jnp.where(inside(bounds, block, rows, cols), 1.0, 0.0)
+        grad = value * keep
         first_next = BETA_FIRST * first[side, i] + (1.0 - BETA_FIRST) * grad
         second_next = BETA_SECOND * second[side, i] + (1.0 - BETA_SECOND) * grad * grad
         first_out[side, i] = first_next
         second_out[side, i] = second_next
-        adam = first_next / (jnp.sqrt(second_next) + ADAM_EPS * BIAS_SECOND**0.5)
-        square = jnp.where(ok, adam * adam, 0.0)
+        root = second_next * lax.rsqrt(second_next)
+        adam = first_next * pl.reciprocal(root + ADAM_EPS * BIAS_SECOND**0.5)
+        square = adam * adam
         square = square[:, :lanes] + square[:, lanes:]
-        square = square[: rows // 2] + square[rows // 2 :]
+        square = (square[: rows // 2] + square[rows // 2 :]) * keep
         piece = jnp.concatenate([grad[:, :lanes], grad[:, lanes:], square], axis=0)
         out[key[block]] = piece.astype(BF16)
 
@@ -155,18 +226,17 @@
     return out, first_next.reshape(first.shape), second_next.reshape(second.shape)
 
 
-def relay_kernel(prev, following, low, high):
-    rows = low.shape[0]
-    low[...] = prev[pl.ds(0, rows), :]
-    high[...] = following[pl.ds(rows, rows), :]
+def relay_kernel(prev, following, up, down):
+    units = up.shape[0]
+    up[...] = prev[pl.ds(0, units)]
+    down[...] = following[pl.ds(0, units)]
 
 
 def relay(prev, following):
-    rows, width = prev.shape
-    half = jax.ShapeDtypeStruct((rows // 2, width), BF16)
+    shape = jax.ShapeDtypeStruct((5, *prev.shape[1:]), BF16)
     return pl.pallas_call(
         relay_kernel,
-        out_shape=(half, half),
+        out_shape=(shape, shape),
         in_specs=[pl.BlockSpec(memory_space=VMEM)] * 2,
         out_specs=(pl.BlockSpec(memory_space=VMEM),) * 2,
         compiler_params=pltpu.CompilerParams(vmem_limit_bytes=6 * MIB),
@@ -179,10 +249,10 @@
 
     def step(block, carry):
         ok = inside(bounds, block, rows, cols)
-        out[block] = jnp.where(ok, back[key[block]].astype(F32), 0.0).astype(BF16)
+        out[block] = jnp.where(ok, back[key[block]], jnp.zeros((), BF16))
         return carry
 
-    lax.fori_loop(0, blocks, step, 0, unroll=4)
+    lax.fori_loop(0, blocks, step, 0, unroll=8)
 
 
 def finish(key, bounds, back):
@@ -199,48 +269,73 @@
 
 def precond_kernel(*refs):
     own_low, own_high, next_low, next_high, far_low, far_high, prev_low, prev_high = refs[:8]
-    roots, lefts, (adam, out, norms, mixed) = refs[8:12], refs[12:17], refs[17:]
+    adam, sources, (out, norms) = refs[8], refs[9:15], refs[15:17]
+    mixed, held, sems = refs[17], refs[18:24], refs[24]
     width, quarter = out.shape
     half = width // 2
     me = lax.axis_index("grp")
     n = width // quarter
+    copies = [pltpu.make_async_copy(*args) for args in zip(sources, held, [sems.at[i] for i in range(6)])]
+    for copy in copies:
+        copy.start()
+    root, up, up_prev, down_next, up_far, down_far = held
+    for copy in copies:
+        copy.wait()
+
+    def joined(low, high):
+        return jnp.concatenate([low, high], axis=0)
+
+    roots = (
+        joined(root[0], root[1]),
+        joined(down_next[9], down_next[10]),
+        joined(up_far[4], down_far[4]),
+        joined(up_prev[9], up_prev[10]),
+    )
     for top, parts in (
         (0, (own_low, next_low, far_low, prev_low)),
         (half, (own_high, next_high, far_high, prev_high)),
     ):
         for row in range(0, half, quarter):
             total = jnp.zeros((quarter, quarter), F32)
-            for piece, root in zip(parts, roots):
-                total += dot(piece[pl.ds(row, quarter), :], root[...], ((1,), (0,)))
+            for piece, right in zip(parts, roots):
+                total += dot(piece[pl.ds(row, quarter), :], right, ((1,), (0,)))
             mixed[pl.ds(top + row, quarter), :] = total.astype(BF16)
     square = jnp.zeros((8, quarter), F32)
-    eighth = quarter // 2
-    places = ((0, 0), (1, 0), (2, 0), (2, eighth), (3, 0))
-    for (step, extra), left in zip(places, lefts):
-        base = lax.rem(me + step, n) * quarter + extra
-        rows = left.shape[0]
-        value = dot(left[...], mixed[...], ((1,), (0,)))
-        out[pl.ds(pl.multiple_of(base, eighth), rows), :] = value
-        square += jnp.sum((value * value).reshape(rows // 8, 8, quarter), axis=0)
+    for step, (low, first), (high, second) in (
+        (0, (up, 0), (up, 5)),
+        (1, (down_next, 5), (down_next, 0)),
+        (2, (up_far, 0), (down_far, 0)),
+        (3, (up_prev, 0), (up_prev, 5)),
+    ):
+        left = jnp.concatenate([joined(low[first + c], high[second + c]) for c in range(n)], axis=1)
+        value = dot(left, mixed[...], ((1,), (0,)))
+        base = ((me + step) & (n - 1)) * quarter
+        out[pl.ds(pl.multiple_of(base, quarter), quarter), :] = value
+        square += jnp.sum((value * value).reshape(quarter // 8, 8, quarter), axis=0)
     norms[...] = jnp.zeros_like(norms)
     norms[0:1, :] = jnp.broadcast_to(jnp.sum(square), (1, 128))
     norms[1:2, :] = jnp.broadcast_to(jnp.sum(adam[...].astype(F32)), (1, 128))
 
 
-def precondition(pieces, roots, lefts, adam):
+def precondition(pieces, adam, sources):
     rows, quarter = pieces[0].shape
-    operands = (*pieces, *map(in_hbm, roots), *map(in_hbm, lefts), adam)
+    operands = (*pieces, adam)
     return pl.pallas_call(
         precond_kernel,
         out_shape=(
             jax.ShapeDtypeStruct((2 * rows, quarter), F32),
             jax.ShapeDtypeStruct((8, 128), F32),
         ),
-        in_specs=[pl.BlockSpec(memory_space=VMEM)] * len(operands),
+        in_specs=[pl.BlockSpec(memory_space=VMEM)] * len(operands)
+        + [pl.BlockSpec(memory_space=pl.ANY)] * len(sources),
         out_specs=(pl.BlockSpec(memory_space=VMEM),) * 2,
-        scratch_shapes=[VMEM((2 * rows, quarter), BF16)],
-        compiler_params=pltpu.CompilerParams(vmem_limit_bytes=12 * MIB),
-    )(*operands)
+        scratch_shapes=[
+            VMEM((2 * rows, quarter), BF16),
+            *[VMEM(source.shape, BF16) for source in sources],
+            pltpu.SemaphoreType.DMA((len(sources),)),
+        ],
+        compiler_params=pltpu.CompilerParams(vmem_limit_bytes=14 * MIB),
+    )(*operands, *map(in_hbm, sources))
 
 
 def graft_kernel(cells, precond, first, second, third, fourth, out):
@@ -288,49 +383,46 @@
     width = grad_parts.shape[3]
     quarter = width // n_grp
     half = total_blocks // 2
-    part = grad_parts[0]
-    place = grp_index.reshape(1).astype(jnp.int32)
-    starts = [((grp_index + step) & (n_grp - 1)) * quarter for step in range(4)]
     turn = ((n_grp - grp_index) & (n_grp - 1)) * quarter
-    part, place, starts, turn = lax.optimization_barrier((part, place, starts, turn))
-
-    def columns(array, step):
-        return slice_at(array, starts[step], quarter, array.ndim - 1)
-
-    far = columns(part, 2)
-    up = columns(part, 1)
-    down = columns(part, 3)
-    far_up = shift(far[:half], 1)
-    far_down = shift(far[half:], -1)
-    up_direct = shift(up[half:], 1)
-    down_direct = shift(down[:half], -1)
-    up_sum = shift((up[:half].astype(F32) + far_up.astype(F32)).astype(BF16), 1)
-    down_sum = shift((down[half:].astype(F32) + far_down.astype(F32)).astype(BF16), -1)
+    first_row = grp_index * quarter
+    grad_parts, turn, first_row = lax.optimization_barrier((grad_parts, turn, first_row))
+
+    far_low, far_high = split(grad_parts, ((0, half, 2), (half, half, 2)), quarter)
+    far_up = shift(far_low, 1)
+    far_down = shift(far_high, -1)
+    later, _, _ = lax.optimization_barrier((grad_parts, far_low, far_high))
+    up_low, up_high, down_low, down_high, own = split(
+        later,
+        ((0, half, 1), (half, half, 1), (0, half, 3), (half, half, 3), (0, total_blocks, 0)),
+        quarter,
+    )
+    up_direct = shift(up_high, 1)
+    down_direct = shift(down_low, -1)
+    up_sum, down_sum = add(up_low, far_up, down_high, far_down)
+    up_sum = shift(up_sum, 1)
+    down_sum = shift(down_sum, -1)
     key, bounds = slots_of(assign, n_own, per_owner), block_bounds.reshape(-1)
-    up_direct, down_direct, key, bounds = lax.optimization_barrier(
-        (up_direct, down_direct, key, bounds)
-    )
-    partial = gather(place, part, up_direct, down_direct)
-
-    left_bf, right_bf = left_root[0].astype(BF16), right_root[0].astype(BF16)
-    right_parts = [columns(right_bf, step) for step in range(4)]
-    left_bf, right_parts, up_sum, down_sum, partial = lax.optimization_barrier(
-        (left_bf, right_parts, up_sum, down_sum, partial)
+    left_root, right_root, _, _ = lax.optimization_barrier((left_root, right_root, far_low, far_high))
+    roots_up, roots_down, root_own = root_pieces(left_root, right_root)
+    up_direct, down_direct, key, bounds, roots_up, roots_down, root_own = lax.optimization_barrier(
+        (up_direct, down_direct, key, bounds, roots_up, roots_down, root_own)
+    )
+    partial = gather(own, up_direct, down_direct)
+
+    roots_up, roots_down, up_sum, down_sum, partial = lax.optimization_barrier(
+        (roots_up, roots_down, up_sum, down_sum, partial)
     )
     sorted_grad, first_next, second_next = pack(
         key, bounds, partial, up_sum, down_sum, first_moment, second_moment
     )
     owned = lax.all_to_all(sorted_grad, "own", split_axis=0, concat_axis=0, tiled=True)
-    left_prev = shift(left_bf, 1)
-    left_next = shift(left_bf, -1)
-    far_halves = relay(left_prev, left_next)
-    left_far_low = shift(far_halves[0], 1)
-    left_far_high = shift(far_halves[1], -1)
-    right_parts, far_halves = lax.optimization_barrier((right_parts, far_halves))
-    roots = [right_parts[0]] + [shift(right_parts[step], step) for step in (3, 2, 1)]
-    lefts = [left_bf, left_next, left_far_low, left_far_high, left_prev]
-
-    owned, lefts, roots = lax.optimization_barrier((owned, lefts, roots))
+    roots_prev = shift(roots_up, 1)
+    roots_next = shift(roots_down, -1)
+    onward = relay(roots_prev, roots_next)
+    far_roots = [shift(onward[0], 1), shift(onward[1], -1)]
+    roots = [root_own, roots_up, roots_prev, roots_next, *far_roots]
+
+    owned, roots = lax.optimization_barrier((owned, roots))
     own_cols = jnp.concatenate(
         [owned[:, :shard_rows], owned[:, shard_rows : 2 * shard_rows]], axis=2
     )
@@ -344,7 +436,7 @@
     far_high = shift(next_high, -1)
     pieces = [low, high, next_low, next_high, far_low, far_high, prev_low, prev_high]
     flat = [piece.reshape(width // 2, quarter) for piece in pieces]
-    precond, norms = precondition(flat, roots, lefts, adam)
+    precond, norms = precondition(flat, adam, roots)
     norms = [norms] + [shift(norms, step) for step in (1, 2, 3)]
     grafted = graft(precond, norms).reshape(n_own, shard_rows, quarter)
     pieces, grafted, assign, bounds = lax.optimization_barrier(
@@ -356,7 +448,7 @@
     whole = jnp.concatenate(
         [jnp.concatenate(pieces[i : i + 2], axis=0) for i in (0, 2, 4, 6)], axis=2
     ).reshape(width, width)
-    rows = slice_at(whole, starts[0], quarter, 0)
+    rows = slice_at(whole, first_row, quarter, 0)
     left_acc = STAT_DECAY * left_stat + dot(rows, whole, ((1,), (1,)))[None]
     cross = dot(whole[:, :quarter], whole, ((0,), (0,)))
     cross = jnp.concatenate([cross, cross], axis=1)

time: 129 us -> 189 us (1.47)
  Pallas kernels: 11.9 us -> 81.2 us
  waiting for transfers between devices: 49.6 us -> 44.2 us
  local copies, waits for them, and re-layouts: 7.16 us -> 3.48 us
  other arithmetic: 7.73 us -> 4.63 us
  starting transfers between devices: 46.7 us -> 49.4 us
    pallas_call x2 -> x6, Pallas kernels: 0.24 us -> 69.7 us  [the longest x2 65.8 us: split(): pl.pallas_call(functools.partial(split_kernel, tuple(((first, step) for f...]
    ppermute x22 -> x19, waiting for transfers between devices: 36.6 us -> 27.7 us  [shift(): return lax.ppermute(array, 'grp', [(i, (i + step) % n) for i in range(n)])]
    all_to_all x1, waiting for transfers between devices: 4.78 us -> 8.29 us  [on_device(): lax.all_to_all(sorted_grad, 'own', split_axis=0, concat_axis=0, tiled=True)]
    ppermute x22 -> x19, starting transfers between devices: 22.3 us -> 25.5 us  [shift(): return lax.ppermute(array, 'grp', [(i, (i + step) % n) for i in range(n)])]
    convert_element_type x3 -> x0, other arithmetic: 3.08 us -> none  [the longest x1 2.14 us: on_device(): (down[half:].astype(F32) + far_down.astype(F32)).astype(BF16)]
    slice x1 -> x0, local copies, waits for them, and re-layouts: 2.77 us -> none  [on_device(): far_down = shift(far[half:], -1)]
  transfers between devices with their start and end apart: 24 -> 21, of which waited for: 16 -> 11; matrix products, arithmetic and copies ran while one was open for 11% -> 5% of each run, Pallas kernels for 4% -> 31%
where the time goes in v5:
time: 189 us; the launch traced here: 188 us
  Pallas kernels  81.2 us (43%)
  starting transfers between devices  49.4 us (26%)
  waiting for transfers between devices  44.2 us (23%)
  other arithmetic  4.63 us (2%)
  matrix products  4.25 us (2%)
  local copies, waits for them, and re-layouts  3.48 us (2%)
    pallas_call x2, Pallas kernels, split(): pl.pallas_call(functools.partial(split_kernel, tuple(((first, step) for f...  65.8 us
    ppermute x19, waiting for transfers between devices, shift(): return lax.ppermute(array, 'grp', [(i, (i + step) % n) for i in range(n)])  27.7 us
    ppermute x19, starting transfers between devices, shift(): return lax.ppermute(array, 'grp', [(i, (i + step) % n) for i in range(n)])  25.5 us
    all_to_all x1, starting transfers between devices, on_device(): lax.all_to_all(sorted_grad, 'own', split_axis=0, concat_axis=0, tiled=True)  15.4 us
    all_to_all x1, starting transfers between devices, on_device(): lax.all_to_all(grafted, 'own', split_axis=0, concat_axis=0, tiled=True)  8.48 us
    all_to_all x1, waiting for transfers between devices, on_device(): lax.all_to_all(sorted_grad, 'own', split_axis=0, concat_axis=0, tiled=True)  8.29 us
    all_to_all x1, waiting for transfers between devices, on_device(): lax.all_to_all(grafted, 'own', split_axis=0, concat_axis=0, tiled=True)  8.25 us
    pallas_call x1, Pallas kernels, pack(): pl.pallas_call(pack_kernel, out_shape=(pltpu.HBM((blocks, piece, 128), BF...  5.05 us
  transfers between devices with their start and end apart: 21, of which 11 were waited for; matrix products, arithmetic and copies ran while one was open for 5% of the time, Pallas kernels for 31%

profile of v5, /device:TPU:1, one launch (start us, length us, event | category | flops | bytes accessed | tf_op | source)
XLA Modules:
  0.0 188.1 jit_solution(5132318226213716673)
XLA Ops:
  0.6 17.0 %shard_map.128 = (bf16[32,16,256]{2,1,0:T(8,128)(2,1)}, bf16[32,16,256]{2,1,0:T(8,128)(2,1)}) custom-call(bf16[1,64,16,1024]{3,2,1,0:T(8,128)(2,1)} %part.1), custom_call_target="tpu_custom_call" | custom-call | tf_op jit(solution)/shard_map/pallas_call | solution.py:69
  17.7 2.2 %collective-permute-start.2 = (bf16[32,16,256]{2,1,0:T(8,128)(2,1)}, bf16[32,16,256]{2,1,0:T(8,128)(2,1)S(1)}, u32[]{:S(2)}, u32[]{:S(2)}) collective-permute-start(bf16[32,16,256]{2,1,0:T(8,128)(2,1)} %get-tuple-element.61), channel_id=1, source_target_pairs={{0,64},{64,128},{128,192},{192,0},{1,65},{65,129},{129,193},{193,1... | collective-permute-start | bytes 786440 | tf_op jit(solution)/shard_map/ppermute | solution.py:26
  19.9 1.5 collective-permute-start.3
  21.4 48.8 %shard_map.129 = (bf16[32,16,256]{2,1,0:T(8,128)(2,1)}, bf16[32,16,256]{2,1,0:T(8,128)(2,1)}, bf16[32,16,256]{2,1,0:T(8,128)(2,1)}, bf16[32,16,256]{2,1,0:T(8,128)(2,1)}, bf16[64,16,256]{2,1,0:T(8,128)(2,1)}) custom-call(bf16[1,64,16,1024]{3,2,1,0:T(8,128)(2,1)} %part.1), custom_call_target="tpu_custom_call" | custom-call | tf_op jit(solution)/shard_map/pallas_call | solution.py:69
  70.3 2.7 %collective-permute-start.1 = (bf16[32,16,256]{2,1,0:T(8,128)(2,1)}, bf16[32,16,256]{2,1,0:T(8,128)(2,1)S(1)}, u32[]{:S(2)}, u32[]{:S(2)}) collective-permute-start(bf16[32,16,256]{2,1,0:T(8,128)(2,1)} %get-tuple-element.65), channel_id=1, source_target_pairs={{0,192},{64,0},{128,64},{192,128},{1,193},{65,1},{129,65},{193,129... | collective-permute-start | bytes 786440 | tf_op jit(solution)/shard_map/ppermute | solution.py:26
  73.2 2.8 %shard_map.130 = (bf16[11,128,256]{2,1,0:T(8,128)(2,1)}, bf16[11,128,256]{2,1,0:T(8,128)(2,1)}, bf16[2,128,256]{2,1,0:T(8,128)(2,1)}) custom-call(f32[1,256,1024]{2,1,0:T(8,128)} %left, f32[1,256,1024]{2,1,0:T(8,128)} %right), custom_call_target="tpu_custom_call" | custom-call | tf_op jit(solution)/shard_map/pallas_call | solution.py:121
  77.0 2.7 %collective-permute-start.5 = (bf16[32,16,256]{2,1,0:T(8,128)(2,1)}, bf16[32,16,256]{2,1,0:T(8,128)(2,1)}, u32[]{:S(2)}, u32[]{:S(2)}) collective-permute-start(bf16[32,16,256]{2,1,0:T(8,128)(2,1)} %get-tuple-element.78), channel_id=1, source_target_pairs={{0,192},{64,0},{128,64},{192,128},{1,193},{65,1},{129,65},{193,129... | collective-permute-start | bytes 786440 | tf_op jit(solution)/shard_map/ppermute | solution.py:26
  79.8 3.9 %collective-permute-done.4.up_sum = bf16[32,16,256]{2,1,0:T(8,128)(2,1)} collective-permute-done((bf16[32,16,256]{2,1,0:T(8,128)(2,1)}, bf16[32,16,256]{2,1,0:T(8,128)(2,1)}, u32[]{:S(2)}, u32[]{:S(2)}) %collective-permute-start.4) | collective-permute-done | bytes 262176 | tf_op jit(solution)/shard_map/ppermute | solution.py:26
  83.7 2.7 %collective-permute-start.7 = (bf16[11,128,256]{2,1,0:T(8,128)(2,1)S(1)}, bf16[11,128,256]{2,1,0:T(8,128)(2,1)S(1)}, u32[]{:S(2)}, u32[]{:S(2)}) collective-permute-start(bf16[11,128,256]{2,1,0:T(8,128)(2,1)S(1)} %copy-done.12), channel_id=1, source_target_pairs={{0,192},{64,0},{128,64},{192,128},{1,193},{65,1},{129,65},{193,129... | collective-permute-start | bytes 2162696 | tf_op jit(solution)/shard_map/ppermute | solution.py:26
  86.4 5.1 %shard_map.133 = (bf16[64,40,128]{2,1,0:T(8,128)(2,1)}, f32[2,32,16,256]{3,2,1,0:T(8,128)}, f32[2,32,16,256]{3,2,1,0:T(8,128)}) custom-call(s32[64]{0:T(128)S(1)} %fusion.9.key, s32[256]{0:T(256)S(1)} %reshape.61.bounds, f32[2,32,16,256]{3,2,1,0:T(8,128)S(1)} %shard_map.132.partial, bf16[32,16,256]{2,1,0:T(8,128)(2,1)} %collective-permute-done.4.up_sum, ...), custom_call_target="tpu_custom_call" | custom-call | tf_op jit(solution)/shard_map/pallas_call | solution.py:197
  91.4 15.4 %all-to-all-start = ((bf16[64,40,128]{2,1,0:T(8,128)(2,1)}), bf16[64,40,128]{2,1,0:T(8,128)(2,1)}, u32[]{:S(2)}, u32[]{:S(2)}) async-start(bf16[64,40,128]{2,1,0:T(8,128)(2,1)} %get-tuple-element.85), calls=%async_computation | async-start | bytes 1310720 | tf_op jit(solution)/shard_map/all_to_all | solution.py:418
  108.0 3.0 %collective-permute-start.9 = (bf16[5,128,256]{2,1,0:T(8,128)(2,1)S(1)}, bf16[5,128,256]{2,1,0:T(8,128)(2,1)S(1)}, u32[]{:S(2)}, u32[]{:S(2)}) collective-permute-start(bf16[5,128,256]{2,1,0:T(8,128)(2,1)S(1)} %get-tuple-element.90), channel_id=1, source_target_pairs={{0,192},{64,0},{128,64},{192,128},{1,193},{65,1},{129,65},{193,129... | collective-permute-start | bytes 983048 | tf_op jit(solution)/shard_map/ppermute | solution.py:26
  110.9 7.7 %collective-permute-done.8.refs_13_ = bf16[5,128,256]{2,1,0:T(8,128)(2,1)S(1)} collective-permute-done((bf16[5,128,256]{2,1,0:T(8,128)(2,1)S(1)}, bf16[5,128,256]{2,1,0:T(8,128)(2,1)S(1)}, u32[]{:S(2)}, u32[]{:S(2)}) %collective-permute-start.8) | collective-permute-done | bytes 327712 | tf_op jit(solution)/shard_map/ppermute | solution.py:26
  118.7 8.3 %all-to-all-done = bf16[64,40,128]{2,1,0:T(8,128)(2,1)} async-done(((bf16[64,40,128]{2,1,0:T(8,128)(2,1)}), bf16[64,40,128]{2,1,0:T(8,128)(2,1)}, u32[]{:S(2)}, u32[]{:S(2)}) %all-to-all-start) | async-done | bytes 655392 | tf_op jit(solution)/shard_map/all_to_all | solution.py:418
  127.0 1.1 fusion.11
  128.1 3.0 %collective-permute-start.11 = (bf16[32,16,256]{2,1,0:T(8,128)(2,1)S(1)}, bf16[32,16,256]{2,1,0:T(8,128)(2,1)S(1)}, u32[]{:S(2)}, u32[]{:S(2)}) collective-permute-start(bf16[32,16,256]{2,1,0:T(8,128)(2,1)S(1)} %get-tuple-element.106), channel_id=1, source_target_pairs={{0,192},{64,0},{128,64},{192,128},{1,193},{65,1},{129,65},{193,129... | collective-permute-start | bytes 786440 | tf_op jit(solution)/shard_map/ppermute | solution.py:26
  131.1 2.7 %collective-permute-start.10 = (bf16[32,16,256]{2,1,0:T(8,128)(2,1)S(1)}, bf16[32,16,256]{2,1,0:T(8,128)(2,1)S(1)}, u32[]{:S(2)}, u32[]{:S(2)}) collective-permute-start(bf16[32,16,256]{2,1,0:T(8,128)(2,1)S(1)} %get-tuple-element.105), channel_id=1, source_target_pairs={{0,192},{64,0},{128,64},{192,128},{1,193},{65,1},{129,65},{193,129... | collective-permute-start | bytes 786440 | tf_op jit(solution)/shard_map/ppermute | solution.py:26
  133.8 2.7 %collective-permute-done.11 = bf16[32,16,256]{2,1,0:T(8,128)(2,1)S(1)} collective-permute-done((bf16[32,16,256]{2,1,0:T(8,128)(2,1)S(1)}, bf16[32,16,256]{2,1,0:T(8,128)(2,1)S(1)}, u32[]{:S(2)}, u32[]{:S(2)}) %collective-permute-start.11) | collective-permute-done | bytes 262176 | tf_op jit(solution)/shard_map/ppermute | solution.py:26
  136.5 3.4 %collective-permute-start.14 = (bf16[32,16,256]{2,1,0:T(8,128)(2,1)S(1)}, bf16[32,16,256]{2,1,0:T(8,128)(2,1)S(1)}, u32[]{:S(2)}, u32[]{:S(2)}) collective-permute-start(bf16[32,16,256]{2,1,0:T(8,128)(2,1)S(1)} %collective-permute-done.11), channel_id=1, source_target_pairs={{0,192},{64,0},{128,64},{192,128},{1,193},{65,1},{129,65},{193,129... | collective-permute-start | bytes 786440 | tf_op jit(solution)/shard_map/ppermute | solution.py:26
  140.9 4.4 %collective-permute-done.15 = bf16[32,16,256]{2,1,0:T(8,128)(2,1)S(1)} collective-permute-done((bf16[32,16,256]{2,1,0:T(8,128)(2,1)S(1)}, bf16[32,16,256]{2,1,0:T(8,128)(2,1)S(1)}, u32[]{:S(2)}, u32[]{:S(2)}) %collective-permute-start.15) | collective-permute-done | bytes 262176 | tf_op jit(solution)/shard_map/ppermute | solution.py:26
  145.3 2.5 %collective-permute-done.14 = bf16[32,16,256]{2,1,0:T(8,128)(2,1)S(1)} collective-permute-done((bf16[32,16,256]{2,1,0:T(8,128)(2,1)S(1)}, bf16[32,16,256]{2,1,0:T(8,128)(2,1)S(1)}, u32[]{:S(2)}, u32[]{:S(2)}) %collective-permute-start.14) | collective-permute-done | bytes 262176 | tf_op jit(solution)/shard_map/ppermute | solution.py:26
  147.8 3.1 %collective-permute-done.13 = bf16[32,16,256]{2,1,0:T(8,128)(2,1)S(1)} collective-permute-done((bf16[32,16,256]{2,1,0:T(8,128)(2,1)S(1)}, bf16[32,16,256]{2,1,0:T(8,128)(2,1)S(1)}, u32[]{:S(2)}, u32[]{:S(2)}) %collective-permute-start.13) | collective-permute-done | bytes 262176 | tf_op jit(solution)/shard_map/ppermute | solution.py:26
  150.9 3.2 %shard_map.135 = (f32[1024,256]{1,0:T(8,128)S(1)}, f32[8,128]{1,0:T(8,128)S(1)}) custom-call(bf16[512,256]{1,0:T(8,128)(2,1)S(1)} %bitcast.27, bf16[512,256]{1,0:T(8,128)(2,1)S(1)} %bitcast.26, bf16[512,256]{1,0:T(8,128)(2,1)S(1)} %bitcast.31, bf16[512,256]{1,0:T(8,128)(2,1)S(1)} %bitcast.28, bf16[512,256]{1,0:T(8,128)(2,1)S(1)} %bitcast.33, ...), custom_call_target="tpu_custom_call" | custom-call | tf_op jit(solution)/shard_map/pallas_call | solution.py:323
  156.6 1.8 collective-permute-done.17.third
  159.0 1.4 shard_map.136
  160.5 8.5 %all-to-all-start.1 = ((bf16[64,16,256]{2,1,0:T(8,128)(2,1)}), bf16[64,16,256]{2,1,0:T(8,128)(2,1)S(1)}, u32[]{:S(2)}, u32[]{:S(2)}) async-start(bf16[64,16,256]{2,1,0:T(8,128)(2,1)} %bitcast.11), calls=%async_computation.1 | async-start | bytes 1048576 | tf_op jit(solution)/shard_map/all_to_all | solution.py:446
  169.0 1.5 maximum_maximum_fusion
  170.7 2.5 %fusion.4 = f32[256,1024]{1,0:T(8,128)S(1)} fusion(bf16[1024,1024]{1,0:T(8,128)(2,1)} %bitcast.34), kind=kOutput, calls=%fused_computation.8 | convolution fusion | flops 536870912 | bytes 3670016 | tf_op jit(solution)/shard_map/dot_general | solution.py:44
  173.3 3.0 %fusion.3 = f32[1,256,1024]{2,1,0:T(8,128)} fusion(s32[]{:T(128)S(6)} %mul.12, f32[256,1024]{1,0:T(8,128)S(1)} %fusion.4, f32[1,256,1024]{2,1,0:T(8,128)} %param.15), kind=kLoop, calls=%fused_computation.7 | loop fusion | flops 786432 | bytes 3145732 | tf_op jit(solution)/shard_map/add | solution.py:456
  176.3 1.7 fusion
  178.0 8.2 %all-to-all-done.1.back = bf16[64,16,256]{2,1,0:T(8,128)(2,1)S(1)} async-done(((bf16[64,16,256]{2,1,0:T(8,128)(2,1)}), bf16[64,16,256]{2,1,0:T(8,128)(2,1)S(1)}, u32[]{:S(2)}, u32[]{:S(2)}) %all-to-all-start.1) | async-done | bytes 524320 | tf_op jit(solution)/shard_map/all_to_all | solution.py:446
  186.3 1.8 shard_map.137
  (63 shorter events, 6.8 us)
Async XLA Ops:
  0.6 72.4 %copy-start.10 = (s32[64,4]{0,1:T(4,128)S(1)}, s32[64,4]{0,1:T(4,128)}, u32[]{:S(2)}) copy-start(s32[64,4]{0,1:T(4,128)} %param.11) | copy-start | bytes 3076
  17.7 58.4 %collective-permute-start.2 = (bf16[32,16,256]{2,1,0:T(8,128)(2,1)}, bf16[32,16,256]{2,1,0:T(8,128)(2,1)S(1)}, u32[]{:S(2)}, u32[]{:S(2)}) collective-permute-start(bf16[32,16,256]{2,1,0:T(8,128)(2,1)} %get-tuple-element.61), channel_id=1, source_target_pairs={{0,64},{64,128},{128,192},{192,0},{1,65},{65,129},{129,193},{193,1... | collective-permute-start | bytes 786440 | tf_op jit(solution)/shard_map/ppermute | solution.py:26
  19.9 56.2 %copy-start.13 = (s32[64]{0:T(128)S(1)}, s32[64]{0:T(128)}, u32[]{:S(2)}) copy-start(s32[64]{0:T(128)} %param.10) | copy-start | bytes 772
  19.9 56.2 %collective-permute-start.3 = (bf16[32,16,256]{2,1,0:T(8,128)(2,1)}, bf16[32,16,256]{2,1,0:T(8,128)(2,1)S(1)}, u32[]{:S(2)}, u32[]{:S(2)}) collective-permute-start(bf16[32,16,256]{2,1,0:T(8,128)(2,1)} %get-tuple-element.62), channel_id=1, source_target_pairs={{0,192},{64,0},{128,64},{192,128},{1,193},{65,1},{129,65},{193,129... | collective-permute-start | bytes 786440 | tf_op jit(solution)/shard_map/ppermute | solution.py:26
  70.2 5.9 %copy-start.2 = (bf16[32,16,256]{2,1,0:T(8,128)(2,1)S(1)}, bf16[32,16,256]{2,1,0:T(8,128)(2,1)}, u32[]{:S(2)}) copy-start(bf16[32,16,256]{2,1,0:T(8,128)(2,1)} %get-tuple-element.75.up) | copy-start | bytes 786436
  70.2 5.9 %copy-start.3 = (bf16[32,16,256]{2,1,0:T(8,128)(2,1)S(1)}, bf16[32,16,256]{2,1,0:T(8,128)(2,1)}, u32[]{:S(2)}) copy-start(bf16[32,16,256]{2,1,0:T(8,128)(2,1)} %get-tuple-element.76.down) | copy-start | bytes 786436
  70.2 9.4 %copy-start.4 = (bf16[64,16,256]{2,1,0:T(8,128)(2,1)S(1)}, bf16[64,16,256]{2,1,0:T(8,128)(2,1)}, u32[]{:S(2)}) copy-start(bf16[64,16,256]{2,1,0:T(8,128)(2,1)} %get-tuple-element.79.own) | copy-start | bytes 1572868
  70.2 9.4 %collective-permute-start = (bf16[32,16,256]{2,1,0:T(8,128)(2,1)}, bf16[32,16,256]{2,1,0:T(8,128)(2,1)S(1)}, u32[]{:S(2)}, u32[]{:S(2)}) collective-permute-start(bf16[32,16,256]{2,1,0:T(8,128)(2,1)} %get-tuple-element.64), channel_id=1, source_target_pairs={{0,64},{64,128},{128,192},{192,0},{1,65},{65,129},{129,193},{193,1... | collective-permute-start | bytes 786440 | tf_op jit(solution)/shard_map/ppermute | solution.py:26
  70.3 9.3 %collective-permute-start.1 = (bf16[32,16,256]{2,1,0:T(8,128)(2,1)}, bf16[32,16,256]{2,1,0:T(8,128)(2,1)S(1)}, u32[]{:S(2)}, u32[]{:S(2)}) collective-permute-start(bf16[32,16,256]{2,1,0:T(8,128)(2,1)} %get-tuple-element.65), channel_id=1, source_target_pairs={{0,192},{64,0},{128,64},{192,128},{1,193},{65,1},{129,65},{193,129... | collective-permute-start | bytes 786440 | tf_op jit(solution)/shard_map/ppermute | solution.py:26
  77.0 6.7 %collective-permute-start.4 = (bf16[32,16,256]{2,1,0:T(8,128)(2,1)}, bf16[32,16,256]{2,1,0:T(8,128)(2,1)}, u32[]{:S(2)}, u32[]{:S(2)}) collective-permute-start(bf16[32,16,256]{2,1,0:T(8,128)(2,1)} %get-tuple-element.77), channel_id=1, source_target_pairs={{0,64},{64,128},{128,192},{192,0},{1,65},{65,129},{129,193},{193,1... | collective-permute-start | bytes 786440 | tf_op jit(solution)/shard_map/ppermute | solution.py:26
  77.0 6.7 %collective-permute-start.5 = (bf16[32,16,256]{2,1,0:T(8,128)(2,1)}, bf16[32,16,256]{2,1,0:T(8,128)(2,1)}, u32[]{:S(2)}, u32[]{:S(2)}) collective-permute-start(bf16[32,16,256]{2,1,0:T(8,128)(2,1)} %get-tuple-element.78), channel_id=1, source_target_pairs={{0,192},{64,0},{128,64},{192,128},{1,193},{65,1},{129,65},{193,129... | collective-permute-start | bytes 786440 | tf_op jit(solution)/shard_map/ppermute | solution.py:26
  79.6 4.1 %copy-start.12 = (bf16[11,128,256]{2,1,0:T(8,128)(2,1)S(1)}, bf16[11,128,256]{2,1,0:T(8,128)(2,1)}, u32[]{:S(2)}) copy-start(bf16[11,128,256]{2,1,0:T(8,128)(2,1)} %get-tuple-element.88) | copy-start | bytes 2162692
  79.7 6.7 %copy-start.7 = (bf16[11,128,256]{2,1,0:T(8,128)(2,1)S(1)}, bf16[11,128,256]{2,1,0:T(8,128)(2,1)}, u32[]{:S(2)}) copy-start(bf16[11,128,256]{2,1,0:T(8,128)(2,1)} %get-tuple-element.93.refs_10_) | copy-start | bytes 2162692
  83.7 23.2 %collective-permute-start.7 = (bf16[11,128,256]{2,1,0:T(8,128)(2,1)S(1)}, bf16[11,128,256]{2,1,0:T(8,128)(2,1)S(1)}, u32[]{:S(2)}, u32[]{:S(2)}) collective-permute-start(bf16[11,128,256]{2,1,0:T(8,128)(2,1)S(1)} %copy-done.12), channel_id=1, source_target_pairs={{0,192},{64,0},{128,64},{192,128},{1,193},{65,1},{129,65},{193,129... | collective-permute-start | bytes 2162696 | tf_op jit(solution)/shard_map/ppermute | solution.py:26
  86.4 20.5 %collective-permute-start.6 = (bf16[11,128,256]{2,1,0:T(8,128)(2,1)S(1)}, bf16[11,128,256]{2,1,0:T(8,128)(2,1)S(1)}, u32[]{:S(2)}, u32[]{:S(2)}) collective-permute-start(bf16[11,128,256]{2,1,0:T(8,128)(2,1)S(1)} %copy-done.7), channel_id=1, source_target_pairs={{0,64},{64,128},{128,192},{192,0},{1,65},{65,129},{129,193},{193,1... | collective-permute-start | bytes 2162696 | tf_op jit(solution)/shard_map/ppermute | solution.py:26
  91.4 35.5 %all-to-all-start = ((bf16[64,40,128]{2,1,0:T(8,128)(2,1)}), bf16[64,40,128]{2,1,0:T(8,128)(2,1)}, u32[]{:S(2)}, u32[]{:S(2)}) async-start(bf16[64,40,128]{2,1,0:T(8,128)(2,1)} %get-tuple-element.85), calls=%async_computation | async-start | bytes 1310720 | tf_op jit(solution)/shard_map/all_to_all | solution.py:418
  108.0 10.7 %collective-permute-start.8 = (bf16[5,128,256]{2,1,0:T(8,128)(2,1)S(1)}, bf16[5,128,256]{2,1,0:T(8,128)(2,1)S(1)}, u32[]{:S(2)}, u32[]{:S(2)}) collective-permute-start(bf16[5,128,256]{2,1,0:T(8,128)(2,1)S(1)} %get-tuple-element.89), channel_id=1, source_target_pairs={{0,64},{64,128},{128,192},{192,0},{1,65},{65,129},{129,193},{193,1... | collective-permute-start | bytes 983048 | tf_op jit(solution)/shard_map/ppermute | solution.py:26
  108.0 10.7 %collective-permute-start.9 = (bf16[5,128,256]{2,1,0:T(8,128)(2,1)S(1)}, bf16[5,128,256]{2,1,0:T(8,128)(2,1)S(1)}, u32[]{:S(2)}, u32[]{:S(2)}) collective-permute-start(bf16[5,128,256]{2,1,0:T(8,128)(2,1)S(1)} %get-tuple-element.90), channel_id=1, source_target_pairs={{0,192},{64,0},{128,64},{192,128},{1,193},{65,1},{129,65},{193,129... | collective-permute-start | bytes 983048 | tf_op jit(solution)/shard_map/ppermute | solution.py:26
  118.7 32.2 %copy-start.8 = (bf16[5,128,256]{2,1,0:T(8,128)(2,1)}, bf16[5,128,256]{2,1,0:T(8,128)(2,1)S(1)}, u32[]{:S(2)}) copy-start(bf16[5,128,256]{2,1,0:T(8,128)(2,1)S(1)} %collective-permute-done.8.refs_13_) | copy-start | bytes 983044
  118.7 32.2 %copy-start.9 = (bf16[5,128,256]{2,1,0:T(8,128)(2,1)}, bf16[5,128,256]{2,1,0:T(8,128)(2,1)S(1)}, u32[]{:S(2)}) copy-start(bf16[5,128,256]{2,1,0:T(8,128)(2,1)S(1)} %collective-permute-done.9.refs_14_) | copy-start | bytes 983044
  128.1 8.4 %collective-permute-start.11 = (bf16[32,16,256]{2,1,0:T(8,128)(2,1)S(1)}, bf16[32,16,256]{2,1,0:T(8,128)(2,1)S(1)}, u32[]{:S(2)}, u32[]{:S(2)}) collective-permute-start(bf16[32,16,256]{2,1,0:T(8,128)(2,1)S(1)} %get-tuple-element.106), channel_id=1, source_target_pairs={{0,192},{64,0},{128,64},{192,128},{1,193},{65,1},{129,65},{193,129... | collective-permute-start | bytes 786440 | tf_op jit(solution)/shard_map/ppermute | solution.py:26
  131.1 8.8 %collective-permute-start.12 = (bf16[32,16,256]{2,1,0:T(8,128)(2,1)S(1)}, bf16[32,16,256]{2,1,0:T(8,128)(2,1)S(1)}, u32[]{:S(2)}, u32[]{:S(2)}) collective-permute-start(bf16[32,16,256]{2,1,0:T(8,128)(2,1)S(1)} %get-tuple-element.105), channel_id=1, source_target_pairs={{0,64},{64,128},{128,192},{192,0},{1,65},{65,129},{129,193},{193,1... | collective-permute-start | bytes 786440 | tf_op jit(solution)/shard_map/ppermute | solution.py:26
  131.1 14.1 %collective-permute-start.15 = (bf16[32,16,256]{2,1,0:T(8,128)(2,1)S(1)}, bf16[32,16,256]{2,1,0:T(8,128)(2,1)S(1)}, u32[]{:S(2)}, u32[]{:S(2)}) collective-permute-start(bf16[32,16,256]{2,1,0:T(8,128)(2,1)S(1)} %get-tuple-element.106), channel_id=1, source_target_pairs={{0,64},{64,128},{128,192},{192,0},{1,65},{65,129},{129,193},{193,1... | collective-permute-start | bytes 786440 | tf_op jit(solution)/shard_map/ppermute | solution.py:26
  131.1 14.1 %collective-permute-start.10 = (bf16[32,16,256]{2,1,0:T(8,128)(2,1)S(1)}, bf16[32,16,256]{2,1,0:T(8,128)(2,1)S(1)}, u32[]{:S(2)}, u32[]{:S(2)}) collective-permute-start(bf16[32,16,256]{2,1,0:T(8,128)(2,1)S(1)} %get-tuple-element.105), channel_id=1, source_target_pairs={{0,192},{64,0},{128,64},{192,128},{1,193},{65,1},{129,65},{193,129... | collective-permute-start | bytes 786440 | tf_op jit(solution)/shard_map/ppermute | solution.py:26
  136.5 11.2 %collective-permute-start.14 = (bf16[32,16,256]{2,1,0:T(8,128)(2,1)S(1)}, bf16[32,16,256]{2,1,0:T(8,128)(2,1)S(1)}, u32[]{:S(2)}, u32[]{:S(2)}) collective-permute-start(bf16[32,16,256]{2,1,0:T(8,128)(2,1)S(1)} %collective-permute-done.11), channel_id=1, source_target_pairs={{0,192},{64,0},{128,64},{192,128},{1,193},{65,1},{129,65},{193,129... | collective-permute-start | bytes 786440 | tf_op jit(solution)/shard_map/ppermute | solution.py:26
  140.0 10.9 %collective-permute-start.13 = (bf16[32,16,256]{2,1,0:T(8,128)(2,1)S(1)}, bf16[32,16,256]{2,1,0:T(8,128)(2,1)S(1)}, u32[]{:S(2)}, u32[]{:S(2)}) collective-permute-start(bf16[32,16,256]{2,1,0:T(8,128)(2,1)S(1)} %collective-permute-done.12), channel_id=1, source_target_pairs={{0,64},{64,128},{128,192},{192,0},{1,65},{65,129},{129,193},{193,1... | collective-permute-start | bytes 786440 | tf_op jit(solution)/shard_map/ppermute | solution.py:26
  154.1 2.5 %collective-permute-start.18 = (f32[8,128]{1,0:T(8,128)S(1)}, f32[8,128]{1,0:T(8,128)S(1)}, u32[]{:S(2)}, u32[]{:S(2)}) collective-permute-start(f32[8,128]{1,0:T(8,128)S(1)} %get-tuple-element.99.first), channel_id=1, source_target_pairs={{0,192},{64,0},{128,64},{192,128},{1,193},{65,1},{129,65},{193,129... | collective-permute-start | bytes 12296 | tf_op jit(solution)/shard_map/ppermute | solution.py:26
  154.5 4.0 %collective-permute-start.17 = (f32[8,128]{1,0:T(8,128)S(1)}, f32[8,128]{1,0:T(8,128)S(1)}, u32[]{:S(2)}, u32[]{:S(2)}) collective-permute-start(f32[8,128]{1,0:T(8,128)S(1)} %get-tuple-element.99.first), channel_id=1, source_target_pairs={{0,128},{64,192},{128,0},{192,64},{1,129},{65,193},{129,1},{193,65... | collective-permute-start | bytes 12296 | tf_op jit(solution)/shard_map/ppermute | solution.py:26
  155.1 4.0 %collective-permute-start.16 = (f32[8,128]{1,0:T(8,128)S(1)}, f32[8,128]{1,0:T(8,128)S(1)}, u32[]{:S(2)}, u32[]{:S(2)}) collective-permute-start(f32[8,128]{1,0:T(8,128)S(1)} %get-tuple-element.99.first), channel_id=1, source_target_pairs={{0,64},{64,128},{128,192},{192,0},{1,65},{65,129},{129,193},{193,1... | collective-permute-start | bytes 12296 | tf_op jit(solution)/shard_map/ppermute | solution.py:26
  160.5 25.8 %all-to-all-start.1 = ((bf16[64,16,256]{2,1,0:T(8,128)(2,1)}), bf16[64,16,256]{2,1,0:T(8,128)(2,1)S(1)}, u32[]{:S(2)}, u32[]{:S(2)}) async-start(bf16[64,16,256]{2,1,0:T(8,128)(2,1)} %bitcast.11), calls=%async_computation.1 | async-start | bytes 1048576 | tf_op jit(solution)/shard_map/all_to_all | solution.py:446
  173.2 3.1 %copy-start.5 = (bf16[64,16,1024]{2,1,0:T(8,128)(2,1)S(1)}, bf16[64,16,1024]{2,1,0:T(8,128)(2,1)}, u32[]{:S(2)}) copy-start(bf16[64,16,1024]{2,1,0:T(8,128)(2,1)} %maximum_maximum_fusion) | copy-start | bytes 6291460
  173.2 3.1 %copy-start.6 = (f32[1,256,1024]{2,1,0:T(8,128)S(1)}, f32[1,256,1024]{2,1,0:T(8,128)}, u32[]{:S(2)}) copy-start(f32[1,256,1024]{2,1,0:T(8,128)} %param.14) | copy-start | bytes 3145732
  (4 other events, 5.0 us)

commit v6 on v5

--- a/solution.py
+++ b/solution.py
@@ -50,34 +50,6 @@
     return (row < n_rows - row_off) & (col < n_cols - col_off)
 
 
-def split_kernel(cuts, part, *refs):
-    outs, sems = refs[: len(cuts)], refs[len(cuts)]
-    quarter = outs[0].shape[2]
-    copies = []
-    for i, ((first, step), out) in enumerate(zip(cuts, outs)):
-        col = ((lax.axis_index("grp") + step) & 3) * quarter
-        source = part.at[0, pl.ds(first, out.shape[0]), :, pl.ds(pl.multiple_of(col, quarter), quarter)]
-        copies.append(pltpu.make_async_copy(source, out, sems.at[i]))
-    for copy in copies:
-        copy.start()
-    for copy in copies:
-        copy.wait()
-
-
-def split(part, cuts, quarter):
-    rows = part.shape[2]
-    return pl.pallas_call(
-        functools.partial(split_kernel, tuple((first, step) for first, _, step in cuts)),
-        out_shape=tuple(
-            pltpu.HBM((count, rows, quarter), BF16) for _, count, _ in cuts
-        ),
-        in_specs=[pl.BlockSpec(memory_space=pl.ANY)],
-        out_specs=(pl.BlockSpec(memory_space=pl.ANY),) * len(cuts),
-        scratch_shapes=[pltpu.SemaphoreType.DMA((len(cuts),))],
-        compiler_params=pltpu.CompilerParams(vmem_limit_bytes=2 * MIB),
-    )(in_hbm(part))
-
-
 def add_kernel(up, far_up, down, far_down, up_out, down_out):
     up_out[...] = (up[...].astype(F32) + far_up[...].astype(F32)).astype(BF16)
     down_out[...] = (down[...].astype(F32) + far_down[...].astype(F32)).astype(BF16)
@@ -132,7 +104,7 @@
     )(in_hbm(left), in_hbm(right))
 
 
-def gather_kernel(own, up_direct, down_direct, out):
+def gather_kernel(own, up_direct, down_direct, first, second, out, first_out, second_out):
     half = up_direct.shape[0]
 
     def step(i, carry):
@@ -141,33 +113,37 @@
         return carry
 
     lax.fori_loop(0, half, step, 0, unroll=4)
-
-
-def gather(own, up_direct, down_direct):
+    first_out[...] = BETA_FIRST * first[...]
+    second_out[...] = BETA_SECOND * second[...]
+
+
+def gather(own, up_direct, down_direct, first, second):
+    shape = jax.ShapeDtypeStruct((2, *up_direct.shape), F32)
     return pl.pallas_call(
         gather_kernel,
-        out_shape=jax.ShapeDtypeStruct((2, *up_direct.shape), F32),
-        in_specs=[pl.BlockSpec(memory_space=VMEM)] * 3,
-        out_specs=pl.BlockSpec(memory_space=VMEM),
-        compiler_params=pltpu.CompilerParams(vmem_limit_bytes=6 * MIB),
+        out_shape=(shape,) * 3,
+        in_specs=[pl.BlockSpec(memory_space=VMEM)] * 5,
+        out_specs=(pl.BlockSpec(memory_space=VMEM),) * 3,
+        compiler_params=pltpu.CompilerParams(vmem_limit_bytes=10 * MIB),
         cost_estimate=LONG,
-    )(own, up_direct, down_direct)
+    )(own, up_direct, down_direct, first.reshape(shape.shape), second.reshape(shape.shape))
 
 
 def pack_kernel(
     key, bounds, partial, up_sum, down_sum, first, second, out, first_out, second_out
 ):
-    _, count, rows, cols = partial.shape
-    half = out.shape[0] // 2
+    _, half, rows, cols = partial.shape
+    count = first_out.shape[1]
     begin = pl.program_id(0) * count
-    lanes = 128
+    lanes = cols // 2
 
     def one(side, i, value):
-        block = side * half + begin + i
+        at = begin + i
+        block = side * half + at
         keep = jnp.where(inside(bounds, block, rows, cols), 1.0, 0.0)
         grad = value * keep
-        first_next = BETA_FIRST * first[side, i] + (1.0 - BETA_FIRST) * grad
-        second_next = BETA_SECOND * second[side, i] + (1.0 - BETA_SECOND) * grad * grad
+        first_next = first[side, at] + (1.0 - BETA_FIRST) * grad
+        second_next = second[side, at] + (1.0 - BETA_SECOND) * grad * grad
         first_out[side, i] = first_next
         second_out[side, i] = second_next
         root = second_next * lax.rsqrt(second_next)
@@ -179,8 +155,9 @@
         out[key[block]] = piece.astype(BF16)
 
     def step(i, carry):
-        one(0, i, partial[0, i] + up_sum[i].astype(F32))
-        one(1, i, partial[1, i] + down_sum[i].astype(F32))
+        at = begin + i
+        one(0, i, partial[0, at] + up_sum[at].astype(F32))
+        one(1, i, partial[1, at] + down_sum[at].astype(F32))
         return carry
 
     lax.fori_loop(0, count, step, 0, unroll=4)
@@ -188,42 +165,24 @@
 
 def pack(key, bounds, partial, up_sum, down_sum, first, second):
     _, half, rows, cols = partial.shape
-    blocks = 2 * half
+    blocks, lanes = 2 * half, cols // 2
     steps = 4 if half >= 16 else 1
-    count = half // steps
-    piece = 2 * rows + rows // 2
-    moment = pl.BlockSpec((2, count, rows, cols), lambda i, *_: (0, i, 0, 0))
-    halves = jax.ShapeDtypeStruct((2, half, rows, cols), F32)
+    moment = pl.BlockSpec((2, half // steps, rows, cols), lambda i, *_: (0, i, 0, 0))
+    halves = pltpu.HBM((2, half, rows, cols), F32)
+    piece = (blocks, 2 * rows + rows // 2, lanes)
     out, first_next, second_next = pl.pallas_call(
         pack_kernel,
-        out_shape=(pltpu.HBM((blocks, piece, 128), BF16), halves, halves),
+        out_shape=(pltpu.HBM(piece, BF16), halves, halves),
         grid_spec=pltpu.PrefetchScalarGridSpec(
             num_scalar_prefetch=2,
             grid=(steps,),
-            in_specs=[
-                moment,
-                pl.BlockSpec((count, rows, cols), lambda i, *_: (i, 0, 0)),
-                pl.BlockSpec((count, rows, cols), lambda i, *_: (i, 0, 0)),
-                moment,
-                moment,
-            ],
-            out_specs=[
-                pl.BlockSpec((blocks, piece, 128), lambda i, *_: (0, 0, 0)),
-                moment,
-                moment,
-            ],
+            in_specs=[pl.BlockSpec(memory_space=VMEM)] * 5,
+            out_specs=[pl.BlockSpec(piece, lambda i, *_: (0, 0, 0)), moment, moment],
         ),
-        compiler_params=pltpu.CompilerParams(vmem_limit_bytes=10 * MIB),
-    )(
-        key,
-        bounds,
-        partial,
-        up_sum,
-        down_sum,
-        in_hbm(first.reshape(halves.shape)),
-        in_hbm(second.reshape(halves.shape)),
-    )
-    return out, first_next.reshape(first.shape), second_next.reshape(second.shape)
+        compiler_params=pltpu.CompilerParams(vmem_limit_bytes=14 * MIB),
+    )(key, bounds, partial, up_sum, down_sum, first, second)
+    shape = (blocks, rows, cols)
+    return out, first_next.reshape(shape), second_next.reshape(shape)
 
 
 def relay_kernel(prev, following, up, down):
@@ -268,38 +227,38 @@
 
 
 def precond_kernel(*refs):
-    own_low, own_high, next_low, next_high, far_low, far_high, prev_low, prev_high = refs[:8]
-    adam, sources, (out, norms) = refs[8], refs[9:15], refs[15:17]
+    pieces, adam, sources, (out, norms) = refs[:8], refs[8], refs[9:15], refs[15:17]
     mixed, held, sems = refs[17], refs[18:24], refs[24]
     width, quarter = out.shape
     half = width // 2
     me = lax.axis_index("grp")
     n = width // quarter
-    copies = [pltpu.make_async_copy(*args) for args in zip(sources, held, [sems.at[i] for i in range(6)])]
+    copies = [
+        pltpu.make_async_copy(source, place, sems.at[i])
+        for i, (source, place) in enumerate(zip(sources, held))
+    ]
     for copy in copies:
         copy.start()
     root, up, up_prev, down_next, up_far, down_far = held
     for copy in copies:
         copy.wait()
-
-    def joined(low, high):
-        return jnp.concatenate([low, high], axis=0)
-
-    roots = (
-        joined(root[0], root[1]),
-        joined(down_next[9], down_next[10]),
-        joined(up_far[4], down_far[4]),
-        joined(up_prev[9], up_prev[10]),
-    )
-    for top, parts in (
-        (0, (own_low, next_low, far_low, prev_low)),
-        (half, (own_high, next_high, far_high, prev_high)),
-    ):
-        for row in range(0, half, quarter):
-            total = jnp.zeros((quarter, quarter), F32)
-            for piece, right in zip(parts, roots):
-                total += dot(piece[pl.ds(row, quarter), :], right, ((1,), (0,)))
-            mixed[pl.ds(top + row, quarter), :] = total.astype(BF16)
+    right = jnp.concatenate(
+        [
+            root[0],
+            root[1],
+            down_next[9],
+            down_next[10],
+            up_far[4],
+            down_far[4],
+            up_prev[9],
+            up_prev[10],
+        ],
+        axis=0,
+    )
+    for row in range(0, width, quarter):
+        parts = [ref[pl.ds(row % half, quarter), :] for ref in pieces[row // half :: 2]]
+        value = dot(jnp.concatenate(parts, axis=1), right, ((1,), (0,)))
+        mixed[pl.ds(row, quarter), :] = value.astype(BF16)
     square = jnp.zeros((8, quarter), F32)
     for step, (low, first), (high, second) in (
         (0, (up, 0), (up, 5)),
@@ -307,8 +266,8 @@
         (2, (up_far, 0), (down_far, 0)),
         (3, (up_prev, 0), (up_prev, 5)),
     ):
-        left = jnp.concatenate([joined(low[first + c], high[second + c]) for c in range(n)], axis=1)
-        value = dot(left, mixed[...], ((1,), (0,)))
+        units = [jnp.concatenate([low[first + c], high[second + c]], axis=0) for c in range(n)]
+        value = dot(jnp.concatenate(units, axis=1), mixed[...], ((1,), (0,)))
         base = ((me + step) & (n - 1)) * quarter
         out[pl.ds(pl.multiple_of(base, quarter), quarter), :] = value
         square += jnp.sum((value * value).reshape(quarter // 8, 8, quarter), axis=0)
@@ -383,18 +342,24 @@
     width = grad_parts.shape[3]
     quarter = width // n_grp
     half = total_blocks // 2
+    starts = [((grp_index + step) & (n_grp - 1)) * quarter for step in range(4)]
     turn = ((n_grp - grp_index) & (n_grp - 1)) * quarter
-    first_row = grp_index * quarter
-    grad_parts, turn, first_row = lax.optimization_barrier((grad_parts, turn, first_row))
-
-    far_low, far_high = split(grad_parts, ((0, half, 2), (half, half, 2)), quarter)
+    grad_parts, starts, turn = lax.optimization_barrier((grad_parts, starts, turn))
+
+    def columns(array, step):
+        return slice_at(array, starts[step], quarter, array.ndim - 1)
+
+    part = grad_parts[0]
+    far = columns(part, 2)
+    far_low, far_high = lax.optimization_barrier((far[:half], far[half:]))
     far_up = shift(far_low, 1)
     far_down = shift(far_high, -1)
-    later, _, _ = lax.optimization_barrier((grad_parts, far_low, far_high))
-    up_low, up_high, down_low, down_high, own = split(
-        later,
-        ((0, half, 1), (half, half, 1), (0, half, 3), (half, half, 3), (0, total_blocks, 0)),
-        quarter,
+    later, left_root, right_root, _, _ = lax.optimization_barrier(
+        (part, left_root, right_root, far_low, far_high)
+    )
+    up, down = columns(later, 1), columns(later, 3)
+    up_low, up_high, down_low, down_high, own = lax.optimization_barrier(
+        (up[:half], up[half:], down[:half], down[half:], columns(later, 0))
     )
     up_direct = shift(up_high, 1)
     down_direct = shift(down_low, -1)
@@ -402,18 +367,17 @@
     up_sum = shift(up_sum, 1)
     down_sum = shift(down_sum, -1)
     key, bounds = slots_of(assign, n_own, per_owner), block_bounds.reshape(-1)
-    left_root, right_root, _, _ = lax.optimization_barrier((left_root, right_root, far_low, far_high))
     roots_up, roots_down, root_own = root_pieces(left_root, right_root)
     up_direct, down_direct, key, bounds, roots_up, roots_down, root_own = lax.optimization_barrier(
         (up_direct, down_direct, key, bounds, roots_up, roots_down, root_own)
     )
-    partial = gather(own, up_direct, down_direct)
+    partial, first, second = gather(own, up_direct, down_direct, first_moment, second_moment)
 
     roots_up, roots_down, up_sum, down_sum, partial = lax.optimization_barrier(
         (roots_up, roots_down, up_sum, down_sum, partial)
     )
     sorted_grad, first_next, second_next = pack(
-        key, bounds, partial, up_sum, down_sum, first_moment, second_moment
+        key, bounds, partial, up_sum, down_sum, first, second
     )
     owned = lax.all_to_all(sorted_grad, "own", split_axis=0, concat_axis=0, tiled=True)
     roots_prev = shift(roots_up, 1)
@@ -426,7 +390,7 @@
     own_cols = jnp.concatenate(
         [owned[:, :shard_rows], owned[:, shard_rows : 2 * shard_rows]], axis=2
     )
-    adam = owned[:, 2 * shard_rows :].reshape(n_own * shard_rows // 2, 128)
+    adam = owned[:, 2 * shard_rows :].reshape(-1, quarter // 2)
     low, high = own_cols[:half], own_cols[half:]
     prev_low = shift(low, 1)
     next_high = shift(high, -1)
@@ -435,7 +399,7 @@
     far_low = shift(prev_low, 1)
     far_high = shift(next_high, -1)
     pieces = [low, high, next_low, next_high, far_low, far_high, prev_low, prev_high]
-    flat = [piece.reshape(width // 2, quarter) for piece in pieces]
+    flat = [piece.reshape(-1, quarter) for piece in pieces]
     precond, norms = precondition(flat, adam, roots)
     norms = [norms] + [shift(norms, step) for step in (1, 2, 3)]
     grafted = graft(precond, norms).reshape(n_own, shard_rows, quarter)
@@ -446,9 +410,9 @@
     back = lax.all_to_all(grafted, "own", split_axis=0, concat_axis=0, tiled=True)
 
     whole = jnp.concatenate(
-        [jnp.concatenate(pieces[i : i + 2], axis=0) for i in (0, 2, 4, 6)], axis=2
+        [jnp.concatenate(pieces[i : i + 2]) for i in (0, 2, 4, 6)], axis=2
     ).reshape(width, width)
-    rows = slice_at(whole, first_row, quarter, 0)
+    rows = slice_at(whole, starts[0], quarter, 0)
     left_acc = STAT_DECAY * left_stat + dot(rows, whole, ((1,), (1,)))[None]
     cross = dot(whole[:, :quarter], whole, ((0,), (0,)))
     cross = jnp.concatenate([cross, cross], axis=1)

time: 189 us -> 128 us (0.68)
  Pallas kernels: 81.2 us -> 14.6 us
  local copies, waits for them, and re-layouts: 3.48 us -> 9.48 us
    pallas_call x4 -> x2, Pallas kernels: 71 us -> 4.36 us  [the longest x1 4.05 us: pack(): pl.pallas_call(pack_kernel, out_shape=(pltpu.HBM(piece, BF16), halves, ha...]
    slice x0 -> x2, local copies, waits for them, and re-layouts: none -> 4.56 us  [the longest x1 2.42 us: on_device(): down[half:]]
  transfers between devices with their start and end apart: 21 -> 21, of which waited for: 11 -> 11; matrix products, arithmetic and copies ran while one was open for 5% -> 11% of each run, Pallas kernels for 31% -> 6%
where the time goes in v6:
time: 128 us; the launch traced here: 127 us
  starting transfers between devices  49.2 us (38%)
  waiting for transfers between devices  44 us (34%)
  Pallas kernels  14.6 us (11%)
  local copies, waits for them, and re-layouts  9.48 us (7%)
  other arithmetic  4.63 us (4%)
  matrix products  4.24 us (3%)
    ppermute x19, waiting for transfers between devices, shift(): return lax.ppermute(array, 'grp', [(i, (i + step) % n) for i in range(n)])  27.5 us
    ppermute x19, starting transfers between devices, shift(): return lax.ppermute(array, 'grp', [(i, (i + step) % n) for i in range(n)])  25.3 us
    all_to_all x1, starting transfers between devices, on_device(): lax.all_to_all(sorted_grad, 'own', split_axis=0, concat_axis=0, tiled=True)  15.4 us
    all_to_all x1, starting transfers between devices, on_device(): lax.all_to_all(grafted, 'own', split_axis=0, concat_axis=0, tiled=True)  8.48 us
    all_to_all x1, waiting for transfers between devices, on_device(): lax.all_to_all(sorted_grad, 'own', split_axis=0, concat_axis=0, tiled=True)  8.29 us
    all_to_all x1, waiting for transfers between devices, on_device(): lax.all_to_all(grafted, 'own', split_axis=0, concat_axis=0, tiled=True)  8.25 us
    dot_general x2, matrix products, dot(): return lax.dot_general(a, b, (dims, ((), ())), preferred_element_type=F32)  4.24 us
    pallas_call x1, Pallas kernels, pack(): pl.pallas_call(pack_kernel, out_shape=(pltpu.HBM(piece, BF16), halves, ha...  4.05 us
  transfers between devices with their start and end apart: 21, of which 11 were waited for; matrix products, arithmetic and copies ran while one was open for 11% of the time, Pallas kernels for 6%

profile of v6, /device:TPU:1, one launch (start us, length us, event | category | flops | bytes accessed | tf_op | source)
XLA Modules:
  0.0 127.1 jit_solution(8455216916056338492)
XLA Ops:
  0.7 2.1 %dynamic-slice_bitcast_fusion = (bf16[32,16,256]{2,1,0:T(8,128)(2,1)}, bf16[32,16,256]{2,1,0:T(8,128)(2,1)}) fusion(bf16[1,64,16,1024]{3,2,1,0:T(8,128)(2,1)} %param.9, s32[]{:T(128)S(6)} %add.42, s32[]{:T(128)S(6)} %mul.23), kind=kLoop, calls=%fused_computation.15 | loop fusion | bytes 1048584 | tf_op jit(solution)/shard_map/slice | solution.py:354
  2.8 2.0 %collective-permute-start.2 = (bf16[32,16,256]{2,1,0:T(8,128)(2,1)}, bf16[32,16,256]{2,1,0:T(8,128)(2,1)S(1)}, u32[]{:S(2)}, u32[]{:S(2)}) collective-permute-start(bf16[32,16,256]{2,1,0:T(8,128)(2,1)} %get-tuple-element.68), channel_id=1, source_target_pairs={{0,64},{64,128},{128,192},{192,0},{1,65},{65,129},{129,193},{193,1... | collective-permute-start | bytes 786440 | tf_op jit(solution)/shard_map/ppermute | solution.py:26
  4.8 1.5 %collective-permute-start.3 = (bf16[32,16,256]{2,1,0:T(8,128)(2,1)}, bf16[32,16,256]{2,1,0:T(8,128)(2,1)S(1)}, u32[]{:S(2)}, u32[]{:S(2)}) collective-permute-start(bf16[32,16,256]{2,1,0:T(8,128)(2,1)} %get-tuple-element.69), channel_id=1, source_target_pairs={{0,192},{64,0},{128,64},{192,128},{1,193},{65,1},{129,65},{193,129... | collective-permute-start | bytes 786440 | tf_op jit(solution)/shard_map/ppermute | solution.py:26
  6.4 2.4 %constant_dynamic-slice_fusion.3 = (bf16[32,16,256]{2,1,0:T(8,128)(2,1)S(1)}, bf16[32,16,256]{2,1,0:T(8,128)(2,1)S(1)}, bf16[32,16,256]{2,1,0:T(8,128)(2,1)S(1)}, bf16[32,16,256]{2,1,0:T(8,128)(2,1)}) fusion(bf16[64,16,1024]{2,1,0:T(8,128)(2,1)} %bitcast.43, s32[]{:T(128)S(6)} %add.42, s32[]{:T(128)S(6)} %mul.24, s32[]{:T(128)S(6)} %mul.22), kind=kLoop, calls=%fused_computation.22 | loop fusion | bytes 2097164 | tf_op jit(solution)/shard_map/slice | solution.py:362
  8.8 1.4 %constant_dynamic-slice_fusion.2.own = bf16[64,16,256]{2,1,0:T(8,128)(2,1)S(1)} fusion(bf16[64,16,1024]{2,1,0:T(8,128)(2,1)} %bitcast.44, s32[]{:T(128)S(6)} %mul.21), kind=kLoop, calls=%fused_computation.21 | loop fusion | bytes 1048580 | tf_op jit(solution)/shard_map/dynamic_slice | solution.py:40
  10.3 2.7 %collective-permute-start.1 = (bf16[32,16,256]{2,1,0:T(8,128)(2,1)S(1)}, bf16[32,16,256]{2,1,0:T(8,128)(2,1)S(1)}, u32[]{:S(2)}, u32[]{:S(2)}) collective-permute-start(bf16[32,16,256]{2,1,0:T(8,128)(2,1)S(1)} %get-tuple-element.75), channel_id=1, source_target_pairs={{0,192},{64,0},{128,64},{192,128},{1,193},{65,1},{129,65},{193,129... | collective-permute-start | bytes 786440 | tf_op jit(solution)/shard_map/ppermute | solution.py:26
  13.2 2.9 %shard_map.128 = (bf16[11,128,256]{2,1,0:T(8,128)(2,1)}, bf16[11,128,256]{2,1,0:T(8,128)(2,1)}, bf16[2,128,256]{2,1,0:T(8,128)(2,1)}) custom-call(f32[1,256,1024]{2,1,0:T(8,128)} %left, f32[1,256,1024]{2,1,0:T(8,128)} %right), custom_call_target="tpu_custom_call" | custom-call | tf_op jit(solution)/shard_map/pallas_call | solution.py:93
  17.0 2.7 %collective-permute-start.5 = (bf16[32,16,256]{2,1,0:T(8,128)(2,1)}, bf16[32,16,256]{2,1,0:T(8,128)(2,1)}, u32[]{:S(2)}, u32[]{:S(2)}) collective-permute-start(bf16[32,16,256]{2,1,0:T(8,128)(2,1)} %get-tuple-element.88), channel_id=1, source_target_pairs={{0,192},{64,0},{128,64},{192,128},{1,193},{65,1},{129,65},{193,129... | collective-permute-start | bytes 786440 | tf_op jit(solution)/shard_map/ppermute | solution.py:26
  20.1 3.7 %collective-permute-done.4.up_sum = bf16[32,16,256]{2,1,0:T(8,128)(2,1)} collective-permute-done((bf16[32,16,256]{2,1,0:T(8,128)(2,1)}, bf16[32,16,256]{2,1,0:T(8,128)(2,1)}, u32[]{:S(2)}, u32[]{:S(2)}) %collective-permute-start.4) | collective-permute-done | bytes 262176 | tf_op jit(solution)/shard_map/ppermute | solution.py:26
  23.8 2.7 %collective-permute-start.7 = (bf16[11,128,256]{2,1,0:T(8,128)(2,1)S(1)}, bf16[11,128,256]{2,1,0:T(8,128)(2,1)S(1)}, u32[]{:S(2)}, u32[]{:S(2)}) collective-permute-start(bf16[11,128,256]{2,1,0:T(8,128)(2,1)S(1)} %copy-done.11), channel_id=1, source_target_pairs={{0,192},{64,0},{128,64},{192,128},{1,193},{65,1},{129,65},{193,129... | collective-permute-start | bytes 2162696 | tf_op jit(solution)/shard_map/ppermute | solution.py:26
  26.4 4.0 %shard_map.131 = (bf16[64,40,128]{2,1,0:T(8,128)(2,1)}, f32[2,32,16,256]{3,2,1,0:T(8,128)}, f32[2,32,16,256]{3,2,1,0:T(8,128)}) custom-call(s32[64]{0:T(128)S(1)} %fusion.9.key, s32[256]{0:T(256)S(1)} %reshape.64.bounds, f32[2,32,16,256]{3,2,1,0:T(8,128)S(1)} %get-tuple-element.93.partial, bf16[32,16,256]{2,1,0:T(8,128)(2,1)} %collective-permute-done.4.up_sum, ...), custom_call_target="tpu_custom_call" | custom-call | tf_op jit(solution)/shard_map/pallas_call | solution.py:173
  30.5 15.4 %all-to-all-start = ((bf16[64,40,128]{2,1,0:T(8,128)(2,1)}), bf16[64,40,128]{2,1,0:T(8,128)(2,1)}, u32[]{:S(2)}, u32[]{:S(2)}) async-start(bf16[64,40,128]{2,1,0:T(8,128)(2,1)} %get-tuple-element.98), calls=%async_computation | async-start | bytes 1310720 | tf_op jit(solution)/shard_map/all_to_all | solution.py:382
  47.0 3.0 %collective-permute-start.9 = (bf16[5,128,256]{2,1,0:T(8,128)(2,1)S(1)}, bf16[5,128,256]{2,1,0:T(8,128)(2,1)S(1)}, u32[]{:S(2)}, u32[]{:S(2)}) collective-permute-start(bf16[5,128,256]{2,1,0:T(8,128)(2,1)S(1)} %get-tuple-element.103), channel_id=1, source_target_pairs={{0,192},{64,0},{128,64},{192,128},{1,193},{65,1},{129,65},{193,129... | collective-permute-start | bytes 983048 | tf_op jit(solution)/shard_map/ppermute | solution.py:26
  50.0 7.7 %collective-permute-done.8.refs_13_ = bf16[5,128,256]{2,1,0:T(8,128)(2,1)S(1)} collective-permute-done((bf16[5,128,256]{2,1,0:T(8,128)(2,1)S(1)}, bf16[5,128,256]{2,1,0:T(8,128)(2,1)S(1)}, u32[]{:S(2)}, u32[]{:S(2)}) %collective-permute-start.8) | collective-permute-done | bytes 327712 | tf_op jit(solution)/shard_map/ppermute | solution.py:26
  57.7 8.3 %all-to-all-done = bf16[64,40,128]{2,1,0:T(8,128)(2,1)} async-done(((bf16[64,40,128]{2,1,0:T(8,128)(2,1)}), bf16[64,40,128]{2,1,0:T(8,128)(2,1)}, u32[]{:S(2)}, u32[]{:S(2)}) %all-to-all-start) | async-done | bytes 655392 | tf_op jit(solution)/shard_map/all_to_all | solution.py:382
  67.1 3.0 %collective-permute-start.11 = (bf16[32,16,256]{2,1,0:T(8,128)(2,1)S(1)}, bf16[32,16,256]{2,1,0:T(8,128)(2,1)S(1)}, u32[]{:S(2)}, u32[]{:S(2)}) collective-permute-start(bf16[32,16,256]{2,1,0:T(8,128)(2,1)S(1)} %get-tuple-element.119), channel_id=1, source_target_pairs={{0,192},{64,0},{128,64},{192,128},{1,193},{65,1},{129,65},{193,129... | collective-permute-start | bytes 786440 | tf_op jit(solution)/shard_map/ppermute | solution.py:26
  70.2 2.7 %collective-permute-start.10 = (bf16[32,16,256]{2,1,0:T(8,128)(2,1)S(1)}, bf16[32,16,256]{2,1,0:T(8,128)(2,1)S(1)}, u32[]{:S(2)}, u32[]{:S(2)}) collective-permute-start(bf16[32,16,256]{2,1,0:T(8,128)(2,1)S(1)} %get-tuple-element.118), channel_id=1, source_target_pairs={{0,192},{64,0},{128,64},{192,128},{1,193},{65,1},{129,65},{193,129... | collective-permute-start | bytes 786440 | tf_op jit(solution)/shard_map/ppermute | solution.py:26
  72.9 2.7 %collective-permute-done.11 = bf16[32,16,256]{2,1,0:T(8,128)(2,1)S(1)} collective-permute-done((bf16[32,16,256]{2,1,0:T(8,128)(2,1)S(1)}, bf16[32,16,256]{2,1,0:T(8,128)(2,1)S(1)}, u32[]{:S(2)}, u32[]{:S(2)}) %collective-permute-start.11) | collective-permute-done | bytes 262176 | tf_op jit(solution)/shard_map/ppermute | solution.py:26
  75.6 3.4 %collective-permute-start.14 = (bf16[32,16,256]{2,1,0:T(8,128)(2,1)S(1)}, bf16[32,16,256]{2,1,0:T(8,128)(2,1)S(1)}, u32[]{:S(2)}, u32[]{:S(2)}) collective-permute-start(bf16[32,16,256]{2,1,0:T(8,128)(2,1)S(1)} %collective-permute-done.11), channel_id=1, source_target_pairs={{0,192},{64,0},{128,64},{192,128},{1,193},{65,1},{129,65},{193,129... | collective-permute-start | bytes 786440 | tf_op jit(solution)/shard_map/ppermute | solution.py:26
  79.9 4.4 %collective-permute-done.15 = bf16[32,16,256]{2,1,0:T(8,128)(2,1)S(1)} collective-permute-done((bf16[32,16,256]{2,1,0:T(8,128)(2,1)S(1)}, bf16[32,16,256]{2,1,0:T(8,128)(2,1)S(1)}, u32[]{:S(2)}, u32[]{:S(2)}) %collective-permute-start.15) | collective-permute-done | bytes 262176 | tf_op jit(solution)/shard_map/ppermute | solution.py:26
  84.3 2.5 %collective-permute-done.14 = bf16[32,16,256]{2,1,0:T(8,128)(2,1)S(1)} collective-permute-done((bf16[32,16,256]{2,1,0:T(8,128)(2,1)S(1)}, bf16[32,16,256]{2,1,0:T(8,128)(2,1)S(1)}, u32[]{:S(2)}, u32[]{:S(2)}) %collective-permute-start.14) | collective-permute-done | bytes 262176 | tf_op jit(solution)/shard_map/ppermute | solution.py:26
  86.8 3.1 %collective-permute-done.13 = bf16[32,16,256]{2,1,0:T(8,128)(2,1)S(1)} collective-permute-done((bf16[32,16,256]{2,1,0:T(8,128)(2,1)S(1)}, bf16[32,16,256]{2,1,0:T(8,128)(2,1)S(1)}, u32[]{:S(2)}, u32[]{:S(2)}) %collective-permute-start.13) | collective-permute-done | bytes 262176 | tf_op jit(solution)/shard_map/ppermute | solution.py:26
  89.9 3.2 %shard_map.133 = (f32[1024,256]{1,0:T(8,128)S(1)}, f32[8,128]{1,0:T(8,128)S(1)}) custom-call(bf16[512,256]{1,0:T(8,128)(2,1)S(1)} %bitcast.32, bf16[512,256]{1,0:T(8,128)(2,1)S(1)} %bitcast.31, bf16[512,256]{1,0:T(8,128)(2,1)S(1)} %bitcast.36, bf16[512,256]{1,0:T(8,128)(2,1)S(1)} %bitcast.33, bf16[512,256]{1,0:T(8,128)(2,1)S(1)} %bitcast.38, ...), custom_call_target="tpu_custom_call" | custom-call | tf_op jit(solution)/shard_map/pallas_call | solution.py:282
  95.7 1.8 %collective-permute-done.17.third = f32[8,128]{1,0:T(8,128)S(1)} collective-permute-done((f32[8,128]{1,0:T(8,128)S(1)}, f32[8,128]{1,0:T(8,128)S(1)}, u32[]{:S(2)}, u32[]{:S(2)}) %collective-permute-start.17) | collective-permute-done | bytes 4128 | tf_op jit(solution)/shard_map/ppermute | solution.py:26
  98.1 1.4 %shard_map.134 = bf16[1024,256]{1,0:T(8,128)(2,1)} custom-call(f32[1024,256]{1,0:T(8,128)S(1)} %get-tuple-element.111.precond, f32[8,128]{1,0:T(8,128)S(1)} %get-tuple-element.112.first, f32[8,128]{1,0:T(8,128)S(1)} %collective-permute-done.16.second, f32[8,128]{1,0:T(8,128)S(1)} %collective-permute-done.17.third, f32[8,128]{1,0:T(8,128)S(1)} %collective-permute-done.18.fourth), custom_call_target="tpu_custom_call" | custom-call | tf_op jit(solution)/shard_map/pallas_call | solution.py:315
  99.5 8.5 %all-to-all-start.1 = ((bf16[64,16,256]{2,1,0:T(8,128)(2,1)}), bf16[64,16,256]{2,1,0:T(8,128)(2,1)S(1)}, u32[]{:S(2)}, u32[]{:S(2)}) async-start(bf16[64,16,256]{2,1,0:T(8,128)(2,1)} %bitcast.14), calls=%async_computation.1 | async-start | bytes 1048576 | tf_op jit(solution)/shard_map/all_to_all | solution.py:410
  108.0 1.5 %maximum_maximum_fusion = bf16[64,16,1024]{2,1,0:T(8,128)(2,1)} fusion(bf16[32,16,256]{2,1,0:T(8,128)(2,1)S(1)} %collective-permute-done.15, bf16[32,16,256]{2,1,0:T(8,128)(2,1)S(1)} %collective-permute-done.12, bf16[32,16,256]{2,1,0:T(8,128)(2,1)S(1)} %collective-permute-done.14, bf16[32,16,256]{2,1,0:T(8,128)(2,1)S(1)} %collective-permute-done.13, ...), kind=kLoop, calls=%fused_computation | loop fusion | flops 16777216 | bytes 4194304 | tf_op jit(solution)/shard_map/concatenate | solution.py:412
  109.8 2.5 %fusion.4 = f32[256,1024]{1,0:T(8,128)S(1)} fusion(bf16[1024,1024]{1,0:T(8,128)(2,1)} %bitcast.41), kind=kOutput, calls=%fused_computation.8 | convolution fusion | flops 536870912 | bytes 3670016 | tf_op jit(solution)/shard_map/dot_general | solution.py:44
  112.3 3.0 %fusion.3 = f32[1,256,1024]{2,1,0:T(8,128)} fusion(s32[]{:T(128)S(6)} %mul.25, f32[256,1024]{1,0:T(8,128)S(1)} %fusion.4, f32[1,256,1024]{2,1,0:T(8,128)} %param.15), kind=kLoop, calls=%fused_computation.7 | loop fusion | flops 786432 | bytes 3145732 | tf_op jit(solution)/shard_map/add | solution.py:420
  115.3 1.7 %fusion = f32[1,256,1024]{2,1,0:T(8,128)} fusion(bf16[1024,1024]{1,0:T(8,128)(2,1)S(1)} %bitcast.42, f32[1,256,1024]{2,1,0:T(8,128)S(1)} %copy-done.5, s32[]{:T(128)S(6)} %mul.21), kind=kOutput, calls=%fused_computation.4 | convolution fusion | flops 537395200 | bytes 4718596 | tf_op jit(solution)/shard_map/dot_general | solution.py:44
  117.1 8.2 %all-to-all-done.1.back = bf16[64,16,256]{2,1,0:T(8,128)(2,1)S(1)} async-done(((bf16[64,16,256]{2,1,0:T(8,128)(2,1)}), bf16[64,16,256]{2,1,0:T(8,128)(2,1)S(1)}, u32[]{:S(2)}, u32[]{:S(2)}) %all-to-all-start.1) | async-done | bytes 524320 | tf_op jit(solution)/shard_map/all_to_all | solution.py:410
  125.3 1.8 %shard_map.135 = bf16[64,16,256]{2,1,0:T(8,128)(2,1)} custom-call(s32[64]{0:T(128)S(1)} %fusion.10.key, s32[256]{0:T(256)S(1)} %reshape.77.bounds, bf16[64,16,256]{2,1,0:T(8,128)(2,1)S(1)} %all-to-all-done.1.back), custom_call_target="tpu_custom_call" | custom-call | tf_op jit(solution)/shard_map/pallas_call | solution.py:219
  (62 shorter events, 8.0 us)
Async XLA Ops:
  0.6 12.4 %copy-start.9 = (s32[64,4]{0,1:T(4,128)S(1)}, s32[64,4]{0,1:T(4,128)}, u32[]{:S(2)}) copy-start(s32[64,4]{0,1:T(4,128)} %param.11) | copy-start | bytes 3076
  2.8 13.3 %collective-permute-start.2 = (bf16[32,16,256]{2,1,0:T(8,128)(2,1)}, bf16[32,16,256]{2,1,0:T(8,128)(2,1)S(1)}, u32[]{:S(2)}, u32[]{:S(2)}) collective-permute-start(bf16[32,16,256]{2,1,0:T(8,128)(2,1)} %get-tuple-element.68), channel_id=1, source_target_pairs={{0,64},{64,128},{128,192},{192,0},{1,65},{65,129},{129,193},{193,1... | collective-permute-start | bytes 786440 | tf_op jit(solution)/shard_map/ppermute | solution.py:26
  4.8 11.3 %collective-permute-start.3 = (bf16[32,16,256]{2,1,0:T(8,128)(2,1)}, bf16[32,16,256]{2,1,0:T(8,128)(2,1)S(1)}, u32[]{:S(2)}, u32[]{:S(2)}) collective-permute-start(bf16[32,16,256]{2,1,0:T(8,128)(2,1)} %get-tuple-element.69), channel_id=1, source_target_pairs={{0,192},{64,0},{128,64},{192,128},{1,193},{65,1},{129,65},{193,129... | collective-permute-start | bytes 786440 | tf_op jit(solution)/shard_map/ppermute | solution.py:26
  8.8 7.3 %copy-start.12 = (s32[64]{0:T(128)S(1)}, s32[64]{0:T(128)}, u32[]{:S(2)}) copy-start(s32[64]{0:T(128)} %param.10) | copy-start | bytes 772
  8.8 10.9 %copy-start.2 = (f32[64,16,256]{2,1,0:T(8,128)S(1)}, f32[64,16,256]{2,1,0:T(8,128)}, u32[]{:S(2)}) copy-start(f32[64,16,256]{2,1,0:T(8,128)} %param.16) | copy-start | bytes 3145732
  10.2 9.5 %collective-permute-start = (bf16[32,16,256]{2,1,0:T(8,128)(2,1)}, bf16[32,16,256]{2,1,0:T(8,128)(2,1)S(1)}, u32[]{:S(2)}, u32[]{:S(2)}) collective-permute-start(bf16[32,16,256]{2,1,0:T(8,128)(2,1)} %get-tuple-element.74), channel_id=1, source_target_pairs={{0,64},{64,128},{128,192},{192,0},{1,65},{65,129},{129,193},{193,1... | collective-permute-start | bytes 786440 | tf_op jit(solution)/shard_map/ppermute | solution.py:26
  10.3 9.4 %collective-permute-start.1 = (bf16[32,16,256]{2,1,0:T(8,128)(2,1)S(1)}, bf16[32,16,256]{2,1,0:T(8,128)(2,1)S(1)}, u32[]{:S(2)}, u32[]{:S(2)}) collective-permute-start(bf16[32,16,256]{2,1,0:T(8,128)(2,1)S(1)} %get-tuple-element.75), channel_id=1, source_target_pairs={{0,192},{64,0},{128,64},{192,128},{1,193},{65,1},{129,65},{193,129... | collective-permute-start | bytes 786440 | tf_op jit(solution)/shard_map/ppermute | solution.py:26
  13.2 6.5 %copy-start.3 = (f32[64,16,256]{2,1,0:T(8,128)S(1)}, f32[64,16,256]{2,1,0:T(8,128)}, u32[]{:S(2)}) copy-start(f32[64,16,256]{2,1,0:T(8,128)} %param.17) | copy-start | bytes 3145732
  17.0 6.7 %collective-permute-start.4 = (bf16[32,16,256]{2,1,0:T(8,128)(2,1)}, bf16[32,16,256]{2,1,0:T(8,128)(2,1)}, u32[]{:S(2)}, u32[]{:S(2)}) collective-permute-start(bf16[32,16,256]{2,1,0:T(8,128)(2,1)} %get-tuple-element.87), channel_id=1, source_target_pairs={{0,64},{64,128},{128,192},{192,0},{1,65},{65,129},{129,193},{193,1... | collective-permute-start | bytes 786440 | tf_op jit(solution)/shard_map/ppermute | solution.py:26
  17.0 6.7 %collective-permute-start.5 = (bf16[32,16,256]{2,1,0:T(8,128)(2,1)}, bf16[32,16,256]{2,1,0:T(8,128)(2,1)}, u32[]{:S(2)}, u32[]{:S(2)}) collective-permute-start(bf16[32,16,256]{2,1,0:T(8,128)(2,1)} %get-tuple-element.88), channel_id=1, source_target_pairs={{0,192},{64,0},{128,64},{192,128},{1,193},{65,1},{129,65},{193,129... | collective-permute-start | bytes 786440 | tf_op jit(solution)/shard_map/ppermute | solution.py:26
  19.7 4.1 %copy-start.11 = (bf16[11,128,256]{2,1,0:T(8,128)(2,1)S(1)}, bf16[11,128,256]{2,1,0:T(8,128)(2,1)}, u32[]{:S(2)}) copy-start(bf16[11,128,256]{2,1,0:T(8,128)(2,1)} %get-tuple-element.101) | copy-start | bytes 2162692
  19.7 6.7 %copy-start.6 = (bf16[11,128,256]{2,1,0:T(8,128)(2,1)S(1)}, bf16[11,128,256]{2,1,0:T(8,128)(2,1)}, u32[]{:S(2)}) copy-start(bf16[11,128,256]{2,1,0:T(8,128)(2,1)} %get-tuple-element.106.refs_10_) | copy-start | bytes 2162692
  23.8 22.2 %collective-permute-start.7 = (bf16[11,128,256]{2,1,0:T(8,128)(2,1)S(1)}, bf16[11,128,256]{2,1,0:T(8,128)(2,1)S(1)}, u32[]{:S(2)}, u32[]{:S(2)}) collective-permute-start(bf16[11,128,256]{2,1,0:T(8,128)(2,1)S(1)} %copy-done.11), channel_id=1, source_target_pairs={{0,192},{64,0},{128,64},{192,128},{1,193},{65,1},{129,65},{193,129... | collective-permute-start | bytes 2162696 | tf_op jit(solution)/shard_map/ppermute | solution.py:26
  26.4 19.5 %collective-permute-start.6 = (bf16[11,128,256]{2,1,0:T(8,128)(2,1)S(1)}, bf16[11,128,256]{2,1,0:T(8,128)(2,1)S(1)}, u32[]{:S(2)}, u32[]{:S(2)}) collective-permute-start(bf16[11,128,256]{2,1,0:T(8,128)(2,1)S(1)} %copy-done.6), channel_id=1, source_target_pairs={{0,64},{64,128},{128,192},{192,0},{1,65},{65,129},{129,193},{193,1... | collective-permute-start | bytes 2162696 | tf_op jit(solution)/shard_map/ppermute | solution.py:26
  30.5 35.5 %all-to-all-start = ((bf16[64,40,128]{2,1,0:T(8,128)(2,1)}), bf16[64,40,128]{2,1,0:T(8,128)(2,1)}, u32[]{:S(2)}, u32[]{:S(2)}) async-start(bf16[64,40,128]{2,1,0:T(8,128)(2,1)} %get-tuple-element.98), calls=%async_computation | async-start | bytes 1310720 | tf_op jit(solution)/shard_map/all_to_all | solution.py:382
  47.0 10.7 %collective-permute-start.8 = (bf16[5,128,256]{2,1,0:T(8,128)(2,1)S(1)}, bf16[5,128,256]{2,1,0:T(8,128)(2,1)S(1)}, u32[]{:S(2)}, u32[]{:S(2)}) collective-permute-start(bf16[5,128,256]{2,1,0:T(8,128)(2,1)S(1)} %get-tuple-element.102), channel_id=1, source_target_pairs={{0,64},{64,128},{128,192},{192,0},{1,65},{65,129},{129,193},{193,1... | collective-permute-start | bytes 983048 | tf_op jit(solution)/shard_map/ppermute | solution.py:26
  47.0 10.7 %collective-permute-start.9 = (bf16[5,128,256]{2,1,0:T(8,128)(2,1)S(1)}, bf16[5,128,256]{2,1,0:T(8,128)(2,1)S(1)}, u32[]{:S(2)}, u32[]{:S(2)}) collective-permute-start(bf16[5,128,256]{2,1,0:T(8,128)(2,1)S(1)} %get-tuple-element.103), channel_id=1, source_target_pairs={{0,192},{64,0},{128,64},{192,128},{1,193},{65,1},{129,65},{193,129... | collective-permute-start | bytes 983048 | tf_op jit(solution)/shard_map/ppermute | solution.py:26
  57.7 32.2 %copy-start.7 = (bf16[5,128,256]{2,1,0:T(8,128)(2,1)}, bf16[5,128,256]{2,1,0:T(8,128)(2,1)S(1)}, u32[]{:S(2)}) copy-start(bf16[5,128,256]{2,1,0:T(8,128)(2,1)S(1)} %collective-permute-done.8.refs_13_) | copy-start | bytes 983044
  57.7 32.2 %copy-start.8 = (bf16[5,128,256]{2,1,0:T(8,128)(2,1)}, bf16[5,128,256]{2,1,0:T(8,128)(2,1)S(1)}, u32[]{:S(2)}) copy-start(bf16[5,128,256]{2,1,0:T(8,128)(2,1)S(1)} %collective-permute-done.9.refs_14_) | copy-start | bytes 983044
  67.1 8.4 %collective-permute-start.11 = (bf16[32,16,256]{2,1,0:T(8,128)(2,1)S(1)}, bf16[32,16,256]{2,1,0:T(8,128)(2,1)S(1)}, u32[]{:S(2)}, u32[]{:S(2)}) collective-permute-start(bf16[32,16,256]{2,1,0:T(8,128)(2,1)S(1)} %get-tuple-element.119), channel_id=1, source_target_pairs={{0,192},{64,0},{128,64},{192,128},{1,193},{65,1},{129,65},{193,129... | collective-permute-start | bytes 786440 | tf_op jit(solution)/shard_map/ppermute | solution.py:26
  70.2 8.8 %collective-permute-start.12 = (bf16[32,16,256]{2,1,0:T(8,128)(2,1)S(1)}, bf16[32,16,256]{2,1,0:T(8,128)(2,1)S(1)}, u32[]{:S(2)}, u32[]{:S(2)}) collective-permute-start(bf16[32,16,256]{2,1,0:T(8,128)(2,1)S(1)} %get-tuple-element.118), channel_id=1, source_target_pairs={{0,64},{64,128},{128,192},{192,0},{1,65},{65,129},{129,193},{193,1... | collective-permute-start | bytes 786440 | tf_op jit(solution)/shard_map/ppermute | solution.py:26
  70.2 14.1 %collective-permute-start.15 = (bf16[32,16,256]{2,1,0:T(8,128)(2,1)S(1)}, bf16[32,16,256]{2,1,0:T(8,128)(2,1)S(1)}, u32[]{:S(2)}, u32[]{:S(2)}) collective-permute-start(bf16[32,16,256]{2,1,0:T(8,128)(2,1)S(1)} %get-tuple-element.119), channel_id=1, source_target_pairs={{0,64},{64,128},{128,192},{192,0},{1,65},{65,129},{129,193},{193,1... | collective-permute-start | bytes 786440 | tf_op jit(solution)/shard_map/ppermute | solution.py:26
  70.2 14.1 %collective-permute-start.10 = (bf16[32,16,256]{2,1,0:T(8,128)(2,1)S(1)}, bf16[32,16,256]{2,1,0:T(8,128)(2,1)S(1)}, u32[]{:S(2)}, u32[]{:S(2)}) collective-permute-start(bf16[32,16,256]{2,1,0:T(8,128)(2,1)S(1)} %get-tuple-element.118), channel_id=1, source_target_pairs={{0,192},{64,0},{128,64},{192,128},{1,193},{65,1},{129,65},{193,129... | collective-permute-start | bytes 786440 | tf_op jit(solution)/shard_map/ppermute | solution.py:26
  75.6 11.2 %collective-permute-start.14 = (bf16[32,16,256]{2,1,0:T(8,128)(2,1)S(1)}, bf16[32,16,256]{2,1,0:T(8,128)(2,1)S(1)}, u32[]{:S(2)}, u32[]{:S(2)}) collective-permute-start(bf16[32,16,256]{2,1,0:T(8,128)(2,1)S(1)} %collective-permute-done.11), channel_id=1, source_target_pairs={{0,192},{64,0},{128,64},{192,128},{1,193},{65,1},{129,65},{193,129... | collective-permute-start | bytes 786440 | tf_op jit(solution)/shard_map/ppermute | solution.py:26
  79.0 10.9 %collective-permute-start.13 = (bf16[32,16,256]{2,1,0:T(8,128)(2,1)S(1)}, bf16[32,16,256]{2,1,0:T(8,128)(2,1)S(1)}, u32[]{:S(2)}, u32[]{:S(2)}) collective-permute-start(bf16[32,16,256]{2,1,0:T(8,128)(2,1)S(1)} %collective-permute-done.12), channel_id=1, source_target_pairs={{0,64},{64,128},{128,192},{192,0},{1,65},{65,129},{129,193},{193,1... | collective-permute-start | bytes 786440 | tf_op jit(solution)/shard_map/ppermute | solution.py:26
  93.1 2.5 %collective-permute-start.18 = (f32[8,128]{1,0:T(8,128)S(1)}, f32[8,128]{1,0:T(8,128)S(1)}, u32[]{:S(2)}, u32[]{:S(2)}) collective-permute-start(f32[8,128]{1,0:T(8,128)S(1)} %get-tuple-element.112.first), channel_id=1, source_target_pairs={{0,192},{64,0},{128,64},{192,128},{1,193},{65,1},{129,65},{193,129... | collective-permute-start | bytes 12296 | tf_op jit(solution)/shard_map/ppermute | solution.py:26
  93.6 4.0 %collective-permute-start.17 = (f32[8,128]{1,0:T(8,128)S(1)}, f32[8,128]{1,0:T(8,128)S(1)}, u32[]{:S(2)}, u32[]{:S(2)}) collective-permute-start(f32[8,128]{1,0:T(8,128)S(1)} %get-tuple-element.112.first), channel_id=1, source_target_pairs={{0,128},{64,192},{128,0},{192,64},{1,129},{65,193},{129,1},{193,65... | collective-permute-start | bytes 12296 | tf_op jit(solution)/shard_map/ppermute | solution.py:26
  94.1 4.0 %collective-permute-start.16 = (f32[8,128]{1,0:T(8,128)S(1)}, f32[8,128]{1,0:T(8,128)S(1)}, u32[]{:S(2)}, u32[]{:S(2)}) collective-permute-start(f32[8,128]{1,0:T(8,128)S(1)} %get-tuple-element.112.first), channel_id=1, source_target_pairs={{0,64},{64,128},{128,192},{192,0},{1,65},{65,129},{129,193},{193,1... | collective-permute-start | bytes 12296 | tf_op jit(solution)/shard_map/ppermute | solution.py:26
  99.5 25.8 %all-to-all-start.1 = ((bf16[64,16,256]{2,1,0:T(8,128)(2,1)}), bf16[64,16,256]{2,1,0:T(8,128)(2,1)S(1)}, u32[]{:S(2)}, u32[]{:S(2)}) async-start(bf16[64,16,256]{2,1,0:T(8,128)(2,1)} %bitcast.14), calls=%async_computation.1 | async-start | bytes 1048576 | tf_op jit(solution)/shard_map/all_to_all | solution.py:410
  108.0 1.5 %copy-start.10 = (s32[64,4]{0,1:T(4,128)S(1)}, s32[64,4]{0,1:T(4,128)}, u32[]{:S(2)}) copy-start(s32[64,4]{0,1:T(4,128)} %param.11) | copy-start | bytes 3076
  112.3 3.1 %copy-start.4 = (bf16[64,16,1024]{2,1,0:T(8,128)(2,1)S(1)}, bf16[64,16,1024]{2,1,0:T(8,128)(2,1)}, u32[]{:S(2)}) copy-start(bf16[64,16,1024]{2,1,0:T(8,128)(2,1)} %maximum_maximum_fusion) | copy-start | bytes 6291460
  112.3 3.1 %copy-start.5 = (f32[1,256,1024]{2,1,0:T(8,128)S(1)}, f32[1,256,1024]{2,1,0:T(8,128)}, u32[]{:S(2)}) copy-start(f32[1,256,1024]{2,1,0:T(8,128)} %param.14) | copy-start | bytes 3145732
  (3 other events, 3.5 us)

commit v7 on v6

--- a/solution.py
+++ b/solution.py
@@ -16,6 +16,12 @@
 NORM_EPS = 1e-06
 F32 = jnp.float32
 BF16 = jnp.bfloat16
+ORDER = (
+    33, 58, 20, 47, 9, 3, 13, 23, 32, 10, 21, 15, 57, 18, 60, 38,
+    49, 11, 52, 31, 40, 34, 61, 55, 0, 27, 53, 46, 24, 2, 28, 54,
+    1, 26, 5, 63, 8, 51, 12, 39, 16, 43, 4, 30, 56, 35, 44, 22,
+    48, 59, 36, 14, 41, 50, 29, 7, 17, 42, 37, 62, 25, 19, 45, 6,
+)
 MIB = 1024 * 1024
 VMEM = pltpu.VMEM
 LONG = pl.CostEstimate(flops=2 * 10**11, bytes_accessed=10**9, transcendentals=0)
@@ -26,8 +32,10 @@
     return lax.ppermute(array, "grp", [(i, (i + step) % n) for i in range(n)])
 
 
-def slots_of(assign, n_own, per_owner):
-    return (assign % n_own * per_owner + assign // n_own).astype(jnp.int32)
+def places_of(assign, n_own, per_owner, order):
+    place = [order.index(slot) for slot in range(len(order))]
+    key = assign % n_own * per_owner + assign // n_own
+    return jnp.asarray(place, jnp.int32)[key]
 
 
 def in_hbm(array):
@@ -201,6 +209,32 @@
         compiler_params=pltpu.CompilerParams(vmem_limit_bytes=6 * MIB),
         cost_estimate=LONG,
     )(prev, following)
+
+
+def unpack_kernel(order, owned, low, high, adam):
+    half, rows, cols = low.shape
+    total = jnp.zeros(adam.shape, F32)
+    for i, place in enumerate(order):
+        piece = owned[i].astype(F32)
+        value = jnp.concatenate([piece[:rows], piece[rows : 2 * rows]], axis=1).astype(BF16)
+        if place < half:
+            low[place] = value
+        else:
+            high[place - half] = value
+        total += piece[2 * rows :]
+    adam[...] = total
+
+
+def unpack(order, owned, rows):
+    half = owned.shape[0] // 2
+    shape = jax.ShapeDtypeStruct((half, rows, 2 * owned.shape[2]), BF16)
+    return pl.pallas_call(
+        functools.partial(unpack_kernel, order),
+        out_shape=(shape, shape, jax.ShapeDtypeStruct((rows // 2, 128), F32)),
+        in_specs=[pl.BlockSpec(memory_space=VMEM)],
+        out_specs=(pl.BlockSpec(memory_space=VMEM),) * 3,
+        compiler_params=pltpu.CompilerParams(vmem_limit_bytes=6 * MIB),
+    )(owned)
 
 
 def finish_kernel(key, bounds, back, out):
@@ -273,7 +307,7 @@
         square += jnp.sum((value * value).reshape(quarter // 8, 8, quarter), axis=0)
     norms[...] = jnp.zeros_like(norms)
     norms[0:1, :] = jnp.broadcast_to(jnp.sum(square), (1, 128))
-    norms[1:2, :] = jnp.broadcast_to(jnp.sum(adam[...].astype(F32)), (1, 128))
+    norms[1:2, :] = jnp.broadcast_to(jnp.sum(adam[...]), (1, 128))
 
 
 def precondition(pieces, adam, sources):
@@ -297,28 +331,28 @@
     )(*operands, *map(in_hbm, sources))
 
 
-def graft_kernel(cells, precond, first, second, third, fourth, out):
+def graft_kernel(cells, order, precond, first, second, third, fourth, out):
     sums = first[...] + second[...] + third[...] + fourth[...]
     pre, adam = sums[0:1, :], sums[1:2, :]
     adam = adam * (BIAS_SECOND / (BIAS_FIRST * BIAS_FIRST))
     scale = -jnp.sqrt(adam / cells) / jnp.sqrt(pre / cells + NORM_EPS)
-    width, quarter = out.shape
+    _, rows, quarter = out.shape
     scale = jnp.concatenate([scale] * (quarter // 128), axis=1)
-    out[...] = (scale * precond[...]).astype(BF16)
-
-
-def graft(precond, norms):
+    for i, place in enumerate(order):
+        out[i] = (scale * precond[pl.ds(place * rows, rows), :]).astype(BF16)
+
+
+def graft(order, precond, norms):
     width, quarter = precond.shape
-    tiles = 4
-    rows = width // tiles
+    shape = (len(order), width // len(order), quarter)
     small = pl.BlockSpec((8, 128), lambda i: (0, 0))
     return pl.pallas_call(
-        functools.partial(graft_kernel, float(width * width)),
-        out_shape=jax.ShapeDtypeStruct((width, quarter), BF16),
-        grid=(tiles,),
-        in_specs=[pl.BlockSpec((rows, quarter), lambda i: (i, 0))] + [small] * 4,
-        out_specs=pl.BlockSpec((rows, quarter), lambda i: (i, 0)),
-        compiler_params=pltpu.CompilerParams(vmem_limit_bytes=6 * MIB),
+        functools.partial(graft_kernel, float(width * width), order),
+        out_shape=pltpu.HBM(shape, BF16),
+        grid=(1,),
+        in_specs=[pl.BlockSpec((width, quarter), lambda i: (0, 0))] + [small] * 4,
+        out_specs=pl.BlockSpec(shape, lambda i: (0, 0, 0)),
+        compiler_params=pltpu.CompilerParams(vmem_limit_bytes=8 * MIB),
     )(precond, *norms)
 
 
@@ -350,6 +384,12 @@
         return slice_at(array, starts[step], quarter, array.ndim - 1)
 
     part = grad_parts[0]
+    order = ORDER if len(ORDER) == n_own else tuple(range(n_own))
+
+    def exchange(array):
+        groups = [list(order)]
+        return lax.all_to_all(array, "own", 0, 0, axis_index_groups=groups, tiled=True)
+
     far = columns(part, 2)
     far_low, far_high = lax.optimization_barrier((far[:half], far[half:]))
     far_up = shift(far_low, 1)
@@ -366,7 +406,7 @@
     up_sum, down_sum = add(up_low, far_up, down_high, far_down)
     up_sum = shift(up_sum, 1)
     down_sum = shift(down_sum, -1)
-    key, bounds = slots_of(assign, n_own, per_owner), block_bounds.reshape(-1)
+    key, bounds = places_of(assign, n_own, per_owner, order), block_bounds.reshape(-1)
     roots_up, roots_down, root_own = root_pieces(left_root, right_root)
     up_direct, down_direct, key, bounds, roots_up, roots_down, root_own = lax.optimization_barrier(
         (up_direct, down_direct, key, bounds, roots_up, roots_down, root_own)
@@ -379,7 +419,7 @@
     sorted_grad, first_next, second_next = pack(
         key, bounds, partial, up_sum, down_sum, first, second
     )
-    owned = lax.all_to_all(sorted_grad, "own", split_axis=0, concat_axis=0, tiled=True)
+    owned = exchange(sorted_grad)
     roots_prev = shift(roots_up, 1)
     roots_next = shift(roots_down, -1)
     onward = relay(roots_prev, roots_next)
@@ -387,11 +427,7 @@
     roots = [root_own, roots_up, roots_prev, roots_next, *far_roots]
 
     owned, roots = lax.optimization_barrier((owned, roots))
-    own_cols = jnp.concatenate(
-        [owned[:, :shard_rows], owned[:, shard_rows : 2 * shard_rows]], axis=2
-    )
-    adam = owned[:, 2 * shard_rows :].reshape(-1, quarter // 2)
-    low, high = own_cols[:half], own_cols[half:]
+    low, high, adam = unpack(order, owned, shard_rows)
     prev_low = shift(low, 1)
     next_high = shift(high, -1)
     prev_high = shift(high, 1)
@@ -402,12 +438,12 @@
     flat = [piece.reshape(-1, quarter) for piece in pieces]
     precond, norms = precondition(flat, adam, roots)
     norms = [norms] + [shift(norms, step) for step in (1, 2, 3)]
-    grafted = graft(precond, norms).reshape(n_own, shard_rows, quarter)
+    grafted = graft(order, precond, norms)
     pieces, grafted, assign, bounds = lax.optimization_barrier(
         (pieces, grafted, assign, block_bounds)
     )
-    key, bounds = slots_of(assign, n_own, per_owner), bounds.reshape(-1)
-    back = lax.all_to_all(grafted, "own", split_axis=0, concat_axis=0, tiled=True)
+    key, bounds = places_of(assign, n_own, per_owner, order), bounds.reshape(-1)
+    back = exchange(grafted)
 
     whole = jnp.concatenate(
         [jnp.concatenate(pieces[i : i + 2]) for i in (0, 2, 4, 6)], axis=2

time: 128 us -> 125 us (0.977)
  waiting for transfers between devices: 44 us -> 40.8 us
  starting transfers between devices: 49.2 us -> 51 us
  local copies, waits for them, and re-layouts: 9.48 us -> 7.83 us
    all_to_all x2, waiting for transfers between devices: 16.5 us -> 13.5 us  [exchange(): lax.all_to_all(array, 'own', 0, 0, axis_index_groups=groups, tiled=True)]
    all_to_all x2, starting transfers between devices: 23.9 us -> 25.7 us  [exchange(): lax.all_to_all(array, 'own', 0, 0, axis_index_groups=groups, tiled=True)]
    gather x0 -> x2, local copies, waits for them, and re-layouts: none -> 1.56 us  [places_of(): return jnp.asarray(place, jnp.int32)[key]]
    slice x1, local copies, waits for them, and re-layouts: 2.42 us -> 1.13 us  [on_device(): down[half:]]
  transfers between devices with their start and end apart: 21 -> 21, of which waited for: 11 -> 10; matrix products, arithmetic and copies ran while one was open for 11% -> 11% of each run, Pallas kernels for 6% -> 7%
where the time goes in v7:
time: 125 us
  starting transfers between devices  51 us (41%)
  waiting for transfers between devices  40.8 us (33%)
  Pallas kernels  15.3 us (12%)
  local copies, waits for them, and re-layouts  7.83 us (6%)
  other arithmetic  4.6 us (4%)
  matrix products  4.24 us (3%)
    ppermute x19, waiting for transfers between devices, shift(): return lax.ppermute(array, 'grp', [(i, (i + step) % n) for i in range(n)])  27.3 us
    all_to_all x2, starting transfers between devices, exchange(): lax.all_to_all(array, 'own', 0, 0, axis_index_groups=groups, tiled=True)  25.7 us
    ppermute x19, starting transfers between devices, shift(): return lax.ppermute(array, 'grp', [(i, (i + step) % n) for i in range(n)])  25.4 us
    all_to_all x2, waiting for transfers between devices, exchange(): lax.all_to_all(array, 'own', 0, 0, axis_index_groups=groups, tiled=True)  13.5 us
    dot_general x2, matrix products, dot(): return lax.dot_general(a, b, (dims, ((), ())), preferred_element_type=F32)  4.24 us
    pallas_call x1, Pallas kernels, pack(): pl.pallas_call(pack_kernel, out_shape=(pltpu.HBM(piece, BF16), halves, ha...  4.04 us
    pallas_call x1, Pallas kernels, precondition(): pl.pallas_call(precond_kernel, out_shape=(jax.ShapeDtypeStruct((2 * rows,...  3.22 us
    add x1, other arithmetic, on_device(): right_acc = STAT_DECAY * right_stat + cross[None]  3.04 us
  transfers between devices with their start and end apart: 21, of which 10 were waited for; matrix products, arithmetic and copies ran while one was open for 11% of the time, Pallas kernels for 7%

profile of v7, /device:TPU:1, one launch (start us, length us, event | category | flops | bytes accessed | tf_op | source)
XLA Modules:
  0.0 124.7 jit_solution(329464337128060990)
XLA Ops:
  0.7 2.3 %dynamic-slice_bitcast_fusion = (bf16[32,16,256]{2,1,0:T(8,128)(2,1)}, bf16[32,16,256]{2,1,0:T(8,128)(2,1)}) fusion(bf16[1,64,16,1024]{3,2,1,0:T(8,128)(2,1)} %param.11, s32[]{:T(128)S(6)} %add.50, s32[]{:T(128)S(6)} %mul.23), kind=kLoop, calls=%fused_computation.13 | loop fusion | bytes 1048584 | tf_op jit(solution)/shard_map/slice | solution.py:394
  3.0 2.0 %collective-permute-start.2 = (bf16[32,16,256]{2,1,0:T(8,128)(2,1)}, bf16[32,16,256]{2,1,0:T(8,128)(2,1)S(1)}, u32[]{:S(2)}, u32[]{:S(2)}) collective-permute-start(bf16[32,16,256]{2,1,0:T(8,128)(2,1)} %get-tuple-element.71), channel_id=1, source_target_pairs={{0,64},{64,128},{128,192},{192,0},{1,65},{65,129},{129,193},{193,1... | collective-permute-start | bytes 786440 | tf_op jit(solution)/shard_map/ppermute | solution.py:32
  5.0 1.5 %collective-permute-start.3 = (bf16[32,16,256]{2,1,0:T(8,128)(2,1)}, bf16[32,16,256]{2,1,0:T(8,128)(2,1)S(1)}, u32[]{:S(2)}, u32[]{:S(2)}) collective-permute-start(bf16[32,16,256]{2,1,0:T(8,128)(2,1)} %get-tuple-element.72), channel_id=1, source_target_pairs={{0,192},{64,0},{128,64},{192,128},{1,193},{65,1},{129,65},{193,129... | collective-permute-start | bytes 786440 | tf_op jit(solution)/shard_map/ppermute | solution.py:32
  6.5 1.4 %constant_dynamic-slice_fusion.2.own = bf16[64,16,256]{2,1,0:T(8,128)(2,1)S(1)} fusion(bf16[64,16,1024]{2,1,0:T(8,128)(2,1)} %bitcast.40, s32[]{:T(128)S(6)} %mul.21), kind=kLoop, calls=%fused_computation.22 | loop fusion | bytes 1048580 | tf_op jit(solution)/shard_map/dynamic_slice | solution.py:48
  7.9 1.1 constant_dynamic-slice_fusion.3
  9.1 2.7 %collective-permute-start.1 = (bf16[32,16,256]{2,1,0:T(8,128)(2,1)S(1)}, bf16[32,16,256]{2,1,0:T(8,128)(2,1)S(1)}, u32[]{:S(2)}, u32[]{:S(2)}) collective-permute-start(bf16[32,16,256]{2,1,0:T(8,128)(2,1)S(1)} %get-tuple-element.78), channel_id=1, source_target_pairs={{0,192},{64,0},{128,64},{192,128},{1,193},{65,1},{129,65},{193,129... | collective-permute-start | bytes 786440 | tf_op jit(solution)/shard_map/ppermute | solution.py:32
  12.8 2.9 %shard_map.146 = (bf16[11,128,256]{2,1,0:T(8,128)(2,1)}, bf16[11,128,256]{2,1,0:T(8,128)(2,1)}, bf16[2,128,256]{2,1,0:T(8,128)(2,1)}) custom-call(f32[1,256,1024]{2,1,0:T(8,128)} %left, f32[1,256,1024]{2,1,0:T(8,128)} %right), custom_call_target="tpu_custom_call" | custom-call | tf_op jit(solution)/shard_map/pallas_call | solution.py:101
  16.5 2.7 %collective-permute-start.5 = (bf16[32,16,256]{2,1,0:T(8,128)(2,1)}, bf16[32,16,256]{2,1,0:T(8,128)(2,1)}, u32[]{:S(2)}, u32[]{:S(2)}) collective-permute-start(bf16[32,16,256]{2,1,0:T(8,128)(2,1)} %get-tuple-element.91), channel_id=1, source_target_pairs={{0,192},{64,0},{128,64},{192,128},{1,193},{65,1},{129,65},{193,129... | collective-permute-start | bytes 786440 | tf_op jit(solution)/shard_map/ppermute | solution.py:32
  19.6 3.7 %collective-permute-done.4.up_sum = bf16[32,16,256]{2,1,0:T(8,128)(2,1)} collective-permute-done((bf16[32,16,256]{2,1,0:T(8,128)(2,1)}, bf16[32,16,256]{2,1,0:T(8,128)(2,1)}, u32[]{:S(2)}, u32[]{:S(2)}) %collective-permute-start.4) | collective-permute-done | bytes 262176 | tf_op jit(solution)/shard_map/ppermute | solution.py:32
  23.3 2.7 %collective-permute-start.7 = (bf16[11,128,256]{2,1,0:T(8,128)(2,1)}, bf16[11,128,256]{2,1,0:T(8,128)(2,1)S(1)}, u32[]{:S(2)}, u32[]{:S(2)}) collective-permute-start(bf16[11,128,256]{2,1,0:T(8,128)(2,1)} %get-tuple-element.104), channel_id=1, source_target_pairs={{0,192},{64,0},{128,64},{192,128},{1,193},{65,1},{129,65},{193,129... | collective-permute-start | bytes 2162696 | tf_op jit(solution)/shard_map/ppermute | solution.py:32
  26.0 4.0 %shard_map.149 = (bf16[64,40,128]{2,1,0:T(8,128)(2,1)}, f32[2,32,16,256]{3,2,1,0:T(8,128)}, f32[2,32,16,256]{3,2,1,0:T(8,128)}) custom-call(s32[64]{0:T(128)S(1)} %gather_fusion, s32[256]{0:T(256)S(1)} %reshape.58.bounds, f32[2,32,16,256]{3,2,1,0:T(8,128)S(1)} %get-tuple-element.96.partial, bf16[32,16,256]{2,1,0:T(8,128)(2,1)} %collective-permute-done.4.up_sum, ...), custom_call_target="tpu_custom_call" | custom-call | tf_op jit(solution)/shard_map/pallas_call | solution.py:181
  30.0 16.0 %all-to-all-start = ((bf16[64,40,128]{2,1,0:T(8,128)(2,1)}), bf16[64,40,128]{2,1,0:T(8,128)(2,1)}, u32[]{:S(2)}, u32[]{:S(2)}) async-start(bf16[64,40,128]{2,1,0:T(8,128)(2,1)} %get-tuple-element.101), calls=%async_computation | async-start | bytes 1310720 | tf_op jit(solution)/shard_map/all_to_all | solution.py:391
  47.2 3.0 %collective-permute-start.9 = (bf16[5,128,256]{2,1,0:T(8,128)(2,1)S(1)}, bf16[5,128,256]{2,1,0:T(8,128)(2,1)S(1)}, u32[]{:S(2)}, u32[]{:S(2)}) collective-permute-start(bf16[5,128,256]{2,1,0:T(8,128)(2,1)S(1)} %get-tuple-element.106), channel_id=1, source_target_pairs={{0,192},{64,0},{128,64},{192,128},{1,193},{65,1},{129,65},{193,129... | collective-permute-start | bytes 983048 | tf_op jit(solution)/shard_map/ppermute | solution.py:32
  50.1 7.9 %collective-permute-done.8.refs_13_ = bf16[5,128,256]{2,1,0:T(8,128)(2,1)S(1)} collective-permute-done((bf16[5,128,256]{2,1,0:T(8,128)(2,1)S(1)}, bf16[5,128,256]{2,1,0:T(8,128)(2,1)S(1)}, u32[]{:S(2)}, u32[]{:S(2)}) %collective-permute-start.8) | collective-permute-done | bytes 327712 | tf_op jit(solution)/shard_map/ppermute | solution.py:32
  58.1 7.1 %all-to-all-done.owned = bf16[64,40,128]{2,1,0:T(8,128)(2,1)} async-done(((bf16[64,40,128]{2,1,0:T(8,128)(2,1)}), bf16[64,40,128]{2,1,0:T(8,128)(2,1)}, u32[]{:S(2)}, u32[]{:S(2)}) %all-to-all-start) | async-done | bytes 655392 | tf_op jit(solution)/shard_map/all_to_all | solution.py:391
  65.2 1.2 shard_map.151
  66.4 3.2 %collective-permute-start.11 = (bf16[32,16,256]{2,1,0:T(8,128)(2,1)S(1)}, bf16[32,16,256]{2,1,0:T(8,128)(2,1)S(1)}, u32[]{:S(2)}, u32[]{:S(2)}) collective-permute-start(bf16[32,16,256]{2,1,0:T(8,128)(2,1)S(1)} %get-tuple-element.125), channel_id=1, source_target_pairs={{0,192},{64,0},{128,64},{192,128},{1,193},{65,1},{129,65},{193,129... | collective-permute-start | bytes 786440 | tf_op jit(solution)/shard_map/ppermute | solution.py:32
  69.6 1.2 collective-permute-start.10
  71.1 3.8 %collective-permute-done.12 = bf16[32,16,256]{2,1,0:T(8,128)(2,1)S(1)} collective-permute-done((bf16[32,16,256]{2,1,0:T(8,128)(2,1)S(1)}, bf16[32,16,256]{2,1,0:T(8,128)(2,1)S(1)}, u32[]{:S(2)}, u32[]{:S(2)}) %collective-permute-start.12) | collective-permute-done | bytes 262176 | tf_op jit(solution)/shard_map/ppermute | solution.py:32
  74.9 2.7 %collective-permute-start.14 = (bf16[32,16,256]{2,1,0:T(8,128)(2,1)S(1)}, bf16[32,16,256]{2,1,0:T(8,128)(2,1)S(1)}, u32[]{:S(2)}, u32[]{:S(2)}) collective-permute-start(bf16[32,16,256]{2,1,0:T(8,128)(2,1)S(1)} %collective-permute-done.11), channel_id=1, source_target_pairs={{0,192},{64,0},{128,64},{192,128},{1,193},{65,1},{129,65},{193,129... | collective-permute-start | bytes 786440 | tf_op jit(solution)/shard_map/ppermute | solution.py:32
  77.6 2.2 %collective-permute-done.10 = bf16[32,16,256]{2,1,0:T(8,128)(2,1)S(1)} collective-permute-done((bf16[32,16,256]{2,1,0:T(8,128)(2,1)S(1)}, bf16[32,16,256]{2,1,0:T(8,128)(2,1)S(1)}, u32[]{:S(2)}, u32[]{:S(2)}) %collective-permute-start.10) | collective-permute-done | bytes 262176 | tf_op jit(solution)/shard_map/ppermute | solution.py:32
  80.5 5.6 %collective-permute-done.13 = bf16[32,16,256]{2,1,0:T(8,128)(2,1)S(1)} collective-permute-done((bf16[32,16,256]{2,1,0:T(8,128)(2,1)S(1)}, bf16[32,16,256]{2,1,0:T(8,128)(2,1)S(1)}, u32[]{:S(2)}, u32[]{:S(2)}) %collective-permute-start.13) | collective-permute-done | bytes 262176 | tf_op jit(solution)/shard_map/ppermute | solution.py:32
  86.2 3.2 %shard_map.152 = (f32[1024,256]{1,0:T(8,128)S(1)}, f32[8,128]{1,0:T(8,128)S(1)}) custom-call(bf16[512,256]{1,0:T(8,128)(2,1)S(1)} %bitcast.28, bf16[512,256]{1,0:T(8,128)(2,1)S(1)} %bitcast.29, bf16[512,256]{1,0:T(8,128)(2,1)S(1)} %bitcast.32, bf16[512,256]{1,0:T(8,128)(2,1)S(1)} %bitcast.31, bf16[512,256]{1,0:T(8,128)(2,1)S(1)} %bitcast.34, ...), custom_call_target="tpu_custom_call" | custom-call | tf_op jit(solution)/shard_map/pallas_call | solution.py:316
  89.4 2.7 %collective-permute-start.18 = (f32[8,128]{1,0:T(8,128)S(1)}, f32[8,128]{1,0:T(8,128)S(1)}, u32[]{:S(2)}, u32[]{:S(2)}) collective-permute-start(f32[8,128]{1,0:T(8,128)S(1)} %get-tuple-element.118.first), channel_id=1, source_target_pairs={{0,192},{64,0},{128,64},{192,128},{1,193},{65,1},{129,65},{193,129... | collective-permute-start | bytes 12296 | tf_op jit(solution)/shard_map/ppermute | solution.py:32
  92.9 3.2 %collective-permute-done.17.third = f32[8,128]{1,0:T(8,128)S(1)} collective-permute-done((f32[8,128]{1,0:T(8,128)S(1)}, f32[8,128]{1,0:T(8,128)S(1)}, u32[]{:S(2)}, u32[]{:S(2)}) %collective-permute-start.17) | collective-permute-done | bytes 4128 | tf_op jit(solution)/shard_map/ppermute | solution.py:32
  97.0 9.6 %all-to-all-start.1 = ((bf16[64,16,256]{2,1,0:T(8,128)(2,1)}), bf16[64,16,256]{2,1,0:T(8,128)(2,1)S(1)}, u32[]{:S(2)}, u32[]{:S(2)}) async-start(bf16[64,16,256]{2,1,0:T(8,128)(2,1)} %shard_map.153), calls=%async_computation.1 | async-start | bytes 1048576 | tf_op jit(solution)/shard_map/all_to_all | solution.py:391
  106.6 1.5 %maximum_maximum_fusion = bf16[64,16,1024]{2,1,0:T(8,128)(2,1)} fusion(bf16[32,16,256]{2,1,0:T(8,128)(2,1)S(1)} %collective-permute-done.15, bf16[32,16,256]{2,1,0:T(8,128)(2,1)S(1)} %collective-permute-done.12, bf16[32,16,256]{2,1,0:T(8,128)(2,1)S(1)} %collective-permute-done.14, bf16[32,16,256]{2,1,0:T(8,128)(2,1)S(1)} %collective-permute-done.13, ...), kind=kLoop, calls=%fused_computation.2 | loop fusion | flops 16777216 | bytes 4194304 | tf_op jit(solution)/shard_map/concatenate | solution.py:448
  109.1 2.5 %fusion.4 = f32[256,1024]{1,0:T(8,128)S(1)} fusion(bf16[1024,1024]{1,0:T(8,128)(2,1)} %bitcast.38), kind=kOutput, calls=%fused_computation.10 | convolution fusion | flops 536870912 | bytes 3670016 | tf_op jit(solution)/shard_map/dot_general | solution.py:52
  111.7 3.0 %fusion.3 = f32[1,256,1024]{2,1,0:T(8,128)} fusion(s32[]{:T(128)S(6)} %mul.25, f32[256,1024]{1,0:T(8,128)S(1)} %fusion.4, f32[1,256,1024]{2,1,0:T(8,128)} %param.17), kind=kLoop, calls=%fused_computation.9 | loop fusion | flops 786432 | bytes 3145732 | tf_op jit(solution)/shard_map/add | solution.py:456
  114.7 1.7 %fusion = f32[1,256,1024]{2,1,0:T(8,128)} fusion(bf16[1024,1024]{1,0:T(8,128)(2,1)S(1)} %bitcast.39, f32[1,256,1024]{2,1,0:T(8,128)S(1)} %copy-done.8, s32[]{:T(128)S(6)} %mul.21), kind=kOutput, calls=%fused_computation.6 | convolution fusion | flops 537395200 | bytes 4718596 | tf_op jit(solution)/shard_map/dot_general | solution.py:52
  116.4 6.4 %all-to-all-done.1.back = bf16[64,16,256]{2,1,0:T(8,128)(2,1)S(1)} async-done(((bf16[64,16,256]{2,1,0:T(8,128)(2,1)}), bf16[64,16,256]{2,1,0:T(8,128)(2,1)S(1)}, u32[]{:S(2)}, u32[]{:S(2)}) %all-to-all-start.1) | async-done | bytes 524320 | tf_op jit(solution)/shard_map/all_to_all | solution.py:391
  122.9 1.8 %shard_map.154 = bf16[64,16,256]{2,1,0:T(8,128)(2,1)} custom-call(s32[64]{0:T(128)S(1)} %gather_fusion.1, s32[256]{0:T(256)S(1)} %reshape.69.bounds, bf16[64,16,256]{2,1,0:T(8,128)(2,1)S(1)} %all-to-all-done.1.back), custom_call_target="tpu_custom_call" | custom-call | tf_op jit(solution)/shard_map/pallas_call | solution.py:253
  (68 shorter events, 7.1 us)
Async XLA Ops:
  0.6 7.3 %copy-start.7 = (bf16[1,64,16,1024]{3,2,1,0:T(8,128)(2,1)S(1)}, bf16[1,64,16,1024]{3,2,1,0:T(8,128)(2,1)}, u32[]{:S(2)}) copy-start(bf16[1,64,16,1024]{3,2,1,0:T(8,128)(2,1)} %param.11) | copy-start | bytes 6291460
  0.7 11.1 %copy-start.12 = (s32[64,4]{0,1:T(4,128)S(1)}, s32[64,4]{0,1:T(4,128)}, u32[]{:S(2)}) copy-start(s32[64,4]{0,1:T(4,128)} %param.13) | copy-start | bytes 3076
  0.7 11.3 %copy-start.14 = (s32[64]{0:T(128)S(1)}, s32[64]{0:T(128)}, u32[]{:S(2)}) copy-start(s32[64]{0:T(128)} %param.12) | copy-start | bytes 772
  0.7 11.3 %copy-start.4 = (s32[64]{0:T(128)S(1)}, s32[64]{0:T(128)}, u32[]{:S(2)}) copy-start(s32[64]{0:T(128)} %constant.63.clone) | copy-start | bytes 772
  3.0 12.7 %collective-permute-start.2 = (bf16[32,16,256]{2,1,0:T(8,128)(2,1)}, bf16[32,16,256]{2,1,0:T(8,128)(2,1)S(1)}, u32[]{:S(2)}, u32[]{:S(2)}) collective-permute-start(bf16[32,16,256]{2,1,0:T(8,128)(2,1)} %get-tuple-element.71), channel_id=1, source_target_pairs={{0,64},{64,128},{128,192},{192,0},{1,65},{65,129},{129,193},{193,1... | collective-permute-start | bytes 786440 | tf_op jit(solution)/shard_map/ppermute | solution.py:32
  5.0 10.7 %collective-permute-start.3 = (bf16[32,16,256]{2,1,0:T(8,128)(2,1)}, bf16[32,16,256]{2,1,0:T(8,128)(2,1)S(1)}, u32[]{:S(2)}, u32[]{:S(2)}) collective-permute-start(bf16[32,16,256]{2,1,0:T(8,128)(2,1)} %get-tuple-element.72), channel_id=1, source_target_pairs={{0,192},{64,0},{128,64},{192,128},{1,193},{65,1},{129,65},{193,129... | collective-permute-start | bytes 786440 | tf_op jit(solution)/shard_map/ppermute | solution.py:32
  9.0 10.2 %copy-start.2 = (f32[64,16,256]{2,1,0:T(8,128)S(1)}, f32[64,16,256]{2,1,0:T(8,128)}, u32[]{:S(2)}) copy-start(f32[64,16,256]{2,1,0:T(8,128)} %param.18) | copy-start | bytes 3145732
  9.1 10.2 %collective-permute-start = (bf16[32,16,256]{2,1,0:T(8,128)(2,1)}, bf16[32,16,256]{2,1,0:T(8,128)(2,1)S(1)}, u32[]{:S(2)}, u32[]{:S(2)}) collective-permute-start(bf16[32,16,256]{2,1,0:T(8,128)(2,1)} %get-tuple-element.77), channel_id=1, source_target_pairs={{0,64},{64,128},{128,192},{192,0},{1,65},{65,129},{129,193},{193,1... | collective-permute-start | bytes 786440 | tf_op jit(solution)/shard_map/ppermute | solution.py:32
  9.1 10.2 %collective-permute-start.1 = (bf16[32,16,256]{2,1,0:T(8,128)(2,1)S(1)}, bf16[32,16,256]{2,1,0:T(8,128)(2,1)S(1)}, u32[]{:S(2)}, u32[]{:S(2)}) collective-permute-start(bf16[32,16,256]{2,1,0:T(8,128)(2,1)S(1)} %get-tuple-element.78), channel_id=1, source_target_pairs={{0,192},{64,0},{128,64},{192,128},{1,193},{65,1},{129,65},{193,129... | collective-permute-start | bytes 786440 | tf_op jit(solution)/shard_map/ppermute | solution.py:32
  12.8 6.5 %copy-start.3 = (f32[64,16,256]{2,1,0:T(8,128)S(1)}, f32[64,16,256]{2,1,0:T(8,128)}, u32[]{:S(2)}) copy-start(f32[64,16,256]{2,1,0:T(8,128)} %param.19) | copy-start | bytes 3145732
  16.5 6.7 %collective-permute-start.4 = (bf16[32,16,256]{2,1,0:T(8,128)(2,1)}, bf16[32,16,256]{2,1,0:T(8,128)(2,1)}, u32[]{:S(2)}, u32[]{:S(2)}) collective-permute-start(bf16[32,16,256]{2,1,0:T(8,128)(2,1)} %get-tuple-element.90), channel_id=1, source_target_pairs={{0,64},{64,128},{128,192},{192,0},{1,65},{65,129},{129,193},{193,1... | collective-permute-start | bytes 786440 | tf_op jit(solution)/shard_map/ppermute | solution.py:32
  16.5 6.7 %collective-permute-start.5 = (bf16[32,16,256]{2,1,0:T(8,128)(2,1)}, bf16[32,16,256]{2,1,0:T(8,128)(2,1)}, u32[]{:S(2)}, u32[]{:S(2)}) collective-permute-start(bf16[32,16,256]{2,1,0:T(8,128)(2,1)} %get-tuple-element.91), channel_id=1, source_target_pairs={{0,192},{64,0},{128,64},{192,128},{1,193},{65,1},{129,65},{193,129... | collective-permute-start | bytes 786440 | tf_op jit(solution)/shard_map/ppermute | solution.py:32
  19.2 6.7 %copy-start.9 = (bf16[11,128,256]{2,1,0:T(8,128)(2,1)S(1)}, bf16[11,128,256]{2,1,0:T(8,128)(2,1)}, u32[]{:S(2)}) copy-start(bf16[11,128,256]{2,1,0:T(8,128)(2,1)} %get-tuple-element.112.refs_10_) | copy-start | bytes 2162692
  23.3 22.8 %collective-permute-start.7 = (bf16[11,128,256]{2,1,0:T(8,128)(2,1)}, bf16[11,128,256]{2,1,0:T(8,128)(2,1)S(1)}, u32[]{:S(2)}, u32[]{:S(2)}) collective-permute-start(bf16[11,128,256]{2,1,0:T(8,128)(2,1)} %get-tuple-element.104), channel_id=1, source_target_pairs={{0,192},{64,0},{128,64},{192,128},{1,193},{65,1},{129,65},{193,129... | collective-permute-start | bytes 2162696 | tf_op jit(solution)/shard_map/ppermute | solution.py:32
  26.0 20.1 %collective-permute-start.6 = (bf16[11,128,256]{2,1,0:T(8,128)(2,1)S(1)}, bf16[11,128,256]{2,1,0:T(8,128)(2,1)S(1)}, u32[]{:S(2)}, u32[]{:S(2)}) collective-permute-start(bf16[11,128,256]{2,1,0:T(8,128)(2,1)S(1)} %copy-done.9), channel_id=1, source_target_pairs={{0,64},{64,128},{128,192},{192,0},{1,65},{65,129},{129,193},{193,1... | collective-permute-start | bytes 2162696 | tf_op jit(solution)/shard_map/ppermute | solution.py:32
  30.0 35.1 %all-to-all-start = ((bf16[64,40,128]{2,1,0:T(8,128)(2,1)}), bf16[64,40,128]{2,1,0:T(8,128)(2,1)}, u32[]{:S(2)}, u32[]{:S(2)}) async-start(bf16[64,40,128]{2,1,0:T(8,128)(2,1)} %get-tuple-element.101), calls=%async_computation | async-start | bytes 1310720 | tf_op jit(solution)/shard_map/all_to_all | solution.py:391
  47.2 10.9 %collective-permute-start.8 = (bf16[5,128,256]{2,1,0:T(8,128)(2,1)S(1)}, bf16[5,128,256]{2,1,0:T(8,128)(2,1)S(1)}, u32[]{:S(2)}, u32[]{:S(2)}) collective-permute-start(bf16[5,128,256]{2,1,0:T(8,128)(2,1)S(1)} %get-tuple-element.105), channel_id=1, source_target_pairs={{0,64},{64,128},{128,192},{192,0},{1,65},{65,129},{129,193},{193,1... | collective-permute-start | bytes 983048 | tf_op jit(solution)/shard_map/ppermute | solution.py:32
  47.2 10.9 %collective-permute-start.9 = (bf16[5,128,256]{2,1,0:T(8,128)(2,1)S(1)}, bf16[5,128,256]{2,1,0:T(8,128)(2,1)S(1)}, u32[]{:S(2)}, u32[]{:S(2)}) collective-permute-start(bf16[5,128,256]{2,1,0:T(8,128)(2,1)S(1)} %get-tuple-element.106), channel_id=1, source_target_pairs={{0,192},{64,0},{128,64},{192,128},{1,193},{65,1},{129,65},{193,129... | collective-permute-start | bytes 983048 | tf_op jit(solution)/shard_map/ppermute | solution.py:32
  58.1 28.1 %copy-start.10 = (bf16[5,128,256]{2,1,0:T(8,128)(2,1)}, bf16[5,128,256]{2,1,0:T(8,128)(2,1)S(1)}, u32[]{:S(2)}) copy-start(bf16[5,128,256]{2,1,0:T(8,128)(2,1)S(1)} %collective-permute-done.8.refs_13_) | copy-start | bytes 983044
  58.1 28.1 %copy-start.11 = (bf16[5,128,256]{2,1,0:T(8,128)(2,1)}, bf16[5,128,256]{2,1,0:T(8,128)(2,1)S(1)}, u32[]{:S(2)}) copy-start(bf16[5,128,256]{2,1,0:T(8,128)(2,1)S(1)} %collective-permute-done.9.refs_14_) | copy-start | bytes 983044
  66.3 8.6 %collective-permute-start.12 = (bf16[32,16,256]{2,1,0:T(8,128)(2,1)S(1)}, bf16[32,16,256]{2,1,0:T(8,128)(2,1)S(1)}, u32[]{:S(2)}, u32[]{:S(2)}) collective-permute-start(bf16[32,16,256]{2,1,0:T(8,128)(2,1)S(1)} %get-tuple-element.124), channel_id=1, source_target_pairs={{0,64},{64,128},{128,192},{192,0},{1,65},{65,129},{129,193},{193,1... | collective-permute-start | bytes 786440 | tf_op jit(solution)/shard_map/ppermute | solution.py:32
  66.4 8.5 %collective-permute-start.11 = (bf16[32,16,256]{2,1,0:T(8,128)(2,1)S(1)}, bf16[32,16,256]{2,1,0:T(8,128)(2,1)S(1)}, u32[]{:S(2)}, u32[]{:S(2)}) collective-permute-start(bf16[32,16,256]{2,1,0:T(8,128)(2,1)S(1)} %get-tuple-element.125), channel_id=1, source_target_pairs={{0,192},{64,0},{128,64},{192,128},{1,193},{65,1},{129,65},{193,129... | collective-permute-start | bytes 786440 | tf_op jit(solution)/shard_map/ppermute | solution.py:32
  69.6 10.1 %collective-permute-start.10 = (bf16[32,16,256]{2,1,0:T(8,128)(2,1)S(1)}, bf16[32,16,256]{2,1,0:T(8,128)(2,1)S(1)}, u32[]{:S(2)}, u32[]{:S(2)}) collective-permute-start(bf16[32,16,256]{2,1,0:T(8,128)(2,1)S(1)} %get-tuple-element.124), channel_id=1, source_target_pairs={{0,192},{64,0},{128,64},{192,128},{1,193},{65,1},{129,65},{193,129... | collective-permute-start | bytes 786440 | tf_op jit(solution)/shard_map/ppermute | solution.py:32
  70.8 9.7 %collective-permute-start.15 = (bf16[32,16,256]{2,1,0:T(8,128)(2,1)S(1)}, bf16[32,16,256]{2,1,0:T(8,128)(2,1)S(1)}, u32[]{:S(2)}, u32[]{:S(2)}) collective-permute-start(bf16[32,16,256]{2,1,0:T(8,128)(2,1)S(1)} %get-tuple-element.125), channel_id=1, source_target_pairs={{0,64},{64,128},{128,192},{192,0},{1,65},{65,129},{129,193},{193,1... | collective-permute-start | bytes 786440 | tf_op jit(solution)/shard_map/ppermute | solution.py:32
  74.9 11.2 %collective-permute-start.13 = (bf16[32,16,256]{2,1,0:T(8,128)(2,1)S(1)}, bf16[32,16,256]{2,1,0:T(8,128)(2,1)S(1)}, u32[]{:S(2)}, u32[]{:S(2)}) collective-permute-start(bf16[32,16,256]{2,1,0:T(8,128)(2,1)S(1)} %collective-permute-done.12), channel_id=1, source_target_pairs={{0,64},{64,128},{128,192},{192,0},{1,65},{65,129},{129,193},{193,1... | collective-permute-start | bytes 786440 | tf_op jit(solution)/shard_map/ppermute | solution.py:32
  74.9 11.2 %collective-permute-start.14 = (bf16[32,16,256]{2,1,0:T(8,128)(2,1)S(1)}, bf16[32,16,256]{2,1,0:T(8,128)(2,1)S(1)}, u32[]{:S(2)}, u32[]{:S(2)}) collective-permute-start(bf16[32,16,256]{2,1,0:T(8,128)(2,1)S(1)} %collective-permute-done.11), channel_id=1, source_target_pairs={{0,192},{64,0},{128,64},{192,128},{1,193},{65,1},{129,65},{193,129... | collective-permute-start | bytes 786440 | tf_op jit(solution)/shard_map/ppermute | solution.py:32
  86.2 10.8 %copy-start.15 = (s32[64]{0:T(128)S(1)}, s32[64]{0:T(128)}, u32[]{:S(2)}) copy-start(s32[64]{0:T(128)} %param.12) | copy-start | bytes 772
  89.4 3.5 %collective-permute-start.18 = (f32[8,128]{1,0:T(8,128)S(1)}, f32[8,128]{1,0:T(8,128)S(1)}, u32[]{:S(2)}, u32[]{:S(2)}) collective-permute-start(f32[8,128]{1,0:T(8,128)S(1)} %get-tuple-element.118.first), channel_id=1, source_target_pairs={{0,192},{64,0},{128,64},{192,128},{1,193},{65,1},{129,65},{193,129... | collective-permute-start | bytes 12296 | tf_op jit(solution)/shard_map/ppermute | solution.py:32
  92.1 4.0 %collective-permute-start.17 = (f32[8,128]{1,0:T(8,128)S(1)}, f32[8,128]{1,0:T(8,128)S(1)}, u32[]{:S(2)}, u32[]{:S(2)}) collective-permute-start(f32[8,128]{1,0:T(8,128)S(1)} %get-tuple-element.118.first), channel_id=1, source_target_pairs={{0,128},{64,192},{128,0},{192,64},{1,129},{65,193},{129,1},{193,65... | collective-permute-start | bytes 12296 | tf_op jit(solution)/shard_map/ppermute | solution.py:32
  92.1 4.0 %collective-permute-start.16 = (f32[8,128]{1,0:T(8,128)S(1)}, f32[8,128]{1,0:T(8,128)S(1)}, u32[]{:S(2)}, u32[]{:S(2)}) collective-permute-start(f32[8,128]{1,0:T(8,128)S(1)} %get-tuple-element.118.first), channel_id=1, source_target_pairs={{0,64},{64,128},{128,192},{192,0},{1,65},{65,129},{129,193},{193,1... | collective-permute-start | bytes 12296 | tf_op jit(solution)/shard_map/ppermute | solution.py:32
  97.0 25.9 %all-to-all-start.1 = ((bf16[64,16,256]{2,1,0:T(8,128)(2,1)}), bf16[64,16,256]{2,1,0:T(8,128)(2,1)S(1)}, u32[]{:S(2)}, u32[]{:S(2)}) async-start(bf16[64,16,256]{2,1,0:T(8,128)(2,1)} %shard_map.153), calls=%async_computation.1 | async-start | bytes 1048576 | tf_op jit(solution)/shard_map/all_to_all | solution.py:391
  111.6 3.1 %copy-start.6 = (bf16[64,16,1024]{2,1,0:T(8,128)(2,1)S(1)}, bf16[64,16,1024]{2,1,0:T(8,128)(2,1)}, u32[]{:S(2)}) copy-start(bf16[64,16,1024]{2,1,0:T(8,128)(2,1)} %maximum_maximum_fusion) | copy-start | bytes 6291460
  (5 other events, 8.9 us)

commit v8 on v7

--- a/solution.py
+++ b/solution.py
@@ -52,10 +52,10 @@
     return lax.dot_general(a, b, (dims, ((), ())), preferred_element_type=F32)
 
 
-def inside(bounds, block, rows, cols):
-    row_off, col_off, n_rows, n_cols = [bounds[4 * block + i] for i in range(4)]
+def inside(bounds, rows, cols):
     row, col = lax.axis_index("own") * rows, lax.axis_index("grp") * cols
-    return (row < n_rows - row_off) & (col < n_cols - col_off)
+    ok = (row < bounds[:, 2] - bounds[:, 0]) & (col < bounds[:, 3] - bounds[:, 1])
+    return ok.astype(jnp.int32)
 
 
 def add_kernel(up, far_up, down, far_down, up_out, down_out):
@@ -138,7 +138,7 @@
 
 
 def pack_kernel(
-    key, bounds, partial, up_sum, down_sum, first, second, out, first_out, second_out
+    key, flags, partial, up_sum, down_sum, first, second, out, first_out, second_out
 ):
     _, half, rows, cols = partial.shape
     count = first_out.shape[1]
@@ -148,7 +148,7 @@
     def one(side, i, value):
         at = begin + i
         block = side * half + at
-        keep = jnp.where(inside(bounds, block, rows, cols), 1.0, 0.0)
+        keep = flags[block].astype(F32)
         grad = value * keep
         first_next = first[side, at] + (1.0 - BETA_FIRST) * grad
         second_next = second[side, at] + (1.0 - BETA_SECOND) * grad * grad
@@ -171,10 +171,10 @@
     lax.fori_loop(0, count, step, 0, unroll=4)
 
 
-def pack(key, bounds, partial, up_sum, down_sum, first, second):
+def pack(key, flags, partial, up_sum, down_sum, first, second):
     _, half, rows, cols = partial.shape
     blocks, lanes = 2 * half, cols // 2
-    steps = 4 if half >= 16 else 1
+    steps = 2 if half >= 16 else 1
     moment = pl.BlockSpec((2, half // steps, rows, cols), lambda i, *_: (0, i, 0, 0))
     halves = pltpu.HBM((2, half, rows, cols), F32)
     piece = (blocks, 2 * rows + rows // 2, lanes)
@@ -187,8 +187,8 @@
             in_specs=[pl.BlockSpec(memory_space=VMEM)] * 5,
             out_specs=[pl.BlockSpec(piece, lambda i, *_: (0, 0, 0)), moment, moment],
         ),
-        compiler_params=pltpu.CompilerParams(vmem_limit_bytes=14 * MIB),
-    )(key, bounds, partial, up_sum, down_sum, first, second)
+        compiler_params=pltpu.CompilerParams(vmem_limit_bytes=16 * MIB),
+    )(key, flags, partial, up_sum, down_sum, first, second)
     shape = (blocks, rows, cols)
     return out, first_next.reshape(shape), second_next.reshape(shape)
 
@@ -237,27 +237,32 @@
     )(owned)
 
 
-def finish_kernel(key, bounds, back, out):
-    blocks, rows, cols = out.shape
-
-    def step(block, carry):
-        ok = inside(bounds, block, rows, cols)
-        out[block] = jnp.where(ok, back[key[block]], jnp.zeros((), BF16))
+def finish_kernel(key, flags, back, out):
+    count, rows, cols = out.shape
+    begin = pl.program_id(0) * count
+
+    def step(i, carry):
+        block = begin + i
+        out[i] = jnp.where(flags[block] != 0, back[key[block]], jnp.zeros((), BF16))
         return carry
 
-    lax.fori_loop(0, blocks, step, 0, unroll=8)
-
-
-def finish(key, bounds, back):
-    whole = pl.BlockSpec(back.shape, lambda i, *_: (0, 0, 0))
+    lax.fori_loop(0, count, step, 0, unroll=8)
+
+
+def finish(key, flags, back):
+    blocks, rows, cols = back.shape
+    steps = 2 if blocks >= 16 else 1
     return pl.pallas_call(
         finish_kernel,
         out_shape=jax.ShapeDtypeStruct(back.shape, BF16),
         grid_spec=pltpu.PrefetchScalarGridSpec(
-            num_scalar_prefetch=2, grid=(1,), in_specs=[whole], out_specs=whole
+            num_scalar_prefetch=2,
+            grid=(steps,),
+            in_specs=[pl.BlockSpec(memory_space=VMEM)],
+            out_specs=pl.BlockSpec((blocks // steps, rows, cols), lambda i, *_: (i, 0, 0)),
         ),
         compiler_params=pltpu.CompilerParams(vmem_limit_bytes=6 * MIB),
-    )(key, bounds, back)
+    )(key, flags, back)
 
 
 def precond_kernel(*refs):
@@ -267,14 +272,17 @@
     half = width // 2
     me = lax.axis_index("grp")
     n = width // quarter
-    copies = [
-        pltpu.make_async_copy(source, place, sems.at[i])
-        for i, (source, place) in enumerate(zip(sources, held))
-    ]
+    root, up, up_prev, down_next, up_far, down_far = held
+    cuts = [(0, 0, 2), (2, 9, 2), (3, 9, 2), (4, 4, 1), (5, 4, 1)]
+    cuts += [(1, 0, 9), (3, 0, 9), (4, 0, 4), (5, 0, 4), (2, 0, 9)]
+    copies = []
+    for i, (which, first, count) in enumerate(cuts):
+        units = pl.ds(first, count)
+        source, place = sources[which].at[units], held[which].at[units]
+        copies.append(pltpu.make_async_copy(source, place, sems.at[i]))
     for copy in copies:
         copy.start()
-    root, up, up_prev, down_next, up_far, down_far = held
-    for copy in copies:
+    for copy in copies[:5]:
         copy.wait()
     right = jnp.concatenate(
         [
@@ -293,6 +301,8 @@
         parts = [ref[pl.ds(row % half, quarter), :] for ref in pieces[row // half :: 2]]
         value = dot(jnp.concatenate(parts, axis=1), right, ((1,), (0,)))
         mixed[pl.ds(row, quarter), :] = value.astype(BF16)
+    for copy in copies[5:]:
+        copy.wait()
     square = jnp.zeros((8, quarter), F32)
     for step, (low, first), (high, second) in (
         (0, (up, 0), (up, 5)),
@@ -325,14 +335,14 @@
         scratch_shapes=[
             VMEM((2 * rows, quarter), BF16),
             *[VMEM(source.shape, BF16) for source in sources],
-            pltpu.SemaphoreType.DMA((len(sources),)),
+            pltpu.SemaphoreType.DMA((10,)),
         ],
         compiler_params=pltpu.CompilerParams(vmem_limit_bytes=14 * MIB),
     )(*operands, *map(in_hbm, sources))
 
 
-def graft_kernel(cells, order, precond, first, second, third, fourth, out):
-    sums = first[...] + second[...] + third[...] + fourth[...]
+def graft_kernel(cells, order, precond, mine, other, out):
+    sums = mine[...] + other[...]
     pre, adam = sums[0:1, :], sums[1:2, :]
     adam = adam * (BIAS_SECOND / (BIAS_FIRST * BIAS_FIRST))
     scale = -jnp.sqrt(adam / cells) / jnp.sqrt(pre / cells + NORM_EPS)
@@ -342,7 +352,7 @@
         out[i] = (scale * precond[pl.ds(place * rows, rows), :]).astype(BF16)
 
 
-def graft(order, precond, norms):
+def graft(order, precond, mine, other):
     width, quarter = precond.shape
     shape = (len(order), width // len(order), quarter)
     small = pl.BlockSpec((8, 128), lambda i: (0, 0))
@@ -350,10 +360,10 @@
         functools.partial(graft_kernel, float(width * width), order),
         out_shape=pltpu.HBM(shape, BF16),
         grid=(1,),
-        in_specs=[pl.BlockSpec((width, quarter), lambda i: (0, 0))] + [small] * 4,
+        in_specs=[pl.BlockSpec((width, quarter), lambda i: (0, 0))] + [small] * 2,
         out_specs=pl.BlockSpec(shape, lambda i: (0, 0, 0)),
         compiler_params=pltpu.CompilerParams(vmem_limit_bytes=8 * MIB),
-    )(precond, *norms)
+    )(precond, mine, other)
 
 
 def on_device(
@@ -394,22 +404,25 @@
     far_low, far_high = lax.optimization_barrier((far[:half], far[half:]))
     far_up = shift(far_low, 1)
     far_down = shift(far_high, -1)
-    later, left_root, right_root, _, _ = lax.optimization_barrier(
-        (part, left_root, right_root, far_low, far_high)
-    )
+    later, _, _ = lax.optimization_barrier((part, far_low, far_high))
     up, down = columns(later, 1), columns(later, 3)
-    up_low, up_high, down_low, down_high, own = lax.optimization_barrier(
-        (up[:half], up[half:], down[:half], down[half:], columns(later, 0))
+    up_low, up_high, down_low, down_high = lax.optimization_barrier(
+        (up[:half], up[half:], down[:half], down[half:])
     )
     up_direct = shift(up_high, 1)
     down_direct = shift(down_low, -1)
     up_sum, down_sum = add(up_low, far_up, down_high, far_down)
+    up_sum, down_sum, left_root, right_root, later = lax.optimization_barrier(
+        (up_sum, down_sum, left_root, right_root, part)
+    )
+    own = columns(later, 0)
     up_sum = shift(up_sum, 1)
     down_sum = shift(down_sum, -1)
-    key, bounds = places_of(assign, n_own, per_owner, order), block_bounds.reshape(-1)
+    key = places_of(assign, n_own, per_owner, order)
+    flags = inside(block_bounds, shard_rows, quarter)
     roots_up, roots_down, root_own = root_pieces(left_root, right_root)
-    up_direct, down_direct, key, bounds, roots_up, roots_down, root_own = lax.optimization_barrier(
-        (up_direct, down_direct, key, bounds, roots_up, roots_down, root_own)
+    up_direct, down_direct, key, flags, roots_up, roots_down, root_own = lax.optimization_barrier(
+        (up_direct, down_direct, key, flags, roots_up, roots_down, root_own)
     )
     partial, first, second = gather(own, up_direct, down_direct, first_moment, second_moment)
 
@@ -417,7 +430,7 @@
         (roots_up, roots_down, up_sum, down_sum, partial)
     )
     sorted_grad, first_next, second_next = pack(
-        key, bounds, partial, up_sum, down_sum, first, second
+        key, flags, partial, up_sum, down_sum, first, second
     )
     owned = exchange(sorted_grad)
     roots_prev = shift(roots_up, 1)
@@ -437,12 +450,10 @@
     pieces = [low, high, next_low, next_high, far_low, far_high, prev_low, prev_high]
     flat = [piece.reshape(-1, quarter) for piece in pieces]
     precond, norms = precondition(flat, adam, roots)
-    norms = [norms] + [shift(norms, step) for step in (1, 2, 3)]
-    grafted = graft(order, precond, norms)
-    pieces, grafted, assign, bounds = lax.optimization_barrier(
-        (pieces, grafted, assign, block_bounds)
-    )
-    key, bounds = places_of(assign, n_own, per_owner, order), bounds.reshape(-1)
+    norms += lax.ppermute(norms, "grp", [(i, i ^ 1) for i in range(n_grp)])
+    others = lax.ppermute(norms, "grp", [(i, i ^ 2) for i in range(n_grp)])
+    grafted = graft(order, precond, norms, others)
+    pieces, grafted = lax.optimization_barrier((pieces, grafted))
     back = exchange(grafted)
 
     whole = jnp.concatenate(
@@ -455,7 +466,7 @@
     cross = slice_at(cross, turn, width, 1)
     right_acc = STAT_DECAY * right_stat + cross[None]
 
-    update = finish(key, bounds, back)
+    update = finish(key, flags, back)
     return (update, first_next, second_next, left_acc, right_acc)
 
 

time: 125 us -> 122 us (0.976)
  waiting for transfers between devices: 40.8 us -> 44.9 us
  other arithmetic: 4.6 us -> 1.94 us
  matrix products: 4.24 us -> 2.47 us
  Pallas kernels: 15.3 us -> 13.8 us
    all_to_all x2, waiting for transfers between devices: 13.5 us -> 19.2 us  [exchange(): lax.all_to_all(array, 'own', 0, 0, axis_index_groups=groups, tiled=True)]
    ppermute x19 -> x16, waiting for transfers between devices: 27.3 us -> 22.2 us  [shift(): return lax.ppermute(array, 'grp', [(i, (i + step) % n) for i in range(n)])]
    ppermute x0 -> x2, waiting for transfers between devices: none -> 3.52 us  [the longest x1 1.91 us: on_device(): norms += lax.ppermute(norms, 'grp', [(i, i ^ 1) for i in range(n_grp)])]
    ppermute x19 -> x16, starting transfers between devices: 25.4 us -> 22.2 us  [shift(): return lax.ppermute(array, 'grp', [(i, (i + step) % n) for i in range(n)])]
    ppermute x0 -> x2, starting transfers between devices: none -> 2.98 us  [the longest x1 2.35 us: on_device(): others = lax.ppermute(norms, 'grp', [(i, i ^ 2) for i in range(n_grp)])]
    dot_general x2, matrix products: 4.24 us -> 2.47 us  [dot(): return lax.dot_general(a, b, (dims, ((), ())), preferred_element_type=F32)]
    add x1, other arithmetic: 3.04 us -> 1.59 us  [on_device(): right_acc = STAT_DECAY * right_stat + cross[None]]
  transfers between devices with their start and end apart: 21 -> 20, of which waited for: 10 -> 10; matrix products, arithmetic and copies ran while one was open for 11% -> 7% of each run, Pallas kernels for 7% -> 6%
where the time goes in v8:
time: 122 us; the launch traced here: 121 us
  starting transfers between devices  50.4 us (41%)
  waiting for transfers between devices  44.9 us (37%)
  Pallas kernels  13.8 us (11%)
  local copies, waits for them, and re-layouts  6.8 us (6%)
  matrix products  2.47 us (2%)
  other arithmetic  1.94 us (2%)
    all_to_all x2, starting transfers between devices, exchange(): lax.all_to_all(array, 'own', 0, 0, axis_index_groups=groups, tiled=True)  25.2 us
    ppermute x16, starting transfers between devices, shift(): return lax.ppermute(array, 'grp', [(i, (i + step) % n) for i in range(n)])  22.2 us
    ppermute x16, waiting for transfers between devices, shift(): return lax.ppermute(array, 'grp', [(i, (i + step) % n) for i in range(n)])  22.2 us
    all_to_all x2, waiting for transfers between devices, exchange(): lax.all_to_all(array, 'own', 0, 0, axis_index_groups=groups, tiled=True)  19.2 us
    pallas_call x1, Pallas kernels, pack(): pl.pallas_call(pack_kernel, out_shape=(pltpu.HBM(piece, BF16), halves, ha...  3.51 us
    pallas_call x1, Pallas kernels, root_pieces(): pl.pallas_call(roots_kernel, out_shape=(pltpu.HBM((11, *unit), BF16), plt...  2.82 us
    pallas_call x1, Pallas kernels, precondition(): pl.pallas_call(precond_kernel, out_shape=(jax.ShapeDtypeStruct((2 * rows,...  2.77 us
    dot_general x2, matrix products, dot(): return lax.dot_general(a, b, (dims, ((), ())), preferred_element_type=F32)  2.47 us
  transfers between devices with their start and end apart: 20, of which 10 were waited for; matrix products, arithmetic and copies ran while one was open for 7% of the time, Pallas kernels for 6%

profile of v8, /device:TPU:1, one launch (start us, length us, event | category | flops | bytes accessed | tf_op | source)
XLA Modules:
  0.0 121.3 jit_solution(6328597220625554019)
XLA Ops:
  0.7 1.4 %dynamic-slice_bitcast_fusion = (bf16[32,16,256]{2,1,0:T(8,128)(2,1)S(1)}, bf16[32,16,256]{2,1,0:T(8,128)(2,1)S(1)}) fusion(bf16[1,64,16,1024]{3,2,1,0:T(8,128)(2,1)} %param.10, s32[]{:T(128)S(6)} %add.41, s32[]{:T(128)S(6)} %mul.29), kind=kLoop, calls=%fused_computation.12 | loop fusion | bytes 1048584 | tf_op jit(solution)/shard_map/slice | solution.py:404
  2.0 2.1 %collective-permute-start.2 = (bf16[32,16,256]{2,1,0:T(8,128)(2,1)S(1)}, bf16[32,16,256]{2,1,0:T(8,128)(2,1)S(1)}, u32[]{:S(2)}, u32[]{:S(2)}) collective-permute-start(bf16[32,16,256]{2,1,0:T(8,128)(2,1)S(1)} %get-tuple-element.71), channel_id=1, source_target_pairs={{0,64},{64,128},{128,192},{192,0},{1,65},{65,129},{129,193},{193,1... | collective-permute-start | bytes 786440 | tf_op jit(solution)/shard_map/ppermute | solution.py:32
  4.2 1.6 %collective-permute-start.3 = (bf16[32,16,256]{2,1,0:T(8,128)(2,1)S(1)}, bf16[32,16,256]{2,1,0:T(8,128)(2,1)S(1)}, u32[]{:S(2)}, u32[]{:S(2)}) collective-permute-start(bf16[32,16,256]{2,1,0:T(8,128)(2,1)S(1)} %get-tuple-element.72), channel_id=1, source_target_pairs={{0,192},{64,0},{128,64},{192,128},{1,193},{65,1},{129,65},{193,129... | collective-permute-start | bytes 786440 | tf_op jit(solution)/shard_map/ppermute | solution.py:32
  5.8 1.7 %constant_dynamic-slice_fusion.3 = (bf16[32,16,256]{2,1,0:T(8,128)(2,1)S(1)}, bf16[32,16,256]{2,1,0:T(8,128)(2,1)S(1)}, bf16[32,16,256]{2,1,0:T(8,128)(2,1)S(1)}, bf16[32,16,256]{2,1,0:T(8,128)(2,1)S(1)}) fusion(bf16[64,16,1024]{2,1,0:T(8,128)(2,1)} %bitcast.42, s32[]{:T(128)S(6)} %add.41, s32[]{:T(128)S(6)} %mul.30, s32[]{:T(128)S(6)} %mul.28), kind=kLoop, calls=%fused_computation.20 | loop fusion | bytes 2097164 | tf_op jit(solution)/shard_map/slice | solution.py:410
  7.6 2.7 %collective-permute-start.1 = (bf16[32,16,256]{2,1,0:T(8,128)(2,1)S(1)}, bf16[32,16,256]{2,1,0:T(8,128)(2,1)S(1)}, u32[]{:S(2)}, u32[]{:S(2)}) collective-permute-start(bf16[32,16,256]{2,1,0:T(8,128)(2,1)S(1)} %get-tuple-element.77), channel_id=1, source_target_pairs={{0,192},{64,0},{128,64},{192,128},{1,193},{65,1},{129,65},{193,129... | collective-permute-start | bytes 786440 | tf_op jit(solution)/shard_map/ppermute | solution.py:32
  12.0 1.2 %collective-permute-start.4 = (bf16[32,16,256]{2,1,0:T(8,128)(2,1)}, bf16[32,16,256]{2,1,0:T(8,128)(2,1)}, u32[]{:S(2)}, u32[]{:S(2)}) collective-permute-start(bf16[32,16,256]{2,1,0:T(8,128)(2,1)} %get-tuple-element.91), channel_id=1, source_target_pairs={{0,64},{64,128},{128,192},{192,0},{1,65},{65,129},{129,193},{193,1... | collective-permute-start | bytes 786440 | tf_op jit(solution)/shard_map/ppermute | solution.py:32
  13.2 1.4 %collective-permute-start.5 = (bf16[32,16,256]{2,1,0:T(8,128)(2,1)}, bf16[32,16,256]{2,1,0:T(8,128)(2,1)}, u32[]{:S(2)}, u32[]{:S(2)}) collective-permute-start(bf16[32,16,256]{2,1,0:T(8,128)(2,1)} %get-tuple-element.92), channel_id=1, source_target_pairs={{0,192},{64,0},{128,64},{192,128},{1,193},{65,1},{129,65},{193,129... | collective-permute-start | bytes 786440 | tf_op jit(solution)/shard_map/ppermute | solution.py:32
  14.7 2.8 %shard_map.138 = (bf16[11,128,256]{2,1,0:T(8,128)(2,1)}, bf16[11,128,256]{2,1,0:T(8,128)(2,1)}, bf16[2,128,256]{2,1,0:T(8,128)(2,1)}) custom-call(f32[1,256,1024]{2,1,0:T(8,128)} %left, f32[1,256,1024]{2,1,0:T(8,128)} %right), custom_call_target="tpu_custom_call" | custom-call | tf_op jit(solution)/shard_map/pallas_call | solution.py:101
  17.5 1.4 %constant_dynamic-slice_fusion.2.own = bf16[64,16,256]{2,1,0:T(8,128)(2,1)S(1)} fusion(bf16[64,16,1024]{2,1,0:T(8,128)(2,1)} %bitcast.43, s32[]{:T(128)S(6)} %mul.27), kind=kLoop, calls=%fused_computation.19 | loop fusion | bytes 1048580 | tf_op jit(solution)/shard_map/dynamic_slice | solution.py:48
  19.3 2.6 %collective-permute-done.4.up_sum = bf16[32,16,256]{2,1,0:T(8,128)(2,1)} collective-permute-done((bf16[32,16,256]{2,1,0:T(8,128)(2,1)}, bf16[32,16,256]{2,1,0:T(8,128)(2,1)}, u32[]{:S(2)}, u32[]{:S(2)}) %collective-permute-start.4) | collective-permute-done | bytes 262176 | tf_op jit(solution)/shard_map/ppermute | solution.py:32
  21.8 2.7 %collective-permute-start.7 = (bf16[11,128,256]{2,1,0:T(8,128)(2,1)S(1)}, bf16[11,128,256]{2,1,0:T(8,128)(2,1)S(1)}, u32[]{:S(2)}, u32[]{:S(2)}) collective-permute-start(bf16[11,128,256]{2,1,0:T(8,128)(2,1)S(1)} %copy-done.15), channel_id=1, source_target_pairs={{0,192},{64,0},{128,64},{192,128},{1,193},{65,1},{129,65},{193,129... | collective-permute-start | bytes 2162696 | tf_op jit(solution)/shard_map/ppermute | solution.py:32
  24.6 3.5 %shard_map.140 = (bf16[64,40,128]{2,1,0:T(8,128)(2,1)}, f32[2,32,16,256]{3,2,1,0:T(8,128)}, f32[2,32,16,256]{3,2,1,0:T(8,128)}) custom-call(s32[64]{0:T(128)S(1)} %gather_fusion, s32[64]{0:T(128)S(1)} %fusion.9.flags, f32[2,32,16,256]{3,2,1,0:T(8,128)S(1)} %get-tuple-element.98.partial, bf16[32,16,256]{2,1,0:T(8,128)(2,1)} %collective-permute-done.4.up_sum, ...), custom_call_target="tpu_custom_call" | custom-call | tf_op jit(solution)/shard_map/pallas_call | solution.py:181
  28.1 15.0 %all-to-all-start = ((bf16[64,40,128]{2,1,0:T(8,128)(2,1)}), bf16[64,40,128]{2,1,0:T(8,128)(2,1)}, u32[]{:S(2)}, u32[]{:S(2)}) async-start(bf16[64,40,128]{2,1,0:T(8,128)(2,1)} %get-tuple-element.103), calls=%async_computation | async-start | bytes 1310720 | tf_op jit(solution)/shard_map/all_to_all | solution.py:401
  44.5 2.7 %collective-permute-start.9 = (bf16[5,128,256]{2,1,0:T(8,128)(2,1)S(1)}, bf16[5,128,256]{2,1,0:T(8,128)(2,1)S(1)}, u32[]{:S(2)}, u32[]{:S(2)}) collective-permute-start(bf16[5,128,256]{2,1,0:T(8,128)(2,1)S(1)} %get-tuple-element.108), channel_id=1, source_target_pairs={{0,192},{64,0},{128,64},{192,128},{1,193},{65,1},{129,65},{193,129... | collective-permute-start | bytes 983048 | tf_op jit(solution)/shard_map/ppermute | solution.py:32
  47.2 7.2 %collective-permute-done.8.refs_13_ = bf16[5,128,256]{2,1,0:T(8,128)(2,1)S(1)} collective-permute-done((bf16[5,128,256]{2,1,0:T(8,128)(2,1)S(1)}, bf16[5,128,256]{2,1,0:T(8,128)(2,1)S(1)}, u32[]{:S(2)}, u32[]{:S(2)}) %collective-permute-start.8) | collective-permute-done | bytes 327712 | tf_op jit(solution)/shard_map/ppermute | solution.py:32
  54.4 7.8 %all-to-all-done.owned = bf16[64,40,128]{2,1,0:T(8,128)(2,1)} async-done(((bf16[64,40,128]{2,1,0:T(8,128)(2,1)}), bf16[64,40,128]{2,1,0:T(8,128)(2,1)}, u32[]{:S(2)}, u32[]{:S(2)}) %all-to-all-start) | async-done | bytes 655392 | tf_op jit(solution)/shard_map/all_to_all | solution.py:401
  62.2 1.2 shard_map.142
  63.8 2.9 %collective-permute-start.11 = (bf16[32,16,256]{2,1,0:T(8,128)(2,1)S(1)}, bf16[32,16,256]{2,1,0:T(8,128)(2,1)S(1)}, u32[]{:S(2)}, u32[]{:S(2)}) collective-permute-start(bf16[32,16,256]{2,1,0:T(8,128)(2,1)S(1)} %get-tuple-element.125), channel_id=1, source_target_pairs={{0,192},{64,0},{128,64},{192,128},{1,193},{65,1},{129,65},{193,129... | collective-permute-start | bytes 786440 | tf_op jit(solution)/shard_map/ppermute | solution.py:32
  66.7 1.2 collective-permute-start.10
  68.2 3.8 %collective-permute-done.12 = bf16[32,16,256]{2,1,0:T(8,128)(2,1)S(1)} collective-permute-done((bf16[32,16,256]{2,1,0:T(8,128)(2,1)S(1)}, bf16[32,16,256]{2,1,0:T(8,128)(2,1)S(1)}, u32[]{:S(2)}, u32[]{:S(2)}) %collective-permute-start.12) | collective-permute-done | bytes 262176 | tf_op jit(solution)/shard_map/ppermute | solution.py:32
  72.0 2.7 %collective-permute-start.14 = (bf16[32,16,256]{2,1,0:T(8,128)(2,1)S(1)}, bf16[32,16,256]{2,1,0:T(8,128)(2,1)S(1)}, u32[]{:S(2)}, u32[]{:S(2)}) collective-permute-start(bf16[32,16,256]{2,1,0:T(8,128)(2,1)S(1)} %collective-permute-done.11), channel_id=1, source_target_pairs={{0,192},{64,0},{128,64},{192,128},{1,193},{65,1},{129,65},{193,129... | collective-permute-start | bytes 786440 | tf_op jit(solution)/shard_map/ppermute | solution.py:32
  74.6 2.2 %collective-permute-done.10 = bf16[32,16,256]{2,1,0:T(8,128)(2,1)S(1)} collective-permute-done((bf16[32,16,256]{2,1,0:T(8,128)(2,1)S(1)}, bf16[32,16,256]{2,1,0:T(8,128)(2,1)S(1)}, u32[]{:S(2)}, u32[]{:S(2)}) %collective-permute-start.10) | collective-permute-done | bytes 262176 | tf_op jit(solution)/shard_map/ppermute | solution.py:32
  77.6 5.6 %collective-permute-done.13 = bf16[32,16,256]{2,1,0:T(8,128)(2,1)S(1)} collective-permute-done((bf16[32,16,256]{2,1,0:T(8,128)(2,1)S(1)}, bf16[32,16,256]{2,1,0:T(8,128)(2,1)S(1)}, u32[]{:S(2)}, u32[]{:S(2)}) %collective-permute-start.13) | collective-permute-done | bytes 262176 | tf_op jit(solution)/shard_map/ppermute | solution.py:32
  83.2 2.8 %shard_map.143 = (f32[1024,256]{1,0:T(8,128)S(1)}, f32[8,128]{1,0:T(8,128)S(1)}) custom-call(bf16[512,256]{1,0:T(8,128)(2,1)S(1)} %bitcast.30, bf16[512,256]{1,0:T(8,128)(2,1)S(1)} %bitcast.31, bf16[512,256]{1,0:T(8,128)(2,1)S(1)} %bitcast.34, bf16[512,256]{1,0:T(8,128)(2,1)S(1)} %bitcast.33, bf16[512,256]{1,0:T(8,128)(2,1)S(1)} %bitcast.36, ...), custom_call_target="tpu_custom_call" | custom-call | tf_op jit(solution)/shard_map/pallas_call | solution.py:326
  86.6 1.9 %collective-permute-done.16 = f32[8,128]{1,0:T(8,128)S(1)} collective-permute-done((f32[8,128]{1,0:T(8,128)S(1)}, f32[8,128]{1,0:T(8,128)S(1)}, u32[]{:S(2)}, u32[]{:S(2)}) %collective-permute-start.16) | collective-permute-done | bytes 4128 | tf_op jit(solution)/shard_map/ppermute | solution.py:453
  88.5 2.4 %collective-permute-start.17 = (f32[8,128]{1,0:T(8,128)S(1)}, f32[8,128]{1,0:T(8,128)S(1)}, u32[]{:S(2)}, u32[]{:S(2)}) collective-permute-start(f32[8,128]{1,0:T(8,128)S(1)} %add.38.mine), channel_id=1, source_target_pairs={{0,128},{64,192},{128,0},{192,64},{1,129},{65,193},{129,1},{193,65... | collective-permute-start | bytes 12296 | tf_op jit(solution)/shard_map/ppermute | solution.py:454
  90.9 1.6 %collective-permute-done.17.other = f32[8,128]{1,0:T(8,128)S(1)} collective-permute-done((f32[8,128]{1,0:T(8,128)S(1)}, f32[8,128]{1,0:T(8,128)S(1)}, u32[]{:S(2)}, u32[]{:S(2)}) %collective-permute-start.17) | collective-permute-done | bytes 4128 | tf_op jit(solution)/shard_map/ppermute | solution.py:454
  93.3 10.2 %all-to-all-start.1 = ((bf16[64,16,256]{2,1,0:T(8,128)(2,1)}), bf16[64,16,256]{2,1,0:T(8,128)(2,1)S(1)}, u32[]{:S(2)}, u32[]{:S(2)}) async-start(bf16[64,16,256]{2,1,0:T(8,128)(2,1)} %shard_map.144), calls=%async_computation.1 | async-start | bytes 1048576 | tf_op jit(solution)/shard_map/all_to_all | solution.py:401
  105.1 1.6 %fusion.3 = f32[1,256,1024]{2,1,0:T(8,128)} fusion(s32[]{:T(128)S(6)} %mul.31, f32[256,1024]{1,0:T(8,128)S(1)} %fusion.4, f32[1,256,1024]{2,1,0:T(8,128)S(1)} %copy-done.10), kind=kLoop, calls=%fused_computation.8 | loop fusion | flops 786432 | bytes 3145732 | tf_op jit(solution)/shard_map/add | solution.py:467
  106.7 1.7 %fusion = f32[1,256,1024]{2,1,0:T(8,128)} fusion(bf16[1024,1024]{1,0:T(8,128)(2,1)S(1)} %bitcast.41, f32[1,256,1024]{2,1,0:T(8,128)S(1)} %copy-done.9, s32[]{:T(128)S(6)} %mul.27), kind=kOutput, calls=%fused_computation.5 | convolution fusion | flops 537395200 | bytes 4718596 | tf_op jit(solution)/shard_map/dot_general | solution.py:52
  108.4 11.4 %all-to-all-done.1.back = bf16[64,16,256]{2,1,0:T(8,128)(2,1)S(1)} async-done(((bf16[64,16,256]{2,1,0:T(8,128)(2,1)}), bf16[64,16,256]{2,1,0:T(8,128)(2,1)S(1)}, u32[]{:S(2)}, u32[]{:S(2)}) %all-to-all-start.1) | async-done | bytes 524320 | tf_op jit(solution)/shard_map/all_to_all | solution.py:401
  119.8 1.5 %shard_map.145 = bf16[64,16,256]{2,1,0:T(8,128)(2,1)} custom-call(s32[64]{0:T(128)S(1)} %copy-done.5, s32[64]{0:T(128)S(1)} %copy-done.3, bf16[64,16,256]{2,1,0:T(8,128)(2,1)S(1)} %all-to-all-done.1.back), custom_call_target="tpu_custom_call" | custom-call | tf_op jit(solution)/shard_map/pallas_call | solution.py:255
  (63 shorter events, 7.9 us)
Async XLA Ops:
  0.6 9.7 %copy-start.8 = (s32[64]{0:T(128)S(1)}, s32[64]{0:T(128)}, u32[]{:S(2)}) copy-start(s32[64]{0:T(128)} %constant.56.clone) | copy-start | bytes 772
  0.6 9.6 %copy-start.16 = (s32[64]{0:T(128)S(1)}, s32[64]{0:T(128)}, u32[]{:S(2)}) copy-start(s32[64]{0:T(128)} %param.11) | copy-start | bytes 772
  0.7 10.4 %copy-start.14 = (s32[64,4]{0,1:T(4,128)S(1)}, s32[64,4]{0,1:T(4,128)}, u32[]{:S(2)}) copy-start(s32[64,4]{0,1:T(4,128)} %param.12) | copy-start | bytes 3076
  2.0 9.1 %collective-permute-start.2 = (bf16[32,16,256]{2,1,0:T(8,128)(2,1)S(1)}, bf16[32,16,256]{2,1,0:T(8,128)(2,1)S(1)}, u32[]{:S(2)}, u32[]{:S(2)}) collective-permute-start(bf16[32,16,256]{2,1,0:T(8,128)(2,1)S(1)} %get-tuple-element.71), channel_id=1, source_target_pairs={{0,64},{64,128},{128,192},{192,0},{1,65},{65,129},{129,193},{193,1... | collective-permute-start | bytes 786440 | tf_op jit(solution)/shard_map/ppermute | solution.py:32
  4.2 7.0 %collective-permute-start.3 = (bf16[32,16,256]{2,1,0:T(8,128)(2,1)S(1)}, bf16[32,16,256]{2,1,0:T(8,128)(2,1)S(1)}, u32[]{:S(2)}, u32[]{:S(2)}) collective-permute-start(bf16[32,16,256]{2,1,0:T(8,128)(2,1)S(1)} %get-tuple-element.72), channel_id=1, source_target_pairs={{0,192},{64,0},{128,64},{192,128},{1,193},{65,1},{129,65},{193,129... | collective-permute-start | bytes 786440 | tf_op jit(solution)/shard_map/ppermute | solution.py:32
  7.5 10.0 %collective-permute-start = (bf16[32,16,256]{2,1,0:T(8,128)(2,1)S(1)}, bf16[32,16,256]{2,1,0:T(8,128)(2,1)S(1)}, u32[]{:S(2)}, u32[]{:S(2)}) collective-permute-start(bf16[32,16,256]{2,1,0:T(8,128)(2,1)S(1)} %get-tuple-element.76), channel_id=1, source_target_pairs={{0,64},{64,128},{128,192},{192,0},{1,65},{65,129},{129,193},{193,1... | collective-permute-start | bytes 786440 | tf_op jit(solution)/shard_map/ppermute | solution.py:32
  7.6 9.9 %collective-permute-start.1 = (bf16[32,16,256]{2,1,0:T(8,128)(2,1)S(1)}, bf16[32,16,256]{2,1,0:T(8,128)(2,1)S(1)}, u32[]{:S(2)}, u32[]{:S(2)}) collective-permute-start(bf16[32,16,256]{2,1,0:T(8,128)(2,1)S(1)} %get-tuple-element.77), channel_id=1, source_target_pairs={{0,192},{64,0},{128,64},{192,128},{1,193},{65,1},{129,65},{193,129... | collective-permute-start | bytes 786440 | tf_op jit(solution)/shard_map/ppermute | solution.py:32
  11.1 13.5 %copy-start.4 = (s32[64]{0:T(128)}, s32[64]{0:T(128)S(1)}, u32[]{:S(2)}) copy-start(s32[64]{0:T(128)S(1)} %gather_fusion) | copy-start | bytes 772
  11.1 13.5 %copy-start.2 = (s32[64]{0:T(128)}, s32[64]{0:T(128)S(1)}, u32[]{:S(2)}) copy-start(s32[64]{0:T(128)S(1)} %fusion.9.flags) | copy-start | bytes 772
  11.1 7.8 %copy-start.6 = (f32[64,16,256]{2,1,0:T(8,128)S(1)}, f32[64,16,256]{2,1,0:T(8,128)}, u32[]{:S(2)}) copy-start(f32[64,16,256]{2,1,0:T(8,128)} %param.17) | copy-start | bytes 3145732
  11.1 7.8 %copy-start.7 = (f32[64,16,256]{2,1,0:T(8,128)S(1)}, f32[64,16,256]{2,1,0:T(8,128)}, u32[]{:S(2)}) copy-start(f32[64,16,256]{2,1,0:T(8,128)} %param.18) | copy-start | bytes 3145732
  12.0 9.8 %collective-permute-start.4 = (bf16[32,16,256]{2,1,0:T(8,128)(2,1)}, bf16[32,16,256]{2,1,0:T(8,128)(2,1)}, u32[]{:S(2)}, u32[]{:S(2)}) collective-permute-start(bf16[32,16,256]{2,1,0:T(8,128)(2,1)} %get-tuple-element.91), channel_id=1, source_target_pairs={{0,64},{64,128},{128,192},{192,0},{1,65},{65,129},{129,193},{193,1... | collective-permute-start | bytes 786440 | tf_op jit(solution)/shard_map/ppermute | solution.py:32
  13.2 8.6 %collective-permute-start.5 = (bf16[32,16,256]{2,1,0:T(8,128)(2,1)}, bf16[32,16,256]{2,1,0:T(8,128)(2,1)}, u32[]{:S(2)}, u32[]{:S(2)}) collective-permute-start(bf16[32,16,256]{2,1,0:T(8,128)(2,1)} %get-tuple-element.92), channel_id=1, source_target_pairs={{0,192},{64,0},{128,64},{192,128},{1,193},{65,1},{129,65},{193,129... | collective-permute-start | bytes 786440 | tf_op jit(solution)/shard_map/ppermute | solution.py:32
  18.9 5.6 %copy-start.11 = (bf16[11,128,256]{2,1,0:T(8,128)(2,1)S(1)}, bf16[11,128,256]{2,1,0:T(8,128)(2,1)}, u32[]{:S(2)}) copy-start(bf16[11,128,256]{2,1,0:T(8,128)(2,1)} %get-tuple-element.114.refs_10_) | copy-start | bytes 2162692
  21.8 21.3 %collective-permute-start.7 = (bf16[11,128,256]{2,1,0:T(8,128)(2,1)S(1)}, bf16[11,128,256]{2,1,0:T(8,128)(2,1)S(1)}, u32[]{:S(2)}, u32[]{:S(2)}) collective-permute-start(bf16[11,128,256]{2,1,0:T(8,128)(2,1)S(1)} %copy-done.15), channel_id=1, source_target_pairs={{0,192},{64,0},{128,64},{192,128},{1,193},{65,1},{129,65},{193,129... | collective-permute-start | bytes 2162696 | tf_op jit(solution)/shard_map/ppermute | solution.py:32
  24.6 18.6 %collective-permute-start.6 = (bf16[11,128,256]{2,1,0:T(8,128)(2,1)S(1)}, bf16[11,128,256]{2,1,0:T(8,128)(2,1)S(1)}, u32[]{:S(2)}, u32[]{:S(2)}) collective-permute-start(bf16[11,128,256]{2,1,0:T(8,128)(2,1)S(1)} %copy-done.11), channel_id=1, source_target_pairs={{0,64},{64,128},{128,192},{192,0},{1,65},{65,129},{129,193},{193,1... | collective-permute-start | bytes 2162696 | tf_op jit(solution)/shard_map/ppermute | solution.py:32
  28.1 34.1 %all-to-all-start = ((bf16[64,40,128]{2,1,0:T(8,128)(2,1)}), bf16[64,40,128]{2,1,0:T(8,128)(2,1)}, u32[]{:S(2)}, u32[]{:S(2)}) async-start(bf16[64,40,128]{2,1,0:T(8,128)(2,1)} %get-tuple-element.103), calls=%async_computation | async-start | bytes 1310720 | tf_op jit(solution)/shard_map/all_to_all | solution.py:401
  44.2 10.2 %collective-permute-start.8 = (bf16[5,128,256]{2,1,0:T(8,128)(2,1)S(1)}, bf16[5,128,256]{2,1,0:T(8,128)(2,1)S(1)}, u32[]{:S(2)}, u32[]{:S(2)}) collective-permute-start(bf16[5,128,256]{2,1,0:T(8,128)(2,1)S(1)} %get-tuple-element.107), channel_id=1, source_target_pairs={{0,64},{64,128},{128,192},{192,0},{1,65},{65,129},{129,193},{193,1... | collective-permute-start | bytes 983048 | tf_op jit(solution)/shard_map/ppermute | solution.py:32
  44.5 9.9 %collective-permute-start.9 = (bf16[5,128,256]{2,1,0:T(8,128)(2,1)S(1)}, bf16[5,128,256]{2,1,0:T(8,128)(2,1)S(1)}, u32[]{:S(2)}, u32[]{:S(2)}) collective-permute-start(bf16[5,128,256]{2,1,0:T(8,128)(2,1)S(1)} %get-tuple-element.108), channel_id=1, source_target_pairs={{0,192},{64,0},{128,64},{192,128},{1,193},{65,1},{129,65},{193,129... | collective-permute-start | bytes 983048 | tf_op jit(solution)/shard_map/ppermute | solution.py:32
  54.4 28.8 %copy-start.12 = (bf16[5,128,256]{2,1,0:T(8,128)(2,1)}, bf16[5,128,256]{2,1,0:T(8,128)(2,1)S(1)}, u32[]{:S(2)}) copy-start(bf16[5,128,256]{2,1,0:T(8,128)(2,1)S(1)} %collective-permute-done.8.refs_13_) | copy-start | bytes 983044
  54.4 28.8 %copy-start.13 = (bf16[5,128,256]{2,1,0:T(8,128)(2,1)}, bf16[5,128,256]{2,1,0:T(8,128)(2,1)S(1)}, u32[]{:S(2)}) copy-start(bf16[5,128,256]{2,1,0:T(8,128)(2,1)S(1)} %collective-permute-done.9.refs_14_) | copy-start | bytes 983044
  63.4 8.5 %collective-permute-start.12 = (bf16[32,16,256]{2,1,0:T(8,128)(2,1)S(1)}, bf16[32,16,256]{2,1,0:T(8,128)(2,1)S(1)}, u32[]{:S(2)}, u32[]{:S(2)}) collective-permute-start(bf16[32,16,256]{2,1,0:T(8,128)(2,1)S(1)} %get-tuple-element.124), channel_id=1, source_target_pairs={{0,64},{64,128},{128,192},{192,0},{1,65},{65,129},{129,193},{193,1... | collective-permute-start | bytes 786440 | tf_op jit(solution)/shard_map/ppermute | solution.py:32
  63.8 8.2 %collective-permute-start.11 = (bf16[32,16,256]{2,1,0:T(8,128)(2,1)S(1)}, bf16[32,16,256]{2,1,0:T(8,128)(2,1)S(1)}, u32[]{:S(2)}, u32[]{:S(2)}) collective-permute-start(bf16[32,16,256]{2,1,0:T(8,128)(2,1)S(1)} %get-tuple-element.125), channel_id=1, source_target_pairs={{0,192},{64,0},{128,64},{192,128},{1,193},{65,1},{129,65},{193,129... | collective-permute-start | bytes 786440 | tf_op jit(solution)/shard_map/ppermute | solution.py:32
  66.7 10.1 %collective-permute-start.10 = (bf16[32,16,256]{2,1,0:T(8,128)(2,1)S(1)}, bf16[32,16,256]{2,1,0:T(8,128)(2,1)S(1)}, u32[]{:S(2)}, u32[]{:S(2)}) collective-permute-start(bf16[32,16,256]{2,1,0:T(8,128)(2,1)S(1)} %get-tuple-element.124), channel_id=1, source_target_pairs={{0,192},{64,0},{128,64},{192,128},{1,193},{65,1},{129,65},{193,129... | collective-permute-start | bytes 786440 | tf_op jit(solution)/shard_map/ppermute | solution.py:32
  67.9 9.7 %collective-permute-start.15 = (bf16[32,16,256]{2,1,0:T(8,128)(2,1)S(1)}, bf16[32,16,256]{2,1,0:T(8,128)(2,1)S(1)}, u32[]{:S(2)}, u32[]{:S(2)}) collective-permute-start(bf16[32,16,256]{2,1,0:T(8,128)(2,1)S(1)} %get-tuple-element.125), channel_id=1, source_target_pairs={{0,64},{64,128},{128,192},{192,0},{1,65},{65,129},{129,193},{193,1... | collective-permute-start | bytes 786440 | tf_op jit(solution)/shard_map/ppermute | solution.py:32
  71.9 11.2 %collective-permute-start.13 = (bf16[32,16,256]{2,1,0:T(8,128)(2,1)S(1)}, bf16[32,16,256]{2,1,0:T(8,128)(2,1)S(1)}, u32[]{:S(2)}, u32[]{:S(2)}) collective-permute-start(bf16[32,16,256]{2,1,0:T(8,128)(2,1)S(1)} %collective-permute-done.12), channel_id=1, source_target_pairs={{0,64},{64,128},{128,192},{192,0},{1,65},{65,129},{129,193},{193,1... | collective-permute-start | bytes 786440 | tf_op jit(solution)/shard_map/ppermute | solution.py:32
  72.0 11.2 %collective-permute-start.14 = (bf16[32,16,256]{2,1,0:T(8,128)(2,1)S(1)}, bf16[32,16,256]{2,1,0:T(8,128)(2,1)S(1)}, u32[]{:S(2)}, u32[]{:S(2)}) collective-permute-start(bf16[32,16,256]{2,1,0:T(8,128)(2,1)S(1)} %collective-permute-done.11), channel_id=1, source_target_pairs={{0,192},{64,0},{128,64},{192,128},{1,193},{65,1},{129,65},{193,129... | collective-permute-start | bytes 786440 | tf_op jit(solution)/shard_map/ppermute | solution.py:32
  86.0 2.5 %collective-permute-start.16 = (f32[8,128]{1,0:T(8,128)S(1)}, f32[8,128]{1,0:T(8,128)S(1)}, u32[]{:S(2)}, u32[]{:S(2)}) collective-permute-start(f32[8,128]{1,0:T(8,128)S(1)} %get-tuple-element.120), channel_id=1, source_target_pairs={{0,64},{64,0},{128,192},{192,128},{1,65},{65,1},{129,193},{193,129... | collective-permute-start | bytes 12296 | tf_op jit(solution)/shard_map/ppermute | solution.py:453
  88.5 4.0 %collective-permute-start.17 = (f32[8,128]{1,0:T(8,128)S(1)}, f32[8,128]{1,0:T(8,128)S(1)}, u32[]{:S(2)}, u32[]{:S(2)}) collective-permute-start(f32[8,128]{1,0:T(8,128)S(1)} %add.38.mine), channel_id=1, source_target_pairs={{0,128},{64,192},{128,0},{192,64},{1,129},{65,193},{129,1},{193,65... | collective-permute-start | bytes 12296 | tf_op jit(solution)/shard_map/ppermute | solution.py:454
  93.3 26.5 %all-to-all-start.1 = ((bf16[64,16,256]{2,1,0:T(8,128)(2,1)}), bf16[64,16,256]{2,1,0:T(8,128)(2,1)S(1)}, u32[]{:S(2)}, u32[]{:S(2)}) async-start(bf16[64,16,256]{2,1,0:T(8,128)(2,1)} %shard_map.144), calls=%async_computation.1 | async-start | bytes 1048576 | tf_op jit(solution)/shard_map/all_to_all | solution.py:401
  106.7 13.1 %copy-start.3 = (s32[64]{0:T(128)S(1)}, s32[64]{0:T(128)}, u32[]{:S(2)}) copy-start(s32[64]{0:T(128)} %copy-done.2) | copy-start | bytes 772
  106.7 13.1 %copy-start.5 = (s32[64]{0:T(128)S(1)}, s32[64]{0:T(128)}, u32[]{:S(2)}) copy-start(s32[64]{0:T(128)} %copy-done.4) | copy-start | bytes 772
  (5 other events, 7.7 us)

commit v9 on v8

--- a/solution.py
+++ b/solution.py
@@ -109,6 +109,7 @@
         in_specs=[pl.BlockSpec(left.shape, lambda i: (0, 0, 0))] * 2,
         out_specs=tuple(pl.BlockSpec((n, *unit), lambda i: (0, 0, 0)) for n in (11, 11, 2)),
         compiler_params=pltpu.CompilerParams(vmem_limit_bytes=8 * MIB),
+        cost_estimate=LONG,
     )(in_hbm(left), in_hbm(right))
 
 
@@ -133,12 +134,11 @@
         in_specs=[pl.BlockSpec(memory_space=VMEM)] * 5,
         out_specs=(pl.BlockSpec(memory_space=VMEM),) * 3,
         compiler_params=pltpu.CompilerParams(vmem_limit_bytes=10 * MIB),
-        cost_estimate=LONG,
     )(own, up_direct, down_direct, first.reshape(shape.shape), second.reshape(shape.shape))
 
 
 def pack_kernel(
-    key, flags, partial, up_sum, down_sum, first, second, out, first_out, second_out
+    key, flags, partial, up_sum, down_sum, first, second, out, squares, first_out, second_out
 ):
     _, half, rows, cols = partial.shape
     count = first_out.shape[1]
@@ -159,8 +159,9 @@
         square = adam * adam
         square = square[:, :lanes] + square[:, lanes:]
         square = (square[: rows // 2] + square[rows // 2 :]) * keep
-        piece = jnp.concatenate([grad[:, :lanes], grad[:, lanes:], square], axis=0)
-        out[key[block]] = piece.astype(BF16)
+        place = key[block]
+        out[place] = grad.astype(BF16)
+        squares[place] = square
 
     def step(i, carry):
         at = begin + i
@@ -177,20 +178,25 @@
     steps = 2 if half >= 16 else 1
     moment = pl.BlockSpec((2, half // steps, rows, cols), lambda i, *_: (0, i, 0, 0))
     halves = pltpu.HBM((2, half, rows, cols), F32)
-    piece = (blocks, 2 * rows + rows // 2, lanes)
-    out, first_next, second_next = pl.pallas_call(
+    piece, tile = (blocks, rows, cols), (blocks, rows // 2, lanes)
+    out, squares, first_next, second_next = pl.pallas_call(
         pack_kernel,
-        out_shape=(pltpu.HBM(piece, BF16), halves, halves),
+        out_shape=(pltpu.HBM(piece, BF16), pltpu.HBM(tile, F32), halves, halves),
         grid_spec=pltpu.PrefetchScalarGridSpec(
             num_scalar_prefetch=2,
             grid=(steps,),
             in_specs=[pl.BlockSpec(memory_space=VMEM)] * 5,
-            out_specs=[pl.BlockSpec(piece, lambda i, *_: (0, 0, 0)), moment, moment],
+            out_specs=[
+                pl.BlockSpec(piece, lambda i, *_: (0, 0, 0)),
+                pl.BlockSpec(tile, lambda i, *_: (0, 0, 0)),
+                moment,
+                moment,
+            ],
         ),
         compiler_params=pltpu.CompilerParams(vmem_limit_bytes=16 * MIB),
     )(key, flags, partial, up_sum, down_sum, first, second)
     shape = (blocks, rows, cols)
-    return out, first_next.reshape(shape), second_next.reshape(shape)
+    return out, squares, first_next.reshape(shape), second_next.reshape(shape)
 
 
 def relay_kernel(prev, following, up, down):
@@ -211,28 +217,22 @@
     )(prev, following)
 
 
-def unpack_kernel(order, owned, low, high, adam):
-    half, rows, cols = low.shape
-    total = jnp.zeros(adam.shape, F32)
+def unpack_kernel(order, owned, low, high):
+    half = low.shape[0]
     for i, place in enumerate(order):
-        piece = owned[i].astype(F32)
-        value = jnp.concatenate([piece[:rows], piece[rows : 2 * rows]], axis=1).astype(BF16)
         if place < half:
-            low[place] = value
+            low[place] = owned[i]
         else:
-            high[place - half] = value
-        total += piece[2 * rows :]
-    adam[...] = total
-
-
-def unpack(order, owned, rows):
-    half = owned.shape[0] // 2
-    shape = jax.ShapeDtypeStruct((half, rows, 2 * owned.shape[2]), BF16)
+            high[place - half] = owned[i]
+
+
+def unpack(order, owned):
+    shape = jax.ShapeDtypeStruct((owned.shape[0] // 2, *owned.shape[1:]), BF16)
     return pl.pallas_call(
         functools.partial(unpack_kernel, order),
-        out_shape=(shape, shape, jax.ShapeDtypeStruct((rows // 2, 128), F32)),
+        out_shape=(shape, shape),
         in_specs=[pl.BlockSpec(memory_space=VMEM)],
-        out_specs=(pl.BlockSpec(memory_space=VMEM),) * 3,
+        out_specs=(pl.BlockSpec(memory_space=VMEM),) * 2,
         compiler_params=pltpu.CompilerParams(vmem_limit_bytes=6 * MIB),
     )(owned)
 
@@ -266,8 +266,8 @@
 
 
 def precond_kernel(*refs):
-    pieces, adam, sources, (out, norms) = refs[:8], refs[8], refs[9:15], refs[15:17]
-    mixed, held, sems = refs[17], refs[18:24], refs[24]
+    pieces, sources, (out, norms) = refs[:8], refs[8:14], refs[14:16]
+    mixed, held, sems = refs[16], refs[17:23], refs[23]
     width, quarter = out.shape
     half = width // 2
     me = lax.axis_index("grp")
@@ -317,21 +317,24 @@
         square += jnp.sum((value * value).reshape(quarter // 8, 8, quarter), axis=0)
     norms[...] = jnp.zeros_like(norms)
     norms[0:1, :] = jnp.broadcast_to(jnp.sum(square), (1, 128))
-    norms[1:2, :] = jnp.broadcast_to(jnp.sum(adam[...]), (1, 128))
-
-
-def precondition(pieces, adam, sources):
+
+
+def precondition(pieces, sources):
     rows, quarter = pieces[0].shape
-    operands = (*pieces, adam)
+    operands = pieces
     return pl.pallas_call(
         precond_kernel,
         out_shape=(
-            jax.ShapeDtypeStruct((2 * rows, quarter), F32),
+            pltpu.HBM((2 * rows, quarter), F32),
             jax.ShapeDtypeStruct((8, 128), F32),
         ),
+        grid=(1,),
         in_specs=[pl.BlockSpec(memory_space=VMEM)] * len(operands)
         + [pl.BlockSpec(memory_space=pl.ANY)] * len(sources),
-        out_specs=(pl.BlockSpec(memory_space=VMEM),) * 2,
+        out_specs=(
+            pl.BlockSpec((2 * rows, quarter), lambda i: (0, 0)),
+            pl.BlockSpec((8, 128), lambda i: (0, 0)),
+        ),
         scratch_shapes=[
             VMEM((2 * rows, quarter), BF16),
             *[VMEM(source.shape, BF16) for source in sources],
@@ -341,9 +344,9 @@
     )(*operands, *map(in_hbm, sources))
 
 
-def graft_kernel(cells, order, precond, mine, other, out):
-    sums = mine[...] + other[...]
-    pre, adam = sums[0:1, :], sums[1:2, :]
+def graft_kernel(cells, order, precond, shares, first, second, third, fourth, out):
+    pre = (first[...] + second[...] + third[...] + fourth[...])[0:1, :]
+    adam = jnp.sum(shares[...], axis=0, keepdims=True)
     adam = adam * (BIAS_SECOND / (BIAS_FIRST * BIAS_FIRST))
     scale = -jnp.sqrt(adam / cells) / jnp.sqrt(pre / cells + NORM_EPS)
     _, rows, quarter = out.shape
@@ -352,18 +355,18 @@
         out[i] = (scale * precond[pl.ds(place * rows, rows), :]).astype(BF16)
 
 
-def graft(order, precond, mine, other):
+def graft(order, precond, shares, norms):
     width, quarter = precond.shape
     shape = (len(order), width // len(order), quarter)
-    small = pl.BlockSpec((8, 128), lambda i: (0, 0))
+    small = [pl.BlockSpec(array.shape, lambda i: (0, 0)) for array in (shares, *norms)]
     return pl.pallas_call(
         functools.partial(graft_kernel, float(width * width), order),
         out_shape=pltpu.HBM(shape, BF16),
         grid=(1,),
-        in_specs=[pl.BlockSpec((width, quarter), lambda i: (0, 0))] + [small] * 2,
+        in_specs=[pl.BlockSpec((width, quarter), lambda i: (0, 0))] + small,
         out_specs=pl.BlockSpec(shape, lambda i: (0, 0, 0)),
         compiler_params=pltpu.CompilerParams(vmem_limit_bytes=8 * MIB),
-    )(precond, mine, other)
+    )(in_hbm(precond), shares, *norms)
 
 
 def on_device(
@@ -415,21 +418,23 @@
     up_sum, down_sum, left_root, right_root, later = lax.optimization_barrier(
         (up_sum, down_sum, left_root, right_root, part)
     )
-    own = columns(later, 0)
     up_sum = shift(up_sum, 1)
     down_sum = shift(down_sum, -1)
     key = places_of(assign, n_own, per_owner, order)
     flags = inside(block_bounds, shard_rows, quarter)
     roots_up, roots_down, root_own = root_pieces(left_root, right_root)
-    up_direct, down_direct, key, flags, roots_up, roots_down, root_own = lax.optimization_barrier(
-        (up_direct, down_direct, key, flags, roots_up, roots_down, root_own)
-    )
+    later, up_direct, down_direct, key, flags, roots_up, roots_down, root_own = (
+        lax.optimization_barrier(
+            (later, up_direct, down_direct, key, flags, roots_up, roots_down, root_own)
+        )
+    )
+    own = columns(later, 0)
     partial, first, second = gather(own, up_direct, down_direct, first_moment, second_moment)
 
     roots_up, roots_down, up_sum, down_sum, partial = lax.optimization_barrier(
         (roots_up, roots_down, up_sum, down_sum, partial)
     )
-    sorted_grad, first_next, second_next = pack(
+    sorted_grad, squares, first_next, second_next = pack(
         key, flags, partial, up_sum, down_sum, first, second
     )
     owned = exchange(sorted_grad)
@@ -439,20 +444,23 @@
     far_roots = [shift(onward[0], 1), shift(onward[1], -1)]
     roots = [root_own, roots_up, roots_prev, roots_next, *far_roots]
 
-    owned, roots = lax.optimization_barrier((owned, roots))
-    low, high, adam = unpack(order, owned, shard_rows)
+    adam_sq = jnp.sum(squares, axis=(1, 2))
+    adam_sq = sum(shift(adam_sq, step) for step in (1, 2, 3)) + adam_sq
+    owned, roots, adam_sq = lax.optimization_barrier((owned, roots, adam_sq))
+    low, high = unpack(order, owned)
     prev_low = shift(low, 1)
     next_high = shift(high, -1)
     prev_high = shift(high, 1)
     next_low = shift(low, -1)
+    prev_low, next_high, adam_sq = lax.optimization_barrier((prev_low, next_high, adam_sq))
+    shares = exchange(jnp.broadcast_to(adam_sq[:, None, None], (n_own, 1, 128)))
     far_low = shift(prev_low, 1)
     far_high = shift(next_high, -1)
     pieces = [low, high, next_low, next_high, far_low, far_high, prev_low, prev_high]
     flat = [piece.reshape(-1, quarter) for piece in pieces]
-    precond, norms = precondition(flat, adam, roots)
-    norms += lax.ppermute(norms, "grp", [(i, i ^ 1) for i in range(n_grp)])
-    others = lax.ppermute(norms, "grp", [(i, i ^ 2) for i in range(n_grp)])
-    grafted = graft(order, precond, norms, others)
+    precond, norms = precondition(flat, roots)
+    norms = [norms] + [shift(norms, step) for step in (1, 2, 3)]
+    grafted = graft(order, precond, shares.reshape(n_own, 128), norms)
     pieces, grafted = lax.optimization_barrier((pieces, grafted))
     back = exchange(grafted)
 

time: 122 us -> 124 us (1.016)
  waiting for transfers between devices: 44.9 us -> 25.9 us
  starting transfers between devices: 50.4 us -> 65.3 us
  Pallas kernels: 13.8 us -> 17.4 us
  local copies, waits for them, and re-layouts: 6.8 us -> 8.44 us
    ppermute x16 -> x22, waiting for transfers between devices: 22.2 us -> 9.78 us  [shift(): return lax.ppermute(array, 'grp', [(i, (i + step) % n) for i in range(n)])]
    all_to_all x2 -> x3, starting transfers between devices: 25.2 us -> 36.3 us  [exchange(): lax.all_to_all(array, 'own', 0, 0, axis_index_groups=groups, tiled=True)]
    ppermute x16 -> x22, starting transfers between devices: 22.2 us -> 29 us  [shift(): return lax.ppermute(array, 'grp', [(i, (i + step) % n) for i in range(n)])]
    ppermute x2 -> x0, waiting for transfers between devices: 3.52 us -> none  [the longest x1 1.91 us: on_device(): norms += lax.ppermute(norms, 'grp', [(i, i ^ 1) for i in range(n_grp)])]
    all_to_all x2 -> x3, waiting for transfers between devices: 19.2 us -> 16.2 us  [exchange(): lax.all_to_all(array, 'own', 0, 0, axis_index_groups=groups, tiled=True)]
    ppermute x2 -> x0, starting transfers between devices: 2.98 us -> none  [the longest x1 2.35 us: on_device(): others = lax.ppermute(norms, 'grp', [(i, i ^ 2) for i in range(n_grp)])]
  transfers between devices with their start and end apart: 20 -> 25, of which waited for: 10 -> 8; matrix products, arithmetic and copies ran while one was open for 7% -> 9% of each run, Pallas kernels for 6% -> 10%
where the time goes in v9:
time: 124 us; the launch traced here: 123 us
  starting transfers between devices  65.3 us (53%)
  waiting for transfers between devices  25.9 us (21%)
  Pallas kernels  17.4 us (14%)
  local copies, waits for them, and re-layouts  8.44 us (7%)
  other arithmetic  2.49 us (2%)
  matrix products  2.49 us (2%)
    all_to_all x3, starting transfers between devices, exchange(): lax.all_to_all(array, 'own', 0, 0, axis_index_groups=groups, tiled=True)  36.3 us
    ppermute x22, starting transfers between devices, shift(): return lax.ppermute(array, 'grp', [(i, (i + step) % n) for i in range(n)])  29 us
    all_to_all x3, waiting for transfers between devices, exchange(): lax.all_to_all(array, 'own', 0, 0, axis_index_groups=groups, tiled=True)  16.2 us
    ppermute x22, waiting for transfers between devices, shift(): return lax.ppermute(array, 'grp', [(i, (i + step) % n) for i in range(n)])  9.78 us
    pallas_call x1, Pallas kernels, precondition(): pl.pallas_call(precond_kernel, out_shape=(pltpu.HBM((2 * rows, quarter),...  3.62 us
    pallas_call x1, Pallas kernels, pack(): pl.pallas_call(pack_kernel, out_shape=(pltpu.HBM(piece, BF16), pltpu.HBM(...  3.6 us
    pallas_call x1, Pallas kernels, root_pieces(): pl.pallas_call(roots_kernel, out_shape=(pltpu.HBM((11, *unit), BF16), plt...  2.97 us
    slice x1, local copies, waits for them, and re-layouts, on_device(): down[half:]  2.5 us
  transfers between devices with their start and end apart: 25, of which 8 were waited for; matrix products, arithmetic and copies ran while one was open for 9% of the time, Pallas kernels for 10%

profile of v9, /device:TPU:1, one launch (start us, length us, event | category | flops | bytes accessed | tf_op | source)
XLA Modules:
  0.0 123.0 jit_solution(4466011993888049455)
XLA Ops:
  0.7 1.4 %dynamic-slice_bitcast_fusion = (bf16[32,16,256]{2,1,0:T(8,128)(2,1)S(1)}, bf16[32,16,256]{2,1,0:T(8,128)(2,1)S(1)}) fusion(bf16[1,64,16,1024]{3,2,1,0:T(8,128)(2,1)} %param.10, s32[]{:T(128)S(6)} %add.49, s32[]{:T(128)S(6)} %mul.29), kind=kLoop, calls=%fused_computation.12 | loop fusion | bytes 1048584 | tf_op jit(solution)/shard_map/slice | solution.py:407
  2.0 2.1 %collective-permute-start = (bf16[32,16,256]{2,1,0:T(8,128)(2,1)S(1)}, bf16[32,16,256]{2,1,0:T(8,128)(2,1)S(1)}, u32[]{:S(2)}, u32[]{:S(2)}) collective-permute-start(bf16[32,16,256]{2,1,0:T(8,128)(2,1)S(1)} %get-tuple-element.76), channel_id=1, source_target_pairs={{0,64},{64,128},{128,192},{192,0},{1,65},{65,129},{129,193},{193,1... | collective-permute-start | bytes 786440 | tf_op jit(solution)/shard_map/ppermute | solution.py:32
  4.2 1.6 %collective-permute-start.1 = (bf16[32,16,256]{2,1,0:T(8,128)(2,1)S(1)}, bf16[32,16,256]{2,1,0:T(8,128)(2,1)S(1)}, u32[]{:S(2)}, u32[]{:S(2)}) collective-permute-start(bf16[32,16,256]{2,1,0:T(8,128)(2,1)S(1)} %get-tuple-element.77), channel_id=1, source_target_pairs={{0,192},{64,0},{128,64},{192,128},{1,193},{65,1},{129,65},{193,129... | collective-permute-start | bytes 786440 | tf_op jit(solution)/shard_map/ppermute | solution.py:32
  5.8 2.5 %constant_dynamic-slice_fusion.3 = (bf16[32,16,256]{2,1,0:T(8,128)(2,1)S(1)}, bf16[32,16,256]{2,1,0:T(8,128)(2,1)}, bf16[32,16,256]{2,1,0:T(8,128)(2,1)S(1)}, bf16[32,16,256]{2,1,0:T(8,128)(2,1)}) fusion(bf16[64,16,1024]{2,1,0:T(8,128)(2,1)} %bitcast.44, s32[]{:T(128)S(6)} %add.49, s32[]{:T(128)S(6)} %mul.30, s32[]{:T(128)S(6)} %mul.28), kind=kLoop, calls=%fused_computation.20 | loop fusion | bytes 2097164 | tf_op jit(solution)/shard_map/slice | solution.py:413
  8.3 2.7 %collective-permute-start.3 = (bf16[32,16,256]{2,1,0:T(8,128)(2,1)}, bf16[32,16,256]{2,1,0:T(8,128)(2,1)}, u32[]{:S(2)}, u32[]{:S(2)}) collective-permute-start(bf16[32,16,256]{2,1,0:T(8,128)(2,1)} %get-tuple-element.87), channel_id=1, source_target_pairs={{0,192},{64,0},{128,64},{192,128},{1,193},{65,1},{129,65},{193,129... | collective-permute-start | bytes 786440 | tf_op jit(solution)/shard_map/ppermute | solution.py:32
  13.3 2.1 %collective-permute-start.5 = (bf16[32,16,256]{2,1,0:T(8,128)(2,1)}, bf16[32,16,256]{2,1,0:T(8,128)(2,1)}, u32[]{:S(2)}, u32[]{:S(2)}) collective-permute-start(bf16[32,16,256]{2,1,0:T(8,128)(2,1)} %get-tuple-element.98), channel_id=1, source_target_pairs={{0,192},{64,0},{128,64},{192,128},{1,193},{65,1},{129,65},{193,129... | collective-permute-start | bytes 786440 | tf_op jit(solution)/shard_map/ppermute | solution.py:32
  15.4 3.0 %shard_map.138 = (bf16[11,128,256]{2,1,0:T(8,128)(2,1)}, bf16[11,128,256]{2,1,0:T(8,128)(2,1)}, bf16[2,128,256]{2,1,0:T(8,128)(2,1)}) custom-call(f32[1,256,1024]{2,1,0:T(8,128)} %left, f32[1,256,1024]{2,1,0:T(8,128)} %right), custom_call_target="tpu_custom_call" | custom-call | flops 199999995904 | bytes 1000000000 | tf_op jit(solution)/shard_map/pallas_call | solution.py:101
  18.4 1.5 %constant_dynamic-slice_fusion.2.own = bf16[64,16,256]{2,1,0:T(8,128)(2,1)S(1)} fusion(bf16[64,16,1024]{2,1,0:T(8,128)(2,1)} %bitcast.45, s32[]{:T(128)S(6)} %mul.27), kind=kLoop, calls=%fused_computation.19 | loop fusion | bytes 1048580 | tf_op jit(solution)/shard_map/dynamic_slice | solution.py:48
  19.9 1.3 %shard_map.139 = (f32[2,32,16,256]{3,2,1,0:T(8,128)S(1)}, f32[2,32,16,256]{3,2,1,0:T(8,128)S(1)}, f32[2,32,16,256]{3,2,1,0:T(8,128)S(1)}) custom-call(bf16[64,16,256]{2,1,0:T(8,128)(2,1)S(1)} %constant_dynamic-slice_fusion.2.own, bf16[32,16,256]{2,1,0:T(8,128)(2,1)} %collective-permute-done.2.up_direct, ...), custom_call_target="tpu_custom_call" | custom-call | tf_op jit(solution)/shard_map/pallas_call | solution.py:131
  21.9 1.6 %collective-permute-start.6 = (bf16[11,128,256]{2,1,0:T(8,128)(2,1)S(1)}, bf16[11,128,256]{2,1,0:T(8,128)(2,1)S(1)}, u32[]{:S(2)}, u32[]{:S(2)}) collective-permute-start(bf16[11,128,256]{2,1,0:T(8,128)(2,1)S(1)} %copy-done.11), channel_id=1, source_target_pairs={{0,64},{64,128},{128,192},{192,0},{1,65},{65,129},{129,193},{193,1... | collective-permute-start | bytes 2162696 | tf_op jit(solution)/shard_map/ppermute | solution.py:32
  23.5 1.4 %collective-permute-start.7 = (bf16[11,128,256]{2,1,0:T(8,128)(2,1)S(1)}, bf16[11,128,256]{2,1,0:T(8,128)(2,1)S(1)}, u32[]{:S(2)}, u32[]{:S(2)}) collective-permute-start(bf16[11,128,256]{2,1,0:T(8,128)(2,1)S(1)} %copy-done.16), channel_id=1, source_target_pairs={{0,192},{64,0},{128,64},{192,128},{1,193},{65,1},{129,65},{193,129... | collective-permute-start | bytes 2162696 | tf_op jit(solution)/shard_map/ppermute | solution.py:32
  25.0 3.6 %shard_map.140 = (bf16[64,16,256]{2,1,0:T(8,128)(2,1)}, f32[64,8,128]{2,1,0:T(8,128)}, f32[2,32,16,256]{3,2,1,0:T(8,128)}, f32[2,32,16,256]{3,2,1,0:T(8,128)}) custom-call(s32[64]{0:T(128)S(1)} %gather_fusion, s32[64]{0:T(128)S(1)} %fusion.9.flags, f32[2,32,16,256]{3,2,1,0:T(8,128)S(1)} %get-tuple-element.104.partial, ...), custom_call_target="tpu_custom_call" | custom-call | tf_op jit(solution)/shard_map/pallas_call | solution.py:182
  28.6 14.8 %all-to-all-start = ((bf16[64,16,256]{2,1,0:T(8,128)(2,1)}), bf16[64,16,256]{2,1,0:T(8,128)(2,1)}, u32[]{:S(2)}, u32[]{:S(2)}) async-start(bf16[64,16,256]{2,1,0:T(8,128)(2,1)} %get-tuple-element.109), calls=%async_computation | async-start | bytes 1048576 | tf_op jit(solution)/shard_map/all_to_all | solution.py:404
  44.7 2.6 %collective-permute-start.9 = (bf16[5,128,256]{2,1,0:T(8,128)(2,1)S(1)}, bf16[5,128,256]{2,1,0:T(8,128)(2,1)S(1)}, u32[]{:S(2)}, u32[]{:S(2)}) collective-permute-start(bf16[5,128,256]{2,1,0:T(8,128)(2,1)S(1)} %get-tuple-element.114), channel_id=1, source_target_pairs={{0,192},{64,0},{128,64},{192,128},{1,193},{65,1},{129,65},{193,129... | collective-permute-start | bytes 983048 | tf_op jit(solution)/shard_map/ppermute | solution.py:32
  47.9 1.5 %collective-permute-start.11 = (f32[64]{0:T(128)S(1)}, f32[64]{0:T(128)S(1)}, u32[]{:S(2)}, u32[]{:S(2)}) collective-permute-start(f32[64]{0:T(128)S(1)} %reduce_sum.9), channel_id=1, source_target_pairs={{0,128},{64,192},{128,0},{192,64},{1,129},{65,193},{129,1},{193,65... | collective-permute-start | bytes 776 | tf_op jit(solution)/shard_map/ppermute | solution.py:32
  50.5 4.3 %collective-permute-done.10 = f32[64]{0:T(128)S(1)} collective-permute-done((f32[64]{0:T(128)S(1)}, f32[64]{0:T(128)S(1)}, u32[]{:S(2)}, u32[]{:S(2)}) %collective-permute-start.10) | collective-permute-done | bytes 288 | tf_op jit(solution)/shard_map/ppermute | solution.py:32
  54.9 4.8 %all-to-all-done.owned = bf16[64,16,256]{2,1,0:T(8,128)(2,1)} async-done(((bf16[64,16,256]{2,1,0:T(8,128)(2,1)}), bf16[64,16,256]{2,1,0:T(8,128)(2,1)}, u32[]{:S(2)}, u32[]{:S(2)}) %all-to-all-start) | async-done | bytes 524320 | tf_op jit(solution)/shard_map/all_to_all | solution.py:404
  59.6 1.3 %shard_map.142 = (bf16[32,16,256]{2,1,0:T(8,128)(2,1)S(1)}, bf16[32,16,256]{2,1,0:T(8,128)(2,1)S(1)}) custom-call(bf16[64,16,256]{2,1,0:T(8,128)(2,1)} %all-to-all-done.owned), custom_call_target="tpu_custom_call" | custom-call | tf_op jit(solution)/shard_map/pallas_call | solution.py:231
  61.1 2.6 %collective-permute-start.15 = (bf16[32,16,256]{2,1,0:T(8,128)(2,1)S(1)}, bf16[32,16,256]{2,1,0:T(8,128)(2,1)S(1)}, u32[]{:S(2)}, u32[]{:S(2)}) collective-permute-start(bf16[32,16,256]{2,1,0:T(8,128)(2,1)S(1)} %get-tuple-element.135), channel_id=1, source_target_pairs={{0,192},{64,0},{128,64},{192,128},{1,193},{65,1},{129,65},{193,129... | collective-permute-start | bytes 786440 | tf_op jit(solution)/shard_map/ppermute | solution.py:32
  63.7 2.7 %collective-permute-start.13 = (bf16[32,16,256]{2,1,0:T(8,128)(2,1)S(1)}, bf16[32,16,256]{2,1,0:T(8,128)(2,1)S(1)}, u32[]{:S(2)}, u32[]{:S(2)}) collective-permute-start(bf16[32,16,256]{2,1,0:T(8,128)(2,1)S(1)} %get-tuple-element.134), channel_id=1, source_target_pairs={{0,192},{64,0},{128,64},{192,128},{1,193},{65,1},{129,65},{193,129... | collective-permute-start | bytes 786440 | tf_op jit(solution)/shard_map/ppermute | solution.py:32
  66.4 2.4 %collective-permute-done.14 = bf16[32,16,256]{2,1,0:T(8,128)(2,1)S(1)} collective-permute-done((bf16[32,16,256]{2,1,0:T(8,128)(2,1)S(1)}, bf16[32,16,256]{2,1,0:T(8,128)(2,1)S(1)}, u32[]{:S(2)}, u32[]{:S(2)}) %collective-permute-start.14) | collective-permute-done | bytes 262176 | tf_op jit(solution)/shard_map/ppermute | solution.py:32
  68.8 2.7 %collective-permute-start.17 = (bf16[32,16,256]{2,1,0:T(8,128)(2,1)S(1)}, bf16[32,16,256]{2,1,0:T(8,128)(2,1)S(1)}, u32[]{:S(2)}, u32[]{:S(2)}) collective-permute-start(bf16[32,16,256]{2,1,0:T(8,128)(2,1)S(1)} %collective-permute-done.15), channel_id=1, source_target_pairs={{0,192},{64,0},{128,64},{192,128},{1,193},{65,1},{129,65},{193,129... | collective-permute-start | bytes 786440 | tf_op jit(solution)/shard_map/ppermute | solution.py:32
  72.3 10.0 %all-to-all-start.1 = ((f32[64,1,128]{2,1,0:T(1,128)}), f32[64,1,128]{2,1,0:T(1,128)S(1)}, u32[]{:S(2)}, u32[]{:S(2)}) async-start(f32[64,1,128]{2,1,0:T(1,128)} %broadcast_in_dim.16), calls=%async_computation.1 | async-start | bytes 65536 | tf_op jit(solution)/shard_map/all_to_all | solution.py:404
  82.3 3.6 %shard_map.143 = (f32[1024,256]{1,0:T(8,128)}, f32[8,128]{1,0:T(8,128)S(1)}) custom-call(bf16[512,256]{1,0:T(8,128)(2,1)S(1)} %bitcast.33, bf16[512,256]{1,0:T(8,128)(2,1)S(1)} %bitcast.34, bf16[512,256]{1,0:T(8,128)(2,1)S(1)} %bitcast.38, bf16[512,256]{1,0:T(8,128)(2,1)S(1)} %bitcast.36, bf16[512,256]{1,0:T(8,128)(2,1)S(1)} %bitcast.39, ...), custom_call_target="tpu_custom_call" | custom-call | tf_op jit(solution)/shard_map/pallas_call | solution.py:325
  86.0 2.9 %collective-permute-start.20 = (f32[8,128]{1,0:T(8,128)S(1)}, f32[8,128]{1,0:T(8,128)S(1)}, u32[]{:S(2)}, u32[]{:S(2)}) collective-permute-start(f32[8,128]{1,0:T(8,128)S(1)} %get-tuple-element.130.first), channel_id=1, source_target_pairs={{0,128},{64,192},{128,0},{192,64},{1,129},{65,193},{129,1},{193,65... | collective-permute-start | bytes 12296 | tf_op jit(solution)/shard_map/ppermute | solution.py:32
  90.0 1.5 %collective-permute-done.21.fourth = f32[8,128]{1,0:T(8,128)S(1)} collective-permute-done((f32[8,128]{1,0:T(8,128)S(1)}, f32[8,128]{1,0:T(8,128)S(1)}, u32[]{:S(2)}, u32[]{:S(2)}) %collective-permute-start.21) | collective-permute-done | bytes 4128 | tf_op jit(solution)/shard_map/ppermute | solution.py:32
  91.6 2.1 %shard_map.144 = bf16[64,16,256]{2,1,0:T(8,128)(2,1)} custom-call(f32[1024,256]{1,0:T(8,128)} %get-tuple-element.128.precond, f32[64,128]{1,0:T(8,128)S(1)} %bitcast.41, f32[8,128]{1,0:T(8,128)S(1)} %get-tuple-element.130.first, f32[8,128]{1,0:T(8,128)S(1)} %collective-permute-done.19.second, f32[8,128]{1,0:T(8,128)S(1)} %collective-permute-done.20.third, ...), custom_call_target="tpu_custom_call" | custom-call | tf_op jit(solution)/shard_map/pallas_call | solution.py:362
  93.7 11.5 %all-to-all-start.2 = ((bf16[64,16,256]{2,1,0:T(8,128)(2,1)}), bf16[64,16,256]{2,1,0:T(8,128)(2,1)S(1)}, u32[]{:S(2)}, u32[]{:S(2)}) async-start(bf16[64,16,256]{2,1,0:T(8,128)(2,1)} %shard_map.144), calls=%async_computation.2 | async-start | bytes 1048576 | tf_op jit(solution)/shard_map/all_to_all | solution.py:404
  106.7 1.6 %fusion.3 = f32[1,256,1024]{2,1,0:T(8,128)} fusion(s32[]{:T(128)S(6)} %mul.31, f32[256,1024]{1,0:T(8,128)S(1)} %fusion.4, f32[1,256,1024]{2,1,0:T(8,128)S(1)} %copy-done.10), kind=kLoop, calls=%fused_computation.8 | loop fusion | flops 786432 | bytes 3145732 | tf_op jit(solution)/shard_map/add | solution.py:475
  108.3 1.7 %fusion = f32[1,256,1024]{2,1,0:T(8,128)} fusion(bf16[1024,1024]{1,0:T(8,128)(2,1)S(1)} %bitcast.43, f32[1,256,1024]{2,1,0:T(8,128)S(1)} %copy-done.9, s32[]{:T(128)S(6)} %mul.27), kind=kOutput, calls=%fused_computation.5 | convolution fusion | flops 537395200 | bytes 4718596 | tf_op jit(solution)/shard_map/dot_general | solution.py:52
  110.1 11.4 %all-to-all-done.2.back = bf16[64,16,256]{2,1,0:T(8,128)(2,1)S(1)} async-done(((bf16[64,16,256]{2,1,0:T(8,128)(2,1)}), bf16[64,16,256]{2,1,0:T(8,128)(2,1)S(1)}, u32[]{:S(2)}, u32[]{:S(2)}) %all-to-all-start.2) | async-done | bytes 524320 | tf_op jit(solution)/shard_map/all_to_all | solution.py:404
  121.5 1.5 %shard_map.145 = bf16[64,16,256]{2,1,0:T(8,128)(2,1)} custom-call(s32[64]{0:T(128)S(1)} %copy-done.7, s32[64]{0:T(128)S(1)} %copy-done.5, bf16[64,16,256]{2,1,0:T(8,128)(2,1)S(1)} %all-to-all-done.2.back), custom_call_target="tpu_custom_call" | custom-call | tf_op jit(solution)/shard_map/pallas_call | solution.py:255
  (77 shorter events, 9.7 us)
Async XLA Ops:
  0.7 11.1 %copy-start.15 = (s32[64,4]{0,1:T(4,128)S(1)}, s32[64,4]{0,1:T(4,128)}, u32[]{:S(2)}) copy-start(s32[64,4]{0,1:T(4,128)} %param.12) | copy-start | bytes 3076
  2.0 9.8 %collective-permute-start = (bf16[32,16,256]{2,1,0:T(8,128)(2,1)S(1)}, bf16[32,16,256]{2,1,0:T(8,128)(2,1)S(1)}, u32[]{:S(2)}, u32[]{:S(2)}) collective-permute-start(bf16[32,16,256]{2,1,0:T(8,128)(2,1)S(1)} %get-tuple-element.76), channel_id=1, source_target_pairs={{0,64},{64,128},{128,192},{192,0},{1,65},{65,129},{129,193},{193,1... | collective-permute-start | bytes 786440 | tf_op jit(solution)/shard_map/ppermute | solution.py:32
  4.2 7.7 %collective-permute-start.1 = (bf16[32,16,256]{2,1,0:T(8,128)(2,1)S(1)}, bf16[32,16,256]{2,1,0:T(8,128)(2,1)S(1)}, u32[]{:S(2)}, u32[]{:S(2)}) collective-permute-start(bf16[32,16,256]{2,1,0:T(8,128)(2,1)S(1)} %get-tuple-element.77), channel_id=1, source_target_pairs={{0,192},{64,0},{128,64},{192,128},{1,193},{65,1},{129,65},{193,129... | collective-permute-start | bytes 786440 | tf_op jit(solution)/shard_map/ppermute | solution.py:32
  8.3 10.1 %collective-permute-start.2 = (bf16[32,16,256]{2,1,0:T(8,128)(2,1)}, bf16[32,16,256]{2,1,0:T(8,128)(2,1)}, u32[]{:S(2)}, u32[]{:S(2)}) collective-permute-start(bf16[32,16,256]{2,1,0:T(8,128)(2,1)} %get-tuple-element.86), channel_id=1, source_target_pairs={{0,64},{64,128},{128,192},{192,0},{1,65},{65,129},{129,193},{193,1... | collective-permute-start | bytes 786440 | tf_op jit(solution)/shard_map/ppermute | solution.py:32
  8.3 10.1 %collective-permute-start.3 = (bf16[32,16,256]{2,1,0:T(8,128)(2,1)}, bf16[32,16,256]{2,1,0:T(8,128)(2,1)}, u32[]{:S(2)}, u32[]{:S(2)}) collective-permute-start(bf16[32,16,256]{2,1,0:T(8,128)(2,1)} %get-tuple-element.87), channel_id=1, source_target_pairs={{0,192},{64,0},{128,64},{192,128},{1,193},{65,1},{129,65},{193,129... | collective-permute-start | bytes 786440 | tf_op jit(solution)/shard_map/ppermute | solution.py:32
  11.8 13.2 %copy-start.6 = (s32[64]{0:T(128)}, s32[64]{0:T(128)S(1)}, u32[]{:S(2)}) copy-start(s32[64]{0:T(128)S(1)} %gather_fusion) | copy-start | bytes 772
  11.8 13.2 %copy-start.4 = (s32[64]{0:T(128)}, s32[64]{0:T(128)S(1)}, u32[]{:S(2)}) copy-start(s32[64]{0:T(128)S(1)} %fusion.9.flags) | copy-start | bytes 772
  12.7 9.2 %collective-permute-start.4 = (bf16[32,16,256]{2,1,0:T(8,128)(2,1)}, bf16[32,16,256]{2,1,0:T(8,128)(2,1)}, u32[]{:S(2)}, u32[]{:S(2)}) collective-permute-start(bf16[32,16,256]{2,1,0:T(8,128)(2,1)} %get-tuple-element.97), channel_id=1, source_target_pairs={{0,64},{64,128},{128,192},{192,0},{1,65},{65,129},{129,193},{193,1... | collective-permute-start | bytes 786440 | tf_op jit(solution)/shard_map/ppermute | solution.py:32
  13.3 8.7 %collective-permute-start.5 = (bf16[32,16,256]{2,1,0:T(8,128)(2,1)}, bf16[32,16,256]{2,1,0:T(8,128)(2,1)}, u32[]{:S(2)}, u32[]{:S(2)}) collective-permute-start(bf16[32,16,256]{2,1,0:T(8,128)(2,1)} %get-tuple-element.98), channel_id=1, source_target_pairs={{0,192},{64,0},{128,64},{192,128},{1,193},{65,1},{129,65},{193,129... | collective-permute-start | bytes 786440 | tf_op jit(solution)/shard_map/ppermute | solution.py:32
  21.9 21.5 %collective-permute-start.6 = (bf16[11,128,256]{2,1,0:T(8,128)(2,1)S(1)}, bf16[11,128,256]{2,1,0:T(8,128)(2,1)S(1)}, u32[]{:S(2)}, u32[]{:S(2)}) collective-permute-start(bf16[11,128,256]{2,1,0:T(8,128)(2,1)S(1)} %copy-done.11), channel_id=1, source_target_pairs={{0,64},{64,128},{128,192},{192,0},{1,65},{65,129},{129,193},{193,1... | collective-permute-start | bytes 2162696 | tf_op jit(solution)/shard_map/ppermute | solution.py:32
  23.5 19.9 %collective-permute-start.7 = (bf16[11,128,256]{2,1,0:T(8,128)(2,1)S(1)}, bf16[11,128,256]{2,1,0:T(8,128)(2,1)S(1)}, u32[]{:S(2)}, u32[]{:S(2)}) collective-permute-start(bf16[11,128,256]{2,1,0:T(8,128)(2,1)S(1)} %copy-done.16), channel_id=1, source_target_pairs={{0,192},{64,0},{128,64},{192,128},{1,193},{65,1},{129,65},{193,129... | collective-permute-start | bytes 2162696 | tf_op jit(solution)/shard_map/ppermute | solution.py:32
  28.6 31.0 %all-to-all-start = ((bf16[64,16,256]{2,1,0:T(8,128)(2,1)}), bf16[64,16,256]{2,1,0:T(8,128)(2,1)}, u32[]{:S(2)}, u32[]{:S(2)}) async-start(bf16[64,16,256]{2,1,0:T(8,128)(2,1)} %get-tuple-element.109), calls=%async_computation | async-start | bytes 1048576 | tf_op jit(solution)/shard_map/all_to_all | solution.py:404
  44.6 15.1 %collective-permute-start.8 = (bf16[5,128,256]{2,1,0:T(8,128)(2,1)S(1)}, bf16[5,128,256]{2,1,0:T(8,128)(2,1)S(1)}, u32[]{:S(2)}, u32[]{:S(2)}) collective-permute-start(bf16[5,128,256]{2,1,0:T(8,128)(2,1)S(1)} %get-tuple-element.113), channel_id=1, source_target_pairs={{0,64},{64,128},{128,192},{192,0},{1,65},{65,129},{129,193},{193,1... | collective-permute-start | bytes 983048 | tf_op jit(solution)/shard_map/ppermute | solution.py:32
  44.7 15.0 %collective-permute-start.9 = (bf16[5,128,256]{2,1,0:T(8,128)(2,1)S(1)}, bf16[5,128,256]{2,1,0:T(8,128)(2,1)S(1)}, u32[]{:S(2)}, u32[]{:S(2)}) collective-permute-start(bf16[5,128,256]{2,1,0:T(8,128)(2,1)S(1)} %get-tuple-element.114), channel_id=1, source_target_pairs={{0,192},{64,0},{128,64},{192,128},{1,193},{65,1},{129,65},{193,129... | collective-permute-start | bytes 983048 | tf_op jit(solution)/shard_map/ppermute | solution.py:32
  47.8 7.0 %collective-permute-start.10 = (f32[64]{0:T(128)S(1)}, f32[64]{0:T(128)S(1)}, u32[]{:S(2)}, u32[]{:S(2)}) collective-permute-start(f32[64]{0:T(128)S(1)} %reduce_sum.9), channel_id=1, source_target_pairs={{0,64},{64,128},{128,192},{192,0},{1,65},{65,129},{129,193},{193,1... | collective-permute-start | bytes 776 | tf_op jit(solution)/shard_map/ppermute | solution.py:32
  47.9 7.0 %collective-permute-start.11 = (f32[64]{0:T(128)S(1)}, f32[64]{0:T(128)S(1)}, u32[]{:S(2)}, u32[]{:S(2)}) collective-permute-start(f32[64]{0:T(128)S(1)} %reduce_sum.9), channel_id=1, source_target_pairs={{0,128},{64,192},{128,0},{192,64},{1,129},{65,193},{129,1},{193,65... | collective-permute-start | bytes 776 | tf_op jit(solution)/shard_map/ppermute | solution.py:32
  49.4 5.5 %collective-permute-start.12 = (f32[64]{0:T(128)S(1)}, f32[64]{0:T(128)S(1)}, u32[]{:S(2)}, u32[]{:S(2)}) collective-permute-start(f32[64]{0:T(128)S(1)} %reduce_sum.9), channel_id=1, source_target_pairs={{0,192},{64,0},{128,64},{192,128},{1,193},{65,1},{129,65},{193,129... | collective-permute-start | bytes 776 | tf_op jit(solution)/shard_map/ppermute | solution.py:32
  59.6 22.6 %copy-start.12 = (bf16[5,128,256]{2,1,0:T(8,128)(2,1)}, bf16[5,128,256]{2,1,0:T(8,128)(2,1)S(1)}, u32[]{:S(2)}) copy-start(bf16[5,128,256]{2,1,0:T(8,128)(2,1)S(1)} %collective-permute-done.8.refs_12_) | copy-start | bytes 983044
  59.6 22.6 %copy-start.13 = (bf16[5,128,256]{2,1,0:T(8,128)(2,1)}, bf16[5,128,256]{2,1,0:T(8,128)(2,1)S(1)}, u32[]{:S(2)}) copy-start(bf16[5,128,256]{2,1,0:T(8,128)(2,1)S(1)} %collective-permute-done.9.refs_13_) | copy-start | bytes 983044
  61.0 7.9 %collective-permute-start.14 = (bf16[32,16,256]{2,1,0:T(8,128)(2,1)S(1)}, bf16[32,16,256]{2,1,0:T(8,128)(2,1)S(1)}, u32[]{:S(2)}, u32[]{:S(2)}) collective-permute-start(bf16[32,16,256]{2,1,0:T(8,128)(2,1)S(1)} %get-tuple-element.134), channel_id=1, source_target_pairs={{0,64},{64,128},{128,192},{192,0},{1,65},{65,129},{129,193},{193,1... | collective-permute-start | bytes 786440 | tf_op jit(solution)/shard_map/ppermute | solution.py:32
  61.1 7.7 %collective-permute-start.15 = (bf16[32,16,256]{2,1,0:T(8,128)(2,1)S(1)}, bf16[32,16,256]{2,1,0:T(8,128)(2,1)S(1)}, u32[]{:S(2)}, u32[]{:S(2)}) collective-permute-start(bf16[32,16,256]{2,1,0:T(8,128)(2,1)S(1)} %get-tuple-element.135), channel_id=1, source_target_pairs={{0,192},{64,0},{128,64},{192,128},{1,193},{65,1},{129,65},{193,129... | collective-permute-start | bytes 786440 | tf_op jit(solution)/shard_map/ppermute | solution.py:32
  63.7 18.5 %collective-permute-start.18 = (bf16[32,16,256]{2,1,0:T(8,128)(2,1)S(1)}, bf16[32,16,256]{2,1,0:T(8,128)(2,1)S(1)}, u32[]{:S(2)}, u32[]{:S(2)}) collective-permute-start(bf16[32,16,256]{2,1,0:T(8,128)(2,1)S(1)} %get-tuple-element.135), channel_id=1, source_target_pairs={{0,64},{64,128},{128,192},{192,0},{1,65},{65,129},{129,193},{193,1... | collective-permute-start | bytes 786440 | tf_op jit(solution)/shard_map/ppermute | solution.py:32
  63.7 18.5 %collective-permute-start.13 = (bf16[32,16,256]{2,1,0:T(8,128)(2,1)S(1)}, bf16[32,16,256]{2,1,0:T(8,128)(2,1)S(1)}, u32[]{:S(2)}, u32[]{:S(2)}) collective-permute-start(bf16[32,16,256]{2,1,0:T(8,128)(2,1)S(1)} %get-tuple-element.134), channel_id=1, source_target_pairs={{0,192},{64,0},{128,64},{192,128},{1,193},{65,1},{129,65},{193,129... | collective-permute-start | bytes 786440 | tf_op jit(solution)/shard_map/ppermute | solution.py:32
  68.8 13.4 %collective-permute-start.16 = (bf16[32,16,256]{2,1,0:T(8,128)(2,1)S(1)}, bf16[32,16,256]{2,1,0:T(8,128)(2,1)S(1)}, u32[]{:S(2)}, u32[]{:S(2)}) collective-permute-start(bf16[32,16,256]{2,1,0:T(8,128)(2,1)S(1)} %collective-permute-done.14), channel_id=1, source_target_pairs={{0,64},{64,128},{128,192},{192,0},{1,65},{65,129},{129,193},{193,1... | collective-permute-start | bytes 786440 | tf_op jit(solution)/shard_map/ppermute | solution.py:32
  68.8 13.4 %collective-permute-start.17 = (bf16[32,16,256]{2,1,0:T(8,128)(2,1)S(1)}, bf16[32,16,256]{2,1,0:T(8,128)(2,1)S(1)}, u32[]{:S(2)}, u32[]{:S(2)}) collective-permute-start(bf16[32,16,256]{2,1,0:T(8,128)(2,1)S(1)} %collective-permute-done.15), channel_id=1, source_target_pairs={{0,192},{64,0},{128,64},{192,128},{1,193},{65,1},{129,65},{193,129... | collective-permute-start | bytes 786440 | tf_op jit(solution)/shard_map/ppermute | solution.py:32
  72.3 17.0 %all-to-all-start.1 = ((f32[64,1,128]{2,1,0:T(1,128)}), f32[64,1,128]{2,1,0:T(1,128)S(1)}, u32[]{:S(2)}, u32[]{:S(2)}) async-start(f32[64,1,128]{2,1,0:T(1,128)} %broadcast_in_dim.16), calls=%async_computation.1 | async-start | bytes 65536 | tf_op jit(solution)/shard_map/all_to_all | solution.py:404
  85.9 3.7 %collective-permute-start.19 = (f32[8,128]{1,0:T(8,128)S(1)}, f32[8,128]{1,0:T(8,128)S(1)}, u32[]{:S(2)}, u32[]{:S(2)}) collective-permute-start(f32[8,128]{1,0:T(8,128)S(1)} %get-tuple-element.130.first), channel_id=1, source_target_pairs={{0,64},{64,128},{128,192},{192,0},{1,65},{65,129},{129,193},{193,1... | collective-permute-start | bytes 12296 | tf_op jit(solution)/shard_map/ppermute | solution.py:32
  86.0 4.0 %collective-permute-start.20 = (f32[8,128]{1,0:T(8,128)S(1)}, f32[8,128]{1,0:T(8,128)S(1)}, u32[]{:S(2)}, u32[]{:S(2)}) collective-permute-start(f32[8,128]{1,0:T(8,128)S(1)} %get-tuple-element.130.first), channel_id=1, source_target_pairs={{0,128},{64,192},{128,0},{192,64},{1,129},{65,193},{129,1},{193,65... | collective-permute-start | bytes 12296 | tf_op jit(solution)/shard_map/ppermute | solution.py:32
  88.9 2.7 %collective-permute-start.21 = (f32[8,128]{1,0:T(8,128)S(1)}, f32[8,128]{1,0:T(8,128)S(1)}, u32[]{:S(2)}, u32[]{:S(2)}) collective-permute-start(f32[8,128]{1,0:T(8,128)S(1)} %get-tuple-element.130.first), channel_id=1, source_target_pairs={{0,192},{64,0},{128,64},{192,128},{1,193},{65,1},{129,65},{193,129... | collective-permute-start | bytes 12296 | tf_op jit(solution)/shard_map/ppermute | solution.py:32
  93.7 27.8 %all-to-all-start.2 = ((bf16[64,16,256]{2,1,0:T(8,128)(2,1)}), bf16[64,16,256]{2,1,0:T(8,128)(2,1)S(1)}, u32[]{:S(2)}, u32[]{:S(2)}) async-start(bf16[64,16,256]{2,1,0:T(8,128)(2,1)} %shard_map.144), calls=%async_computation.2 | async-start | bytes 1048576 | tf_op jit(solution)/shard_map/all_to_all | solution.py:404
  108.3 13.1 %copy-start.5 = (s32[64]{0:T(128)S(1)}, s32[64]{0:T(128)}, u32[]{:S(2)}) copy-start(s32[64]{0:T(128)} %copy-done.4) | copy-start | bytes 772
  108.3 13.1 %copy-start.7 = (s32[64]{0:T(128)S(1)}, s32[64]{0:T(128)}, u32[]{:S(2)}) copy-start(s32[64]{0:T(128)} %copy-done.6) | copy-start | bytes 772
  (11 other events, 46.9 us)

commit v10 on v8

--- a/solution.py
+++ b/solution.py
@@ -174,7 +174,7 @@
 def pack(key, flags, partial, up_sum, down_sum, first, second):
     _, half, rows, cols = partial.shape
     blocks, lanes = 2 * half, cols // 2
-    steps = 2 if half >= 16 else 1
+    steps = 4 if half >= 16 else 1
     moment = pl.BlockSpec((2, half // steps, rows, cols), lambda i, *_: (0, i, 0, 0))
     halves = pltpu.HBM((2, half, rows, cols), F32)
     piece = (blocks, 2 * rows + rows // 2, lanes)
@@ -215,13 +215,13 @@
     half, rows, cols = low.shape
     total = jnp.zeros(adam.shape, F32)
     for i, place in enumerate(order):
-        piece = owned[i].astype(F32)
-        value = jnp.concatenate([piece[:rows], piece[rows : 2 * rows]], axis=1).astype(BF16)
+        piece = owned[i]
+        value = jnp.concatenate([piece[:rows], piece[rows : 2 * rows]], axis=1)
         if place < half:
             low[place] = value
         else:
             high[place - half] = value
-        total += piece[2 * rows :]
+        total += piece.astype(F32)[2 * rows :]
     adam[...] = total
 
 
@@ -341,8 +341,8 @@
     )(*operands, *map(in_hbm, sources))
 
 
-def graft_kernel(cells, order, precond, mine, other, out):
-    sums = mine[...] + other[...]
+def graft_kernel(cells, order, precond, first, second, third, fourth, out):
+    sums = first[...] + second[...] + third[...] + fourth[...]
     pre, adam = sums[0:1, :], sums[1:2, :]
     adam = adam * (BIAS_SECOND / (BIAS_FIRST * BIAS_FIRST))
     scale = -jnp.sqrt(adam / cells) / jnp.sqrt(pre / cells + NORM_EPS)
@@ -352,7 +352,7 @@
         out[i] = (scale * precond[pl.ds(place * rows, rows), :]).astype(BF16)
 
 
-def graft(order, precond, mine, other):
+def graft(order, precond, norms):
     width, quarter = precond.shape
     shape = (len(order), width // len(order), quarter)
     small = pl.BlockSpec((8, 128), lambda i: (0, 0))
@@ -360,10 +360,10 @@
         functools.partial(graft_kernel, float(width * width), order),
         out_shape=pltpu.HBM(shape, BF16),
         grid=(1,),
-        in_specs=[pl.BlockSpec((width, quarter), lambda i: (0, 0))] + [small] * 2,
+        in_specs=[pl.BlockSpec((width, quarter), lambda i: (0, 0))] + [small] * 4,
         out_specs=pl.BlockSpec(shape, lambda i: (0, 0, 0)),
         compiler_params=pltpu.CompilerParams(vmem_limit_bytes=8 * MIB),
-    )(precond, mine, other)
+    )(precond, *norms)
 
 
 def on_device(
@@ -450,9 +450,8 @@
     pieces = [low, high, next_low, next_high, far_low, far_high, prev_low, prev_high]
     flat = [piece.reshape(-1, quarter) for piece in pieces]
     precond, norms = precondition(flat, adam, roots)
-    norms += lax.ppermute(norms, "grp", [(i, i ^ 1) for i in range(n_grp)])
-    others = lax.ppermute(norms, "grp", [(i, i ^ 2) for i in range(n_grp)])
-    grafted = graft(order, precond, norms, others)
+    norms = [norms] + [shift(norms, step) for step in (1, 2, 3)]
+    grafted = graft(order, precond, norms)
     pieces, grafted = lax.optimization_barrier((pieces, grafted))
     back = exchange(grafted)
 

time: 122 us -> 122 us (level)
    ppermute x16 -> x19, waiting for transfers between devices: 22.2 us -> 25.9 us  [shift(): return lax.ppermute(array, 'grp', [(i, (i + step) % n) for i in range(n)])]
    ppermute x2 -> x0, waiting for transfers between devices: 3.52 us -> none  [the longest x1 1.91 us: on_device(): norms += lax.ppermute(norms, 'grp', [(i, i ^ 1) for i in range(n_grp)])]
    ppermute x16 -> x19, starting transfers between devices: 22.2 us -> 25.6 us  [shift(): return lax.ppermute(array, 'grp', [(i, (i + step) % n) for i in range(n)])]
    ppermute x2 -> x0, starting transfers between devices: 2.98 us -> none  [the longest x1 2.35 us: on_device(): others = lax.ppermute(norms, 'grp', [(i, i ^ 2) for i in range(n_grp)])]
  transfers between devices with their start and end apart: 20 -> 21, of which waited for: 10 -> 10; matrix products, arithmetic and copies ran while one was open for 7% -> 7% of each run, Pallas kernels for 6% -> 7%
where the time goes in v10:
time: 122 us; the launch traced here: 121 us
  starting transfers between devices  50.3 us (41%)
  waiting for transfers between devices  44.7 us (37%)
  Pallas kernels  14.3 us (12%)
  local copies, waits for them, and re-layouts  6.8 us (6%)
  matrix products  2.48 us (2%)
  other arithmetic  1.93 us (2%)
    ppermute x19, waiting for transfers between devices, shift(): return lax.ppermute(array, 'grp', [(i, (i + step) % n) for i in range(n)])  25.9 us
    ppermute x19, starting transfers between devices, shift(): return lax.ppermute(array, 'grp', [(i, (i + step) % n) for i in range(n)])  25.6 us
    all_to_all x2, starting transfers between devices, exchange(): lax.all_to_all(array, 'own', 0, 0, axis_index_groups=groups, tiled=True)  24.6 us
    all_to_all x2, waiting for transfers between devices, exchange(): lax.all_to_all(array, 'own', 0, 0, axis_index_groups=groups, tiled=True)  18.7 us
    pallas_call x1, Pallas kernels, pack(): pl.pallas_call(pack_kernel, out_shape=(pltpu.HBM(piece, BF16), halves, ha...  3.95 us
    pallas_call x1, Pallas kernels, root_pieces(): pl.pallas_call(roots_kernel, out_shape=(pltpu.HBM((11, *unit), BF16), plt...  2.82 us
    pallas_call x1, Pallas kernels, precondition(): pl.pallas_call(precond_kernel, out_shape=(jax.ShapeDtypeStruct((2 * rows,...  2.77 us
    dot_general x2, matrix products, dot(): return lax.dot_general(a, b, (dims, ((), ())), preferred_element_type=F32)  2.48 us
  transfers between devices with their start and end apart: 21, of which 10 were waited for; matrix products, arithmetic and copies ran while one was open for 7% of the time, Pallas kernels for 7%

profile of v10, /device:TPU:1, one launch (start us, length us, event | category | flops | bytes accessed | tf_op | source)
XLA Modules:
  0.0 121.3 jit_solution(3482730680850262753)
XLA Ops:
  0.7 1.4 %dynamic-slice_bitcast_fusion = (bf16[32,16,256]{2,1,0:T(8,128)(2,1)S(1)}, bf16[32,16,256]{2,1,0:T(8,128)(2,1)S(1)}) fusion(bf16[1,64,16,1024]{3,2,1,0:T(8,128)(2,1)} %param.10, s32[]{:T(128)S(6)} %add.37, s32[]{:T(128)S(6)} %mul.29), kind=kLoop, calls=%fused_computation.12 | loop fusion | bytes 1048584 | tf_op jit(solution)/shard_map/slice | solution.py:404
  2.0 2.1 %collective-permute-start.2 = (bf16[32,16,256]{2,1,0:T(8,128)(2,1)S(1)}, bf16[32,16,256]{2,1,0:T(8,128)(2,1)S(1)}, u32[]{:S(2)}, u32[]{:S(2)}) collective-permute-start(bf16[32,16,256]{2,1,0:T(8,128)(2,1)S(1)} %get-tuple-element.71), channel_id=1, source_target_pairs={{0,64},{64,128},{128,192},{192,0},{1,65},{65,129},{129,193},{193,1... | collective-permute-start | bytes 786440 | tf_op jit(solution)/shard_map/ppermute | solution.py:32
  4.2 1.6 %collective-permute-start.3 = (bf16[32,16,256]{2,1,0:T(8,128)(2,1)S(1)}, bf16[32,16,256]{2,1,0:T(8,128)(2,1)S(1)}, u32[]{:S(2)}, u32[]{:S(2)}) collective-permute-start(bf16[32,16,256]{2,1,0:T(8,128)(2,1)S(1)} %get-tuple-element.72), channel_id=1, source_target_pairs={{0,192},{64,0},{128,64},{192,128},{1,193},{65,1},{129,65},{193,129... | collective-permute-start | bytes 786440 | tf_op jit(solution)/shard_map/ppermute | solution.py:32
  5.8 1.7 %constant_dynamic-slice_fusion.3 = (bf16[32,16,256]{2,1,0:T(8,128)(2,1)S(1)}, bf16[32,16,256]{2,1,0:T(8,128)(2,1)S(1)}, bf16[32,16,256]{2,1,0:T(8,128)(2,1)S(1)}, bf16[32,16,256]{2,1,0:T(8,128)(2,1)S(1)}) fusion(bf16[64,16,1024]{2,1,0:T(8,128)(2,1)} %bitcast.42, s32[]{:T(128)S(6)} %add.37, s32[]{:T(128)S(6)} %mul.30, s32[]{:T(128)S(6)} %mul.28), kind=kLoop, calls=%fused_computation.20 | loop fusion | bytes 2097164 | tf_op jit(solution)/shard_map/slice | solution.py:410
  7.6 2.7 %collective-permute-start.1 = (bf16[32,16,256]{2,1,0:T(8,128)(2,1)S(1)}, bf16[32,16,256]{2,1,0:T(8,128)(2,1)S(1)}, u32[]{:S(2)}, u32[]{:S(2)}) collective-permute-start(bf16[32,16,256]{2,1,0:T(8,128)(2,1)S(1)} %get-tuple-element.77), channel_id=1, source_target_pairs={{0,192},{64,0},{128,64},{192,128},{1,193},{65,1},{129,65},{193,129... | collective-permute-start | bytes 786440 | tf_op jit(solution)/shard_map/ppermute | solution.py:32
  12.0 1.2 %collective-permute-start.4 = (bf16[32,16,256]{2,1,0:T(8,128)(2,1)}, bf16[32,16,256]{2,1,0:T(8,128)(2,1)}, u32[]{:S(2)}, u32[]{:S(2)}) collective-permute-start(bf16[32,16,256]{2,1,0:T(8,128)(2,1)} %get-tuple-element.91), channel_id=1, source_target_pairs={{0,64},{64,128},{128,192},{192,0},{1,65},{65,129},{129,193},{193,1... | collective-permute-start | bytes 786440 | tf_op jit(solution)/shard_map/ppermute | solution.py:32
  13.2 1.4 %collective-permute-start.5 = (bf16[32,16,256]{2,1,0:T(8,128)(2,1)}, bf16[32,16,256]{2,1,0:T(8,128)(2,1)}, u32[]{:S(2)}, u32[]{:S(2)}) collective-permute-start(bf16[32,16,256]{2,1,0:T(8,128)(2,1)} %get-tuple-element.92), channel_id=1, source_target_pairs={{0,192},{64,0},{128,64},{192,128},{1,193},{65,1},{129,65},{193,129... | collective-permute-start | bytes 786440 | tf_op jit(solution)/shard_map/ppermute | solution.py:32
  14.7 2.8 %shard_map.138 = (bf16[11,128,256]{2,1,0:T(8,128)(2,1)}, bf16[11,128,256]{2,1,0:T(8,128)(2,1)}, bf16[2,128,256]{2,1,0:T(8,128)(2,1)}) custom-call(f32[1,256,1024]{2,1,0:T(8,128)} %left, f32[1,256,1024]{2,1,0:T(8,128)} %right), custom_call_target="tpu_custom_call" | custom-call | tf_op jit(solution)/shard_map/pallas_call | solution.py:101
  17.5 1.4 %constant_dynamic-slice_fusion.2.own = bf16[64,16,256]{2,1,0:T(8,128)(2,1)S(1)} fusion(bf16[64,16,1024]{2,1,0:T(8,128)(2,1)} %bitcast.43, s32[]{:T(128)S(6)} %mul.27), kind=kLoop, calls=%fused_computation.19 | loop fusion | bytes 1048580 | tf_op jit(solution)/shard_map/dynamic_slice | solution.py:48
  19.3 2.6 %collective-permute-done.4.up_sum = bf16[32,16,256]{2,1,0:T(8,128)(2,1)} collective-permute-done((bf16[32,16,256]{2,1,0:T(8,128)(2,1)}, bf16[32,16,256]{2,1,0:T(8,128)(2,1)}, u32[]{:S(2)}, u32[]{:S(2)}) %collective-permute-start.4) | collective-permute-done | bytes 262176 | tf_op jit(solution)/shard_map/ppermute | solution.py:32
  21.8 2.7 %collective-permute-start.7 = (bf16[11,128,256]{2,1,0:T(8,128)(2,1)S(1)}, bf16[11,128,256]{2,1,0:T(8,128)(2,1)S(1)}, u32[]{:S(2)}, u32[]{:S(2)}) collective-permute-start(bf16[11,128,256]{2,1,0:T(8,128)(2,1)S(1)} %copy-done.15), channel_id=1, source_target_pairs={{0,192},{64,0},{128,64},{192,128},{1,193},{65,1},{129,65},{193,129... | collective-permute-start | bytes 2162696 | tf_op jit(solution)/shard_map/ppermute | solution.py:32
  24.6 4.0 %shard_map.140 = (bf16[64,40,128]{2,1,0:T(8,128)(2,1)}, f32[2,32,16,256]{3,2,1,0:T(8,128)}, f32[2,32,16,256]{3,2,1,0:T(8,128)}) custom-call(s32[64]{0:T(128)S(1)} %gather_fusion, s32[64]{0:T(128)S(1)} %fusion.9.flags, f32[2,32,16,256]{3,2,1,0:T(8,128)S(1)} %get-tuple-element.98.partial, bf16[32,16,256]{2,1,0:T(8,128)(2,1)} %collective-permute-done.4.up_sum, ...), custom_call_target="tpu_custom_call" | custom-call | tf_op jit(solution)/shard_map/pallas_call | solution.py:181
  28.5 15.0 %all-to-all-start = ((bf16[64,40,128]{2,1,0:T(8,128)(2,1)}), bf16[64,40,128]{2,1,0:T(8,128)(2,1)}, u32[]{:S(2)}, u32[]{:S(2)}) async-start(bf16[64,40,128]{2,1,0:T(8,128)(2,1)} %get-tuple-element.103), calls=%async_computation | async-start | bytes 1310720 | tf_op jit(solution)/shard_map/all_to_all | solution.py:401
  45.0 2.7 %collective-permute-start.9 = (bf16[5,128,256]{2,1,0:T(8,128)(2,1)S(1)}, bf16[5,128,256]{2,1,0:T(8,128)(2,1)S(1)}, u32[]{:S(2)}, u32[]{:S(2)}) collective-permute-start(bf16[5,128,256]{2,1,0:T(8,128)(2,1)S(1)} %get-tuple-element.108), channel_id=1, source_target_pairs={{0,192},{64,0},{128,64},{192,128},{1,193},{65,1},{129,65},{193,129... | collective-permute-start | bytes 983048 | tf_op jit(solution)/shard_map/ppermute | solution.py:32
  47.6 7.7 %collective-permute-done.8.refs_13_ = bf16[5,128,256]{2,1,0:T(8,128)(2,1)S(1)} collective-permute-done((bf16[5,128,256]{2,1,0:T(8,128)(2,1)S(1)}, bf16[5,128,256]{2,1,0:T(8,128)(2,1)S(1)}, u32[]{:S(2)}, u32[]{:S(2)}) %collective-permute-start.8) | collective-permute-done | bytes 327712 | tf_op jit(solution)/shard_map/ppermute | solution.py:32
  55.3 7.3 %all-to-all-done.owned = bf16[64,40,128]{2,1,0:T(8,128)(2,1)} async-done(((bf16[64,40,128]{2,1,0:T(8,128)(2,1)}), bf16[64,40,128]{2,1,0:T(8,128)(2,1)}, u32[]{:S(2)}, u32[]{:S(2)}) %all-to-all-start) | async-done | bytes 655392 | tf_op jit(solution)/shard_map/all_to_all | solution.py:401
  62.7 1.2 shard_map.142
  64.2 2.9 %collective-permute-start.11 = (bf16[32,16,256]{2,1,0:T(8,128)(2,1)S(1)}, bf16[32,16,256]{2,1,0:T(8,128)(2,1)S(1)}, u32[]{:S(2)}, u32[]{:S(2)}) collective-permute-start(bf16[32,16,256]{2,1,0:T(8,128)(2,1)S(1)} %get-tuple-element.125), channel_id=1, source_target_pairs={{0,192},{64,0},{128,64},{192,128},{1,193},{65,1},{129,65},{193,129... | collective-permute-start | bytes 786440 | tf_op jit(solution)/shard_map/ppermute | solution.py:32
  67.1 1.2 collective-permute-start.10
  68.6 3.8 %collective-permute-done.12 = bf16[32,16,256]{2,1,0:T(8,128)(2,1)S(1)} collective-permute-done((bf16[32,16,256]{2,1,0:T(8,128)(2,1)S(1)}, bf16[32,16,256]{2,1,0:T(8,128)(2,1)S(1)}, u32[]{:S(2)}, u32[]{:S(2)}) %collective-permute-start.12) | collective-permute-done | bytes 262176 | tf_op jit(solution)/shard_map/ppermute | solution.py:32
  72.4 2.7 %collective-permute-start.14 = (bf16[32,16,256]{2,1,0:T(8,128)(2,1)S(1)}, bf16[32,16,256]{2,1,0:T(8,128)(2,1)S(1)}, u32[]{:S(2)}, u32[]{:S(2)}) collective-permute-start(bf16[32,16,256]{2,1,0:T(8,128)(2,1)S(1)} %collective-permute-done.11), channel_id=1, source_target_pairs={{0,192},{64,0},{128,64},{192,128},{1,193},{65,1},{129,65},{193,129... | collective-permute-start | bytes 786440 | tf_op jit(solution)/shard_map/ppermute | solution.py:32
  75.1 2.2 %collective-permute-done.10 = bf16[32,16,256]{2,1,0:T(8,128)(2,1)S(1)} collective-permute-done((bf16[32,16,256]{2,1,0:T(8,128)(2,1)S(1)}, bf16[32,16,256]{2,1,0:T(8,128)(2,1)S(1)}, u32[]{:S(2)}, u32[]{:S(2)}) %collective-permute-start.10) | collective-permute-done | bytes 262176 | tf_op jit(solution)/shard_map/ppermute | solution.py:32
  78.0 5.6 %collective-permute-done.13 = bf16[32,16,256]{2,1,0:T(8,128)(2,1)S(1)} collective-permute-done((bf16[32,16,256]{2,1,0:T(8,128)(2,1)S(1)}, bf16[32,16,256]{2,1,0:T(8,128)(2,1)S(1)}, u32[]{:S(2)}, u32[]{:S(2)}) %collective-permute-start.13) | collective-permute-done | bytes 262176 | tf_op jit(solution)/shard_map/ppermute | solution.py:32
  83.6 2.8 %shard_map.143 = (f32[1024,256]{1,0:T(8,128)S(1)}, f32[8,128]{1,0:T(8,128)S(1)}) custom-call(bf16[512,256]{1,0:T(8,128)(2,1)S(1)} %bitcast.30, bf16[512,256]{1,0:T(8,128)(2,1)S(1)} %bitcast.31, bf16[512,256]{1,0:T(8,128)(2,1)S(1)} %bitcast.34, bf16[512,256]{1,0:T(8,128)(2,1)S(1)} %bitcast.33, bf16[512,256]{1,0:T(8,128)(2,1)S(1)} %bitcast.36, ...), custom_call_target="tpu_custom_call" | custom-call | tf_op jit(solution)/shard_map/pallas_call | solution.py:326
  86.4 2.7 %collective-permute-start.18 = (f32[8,128]{1,0:T(8,128)S(1)}, f32[8,128]{1,0:T(8,128)S(1)}, u32[]{:S(2)}, u32[]{:S(2)}) collective-permute-start(f32[8,128]{1,0:T(8,128)S(1)} %get-tuple-element.120.first), channel_id=1, source_target_pairs={{0,192},{64,0},{128,64},{192,128},{1,193},{65,1},{129,65},{193,129... | collective-permute-start | bytes 12296 | tf_op jit(solution)/shard_map/ppermute | solution.py:32
  89.9 3.2 %collective-permute-done.17.third = f32[8,128]{1,0:T(8,128)S(1)} collective-permute-done((f32[8,128]{1,0:T(8,128)S(1)}, f32[8,128]{1,0:T(8,128)S(1)}, u32[]{:S(2)}, u32[]{:S(2)}) %collective-permute-start.17) | collective-permute-done | bytes 4128 | tf_op jit(solution)/shard_map/ppermute | solution.py:32
  93.1 0.9 shard_map.144
  94.0 9.6 %all-to-all-start.1 = ((bf16[64,16,256]{2,1,0:T(8,128)(2,1)}), bf16[64,16,256]{2,1,0:T(8,128)(2,1)S(1)}, u32[]{:S(2)}, u32[]{:S(2)}) async-start(bf16[64,16,256]{2,1,0:T(8,128)(2,1)} %shard_map.144), calls=%async_computation.1 | async-start | bytes 1048576 | tf_op jit(solution)/shard_map/all_to_all | solution.py:401
  105.1 1.6 %fusion.3 = f32[1,256,1024]{2,1,0:T(8,128)} fusion(s32[]{:T(128)S(6)} %mul.31, f32[256,1024]{1,0:T(8,128)S(1)} %fusion.4, f32[1,256,1024]{2,1,0:T(8,128)S(1)} %copy-done.10), kind=kLoop, calls=%fused_computation.8 | loop fusion | flops 786432 | bytes 3145732 | tf_op jit(solution)/shard_map/add | solution.py:466
  106.7 1.7 %fusion = f32[1,256,1024]{2,1,0:T(8,128)} fusion(bf16[1024,1024]{1,0:T(8,128)(2,1)S(1)} %bitcast.41, f32[1,256,1024]{2,1,0:T(8,128)S(1)} %copy-done.9, s32[]{:T(128)S(6)} %mul.27), kind=kOutput, calls=%fused_computation.5 | convolution fusion | flops 537395200 | bytes 4718596 | tf_op jit(solution)/shard_map/dot_general | solution.py:52
  108.5 11.4 %all-to-all-done.1.back = bf16[64,16,256]{2,1,0:T(8,128)(2,1)S(1)} async-done(((bf16[64,16,256]{2,1,0:T(8,128)(2,1)}), bf16[64,16,256]{2,1,0:T(8,128)(2,1)S(1)}, u32[]{:S(2)}, u32[]{:S(2)}) %all-to-all-start.1) | async-done | bytes 524320 | tf_op jit(solution)/shard_map/all_to_all | solution.py:401
  119.9 1.5 %shard_map.145 = bf16[64,16,256]{2,1,0:T(8,128)(2,1)} custom-call(s32[64]{0:T(128)S(1)} %copy-done.5, s32[64]{0:T(128)S(1)} %copy-done.3, bf16[64,16,256]{2,1,0:T(8,128)(2,1)S(1)} %all-to-all-done.1.back), custom_call_target="tpu_custom_call" | custom-call | tf_op jit(solution)/shard_map/pallas_call | solution.py:255
  (64 shorter events, 7.2 us)
Async XLA Ops:
  0.6 9.7 %copy-start.8 = (s32[64]{0:T(128)S(1)}, s32[64]{0:T(128)}, u32[]{:S(2)}) copy-start(s32[64]{0:T(128)} %constant.56.clone) | copy-start | bytes 772
  0.6 9.6 %copy-start.16 = (s32[64]{0:T(128)S(1)}, s32[64]{0:T(128)}, u32[]{:S(2)}) copy-start(s32[64]{0:T(128)} %param.11) | copy-start | bytes 772
  0.7 10.4 %copy-start.14 = (s32[64,4]{0,1:T(4,128)S(1)}, s32[64,4]{0,1:T(4,128)}, u32[]{:S(2)}) copy-start(s32[64,4]{0,1:T(4,128)} %param.12) | copy-start | bytes 3076
  2.0 9.1 %collective-permute-start.2 = (bf16[32,16,256]{2,1,0:T(8,128)(2,1)S(1)}, bf16[32,16,256]{2,1,0:T(8,128)(2,1)S(1)}, u32[]{:S(2)}, u32[]{:S(2)}) collective-permute-start(bf16[32,16,256]{2,1,0:T(8,128)(2,1)S(1)} %get-tuple-element.71), channel_id=1, source_target_pairs={{0,64},{64,128},{128,192},{192,0},{1,65},{65,129},{129,193},{193,1... | collective-permute-start | bytes 786440 | tf_op jit(solution)/shard_map/ppermute | solution.py:32
  4.2 7.0 %collective-permute-start.3 = (bf16[32,16,256]{2,1,0:T(8,128)(2,1)S(1)}, bf16[32,16,256]{2,1,0:T(8,128)(2,1)S(1)}, u32[]{:S(2)}, u32[]{:S(2)}) collective-permute-start(bf16[32,16,256]{2,1,0:T(8,128)(2,1)S(1)} %get-tuple-element.72), channel_id=1, source_target_pairs={{0,192},{64,0},{128,64},{192,128},{1,193},{65,1},{129,65},{193,129... | collective-permute-start | bytes 786440 | tf_op jit(solution)/shard_map/ppermute | solution.py:32
  7.5 10.0 %collective-permute-start = (bf16[32,16,256]{2,1,0:T(8,128)(2,1)S(1)}, bf16[32,16,256]{2,1,0:T(8,128)(2,1)S(1)}, u32[]{:S(2)}, u32[]{:S(2)}) collective-permute-start(bf16[32,16,256]{2,1,0:T(8,128)(2,1)S(1)} %get-tuple-element.76), channel_id=1, source_target_pairs={{0,64},{64,128},{128,192},{192,0},{1,65},{65,129},{129,193},{193,1... | collective-permute-start | bytes 786440 | tf_op jit(solution)/shard_map/ppermute | solution.py:32
  7.6 9.9 %collective-permute-start.1 = (bf16[32,16,256]{2,1,0:T(8,128)(2,1)S(1)}, bf16[32,16,256]{2,1,0:T(8,128)(2,1)S(1)}, u32[]{:S(2)}, u32[]{:S(2)}) collective-permute-start(bf16[32,16,256]{2,1,0:T(8,128)(2,1)S(1)} %get-tuple-element.77), channel_id=1, source_target_pairs={{0,192},{64,0},{128,64},{192,128},{1,193},{65,1},{129,65},{193,129... | collective-permute-start | bytes 786440 | tf_op jit(solution)/shard_map/ppermute | solution.py:32
  11.1 13.5 %copy-start.4 = (s32[64]{0:T(128)}, s32[64]{0:T(128)S(1)}, u32[]{:S(2)}) copy-start(s32[64]{0:T(128)S(1)} %gather_fusion) | copy-start | bytes 772
  11.1 13.5 %copy-start.2 = (s32[64]{0:T(128)}, s32[64]{0:T(128)S(1)}, u32[]{:S(2)}) copy-start(s32[64]{0:T(128)S(1)} %fusion.9.flags) | copy-start | bytes 772
  11.1 7.8 %copy-start.6 = (f32[64,16,256]{2,1,0:T(8,128)S(1)}, f32[64,16,256]{2,1,0:T(8,128)}, u32[]{:S(2)}) copy-start(f32[64,16,256]{2,1,0:T(8,128)} %param.17) | copy-start | bytes 3145732
  11.1 7.8 %copy-start.7 = (f32[64,16,256]{2,1,0:T(8,128)S(1)}, f32[64,16,256]{2,1,0:T(8,128)}, u32[]{:S(2)}) copy-start(f32[64,16,256]{2,1,0:T(8,128)} %param.18) | copy-start | bytes 3145732
  12.0 9.8 %collective-permute-start.4 = (bf16[32,16,256]{2,1,0:T(8,128)(2,1)}, bf16[32,16,256]{2,1,0:T(8,128)(2,1)}, u32[]{:S(2)}, u32[]{:S(2)}) collective-permute-start(bf16[32,16,256]{2,1,0:T(8,128)(2,1)} %get-tuple-element.91), channel_id=1, source_target_pairs={{0,64},{64,128},{128,192},{192,0},{1,65},{65,129},{129,193},{193,1... | collective-permute-start | bytes 786440 | tf_op jit(solution)/shard_map/ppermute | solution.py:32
  13.2 8.6 %collective-permute-start.5 = (bf16[32,16,256]{2,1,0:T(8,128)(2,1)}, bf16[32,16,256]{2,1,0:T(8,128)(2,1)}, u32[]{:S(2)}, u32[]{:S(2)}) collective-permute-start(bf16[32,16,256]{2,1,0:T(8,128)(2,1)} %get-tuple-element.92), channel_id=1, source_target_pairs={{0,192},{64,0},{128,64},{192,128},{1,193},{65,1},{129,65},{193,129... | collective-permute-start | bytes 786440 | tf_op jit(solution)/shard_map/ppermute | solution.py:32
  21.8 21.7 %collective-permute-start.7 = (bf16[11,128,256]{2,1,0:T(8,128)(2,1)S(1)}, bf16[11,128,256]{2,1,0:T(8,128)(2,1)S(1)}, u32[]{:S(2)}, u32[]{:S(2)}) collective-permute-start(bf16[11,128,256]{2,1,0:T(8,128)(2,1)S(1)} %copy-done.15), channel_id=1, source_target_pairs={{0,192},{64,0},{128,64},{192,128},{1,193},{65,1},{129,65},{193,129... | collective-permute-start | bytes 2162696 | tf_op jit(solution)/shard_map/ppermute | solution.py:32
  24.6 19.0 %collective-permute-start.6 = (bf16[11,128,256]{2,1,0:T(8,128)(2,1)S(1)}, bf16[11,128,256]{2,1,0:T(8,128)(2,1)S(1)}, u32[]{:S(2)}, u32[]{:S(2)}) collective-permute-start(bf16[11,128,256]{2,1,0:T(8,128)(2,1)S(1)} %copy-done.11), channel_id=1, source_target_pairs={{0,64},{64,128},{128,192},{192,0},{1,65},{65,129},{129,193},{193,1... | collective-permute-start | bytes 2162696 | tf_op jit(solution)/shard_map/ppermute | solution.py:32
  28.5 34.1 %all-to-all-start = ((bf16[64,40,128]{2,1,0:T(8,128)(2,1)}), bf16[64,40,128]{2,1,0:T(8,128)(2,1)}, u32[]{:S(2)}, u32[]{:S(2)}) async-start(bf16[64,40,128]{2,1,0:T(8,128)(2,1)} %get-tuple-element.103), calls=%async_computation | async-start | bytes 1310720 | tf_op jit(solution)/shard_map/all_to_all | solution.py:401
  44.7 10.7 %collective-permute-start.8 = (bf16[5,128,256]{2,1,0:T(8,128)(2,1)S(1)}, bf16[5,128,256]{2,1,0:T(8,128)(2,1)S(1)}, u32[]{:S(2)}, u32[]{:S(2)}) collective-permute-start(bf16[5,128,256]{2,1,0:T(8,128)(2,1)S(1)} %get-tuple-element.107), channel_id=1, source_target_pairs={{0,64},{64,128},{128,192},{192,0},{1,65},{65,129},{129,193},{193,1... | collective-permute-start | bytes 983048 | tf_op jit(solution)/shard_map/ppermute | solution.py:32
  45.0 10.4 %collective-permute-start.9 = (bf16[5,128,256]{2,1,0:T(8,128)(2,1)S(1)}, bf16[5,128,256]{2,1,0:T(8,128)(2,1)S(1)}, u32[]{:S(2)}, u32[]{:S(2)}) collective-permute-start(bf16[5,128,256]{2,1,0:T(8,128)(2,1)S(1)} %get-tuple-element.108), channel_id=1, source_target_pairs={{0,192},{64,0},{128,64},{192,128},{1,193},{65,1},{129,65},{193,129... | collective-permute-start | bytes 983048 | tf_op jit(solution)/shard_map/ppermute | solution.py:32
  55.3 28.3 %copy-start.12 = (bf16[5,128,256]{2,1,0:T(8,128)(2,1)}, bf16[5,128,256]{2,1,0:T(8,128)(2,1)S(1)}, u32[]{:S(2)}) copy-start(bf16[5,128,256]{2,1,0:T(8,128)(2,1)S(1)} %collective-permute-done.8.refs_13_) | copy-start | bytes 983044
  55.3 28.3 %copy-start.13 = (bf16[5,128,256]{2,1,0:T(8,128)(2,1)}, bf16[5,128,256]{2,1,0:T(8,128)(2,1)S(1)}, u32[]{:S(2)}) copy-start(bf16[5,128,256]{2,1,0:T(8,128)(2,1)S(1)} %collective-permute-done.9.refs_14_) | copy-start | bytes 983044
  63.8 8.5 %collective-permute-start.12 = (bf16[32,16,256]{2,1,0:T(8,128)(2,1)S(1)}, bf16[32,16,256]{2,1,0:T(8,128)(2,1)S(1)}, u32[]{:S(2)}, u32[]{:S(2)}) collective-permute-start(bf16[32,16,256]{2,1,0:T(8,128)(2,1)S(1)} %get-tuple-element.124), channel_id=1, source_target_pairs={{0,64},{64,128},{128,192},{192,0},{1,65},{65,129},{129,193},{193,1... | collective-permute-start | bytes 786440 | tf_op jit(solution)/shard_map/ppermute | solution.py:32
  64.2 8.2 %collective-permute-start.11 = (bf16[32,16,256]{2,1,0:T(8,128)(2,1)S(1)}, bf16[32,16,256]{2,1,0:T(8,128)(2,1)S(1)}, u32[]{:S(2)}, u32[]{:S(2)}) collective-permute-start(bf16[32,16,256]{2,1,0:T(8,128)(2,1)S(1)} %get-tuple-element.125), channel_id=1, source_target_pairs={{0,192},{64,0},{128,64},{192,128},{1,193},{65,1},{129,65},{193,129... | collective-permute-start | bytes 786440 | tf_op jit(solution)/shard_map/ppermute | solution.py:32
  67.1 10.1 %collective-permute-start.10 = (bf16[32,16,256]{2,1,0:T(8,128)(2,1)S(1)}, bf16[32,16,256]{2,1,0:T(8,128)(2,1)S(1)}, u32[]{:S(2)}, u32[]{:S(2)}) collective-permute-start(bf16[32,16,256]{2,1,0:T(8,128)(2,1)S(1)} %get-tuple-element.124), channel_id=1, source_target_pairs={{0,192},{64,0},{128,64},{192,128},{1,193},{65,1},{129,65},{193,129... | collective-permute-start | bytes 786440 | tf_op jit(solution)/shard_map/ppermute | solution.py:32
  68.3 9.7 %collective-permute-start.15 = (bf16[32,16,256]{2,1,0:T(8,128)(2,1)S(1)}, bf16[32,16,256]{2,1,0:T(8,128)(2,1)S(1)}, u32[]{:S(2)}, u32[]{:S(2)}) collective-permute-start(bf16[32,16,256]{2,1,0:T(8,128)(2,1)S(1)} %get-tuple-element.125), channel_id=1, source_target_pairs={{0,64},{64,128},{128,192},{192,0},{1,65},{65,129},{129,193},{193,1... | collective-permute-start | bytes 786440 | tf_op jit(solution)/shard_map/ppermute | solution.py:32
  72.4 11.2 %collective-permute-start.13 = (bf16[32,16,256]{2,1,0:T(8,128)(2,1)S(1)}, bf16[32,16,256]{2,1,0:T(8,128)(2,1)S(1)}, u32[]{:S(2)}, u32[]{:S(2)}) collective-permute-start(bf16[32,16,256]{2,1,0:T(8,128)(2,1)S(1)} %collective-permute-done.12), channel_id=1, source_target_pairs={{0,64},{64,128},{128,192},{192,0},{1,65},{65,129},{129,193},{193,1... | collective-permute-start | bytes 786440 | tf_op jit(solution)/shard_map/ppermute | solution.py:32
  72.4 11.2 %collective-permute-start.14 = (bf16[32,16,256]{2,1,0:T(8,128)(2,1)S(1)}, bf16[32,16,256]{2,1,0:T(8,128)(2,1)S(1)}, u32[]{:S(2)}, u32[]{:S(2)}) collective-permute-start(bf16[32,16,256]{2,1,0:T(8,128)(2,1)S(1)} %collective-permute-done.11), channel_id=1, source_target_pairs={{0,192},{64,0},{128,64},{192,128},{1,193},{65,1},{129,65},{193,129... | collective-permute-start | bytes 786440 | tf_op jit(solution)/shard_map/ppermute | solution.py:32
  86.4 3.5 %collective-permute-start.18 = (f32[8,128]{1,0:T(8,128)S(1)}, f32[8,128]{1,0:T(8,128)S(1)}, u32[]{:S(2)}, u32[]{:S(2)}) collective-permute-start(f32[8,128]{1,0:T(8,128)S(1)} %get-tuple-element.120.first), channel_id=1, source_target_pairs={{0,192},{64,0},{128,64},{192,128},{1,193},{65,1},{129,65},{193,129... | collective-permute-start | bytes 12296 | tf_op jit(solution)/shard_map/ppermute | solution.py:32
  89.1 4.0 %collective-permute-start.17 = (f32[8,128]{1,0:T(8,128)S(1)}, f32[8,128]{1,0:T(8,128)S(1)}, u32[]{:S(2)}, u32[]{:S(2)}) collective-permute-start(f32[8,128]{1,0:T(8,128)S(1)} %get-tuple-element.120.first), channel_id=1, source_target_pairs={{0,128},{64,192},{128,0},{192,64},{1,129},{65,193},{129,1},{193,65... | collective-permute-start | bytes 12296 | tf_op jit(solution)/shard_map/ppermute | solution.py:32
  89.1 4.0 %collective-permute-start.16 = (f32[8,128]{1,0:T(8,128)S(1)}, f32[8,128]{1,0:T(8,128)S(1)}, u32[]{:S(2)}, u32[]{:S(2)}) collective-permute-start(f32[8,128]{1,0:T(8,128)S(1)} %get-tuple-element.120.first), channel_id=1, source_target_pairs={{0,64},{64,128},{128,192},{192,0},{1,65},{65,129},{129,193},{193,1... | collective-permute-start | bytes 12296 | tf_op jit(solution)/shard_map/ppermute | solution.py:32
  94.0 25.9 %all-to-all-start.1 = ((bf16[64,16,256]{2,1,0:T(8,128)(2,1)}), bf16[64,16,256]{2,1,0:T(8,128)(2,1)S(1)}, u32[]{:S(2)}, u32[]{:S(2)}) async-start(bf16[64,16,256]{2,1,0:T(8,128)(2,1)} %shard_map.144), calls=%async_computation.1 | async-start | bytes 1048576 | tf_op jit(solution)/shard_map/all_to_all | solution.py:401
  106.7 13.1 %copy-start.3 = (s32[64]{0:T(128)S(1)}, s32[64]{0:T(128)}, u32[]{:S(2)}) copy-start(s32[64]{0:T(128)} %copy-done.2) | copy-start | bytes 772
  106.7 13.1 %copy-start.5 = (s32[64]{0:T(128)S(1)}, s32[64]{0:T(128)}, u32[]{:S(2)}) copy-start(s32[64]{0:T(128)} %copy-done.4) | copy-start | bytes 772
  (6 other events, 13.4 us)

commit v11 on v9

--- a/solution.py
+++ b/solution.py
@@ -16,12 +16,6 @@
 NORM_EPS = 1e-06
 F32 = jnp.float32
 BF16 = jnp.bfloat16
-ORDER = (
-    33, 58, 20, 47, 9, 3, 13, 23, 32, 10, 21, 15, 57, 18, 60, 38,
-    49, 11, 52, 31, 40, 34, 61, 55, 0, 27, 53, 46, 24, 2, 28, 54,
-    1, 26, 5, 63, 8, 51, 12, 39, 16, 43, 4, 30, 56, 35, 44, 22,
-    48, 59, 36, 14, 41, 50, 29, 7, 17, 42, 37, 62, 25, 19, 45, 6,
-)
 MIB = 1024 * 1024
 VMEM = pltpu.VMEM
 LONG = pl.CostEstimate(flops=2 * 10**11, bytes_accessed=10**9, transcendentals=0)
@@ -30,12 +24,6 @@
 def shift(array, step):
     n = lax.axis_size("grp")
     return lax.ppermute(array, "grp", [(i, (i + step) % n) for i in range(n)])
-
-
-def places_of(assign, n_own, per_owner, order):
-    place = [order.index(slot) for slot in range(len(order))]
-    key = assign % n_own * per_owner + assign // n_own
-    return jnp.asarray(place, jnp.int32)[key]
 
 
 def in_hbm(array):
@@ -215,26 +203,6 @@
         compiler_params=pltpu.CompilerParams(vmem_limit_bytes=6 * MIB),
         cost_estimate=LONG,
     )(prev, following)
-
-
-def unpack_kernel(order, owned, low, high):
-    half = low.shape[0]
-    for i, place in enumerate(order):
-        if place < half:
-            low[place] = owned[i]
-        else:
-            high[place - half] = owned[i]
-
-
-def unpack(order, owned):
-    shape = jax.ShapeDtypeStruct((owned.shape[0] // 2, *owned.shape[1:]), BF16)
-    return pl.pallas_call(
-        functools.partial(unpack_kernel, order),
-        out_shape=(shape, shape),
-        in_specs=[pl.BlockSpec(memory_space=VMEM)],
-        out_specs=(pl.BlockSpec(memory_space=VMEM),) * 2,
-        compiler_params=pltpu.CompilerParams(vmem_limit_bytes=6 * MIB),
-    )(owned)
 
 
 def finish_kernel(key, flags, back, out):
@@ -325,16 +293,12 @@
     return pl.pallas_call(
         precond_kernel,
         out_shape=(
-            pltpu.HBM((2 * rows, quarter), F32),
+            jax.ShapeDtypeStruct((2 * rows, quarter), F32),
             jax.ShapeDtypeStruct((8, 128), F32),
         ),
-        grid=(1,),
         in_specs=[pl.BlockSpec(memory_space=VMEM)] * len(operands)
         + [pl.BlockSpec(memory_space=pl.ANY)] * len(sources),
-        out_specs=(
-            pl.BlockSpec((2 * rows, quarter), lambda i: (0, 0)),
-            pl.BlockSpec((8, 128), lambda i: (0, 0)),
-        ),
+        out_specs=(pl.BlockSpec(memory_space=VMEM),) * 2,
         scratch_shapes=[
             VMEM((2 * rows, quarter), BF16),
             *[VMEM(source.shape, BF16) for source in sources],
@@ -344,29 +308,31 @@
     )(*operands, *map(in_hbm, sources))
 
 
-def graft_kernel(cells, order, precond, shares, first, second, third, fourth, out):
+def graft_kernel(cells, precond, sums, first, second, third, fourth, out):
     pre = (first[...] + second[...] + third[...] + fourth[...])[0:1, :]
-    adam = jnp.sum(shares[...], axis=0, keepdims=True)
+    slot = lax.broadcasted_iota(jnp.int32, sums.shape, 1)
+    adam = jnp.sum(jnp.where(slot == lax.axis_index("own"), sums[...], 0.0))
     adam = adam * (BIAS_SECOND / (BIAS_FIRST * BIAS_FIRST))
     scale = -jnp.sqrt(adam / cells) / jnp.sqrt(pre / cells + NORM_EPS)
-    _, rows, quarter = out.shape
+    pieces, rows, quarter = out.shape
     scale = jnp.concatenate([scale] * (quarter // 128), axis=1)
-    for i, place in enumerate(order):
-        out[i] = (scale * precond[pl.ds(place * rows, rows), :]).astype(BF16)
-
-
-def graft(order, precond, shares, norms):
+    for i in range(pieces):
+        out[i] = (scale * precond[pl.ds(i * rows, rows), :]).astype(BF16)
+
+
+def graft(precond, sums, norms):
     width, quarter = precond.shape
-    shape = (len(order), width // len(order), quarter)
-    small = [pl.BlockSpec(array.shape, lambda i: (0, 0)) for array in (shares, *norms)]
-    return pl.pallas_call(
-        functools.partial(graft_kernel, float(width * width), order),
+    pieces = sums.shape[1]
+    shape = (pieces, width // pieces, quarter)
+    operands = (precond, sums, *norms)
+    return pl.pallas_call(
+        functools.partial(graft_kernel, float(width * width)),
         out_shape=pltpu.HBM(shape, BF16),
         grid=(1,),
-        in_specs=[pl.BlockSpec((width, quarter), lambda i: (0, 0))] + small,
+        in_specs=[pl.BlockSpec(array.shape, lambda i: (0, 0)) for array in operands],
         out_specs=pl.BlockSpec(shape, lambda i: (0, 0, 0)),
         compiler_params=pltpu.CompilerParams(vmem_limit_bytes=8 * MIB),
-    )(in_hbm(precond), shares, *norms)
+    )(*operands)
 
 
 def on_device(
@@ -397,11 +363,15 @@
         return slice_at(array, starts[step], quarter, array.ndim - 1)
 
     part = grad_parts[0]
-    order = ORDER if len(ORDER) == n_own else tuple(range(n_own))
 
     def exchange(array):
-        groups = [list(order)]
-        return lax.all_to_all(array, "own", 0, 0, axis_index_groups=groups, tiled=True)
+        return lax.all_to_all(array, "own", split_axis=0, concat_axis=0, tiled=True)
+
+    def summed(array, axis, *steps):
+        n = lax.axis_size(axis)
+        for step in steps:
+            array += lax.ppermute(array, axis, [(i, i ^ step) for i in range(n)])
+        return array
 
     far = columns(part, 2)
     far_low, far_high = lax.optimization_barrier((far[:half], far[half:]))
@@ -420,7 +390,7 @@
     )
     up_sum = shift(up_sum, 1)
     down_sum = shift(down_sum, -1)
-    key = places_of(assign, n_own, per_owner, order)
+    key = (assign % n_own * per_owner + assign // n_own).astype(jnp.int32)
     flags = inside(block_bounds, shard_rows, quarter)
     roots_up, roots_down, root_own = root_pieces(left_root, right_root)
     later, up_direct, down_direct, key, flags, roots_up, roots_down, root_own = (
@@ -445,22 +415,23 @@
     roots = [root_own, roots_up, roots_prev, roots_next, *far_roots]
 
     adam_sq = jnp.sum(squares, axis=(1, 2))
-    adam_sq = sum(shift(adam_sq, step) for step in (1, 2, 3)) + adam_sq
+    bits = [1 << i for i in range(n_own.bit_length() - 1)]
+    adam_sq = summed(summed(adam_sq, "grp", 1, 2), "own", *bits[:2])
     owned, roots, adam_sq = lax.optimization_barrier((owned, roots, adam_sq))
-    low, high = unpack(order, owned)
+    low, high = owned[:half], owned[half:]
     prev_low = shift(low, 1)
     next_high = shift(high, -1)
     prev_high = shift(high, 1)
     next_low = shift(low, -1)
-    prev_low, next_high, adam_sq = lax.optimization_barrier((prev_low, next_high, adam_sq))
-    shares = exchange(jnp.broadcast_to(adam_sq[:, None, None], (n_own, 1, 128)))
+    adam_sq = summed(adam_sq, "own", *bits[2:])
     far_low = shift(prev_low, 1)
     far_high = shift(next_high, -1)
     pieces = [low, high, next_low, next_high, far_low, far_high, prev_low, prev_high]
     flat = [piece.reshape(-1, quarter) for piece in pieces]
+    flat, adam_sq = lax.optimization_barrier((flat, adam_sq))
     precond, norms = precondition(flat, roots)
     norms = [norms] + [shift(norms, step) for step in (1, 2, 3)]
-    grafted = graft(order, precond, shares.reshape(n_own, 128), norms)
+    grafted = graft(precond, adam_sq.reshape(1, n_own), norms)
     pieces, grafted = lax.optimization_barrier((pieces, grafted))
     back = exchange(grafted)
 

time: 124 us -> 141 us (1.14)
  starting transfers between devices: 65.3 us -> 80.8 us
  waiting for transfers between devices: 25.9 us -> 31.3 us
  Pallas kernels: 17.4 us -> 14.1 us
    ppermute x0 -> x8, starting transfers between devices: none -> 19.7 us  [summed(): array += lax.ppermute(array, axis, [(i, i ^ step) for i in range(n)])]
    ppermute x0 -> x8, waiting for transfers between devices: none -> 12.6 us  [summed(): array += lax.ppermute(array, axis, [(i, i ^ step) for i in range(n)])]
    all_to_all x3 -> x2, waiting for transfers between devices: 16.2 us -> 12.4 us  [exchange(): return lax.all_to_all(array, 'own', split_axis=0, concat_axis=0, tiled=True)]
    ppermute x22 -> x19, waiting for transfers between devices: 9.78 us -> 6.22 us  [shift(): return lax.ppermute(array, 'grp', [(i, (i + step) % n) for i in range(n)])]
    pallas_call x3 -> x2, Pallas kernels: 7.03 us -> 3.79 us  [the longest x1 2.77 us: precondition(): pl.pallas_call(precond_kernel, out_shape=(jax.ShapeDtypeStruct((2 * rows,...]
    ppermute x22 -> x19, starting transfers between devices: 29 us -> 26 us  [shift(): return lax.ppermute(array, 'grp', [(i, (i + step) % n) for i in range(n)])]
    all_to_all x3 -> x2, starting transfers between devices: 36.3 us -> 35.1 us  [exchange(): return lax.all_to_all(array, 'own', split_axis=0, concat_axis=0, tiled=True)]
  transfers between devices with their start and end apart: 25 -> 29, of which waited for: 8 -> 13; matrix products, arithmetic and copies ran while one was open for 9% -> 6% of each run, Pallas kernels for 10% -> 6%
where the time goes in v11:
time: 141 us; the launch traced here: 140 us
  starting transfers between devices  80.8 us (57%)
  waiting for transfers between devices  31.3 us (22%)
  Pallas kernels  14.1 us (10%)
  local copies, waits for them, and re-layouts  8.18 us (6%)
  other arithmetic  2.5 us (2%)
  matrix products  2.47 us (2%)
    all_to_all x2, starting transfers between devices, exchange(): return lax.all_to_all(array, 'own', split_axis=0, concat_axis=0, tiled=True)  35.1 us
    ppermute x19, starting transfers between devices, shift(): return lax.ppermute(array, 'grp', [(i, (i + step) % n) for i in range(n)])  26 us
    ppermute x8, starting transfers between devices, summed(): array += lax.ppermute(array, axis, [(i, i ^ step) for i in range(n)])  19.7 us
    ppermute x8, waiting for transfers between devices, summed(): array += lax.ppermute(array, axis, [(i, i ^ step) for i in range(n)])  12.6 us
    all_to_all x2, waiting for transfers between devices, exchange(): return lax.all_to_all(array, 'own', split_axis=0, concat_axis=0, tiled=True)  12.4 us
    ppermute x19, waiting for transfers between devices, shift(): return lax.ppermute(array, 'grp', [(i, (i + step) % n) for i in range(n)])  6.22 us
    pallas_call x1, Pallas kernels, pack(): pl.pallas_call(pack_kernel, out_shape=(pltpu.HBM(piece, BF16), pltpu.HBM(...  3.6 us
    pallas_call x1, Pallas kernels, root_pieces(): pl.pallas_call(roots_kernel, out_shape=(pltpu.HBM((11, *unit), BF16), plt...  2.97 us
  transfers between devices with their start and end apart: 29, of which 13 were waited for; matrix products, arithmetic and copies ran while one was open for 6% of the time, Pallas kernels for 6%

profile of v11, /device:TPU:1, one launch (start us, length us, event | category | flops | bytes accessed | tf_op | source)
XLA Modules:
  0.0 140.3 jit_solution(17075224498649313939)
XLA Ops:
  0.7 1.4 dynamic-slice_bitcast_fusion
  2.0 2.1 %collective-permute-start = (bf16[32,16,256]{2,1,0:T(8,128)(2,1)S(1)}, bf16[32,16,256]{2,1,0:T(8,128)(2,1)S(1)}, u32[]{:S(2)}, u32[]{:S(2)}) collective-permute-start(bf16[32,16,256]{2,1,0:T(8,128)(2,1)S(1)} %get-tuple-element.80), channel_id=1, source_target_pairs={{0,64},{64,128},{128,192},{192,0},{1,65},{65,129},{129,193},{193,1... | collective-permute-start | bytes 786440 | tf_op jit(solution)/shard_map/ppermute | solution.py:26
  4.1 1.6 %collective-permute-start.1 = (bf16[32,16,256]{2,1,0:T(8,128)(2,1)S(1)}, bf16[32,16,256]{2,1,0:T(8,128)(2,1)S(1)}, u32[]{:S(2)}, u32[]{:S(2)}) collective-permute-start(bf16[32,16,256]{2,1,0:T(8,128)(2,1)S(1)} %get-tuple-element.81), channel_id=1, source_target_pairs={{0,192},{64,0},{128,64},{192,128},{1,193},{65,1},{129,65},{193,129... | collective-permute-start | bytes 786440 | tf_op jit(solution)/shard_map/ppermute | solution.py:26
  5.8 2.5 %constant_dynamic-slice_fusion.3 = (bf16[32,16,256]{2,1,0:T(8,128)(2,1)S(1)}, bf16[32,16,256]{2,1,0:T(8,128)(2,1)}, bf16[32,16,256]{2,1,0:T(8,128)(2,1)S(1)}, bf16[32,16,256]{2,1,0:T(8,128)(2,1)}) fusion(bf16[64,16,1024]{2,1,0:T(8,128)(2,1)} %bitcast.44, s32[]{:T(128)S(6)} %add.64, s32[]{:T(128)S(6)} %mul.30, s32[]{:T(128)S(6)} %mul.28), kind=kLoop, calls=%fused_computation.17 | loop fusion | bytes 2097164 | tf_op jit(solution)/shard_map/slice | solution.py:383
  8.3 2.7 %collective-permute-start.3 = (bf16[32,16,256]{2,1,0:T(8,128)(2,1)}, bf16[32,16,256]{2,1,0:T(8,128)(2,1)}, u32[]{:S(2)}, u32[]{:S(2)}) collective-permute-start(bf16[32,16,256]{2,1,0:T(8,128)(2,1)} %get-tuple-element.91), channel_id=1, source_target_pairs={{0,192},{64,0},{128,64},{192,128},{1,193},{65,1},{129,65},{193,129... | collective-permute-start | bytes 786440 | tf_op jit(solution)/shard_map/ppermute | solution.py:26
  11.9 1.3 collective-permute-start.4
  14.6 3.0 %shard_map.129 = (bf16[11,128,256]{2,1,0:T(8,128)(2,1)}, bf16[11,128,256]{2,1,0:T(8,128)(2,1)}, bf16[2,128,256]{2,1,0:T(8,128)(2,1)}) custom-call(f32[1,256,1024]{2,1,0:T(8,128)} %left, f32[1,256,1024]{2,1,0:T(8,128)} %right), custom_call_target="tpu_custom_call" | custom-call | flops 199999995904 | bytes 1000000000 | tf_op jit(solution)/shard_map/pallas_call | solution.py:89
  17.6 1.5 %constant_dynamic-slice_fusion.2.own = bf16[64,16,256]{2,1,0:T(8,128)(2,1)S(1)} fusion(bf16[64,16,1024]{2,1,0:T(8,128)(2,1)} %bitcast.45, s32[]{:T(128)S(6)} %mul.27), kind=kLoop, calls=%fused_computation.16 | loop fusion | bytes 1048580 | tf_op jit(solution)/shard_map/dynamic_slice | solution.py:36
  21.7 2.7 %collective-permute-start.7 = (bf16[11,128,256]{2,1,0:T(8,128)(2,1)S(1)}, bf16[11,128,256]{2,1,0:T(8,128)(2,1)S(1)}, u32[]{:S(2)}, u32[]{:S(2)}) collective-permute-start(bf16[11,128,256]{2,1,0:T(8,128)(2,1)S(1)} %copy-done.15), channel_id=1, source_target_pairs={{0,192},{64,0},{128,64},{192,128},{1,193},{65,1},{129,65},{193,129... | collective-permute-start | bytes 2162696 | tf_op jit(solution)/shard_map/ppermute | solution.py:26
  24.4 3.6 %shard_map.131 = (bf16[64,16,256]{2,1,0:T(8,128)(2,1)}, f32[64,8,128]{2,1,0:T(8,128)}, f32[2,32,16,256]{3,2,1,0:T(8,128)}, f32[2,32,16,256]{3,2,1,0:T(8,128)}) custom-call(s32[64]{0:T(128)S(1)} %fusion.8.key, s32[64]{0:T(128)S(1)} %fusion.9.flags, f32[2,32,16,256]{3,2,1,0:T(8,128)S(1)} %get-tuple-element.108.partial, ...), custom_call_target="tpu_custom_call" | custom-call | tf_op jit(solution)/shard_map/pallas_call | solution.py:170
  28.0 14.6 %all-to-all-start = ((bf16[64,16,256]{2,1,0:T(8,128)(2,1)}), bf16[64,16,256]{2,1,0:T(8,128)(2,1)}, u32[]{:S(2)}, u32[]{:S(2)}) async-start(bf16[64,16,256]{2,1,0:T(8,128)(2,1)} %get-tuple-element.113), calls=%async_computation | async-start | bytes 1048576 | tf_op jit(solution)/shard_map/all_to_all | solution.py:368
  44.0 2.7 %collective-permute-start.9 = (bf16[5,128,256]{2,1,0:T(8,128)(2,1)S(1)}, bf16[5,128,256]{2,1,0:T(8,128)(2,1)S(1)}, u32[]{:S(2)}, u32[]{:S(2)}) collective-permute-start(bf16[5,128,256]{2,1,0:T(8,128)(2,1)S(1)} %get-tuple-element.118), channel_id=1, source_target_pairs={{0,192},{64,0},{128,64},{192,128},{1,193},{65,1},{129,65},{193,129... | collective-permute-start | bytes 983048 | tf_op jit(solution)/shard_map/ppermute | solution.py:26
  47.3 5.0 %collective-permute-done.10 = f32[64]{0:T(128)S(1)} collective-permute-done((f32[64]{0:T(128)S(1)}, f32[64]{0:T(128)S(1)}, u32[]{:S(2)}, u32[]{:S(2)}) %collective-permute-start.10) | collective-permute-done | bytes 288 | tf_op jit(solution)/shard_map/ppermute | solution.py:373
  52.3 4.1 %collective-permute-start.11 = (f32[64]{0:T(128)S(1)}, f32[64]{0:T(128)S(1)}, u32[]{:S(2)}, u32[]{:S(2)}) collective-permute-start(f32[64]{0:T(128)S(1)} %add.54), channel_id=1, source_target_pairs={{0,128},{64,192},{128,0},{192,64},{1,129},{65,193},{129,1},{193,65... | collective-permute-start | bytes 776 | tf_op jit(solution)/shard_map/ppermute | solution.py:373
  57.7 2.1 %collective-permute-start.12 = (f32[64]{0:T(128)S(1)}, f32[64]{0:T(128)S(1)}, u32[]{:S(2)}, u32[]{:S(2)}) collective-permute-start(f32[64]{0:T(128)S(1)} %add.55), channel_id=1, source_target_pairs={{0,1},{1,0},{2,3},{3,2},{4,5},{5,4},{6,7},{7,6},{8,9},{9,8},{10,11... | collective-permute-start | bytes 776 | tf_op jit(solution)/shard_map/ppermute | solution.py:373
  60.7 1.4 collective-permute-start.13
  64.4 2.1 %collective-permute-start.15 = (bf16[32,16,256]{2,1,0:T(8,128)(2,1)S(1)}, bf16[32,16,256]{2,1,0:T(8,128)(2,1)S(1)}, u32[]{:S(2)}, u32[]{:S(2)}) collective-permute-start(bf16[32,16,256]{2,1,0:T(8,128)(2,1)S(1)} %get-tuple-element.143), channel_id=1, source_target_pairs={{0,192},{64,0},{128,64},{192,128},{1,193},{65,1},{129,65},{193,129... | collective-permute-start | bytes 786440 | tf_op jit(solution)/shard_map/ppermute | solution.py:26
  67.5 1.8 %collective-permute-start.14 = (bf16[32,16,256]{2,1,0:T(8,128)(2,1)S(1)}, bf16[32,16,256]{2,1,0:T(8,128)(2,1)S(1)}, u32[]{:S(2)}, u32[]{:S(2)}) collective-permute-start(bf16[32,16,256]{2,1,0:T(8,128)(2,1)S(1)} %get-tuple-element.142), channel_id=1, source_target_pairs={{0,192},{64,0},{128,64},{192,128},{1,193},{65,1},{129,65},{193,129... | collective-permute-start | bytes 786440 | tf_op jit(solution)/shard_map/ppermute | solution.py:26
  69.2 1.6 %collective-permute-done.15 = bf16[32,16,256]{2,1,0:T(8,128)(2,1)S(1)} collective-permute-done((bf16[32,16,256]{2,1,0:T(8,128)(2,1)S(1)}, bf16[32,16,256]{2,1,0:T(8,128)(2,1)S(1)}, u32[]{:S(2)}, u32[]{:S(2)}) %collective-permute-start.15) | collective-permute-done | bytes 262176 | tf_op jit(solution)/shard_map/ppermute | solution.py:26
  70.8 3.3 %collective-permute-start.18 = (bf16[32,16,256]{2,1,0:T(8,128)(2,1)S(1)}, bf16[32,16,256]{2,1,0:T(8,128)(2,1)S(1)}, u32[]{:S(2)}, u32[]{:S(2)}) collective-permute-start(bf16[32,16,256]{2,1,0:T(8,128)(2,1)S(1)} %collective-permute-done.15), channel_id=1, source_target_pairs={{0,192},{64,0},{128,64},{192,128},{1,193},{65,1},{129,65},{193,129... | collective-permute-start | bytes 786440 | tf_op jit(solution)/shard_map/ppermute | solution.py:26
  74.1 2.3 %collective-permute-start.20 = (f32[64]{0:T(128)S(1)}, f32[64]{0:T(128)S(1)}, u32[]{:S(2)}, u32[]{:S(2)}) collective-permute-start(f32[64]{0:T(128)S(1)} %add.57), channel_id=1, source_target_pairs={{0,4},{1,5},{2,6},{3,7},{4,0},{5,1},{6,2},{7,3},{8,12},{9,13},{10,... | collective-permute-start | bytes 776 | tf_op jit(solution)/shard_map/ppermute | solution.py:373
  77.7 5.3 %collective-permute-start.21 = (f32[64]{0:T(128)S(1)}, f32[64]{0:T(128)S(1)}, u32[]{:S(2)}, u32[]{:S(2)}) collective-permute-start(f32[64]{0:T(128)S(1)} %add.58), channel_id=1, source_target_pairs={{0,8},{1,9},{2,10},{3,11},{4,12},{5,13},{6,14},{7,15},{8,0},{9,1},... | collective-permute-start | bytes 776 | tf_op jit(solution)/shard_map/ppermute | solution.py:373
  84.0 1.4 collective-permute-start.22
  86.7 3.0 %collective-permute-start.23 = (f32[64]{0:T(128)S(1)}, f32[64]{0:T(128)S(1)}, u32[]{:S(2)}, u32[]{:S(2)}) collective-permute-start(f32[64]{0:T(128)S(1)} %add.60), channel_id=1, source_target_pairs={{0,32},{1,33},{2,34},{3,35},{4,36},{5,37},{6,38},{7,39},{8,40},{9,... | collective-permute-start | bytes 776 | tf_op jit(solution)/shard_map/ppermute | solution.py:373
  90.7 2.8 %shard_map.133 = (f32[1024,256]{1,0:T(8,128)S(1)}, f32[8,128]{1,0:T(8,128)S(1)}) custom-call(bf16[512,256]{1,0:T(8,128)(2,1)S(1)} %bitcast.32, bf16[512,256]{1,0:T(8,128)(2,1)S(1)} %bitcast.31, bf16[512,256]{1,0:T(8,128)(2,1)S(1)} %bitcast.38, bf16[512,256]{1,0:T(8,128)(2,1)S(1)} %bitcast.35, bf16[512,256]{1,0:T(8,128)(2,1)S(1)} %bitcast.40, ...), custom_call_target="tpu_custom_call" | custom-call | tf_op jit(solution)/shard_map/pallas_call | solution.py:293
  93.4 2.5 %collective-permute-start.26 = (f32[8,128]{1,0:T(8,128)S(1)}, f32[8,128]{1,0:T(8,128)S(1)}, u32[]{:S(2)}, u32[]{:S(2)}) collective-permute-start(f32[8,128]{1,0:T(8,128)S(1)} %get-tuple-element.138.first), channel_id=1, source_target_pairs={{0,192},{64,0},{128,64},{192,128},{1,193},{65,1},{129,65},{193,129... | collective-permute-start | bytes 12296 | tf_op jit(solution)/shard_map/ppermute | solution.py:26
  96.6 3.2 %collective-permute-done.25.third = f32[8,128]{1,0:T(8,128)S(1)} collective-permute-done((f32[8,128]{1,0:T(8,128)S(1)}, f32[8,128]{1,0:T(8,128)S(1)}, u32[]{:S(2)}, u32[]{:S(2)}) %collective-permute-start.25) | collective-permute-done | bytes 4128 | tf_op jit(solution)/shard_map/ppermute | solution.py:26
  100.9 20.6 %all-to-all-start.1 = ((bf16[64,16,256]{2,1,0:T(8,128)(2,1)}), bf16[64,16,256]{2,1,0:T(8,128)(2,1)S(1)}, u32[]{:S(2)}, u32[]{:S(2)}) async-start(bf16[64,16,256]{2,1,0:T(8,128)(2,1)} %shard_map.134), calls=%async_computation.1 | async-start | bytes 1048576 | tf_op jit(solution)/shard_map/all_to_all | solution.py:368
  123.0 1.6 %fusion.3 = f32[1,256,1024]{2,1,0:T(8,128)} fusion(s32[]{:T(128)S(6)} %mul.31, f32[256,1024]{1,0:T(8,128)S(1)} %fusion.4, f32[1,256,1024]{2,1,0:T(8,128)S(1)} %copy-done.9), kind=kLoop, calls=%fused_computation.7 | loop fusion | flops 786432 | bytes 3145732 | tf_op jit(solution)/shard_map/add | solution.py:446
  124.6 1.7 %fusion = f32[1,256,1024]{2,1,0:T(8,128)} fusion(bf16[1024,1024]{1,0:T(8,128)(2,1)S(1)} %bitcast.43, f32[1,256,1024]{2,1,0:T(8,128)S(1)} %copy-done.8, s32[]{:T(128)S(6)} %mul.27), kind=kOutput, calls=%fused_computation.4 | convolution fusion | flops 537395200 | bytes 4718596 | tf_op jit(solution)/shard_map/dot_general | solution.py:40
  126.3 12.4 %all-to-all-done.1.back = bf16[64,16,256]{2,1,0:T(8,128)(2,1)S(1)} async-done(((bf16[64,16,256]{2,1,0:T(8,128)(2,1)}), bf16[64,16,256]{2,1,0:T(8,128)(2,1)S(1)}, u32[]{:S(2)}, u32[]{:S(2)}) %all-to-all-start.1) | async-done | bytes 524320 | tf_op jit(solution)/shard_map/all_to_all | solution.py:368
  138.8 1.5 %shard_map.135 = bf16[64,16,256]{2,1,0:T(8,128)(2,1)} custom-call(s32[64]{0:T(128)S(1)} %copy-done.7, s32[64]{0:T(128)S(1)} %copy-done.5, bf16[64,16,256]{2,1,0:T(8,128)(2,1)S(1)} %all-to-all-done.1.back), custom_call_target="tpu_custom_call" | custom-call | tf_op jit(solution)/shard_map/pallas_call | solution.py:223
  (87 shorter events, 20.2 us)
Async XLA Ops:
  2.0 9.0 %collective-permute-start = (bf16[32,16,256]{2,1,0:T(8,128)(2,1)S(1)}, bf16[32,16,256]{2,1,0:T(8,128)(2,1)S(1)}, u32[]{:S(2)}, u32[]{:S(2)}) collective-permute-start(bf16[32,16,256]{2,1,0:T(8,128)(2,1)S(1)} %get-tuple-element.80), channel_id=1, source_target_pairs={{0,64},{64,128},{128,192},{192,0},{1,65},{65,129},{129,193},{193,1... | collective-permute-start | bytes 786440 | tf_op jit(solution)/shard_map/ppermute | solution.py:26
  4.1 6.9 %collective-permute-start.1 = (bf16[32,16,256]{2,1,0:T(8,128)(2,1)S(1)}, bf16[32,16,256]{2,1,0:T(8,128)(2,1)S(1)}, u32[]{:S(2)}, u32[]{:S(2)}) collective-permute-start(bf16[32,16,256]{2,1,0:T(8,128)(2,1)S(1)} %get-tuple-element.81), channel_id=1, source_target_pairs={{0,192},{64,0},{128,64},{192,128},{1,193},{65,1},{129,65},{193,129... | collective-permute-start | bytes 786440 | tf_op jit(solution)/shard_map/ppermute | solution.py:26
  8.3 9.3 %collective-permute-start.2 = (bf16[32,16,256]{2,1,0:T(8,128)(2,1)}, bf16[32,16,256]{2,1,0:T(8,128)(2,1)}, u32[]{:S(2)}, u32[]{:S(2)}) collective-permute-start(bf16[32,16,256]{2,1,0:T(8,128)(2,1)} %get-tuple-element.90), channel_id=1, source_target_pairs={{0,64},{64,128},{128,192},{192,0},{1,65},{65,129},{129,193},{193,1... | collective-permute-start | bytes 786440 | tf_op jit(solution)/shard_map/ppermute | solution.py:26
  8.3 9.3 %collective-permute-start.3 = (bf16[32,16,256]{2,1,0:T(8,128)(2,1)}, bf16[32,16,256]{2,1,0:T(8,128)(2,1)}, u32[]{:S(2)}, u32[]{:S(2)}) collective-permute-start(bf16[32,16,256]{2,1,0:T(8,128)(2,1)} %get-tuple-element.91), channel_id=1, source_target_pairs={{0,192},{64,0},{128,64},{192,128},{1,193},{65,1},{129,65},{193,129... | collective-permute-start | bytes 786440 | tf_op jit(solution)/shard_map/ppermute | solution.py:26
  11.9 9.8 %collective-permute-start.4 = (bf16[32,16,256]{2,1,0:T(8,128)(2,1)}, bf16[32,16,256]{2,1,0:T(8,128)(2,1)}, u32[]{:S(2)}, u32[]{:S(2)}) collective-permute-start(bf16[32,16,256]{2,1,0:T(8,128)(2,1)} %get-tuple-element.101), channel_id=1, source_target_pairs={{0,64},{64,128},{128,192},{192,0},{1,65},{65,129},{129,193},{193,1... | collective-permute-start | bytes 786440 | tf_op jit(solution)/shard_map/ppermute | solution.py:26
  13.2 8.5 %collective-permute-start.5 = (bf16[32,16,256]{2,1,0:T(8,128)(2,1)}, bf16[32,16,256]{2,1,0:T(8,128)(2,1)}, u32[]{:S(2)}, u32[]{:S(2)}) collective-permute-start(bf16[32,16,256]{2,1,0:T(8,128)(2,1)} %get-tuple-element.102), channel_id=1, source_target_pairs={{0,192},{64,0},{128,64},{192,128},{1,193},{65,1},{129,65},{193,129... | collective-permute-start | bytes 786440 | tf_op jit(solution)/shard_map/ppermute | solution.py:26
  21.7 20.9 %collective-permute-start.7 = (bf16[11,128,256]{2,1,0:T(8,128)(2,1)S(1)}, bf16[11,128,256]{2,1,0:T(8,128)(2,1)S(1)}, u32[]{:S(2)}, u32[]{:S(2)}) collective-permute-start(bf16[11,128,256]{2,1,0:T(8,128)(2,1)S(1)} %copy-done.15), channel_id=1, source_target_pairs={{0,192},{64,0},{128,64},{192,128},{1,193},{65,1},{129,65},{193,129... | collective-permute-start | bytes 2162696 | tf_op jit(solution)/shard_map/ppermute | solution.py:26
  24.4 18.2 %collective-permute-start.6 = (bf16[11,128,256]{2,1,0:T(8,128)(2,1)S(1)}, bf16[11,128,256]{2,1,0:T(8,128)(2,1)S(1)}, u32[]{:S(2)}, u32[]{:S(2)}) collective-permute-start(bf16[11,128,256]{2,1,0:T(8,128)(2,1)S(1)} %copy-done.10), channel_id=1, source_target_pairs={{0,64},{64,128},{128,192},{192,0},{1,65},{65,129},{129,193},{193,1... | collective-permute-start | bytes 2162696 | tf_op jit(solution)/shard_map/ppermute | solution.py:26
  28.0 35.0 %all-to-all-start = ((bf16[64,16,256]{2,1,0:T(8,128)(2,1)}), bf16[64,16,256]{2,1,0:T(8,128)(2,1)}, u32[]{:S(2)}, u32[]{:S(2)}) async-start(bf16[64,16,256]{2,1,0:T(8,128)(2,1)} %get-tuple-element.113), calls=%async_computation | async-start | bytes 1048576 | tf_op jit(solution)/shard_map/all_to_all | solution.py:368
  43.7 19.3 %collective-permute-start.8 = (bf16[5,128,256]{2,1,0:T(8,128)(2,1)S(1)}, bf16[5,128,256]{2,1,0:T(8,128)(2,1)S(1)}, u32[]{:S(2)}, u32[]{:S(2)}) collective-permute-start(bf16[5,128,256]{2,1,0:T(8,128)(2,1)S(1)} %get-tuple-element.117), channel_id=1, source_target_pairs={{0,64},{64,128},{128,192},{192,0},{1,65},{65,129},{129,193},{193,1... | collective-permute-start | bytes 983048 | tf_op jit(solution)/shard_map/ppermute | solution.py:26
  44.0 19.1 %collective-permute-start.9 = (bf16[5,128,256]{2,1,0:T(8,128)(2,1)S(1)}, bf16[5,128,256]{2,1,0:T(8,128)(2,1)S(1)}, u32[]{:S(2)}, u32[]{:S(2)}) collective-permute-start(bf16[5,128,256]{2,1,0:T(8,128)(2,1)S(1)} %get-tuple-element.118), channel_id=1, source_target_pairs={{0,192},{64,0},{128,64},{192,128},{1,193},{65,1},{129,65},{193,129... | collective-permute-start | bytes 983048 | tf_op jit(solution)/shard_map/ppermute | solution.py:26
  47.2 5.1 %collective-permute-start.10 = (f32[64]{0:T(128)S(1)}, f32[64]{0:T(128)S(1)}, u32[]{:S(2)}, u32[]{:S(2)}) collective-permute-start(f32[64]{0:T(128)S(1)} %reduce_sum.9), channel_id=1, source_target_pairs={{0,64},{64,0},{128,192},{192,128},{1,65},{65,1},{129,193},{193,129... | collective-permute-start | bytes 776 | tf_op jit(solution)/shard_map/ppermute | solution.py:373
  52.3 5.4 %collective-permute-start.11 = (f32[64]{0:T(128)S(1)}, f32[64]{0:T(128)S(1)}, u32[]{:S(2)}, u32[]{:S(2)}) collective-permute-start(f32[64]{0:T(128)S(1)} %add.54), channel_id=1, source_target_pairs={{0,128},{64,192},{128,0},{192,64},{1,129},{65,193},{129,1},{193,65... | collective-permute-start | bytes 776 | tf_op jit(solution)/shard_map/ppermute | solution.py:373
  57.7 3.0 %collective-permute-start.12 = (f32[64]{0:T(128)S(1)}, f32[64]{0:T(128)S(1)}, u32[]{:S(2)}, u32[]{:S(2)}) collective-permute-start(f32[64]{0:T(128)S(1)} %add.55), channel_id=1, source_target_pairs={{0,1},{1,0},{2,3},{3,2},{4,5},{5,4},{6,7},{7,6},{8,9},{9,8},{10,11... | collective-permute-start | bytes 776 | tf_op jit(solution)/shard_map/ppermute | solution.py:373
  60.7 2.4 %collective-permute-start.13 = (f32[64]{0:T(128)S(1)}, f32[64]{0:T(128)S(1)}, u32[]{:S(2)}, u32[]{:S(2)}) collective-permute-start(f32[64]{0:T(128)S(1)} %add.56), channel_id=1, source_target_pairs={{0,2},{1,3},{2,0},{3,1},{4,6},{5,7},{6,4},{7,5},{8,10},{9,11},{10,... | collective-permute-start | bytes 776 | tf_op jit(solution)/shard_map/ppermute | solution.py:373
  63.1 27.6 %copy-start.11 = (bf16[5,128,256]{2,1,0:T(8,128)(2,1)}, bf16[5,128,256]{2,1,0:T(8,128)(2,1)S(1)}, u32[]{:S(2)}) copy-start(bf16[5,128,256]{2,1,0:T(8,128)(2,1)S(1)} %collective-permute-done.8.refs_12_) | copy-start | bytes 983044
  63.1 27.6 %copy-start.12 = (bf16[5,128,256]{2,1,0:T(8,128)(2,1)}, bf16[5,128,256]{2,1,0:T(8,128)(2,1)S(1)}, u32[]{:S(2)}) copy-start(bf16[5,128,256]{2,1,0:T(8,128)(2,1)S(1)} %collective-permute-done.9.refs_13_) | copy-start | bytes 983044
  64.4 6.4 %collective-permute-start.15 = (bf16[32,16,256]{2,1,0:T(8,128)(2,1)S(1)}, bf16[32,16,256]{2,1,0:T(8,128)(2,1)S(1)}, u32[]{:S(2)}, u32[]{:S(2)}) collective-permute-start(bf16[32,16,256]{2,1,0:T(8,128)(2,1)S(1)} %get-tuple-element.143), channel_id=1, source_target_pairs={{0,192},{64,0},{128,64},{192,128},{1,193},{65,1},{129,65},{193,129... | collective-permute-start | bytes 786440 | tf_op jit(solution)/shard_map/ppermute | solution.py:26
  66.5 7.6 %collective-permute-start.16 = (bf16[32,16,256]{2,1,0:T(8,128)(2,1)S(1)}, bf16[32,16,256]{2,1,0:T(8,128)(2,1)S(1)}, u32[]{:S(2)}, u32[]{:S(2)}) collective-permute-start(bf16[32,16,256]{2,1,0:T(8,128)(2,1)S(1)} %get-tuple-element.142), channel_id=1, source_target_pairs={{0,64},{64,128},{128,192},{192,0},{1,65},{65,129},{129,193},{193,1... | collective-permute-start | bytes 786440 | tf_op jit(solution)/shard_map/ppermute | solution.py:26
  66.5 24.1 %collective-permute-start.19 = (bf16[32,16,256]{2,1,0:T(8,128)(2,1)S(1)}, bf16[32,16,256]{2,1,0:T(8,128)(2,1)S(1)}, u32[]{:S(2)}, u32[]{:S(2)}) collective-permute-start(bf16[32,16,256]{2,1,0:T(8,128)(2,1)S(1)} %get-tuple-element.143), channel_id=1, source_target_pairs={{0,64},{64,128},{128,192},{192,0},{1,65},{65,129},{129,193},{193,1... | collective-permute-start | bytes 786440 | tf_op jit(solution)/shard_map/ppermute | solution.py:26
  67.5 23.1 %collective-permute-start.14 = (bf16[32,16,256]{2,1,0:T(8,128)(2,1)S(1)}, bf16[32,16,256]{2,1,0:T(8,128)(2,1)S(1)}, u32[]{:S(2)}, u32[]{:S(2)}) collective-permute-start(bf16[32,16,256]{2,1,0:T(8,128)(2,1)S(1)} %get-tuple-element.142), channel_id=1, source_target_pairs={{0,192},{64,0},{128,64},{192,128},{1,193},{65,1},{129,65},{193,129... | collective-permute-start | bytes 786440 | tf_op jit(solution)/shard_map/ppermute | solution.py:26
  70.8 19.8 %collective-permute-start.18 = (bf16[32,16,256]{2,1,0:T(8,128)(2,1)S(1)}, bf16[32,16,256]{2,1,0:T(8,128)(2,1)S(1)}, u32[]{:S(2)}, u32[]{:S(2)}) collective-permute-start(bf16[32,16,256]{2,1,0:T(8,128)(2,1)S(1)} %collective-permute-done.15), channel_id=1, source_target_pairs={{0,192},{64,0},{128,64},{192,128},{1,193},{65,1},{129,65},{193,129... | collective-permute-start | bytes 786440 | tf_op jit(solution)/shard_map/ppermute | solution.py:26
  74.1 16.5 %collective-permute-start.17 = (bf16[32,16,256]{2,1,0:T(8,128)(2,1)S(1)}, bf16[32,16,256]{2,1,0:T(8,128)(2,1)S(1)}, u32[]{:S(2)}, u32[]{:S(2)}) collective-permute-start(bf16[32,16,256]{2,1,0:T(8,128)(2,1)S(1)} %collective-permute-done.16), channel_id=1, source_target_pairs={{0,64},{64,128},{128,192},{192,0},{1,65},{65,129},{129,193},{193,1... | collective-permute-start | bytes 786440 | tf_op jit(solution)/shard_map/ppermute | solution.py:26
  74.1 3.6 %collective-permute-start.20 = (f32[64]{0:T(128)S(1)}, f32[64]{0:T(128)S(1)}, u32[]{:S(2)}, u32[]{:S(2)}) collective-permute-start(f32[64]{0:T(128)S(1)} %add.57), channel_id=1, source_target_pairs={{0,4},{1,5},{2,6},{3,7},{4,0},{5,1},{6,2},{7,3},{8,12},{9,13},{10,... | collective-permute-start | bytes 776 | tf_op jit(solution)/shard_map/ppermute | solution.py:373
  77.7 6.3 %collective-permute-start.21 = (f32[64]{0:T(128)S(1)}, f32[64]{0:T(128)S(1)}, u32[]{:S(2)}, u32[]{:S(2)}) collective-permute-start(f32[64]{0:T(128)S(1)} %add.58), channel_id=1, source_target_pairs={{0,8},{1,9},{2,10},{3,11},{4,12},{5,13},{6,14},{7,15},{8,0},{9,1},... | collective-permute-start | bytes 776 | tf_op jit(solution)/shard_map/ppermute | solution.py:373
  84.0 2.7 %collective-permute-start.22 = (f32[64]{0:T(128)S(1)}, f32[64]{0:T(128)S(1)}, u32[]{:S(2)}, u32[]{:S(2)}) collective-permute-start(f32[64]{0:T(128)S(1)} %add.59), channel_id=1, source_target_pairs={{0,16},{1,17},{2,18},{3,19},{4,20},{5,21},{6,22},{7,23},{8,24},{9,... | collective-permute-start | bytes 776 | tf_op jit(solution)/shard_map/ppermute | solution.py:373
  86.7 3.9 %collective-permute-start.23 = (f32[64]{0:T(128)S(1)}, f32[64]{0:T(128)S(1)}, u32[]{:S(2)}, u32[]{:S(2)}) collective-permute-start(f32[64]{0:T(128)S(1)} %add.60), channel_id=1, source_target_pairs={{0,32},{1,33},{2,34},{3,35},{4,36},{5,37},{6,38},{7,39},{8,40},{9,... | collective-permute-start | bytes 776 | tf_op jit(solution)/shard_map/ppermute | solution.py:373
  93.4 3.2 %collective-permute-start.26 = (f32[8,128]{1,0:T(8,128)S(1)}, f32[8,128]{1,0:T(8,128)S(1)}, u32[]{:S(2)}, u32[]{:S(2)}) collective-permute-start(f32[8,128]{1,0:T(8,128)S(1)} %get-tuple-element.138.first), channel_id=1, source_target_pairs={{0,192},{64,0},{128,64},{192,128},{1,193},{65,1},{129,65},{193,129... | collective-permute-start | bytes 12296 | tf_op jit(solution)/shard_map/ppermute | solution.py:26
  95.9 4.0 %collective-permute-start.25 = (f32[8,128]{1,0:T(8,128)S(1)}, f32[8,128]{1,0:T(8,128)S(1)}, u32[]{:S(2)}, u32[]{:S(2)}) collective-permute-start(f32[8,128]{1,0:T(8,128)S(1)} %get-tuple-element.138.first), channel_id=1, source_target_pairs={{0,128},{64,192},{128,0},{192,64},{1,129},{65,193},{129,1},{193,65... | collective-permute-start | bytes 12296 | tf_op jit(solution)/shard_map/ppermute | solution.py:26
  95.9 4.0 %collective-permute-start.24 = (f32[8,128]{1,0:T(8,128)S(1)}, f32[8,128]{1,0:T(8,128)S(1)}, u32[]{:S(2)}, u32[]{:S(2)}) collective-permute-start(f32[8,128]{1,0:T(8,128)S(1)} %get-tuple-element.138.first), channel_id=1, source_target_pairs={{0,64},{64,128},{128,192},{192,0},{1,65},{65,129},{129,193},{193,1... | collective-permute-start | bytes 12296 | tf_op jit(solution)/shard_map/ppermute | solution.py:26
  100.9 37.9 %all-to-all-start.1 = ((bf16[64,16,256]{2,1,0:T(8,128)(2,1)}), bf16[64,16,256]{2,1,0:T(8,128)(2,1)S(1)}, u32[]{:S(2)}, u32[]{:S(2)}) async-start(bf16[64,16,256]{2,1,0:T(8,128)(2,1)} %shard_map.134), calls=%async_computation.1 | async-start | bytes 1048576 | tf_op jit(solution)/shard_map/all_to_all | solution.py:368
  124.6 14.2 %copy-start.7 = (s32[64]{0:T(128)S(1)}, s32[64]{0:T(128)}, u32[]{:S(2)}) copy-start(s32[64]{0:T(128)} %copy-done.6) | copy-start | bytes 772
  (14 other events, 90.5 us)

commit v12 on v10

--- a/solution.py
+++ b/solution.py
@@ -174,7 +174,7 @@
 def pack(key, flags, partial, up_sum, down_sum, first, second):
     _, half, rows, cols = partial.shape
     blocks, lanes = 2 * half, cols // 2
-    steps = 4 if half >= 16 else 1
+    steps = 2 if half >= 16 else 1
     moment = pl.BlockSpec((2, half // steps, rows, cols), lambda i, *_: (0, i, 0, 0))
     halves = pltpu.HBM((2, half, rows, cols), F32)
     piece = (blocks, 2 * rows + rows // 2, lanes)

time: 122 us -> 121 us (level)
  transfers between devices with their start and end apart: 21 -> 21, of which waited for: 10 -> 10; matrix products, arithmetic and copies ran while one was open for 7% -> 7% of each run, Pallas kernels for 7% -> 6%
where the time goes in v12:
time: 121 us
  starting transfers between devices  50.3 us (42%)
  waiting for transfers between devices  44.7 us (37%)
  Pallas kernels  13.9 us (11%)
  local copies, waits for them, and re-layouts  6.8 us (6%)
  matrix products  2.48 us (2%)
  other arithmetic  1.93 us (2%)
    ppermute x19, starting transfers between devices, shift(): return lax.ppermute(array, 'grp', [(i, (i + step) % n) for i in range(n)])  25.6 us
    ppermute x19, waiting for transfers between devices, shift(): return lax.ppermute(array, 'grp', [(i, (i + step) % n) for i in range(n)])  25.5 us
    all_to_all x2, starting transfers between devices, exchange(): lax.all_to_all(array, 'own', 0, 0, axis_index_groups=groups, tiled=True)  24.6 us
    all_to_all x2, waiting for transfers between devices, exchange(): lax.all_to_all(array, 'own', 0, 0, axis_index_groups=groups, tiled=True)  19.2 us
    pallas_call x1, Pallas kernels, pack(): pl.pallas_call(pack_kernel, out_shape=(pltpu.HBM(piece, BF16), halves, ha...  3.51 us
    pallas_call x1, Pallas kernels, root_pieces(): pl.pallas_call(roots_kernel, out_shape=(pltpu.HBM((11, *unit), BF16), plt...  2.82 us
    pallas_call x1, Pallas kernels, precondition(): pl.pallas_call(precond_kernel, out_shape=(jax.ShapeDtypeStruct((2 * rows,...  2.77 us
    dot_general x2, matrix products, dot(): return lax.dot_general(a, b, (dims, ((), ())), preferred_element_type=F32)  2.48 us
  transfers between devices with their start and end apart: 21, of which 10 were waited for; matrix products, arithmetic and copies ran while one was open for 7% of the time, Pallas kernels for 6%

profile of v12, /device:TPU:1, one launch (start us, length us, event | category | flops | bytes accessed | tf_op | source)
XLA Modules:
  0.0 120.9 jit_solution(16245839502719641902)
XLA Ops:
  0.7 1.4 %dynamic-slice_bitcast_fusion = (bf16[32,16,256]{2,1,0:T(8,128)(2,1)S(1)}, bf16[32,16,256]{2,1,0:T(8,128)(2,1)S(1)}) fusion(bf16[1,64,16,1024]{3,2,1,0:T(8,128)(2,1)} %param.10, s32[]{:T(128)S(6)} %add.37, s32[]{:T(128)S(6)} %mul.29), kind=kLoop, calls=%fused_computation.12 | loop fusion | bytes 1048584 | tf_op jit(solution)/shard_map/slice | solution.py:404
  2.0 2.1 %collective-permute-start.2 = (bf16[32,16,256]{2,1,0:T(8,128)(2,1)S(1)}, bf16[32,16,256]{2,1,0:T(8,128)(2,1)S(1)}, u32[]{:S(2)}, u32[]{:S(2)}) collective-permute-start(bf16[32,16,256]{2,1,0:T(8,128)(2,1)S(1)} %get-tuple-element.71), channel_id=1, source_target_pairs={{0,64},{64,128},{128,192},{192,0},{1,65},{65,129},{129,193},{193,1... | collective-permute-start | bytes 786440 | tf_op jit(solution)/shard_map/ppermute | solution.py:32
  4.2 1.6 %collective-permute-start.3 = (bf16[32,16,256]{2,1,0:T(8,128)(2,1)S(1)}, bf16[32,16,256]{2,1,0:T(8,128)(2,1)S(1)}, u32[]{:S(2)}, u32[]{:S(2)}) collective-permute-start(bf16[32,16,256]{2,1,0:T(8,128)(2,1)S(1)} %get-tuple-element.72), channel_id=1, source_target_pairs={{0,192},{64,0},{128,64},{192,128},{1,193},{65,1},{129,65},{193,129... | collective-permute-start | bytes 786440 | tf_op jit(solution)/shard_map/ppermute | solution.py:32
  5.8 1.7 %constant_dynamic-slice_fusion.3 = (bf16[32,16,256]{2,1,0:T(8,128)(2,1)S(1)}, bf16[32,16,256]{2,1,0:T(8,128)(2,1)S(1)}, bf16[32,16,256]{2,1,0:T(8,128)(2,1)S(1)}, bf16[32,16,256]{2,1,0:T(8,128)(2,1)S(1)}) fusion(bf16[64,16,1024]{2,1,0:T(8,128)(2,1)} %bitcast.42, s32[]{:T(128)S(6)} %add.37, s32[]{:T(128)S(6)} %mul.30, s32[]{:T(128)S(6)} %mul.28), kind=kLoop, calls=%fused_computation.20 | loop fusion | bytes 2097164 | tf_op jit(solution)/shard_map/slice | solution.py:410
  7.6 2.7 %collective-permute-start.1 = (bf16[32,16,256]{2,1,0:T(8,128)(2,1)S(1)}, bf16[32,16,256]{2,1,0:T(8,128)(2,1)S(1)}, u32[]{:S(2)}, u32[]{:S(2)}) collective-permute-start(bf16[32,16,256]{2,1,0:T(8,128)(2,1)S(1)} %get-tuple-element.77), channel_id=1, source_target_pairs={{0,192},{64,0},{128,64},{192,128},{1,193},{65,1},{129,65},{193,129... | collective-permute-start | bytes 786440 | tf_op jit(solution)/shard_map/ppermute | solution.py:32
  12.0 1.2 %collective-permute-start.4 = (bf16[32,16,256]{2,1,0:T(8,128)(2,1)}, bf16[32,16,256]{2,1,0:T(8,128)(2,1)}, u32[]{:S(2)}, u32[]{:S(2)}) collective-permute-start(bf16[32,16,256]{2,1,0:T(8,128)(2,1)} %get-tuple-element.91), channel_id=1, source_target_pairs={{0,64},{64,128},{128,192},{192,0},{1,65},{65,129},{129,193},{193,1... | collective-permute-start | bytes 786440 | tf_op jit(solution)/shard_map/ppermute | solution.py:32
  13.2 1.4 %collective-permute-start.5 = (bf16[32,16,256]{2,1,0:T(8,128)(2,1)}, bf16[32,16,256]{2,1,0:T(8,128)(2,1)}, u32[]{:S(2)}, u32[]{:S(2)}) collective-permute-start(bf16[32,16,256]{2,1,0:T(8,128)(2,1)} %get-tuple-element.92), channel_id=1, source_target_pairs={{0,192},{64,0},{128,64},{192,128},{1,193},{65,1},{129,65},{193,129... | collective-permute-start | bytes 786440 | tf_op jit(solution)/shard_map/ppermute | solution.py:32
  14.7 2.8 %shard_map.138 = (bf16[11,128,256]{2,1,0:T(8,128)(2,1)}, bf16[11,128,256]{2,1,0:T(8,128)(2,1)}, bf16[2,128,256]{2,1,0:T(8,128)(2,1)}) custom-call(f32[1,256,1024]{2,1,0:T(8,128)} %left, f32[1,256,1024]{2,1,0:T(8,128)} %right), custom_call_target="tpu_custom_call" | custom-call | tf_op jit(solution)/shard_map/pallas_call | solution.py:101
  17.5 1.4 %constant_dynamic-slice_fusion.2.own = bf16[64,16,256]{2,1,0:T(8,128)(2,1)S(1)} fusion(bf16[64,16,1024]{2,1,0:T(8,128)(2,1)} %bitcast.43, s32[]{:T(128)S(6)} %mul.27), kind=kLoop, calls=%fused_computation.19 | loop fusion | bytes 1048580 | tf_op jit(solution)/shard_map/dynamic_slice | solution.py:48
  19.3 2.6 %collective-permute-done.4.up_sum = bf16[32,16,256]{2,1,0:T(8,128)(2,1)} collective-permute-done((bf16[32,16,256]{2,1,0:T(8,128)(2,1)}, bf16[32,16,256]{2,1,0:T(8,128)(2,1)}, u32[]{:S(2)}, u32[]{:S(2)}) %collective-permute-start.4) | collective-permute-done | bytes 262176 | tf_op jit(solution)/shard_map/ppermute | solution.py:32
  21.8 2.7 %collective-permute-start.7 = (bf16[11,128,256]{2,1,0:T(8,128)(2,1)S(1)}, bf16[11,128,256]{2,1,0:T(8,128)(2,1)S(1)}, u32[]{:S(2)}, u32[]{:S(2)}) collective-permute-start(bf16[11,128,256]{2,1,0:T(8,128)(2,1)S(1)} %copy-done.15), channel_id=1, source_target_pairs={{0,192},{64,0},{128,64},{192,128},{1,193},{65,1},{129,65},{193,129... | collective-permute-start | bytes 2162696 | tf_op jit(solution)/shard_map/ppermute | solution.py:32
  24.6 3.5 %shard_map.140 = (bf16[64,40,128]{2,1,0:T(8,128)(2,1)}, f32[2,32,16,256]{3,2,1,0:T(8,128)}, f32[2,32,16,256]{3,2,1,0:T(8,128)}) custom-call(s32[64]{0:T(128)S(1)} %gather_fusion, s32[64]{0:T(128)S(1)} %fusion.9.flags, f32[2,32,16,256]{3,2,1,0:T(8,128)S(1)} %get-tuple-element.98.partial, bf16[32,16,256]{2,1,0:T(8,128)(2,1)} %collective-permute-done.4.up_sum, ...), custom_call_target="tpu_custom_call" | custom-call | tf_op jit(solution)/shard_map/pallas_call | solution.py:181
  28.1 15.0 %all-to-all-start = ((bf16[64,40,128]{2,1,0:T(8,128)(2,1)}), bf16[64,40,128]{2,1,0:T(8,128)(2,1)}, u32[]{:S(2)}, u32[]{:S(2)}) async-start(bf16[64,40,128]{2,1,0:T(8,128)(2,1)} %get-tuple-element.103), calls=%async_computation | async-start | bytes 1310720 | tf_op jit(solution)/shard_map/all_to_all | solution.py:401
  44.5 2.7 %collective-permute-start.9 = (bf16[5,128,256]{2,1,0:T(8,128)(2,1)S(1)}, bf16[5,128,256]{2,1,0:T(8,128)(2,1)S(1)}, u32[]{:S(2)}, u32[]{:S(2)}) collective-permute-start(bf16[5,128,256]{2,1,0:T(8,128)(2,1)S(1)} %get-tuple-element.108), channel_id=1, source_target_pairs={{0,192},{64,0},{128,64},{192,128},{1,193},{65,1},{129,65},{193,129... | collective-permute-start | bytes 983048 | tf_op jit(solution)/shard_map/ppermute | solution.py:32
  47.2 7.2 %collective-permute-done.8.refs_13_ = bf16[5,128,256]{2,1,0:T(8,128)(2,1)S(1)} collective-permute-done((bf16[5,128,256]{2,1,0:T(8,128)(2,1)S(1)}, bf16[5,128,256]{2,1,0:T(8,128)(2,1)S(1)}, u32[]{:S(2)}, u32[]{:S(2)}) %collective-permute-start.8) | collective-permute-done | bytes 327712 | tf_op jit(solution)/shard_map/ppermute | solution.py:32
  54.4 7.8 %all-to-all-done.owned = bf16[64,40,128]{2,1,0:T(8,128)(2,1)} async-done(((bf16[64,40,128]{2,1,0:T(8,128)(2,1)}), bf16[64,40,128]{2,1,0:T(8,128)(2,1)}, u32[]{:S(2)}, u32[]{:S(2)}) %all-to-all-start) | async-done | bytes 655392 | tf_op jit(solution)/shard_map/all_to_all | solution.py:401
  62.2 1.2 shard_map.142
  63.8 2.9 %collective-permute-start.11 = (bf16[32,16,256]{2,1,0:T(8,128)(2,1)S(1)}, bf16[32,16,256]{2,1,0:T(8,128)(2,1)S(1)}, u32[]{:S(2)}, u32[]{:S(2)}) collective-permute-start(bf16[32,16,256]{2,1,0:T(8,128)(2,1)S(1)} %get-tuple-element.125), channel_id=1, source_target_pairs={{0,192},{64,0},{128,64},{192,128},{1,193},{65,1},{129,65},{193,129... | collective-permute-start | bytes 786440 | tf_op jit(solution)/shard_map/ppermute | solution.py:32
  66.7 1.2 collective-permute-start.10
  68.2 3.8 %collective-permute-done.12 = bf16[32,16,256]{2,1,0:T(8,128)(2,1)S(1)} collective-permute-done((bf16[32,16,256]{2,1,0:T(8,128)(2,1)S(1)}, bf16[32,16,256]{2,1,0:T(8,128)(2,1)S(1)}, u32[]{:S(2)}, u32[]{:S(2)}) %collective-permute-start.12) | collective-permute-done | bytes 262176 | tf_op jit(solution)/shard_map/ppermute | solution.py:32
  72.0 2.7 %collective-permute-start.14 = (bf16[32,16,256]{2,1,0:T(8,128)(2,1)S(1)}, bf16[32,16,256]{2,1,0:T(8,128)(2,1)S(1)}, u32[]{:S(2)}, u32[]{:S(2)}) collective-permute-start(bf16[32,16,256]{2,1,0:T(8,128)(2,1)S(1)} %collective-permute-done.11), channel_id=1, source_target_pairs={{0,192},{64,0},{128,64},{192,128},{1,193},{65,1},{129,65},{193,129... | collective-permute-start | bytes 786440 | tf_op jit(solution)/shard_map/ppermute | solution.py:32
  74.6 2.2 %collective-permute-done.10 = bf16[32,16,256]{2,1,0:T(8,128)(2,1)S(1)} collective-permute-done((bf16[32,16,256]{2,1,0:T(8,128)(2,1)S(1)}, bf16[32,16,256]{2,1,0:T(8,128)(2,1)S(1)}, u32[]{:S(2)}, u32[]{:S(2)}) %collective-permute-start.10) | collective-permute-done | bytes 262176 | tf_op jit(solution)/shard_map/ppermute | solution.py:32
  77.6 5.6 %collective-permute-done.13 = bf16[32,16,256]{2,1,0:T(8,128)(2,1)S(1)} collective-permute-done((bf16[32,16,256]{2,1,0:T(8,128)(2,1)S(1)}, bf16[32,16,256]{2,1,0:T(8,128)(2,1)S(1)}, u32[]{:S(2)}, u32[]{:S(2)}) %collective-permute-start.13) | collective-permute-done | bytes 262176 | tf_op jit(solution)/shard_map/ppermute | solution.py:32
  83.2 2.8 %shard_map.143 = (f32[1024,256]{1,0:T(8,128)S(1)}, f32[8,128]{1,0:T(8,128)S(1)}) custom-call(bf16[512,256]{1,0:T(8,128)(2,1)S(1)} %bitcast.30, bf16[512,256]{1,0:T(8,128)(2,1)S(1)} %bitcast.31, bf16[512,256]{1,0:T(8,128)(2,1)S(1)} %bitcast.34, bf16[512,256]{1,0:T(8,128)(2,1)S(1)} %bitcast.33, bf16[512,256]{1,0:T(8,128)(2,1)S(1)} %bitcast.36, ...), custom_call_target="tpu_custom_call" | custom-call | tf_op jit(solution)/shard_map/pallas_call | solution.py:326
  86.0 2.7 %collective-permute-start.18 = (f32[8,128]{1,0:T(8,128)S(1)}, f32[8,128]{1,0:T(8,128)S(1)}, u32[]{:S(2)}, u32[]{:S(2)}) collective-permute-start(f32[8,128]{1,0:T(8,128)S(1)} %get-tuple-element.120.first), channel_id=1, source_target_pairs={{0,192},{64,0},{128,64},{192,128},{1,193},{65,1},{129,65},{193,129... | collective-permute-start | bytes 12296 | tf_op jit(solution)/shard_map/ppermute | solution.py:32
  89.4 3.2 %collective-permute-done.17.third = f32[8,128]{1,0:T(8,128)S(1)} collective-permute-done((f32[8,128]{1,0:T(8,128)S(1)}, f32[8,128]{1,0:T(8,128)S(1)}, u32[]{:S(2)}, u32[]{:S(2)}) %collective-permute-start.17) | collective-permute-done | bytes 4128 | tf_op jit(solution)/shard_map/ppermute | solution.py:32
  92.6 0.9 shard_map.144
  93.5 9.6 %all-to-all-start.1 = ((bf16[64,16,256]{2,1,0:T(8,128)(2,1)}), bf16[64,16,256]{2,1,0:T(8,128)(2,1)S(1)}, u32[]{:S(2)}, u32[]{:S(2)}) async-start(bf16[64,16,256]{2,1,0:T(8,128)(2,1)} %shard_map.144), calls=%async_computation.1 | async-start | bytes 1048576 | tf_op jit(solution)/shard_map/all_to_all | solution.py:401
  104.7 1.6 %fusion.3 = f32[1,256,1024]{2,1,0:T(8,128)} fusion(s32[]{:T(128)S(6)} %mul.31, f32[256,1024]{1,0:T(8,128)S(1)} %fusion.4, f32[1,256,1024]{2,1,0:T(8,128)S(1)} %copy-done.10), kind=kLoop, calls=%fused_computation.8 | loop fusion | flops 786432 | bytes 3145732 | tf_op jit(solution)/shard_map/add | solution.py:466
  106.3 1.7 %fusion = f32[1,256,1024]{2,1,0:T(8,128)} fusion(bf16[1024,1024]{1,0:T(8,128)(2,1)S(1)} %bitcast.41, f32[1,256,1024]{2,1,0:T(8,128)S(1)} %copy-done.9, s32[]{:T(128)S(6)} %mul.27), kind=kOutput, calls=%fused_computation.5 | convolution fusion | flops 537395200 | bytes 4718596 | tf_op jit(solution)/shard_map/dot_general | solution.py:52
  108.0 11.4 %all-to-all-done.1.back = bf16[64,16,256]{2,1,0:T(8,128)(2,1)S(1)} async-done(((bf16[64,16,256]{2,1,0:T(8,128)(2,1)}), bf16[64,16,256]{2,1,0:T(8,128)(2,1)S(1)}, u32[]{:S(2)}, u32[]{:S(2)}) %all-to-all-start.1) | async-done | bytes 524320 | tf_op jit(solution)/shard_map/all_to_all | solution.py:401
  119.4 1.5 %shard_map.145 = bf16[64,16,256]{2,1,0:T(8,128)(2,1)} custom-call(s32[64]{0:T(128)S(1)} %copy-done.5, s32[64]{0:T(128)S(1)} %copy-done.3, bf16[64,16,256]{2,1,0:T(8,128)(2,1)S(1)} %all-to-all-done.1.back), custom_call_target="tpu_custom_call" | custom-call | tf_op jit(solution)/shard_map/pallas_call | solution.py:255
  (64 shorter events, 7.2 us)
Async XLA Ops:
  0.6 9.7 %copy-start.8 = (s32[64]{0:T(128)S(1)}, s32[64]{0:T(128)}, u32[]{:S(2)}) copy-start(s32[64]{0:T(128)} %constant.56.clone) | copy-start | bytes 772
  0.6 9.6 %copy-start.16 = (s32[64]{0:T(128)S(1)}, s32[64]{0:T(128)}, u32[]{:S(2)}) copy-start(s32[64]{0:T(128)} %param.11) | copy-start | bytes 772
  0.7 10.4 %copy-start.14 = (s32[64,4]{0,1:T(4,128)S(1)}, s32[64,4]{0,1:T(4,128)}, u32[]{:S(2)}) copy-start(s32[64,4]{0,1:T(4,128)} %param.12) | copy-start | bytes 3076
  2.0 9.1 %collective-permute-start.2 = (bf16[32,16,256]{2,1,0:T(8,128)(2,1)S(1)}, bf16[32,16,256]{2,1,0:T(8,128)(2,1)S(1)}, u32[]{:S(2)}, u32[]{:S(2)}) collective-permute-start(bf16[32,16,256]{2,1,0:T(8,128)(2,1)S(1)} %get-tuple-element.71), channel_id=1, source_target_pairs={{0,64},{64,128},{128,192},{192,0},{1,65},{65,129},{129,193},{193,1... | collective-permute-start | bytes 786440 | tf_op jit(solution)/shard_map/ppermute | solution.py:32
  4.2 7.0 %collective-permute-start.3 = (bf16[32,16,256]{2,1,0:T(8,128)(2,1)S(1)}, bf16[32,16,256]{2,1,0:T(8,128)(2,1)S(1)}, u32[]{:S(2)}, u32[]{:S(2)}) collective-permute-start(bf16[32,16,256]{2,1,0:T(8,128)(2,1)S(1)} %get-tuple-element.72), channel_id=1, source_target_pairs={{0,192},{64,0},{128,64},{192,128},{1,193},{65,1},{129,65},{193,129... | collective-permute-start | bytes 786440 | tf_op jit(solution)/shard_map/ppermute | solution.py:32
  7.5 10.0 %collective-permute-start = (bf16[32,16,256]{2,1,0:T(8,128)(2,1)S(1)}, bf16[32,16,256]{2,1,0:T(8,128)(2,1)S(1)}, u32[]{:S(2)}, u32[]{:S(2)}) collective-permute-start(bf16[32,16,256]{2,1,0:T(8,128)(2,1)S(1)} %get-tuple-element.76), channel_id=1, source_target_pairs={{0,64},{64,128},{128,192},{192,0},{1,65},{65,129},{129,193},{193,1... | collective-permute-start | bytes 786440 | tf_op jit(solution)/shard_map/ppermute | solution.py:32
  7.6 9.9 %collective-permute-start.1 = (bf16[32,16,256]{2,1,0:T(8,128)(2,1)S(1)}, bf16[32,16,256]{2,1,0:T(8,128)(2,1)S(1)}, u32[]{:S(2)}, u32[]{:S(2)}) collective-permute-start(bf16[32,16,256]{2,1,0:T(8,128)(2,1)S(1)} %get-tuple-element.77), channel_id=1, source_target_pairs={{0,192},{64,0},{128,64},{192,128},{1,193},{65,1},{129,65},{193,129... | collective-permute-start | bytes 786440 | tf_op jit(solution)/shard_map/ppermute | solution.py:32
  11.1 13.5 %copy-start.4 = (s32[64]{0:T(128)}, s32[64]{0:T(128)S(1)}, u32[]{:S(2)}) copy-start(s32[64]{0:T(128)S(1)} %gather_fusion) | copy-start | bytes 772
  11.1 13.5 %copy-start.2 = (s32[64]{0:T(128)}, s32[64]{0:T(128)S(1)}, u32[]{:S(2)}) copy-start(s32[64]{0:T(128)S(1)} %fusion.9.flags) | copy-start | bytes 772
  11.1 7.8 %copy-start.6 = (f32[64,16,256]{2,1,0:T(8,128)S(1)}, f32[64,16,256]{2,1,0:T(8,128)}, u32[]{:S(2)}) copy-start(f32[64,16,256]{2,1,0:T(8,128)} %param.17) | copy-start | bytes 3145732
  11.1 7.8 %copy-start.7 = (f32[64,16,256]{2,1,0:T(8,128)S(1)}, f32[64,16,256]{2,1,0:T(8,128)}, u32[]{:S(2)}) copy-start(f32[64,16,256]{2,1,0:T(8,128)} %param.18) | copy-start | bytes 3145732
  12.0 9.8 %collective-permute-start.4 = (bf16[32,16,256]{2,1,0:T(8,128)(2,1)}, bf16[32,16,256]{2,1,0:T(8,128)(2,1)}, u32[]{:S(2)}, u32[]{:S(2)}) collective-permute-start(bf16[32,16,256]{2,1,0:T(8,128)(2,1)} %get-tuple-element.91), channel_id=1, source_target_pairs={{0,64},{64,128},{128,192},{192,0},{1,65},{65,129},{129,193},{193,1... | collective-permute-start | bytes 786440 | tf_op jit(solution)/shard_map/ppermute | solution.py:32
  13.2 8.6 %collective-permute-start.5 = (bf16[32,16,256]{2,1,0:T(8,128)(2,1)}, bf16[32,16,256]{2,1,0:T(8,128)(2,1)}, u32[]{:S(2)}, u32[]{:S(2)}) collective-permute-start(bf16[32,16,256]{2,1,0:T(8,128)(2,1)} %get-tuple-element.92), channel_id=1, source_target_pairs={{0,192},{64,0},{128,64},{192,128},{1,193},{65,1},{129,65},{193,129... | collective-permute-start | bytes 786440 | tf_op jit(solution)/shard_map/ppermute | solution.py:32
  21.8 21.3 %collective-permute-start.7 = (bf16[11,128,256]{2,1,0:T(8,128)(2,1)S(1)}, bf16[11,128,256]{2,1,0:T(8,128)(2,1)S(1)}, u32[]{:S(2)}, u32[]{:S(2)}) collective-permute-start(bf16[11,128,256]{2,1,0:T(8,128)(2,1)S(1)} %copy-done.15), channel_id=1, source_target_pairs={{0,192},{64,0},{128,64},{192,128},{1,193},{65,1},{129,65},{193,129... | collective-permute-start | bytes 2162696 | tf_op jit(solution)/shard_map/ppermute | solution.py:32
  24.6 18.6 %collective-permute-start.6 = (bf16[11,128,256]{2,1,0:T(8,128)(2,1)S(1)}, bf16[11,128,256]{2,1,0:T(8,128)(2,1)S(1)}, u32[]{:S(2)}, u32[]{:S(2)}) collective-permute-start(bf16[11,128,256]{2,1,0:T(8,128)(2,1)S(1)} %copy-done.11), channel_id=1, source_target_pairs={{0,64},{64,128},{128,192},{192,0},{1,65},{65,129},{129,193},{193,1... | collective-permute-start | bytes 2162696 | tf_op jit(solution)/shard_map/ppermute | solution.py:32
  28.1 34.1 %all-to-all-start = ((bf16[64,40,128]{2,1,0:T(8,128)(2,1)}), bf16[64,40,128]{2,1,0:T(8,128)(2,1)}, u32[]{:S(2)}, u32[]{:S(2)}) async-start(bf16[64,40,128]{2,1,0:T(8,128)(2,1)} %get-tuple-element.103), calls=%async_computation | async-start | bytes 1310720 | tf_op jit(solution)/shard_map/all_to_all | solution.py:401
  44.2 10.2 %collective-permute-start.8 = (bf16[5,128,256]{2,1,0:T(8,128)(2,1)S(1)}, bf16[5,128,256]{2,1,0:T(8,128)(2,1)S(1)}, u32[]{:S(2)}, u32[]{:S(2)}) collective-permute-start(bf16[5,128,256]{2,1,0:T(8,128)(2,1)S(1)} %get-tuple-element.107), channel_id=1, source_target_pairs={{0,64},{64,128},{128,192},{192,0},{1,65},{65,129},{129,193},{193,1... | collective-permute-start | bytes 983048 | tf_op jit(solution)/shard_map/ppermute | solution.py:32
  44.5 9.9 %collective-permute-start.9 = (bf16[5,128,256]{2,1,0:T(8,128)(2,1)S(1)}, bf16[5,128,256]{2,1,0:T(8,128)(2,1)S(1)}, u32[]{:S(2)}, u32[]{:S(2)}) collective-permute-start(bf16[5,128,256]{2,1,0:T(8,128)(2,1)S(1)} %get-tuple-element.108), channel_id=1, source_target_pairs={{0,192},{64,0},{128,64},{192,128},{1,193},{65,1},{129,65},{193,129... | collective-permute-start | bytes 983048 | tf_op jit(solution)/shard_map/ppermute | solution.py:32
  54.4 28.8 %copy-start.12 = (bf16[5,128,256]{2,1,0:T(8,128)(2,1)}, bf16[5,128,256]{2,1,0:T(8,128)(2,1)S(1)}, u32[]{:S(2)}) copy-start(bf16[5,128,256]{2,1,0:T(8,128)(2,1)S(1)} %collective-permute-done.8.refs_13_) | copy-start | bytes 983044
  54.4 28.8 %copy-start.13 = (bf16[5,128,256]{2,1,0:T(8,128)(2,1)}, bf16[5,128,256]{2,1,0:T(8,128)(2,1)S(1)}, u32[]{:S(2)}) copy-start(bf16[5,128,256]{2,1,0:T(8,128)(2,1)S(1)} %collective-permute-done.9.refs_14_) | copy-start | bytes 983044
  63.4 8.5 %collective-permute-start.12 = (bf16[32,16,256]{2,1,0:T(8,128)(2,1)S(1)}, bf16[32,16,256]{2,1,0:T(8,128)(2,1)S(1)}, u32[]{:S(2)}, u32[]{:S(2)}) collective-permute-start(bf16[32,16,256]{2,1,0:T(8,128)(2,1)S(1)} %get-tuple-element.124), channel_id=1, source_target_pairs={{0,64},{64,128},{128,192},{192,0},{1,65},{65,129},{129,193},{193,1... | collective-permute-start | bytes 786440 | tf_op jit(solution)/shard_map/ppermute | solution.py:32
  63.8 8.2 %collective-permute-start.11 = (bf16[32,16,256]{2,1,0:T(8,128)(2,1)S(1)}, bf16[32,16,256]{2,1,0:T(8,128)(2,1)S(1)}, u32[]{:S(2)}, u32[]{:S(2)}) collective-permute-start(bf16[32,16,256]{2,1,0:T(8,128)(2,1)S(1)} %get-tuple-element.125), channel_id=1, source_target_pairs={{0,192},{64,0},{128,64},{192,128},{1,193},{65,1},{129,65},{193,129... | collective-permute-start | bytes 786440 | tf_op jit(solution)/shard_map/ppermute | solution.py:32
  66.7 10.1 %collective-permute-start.10 = (bf16[32,16,256]{2,1,0:T(8,128)(2,1)S(1)}, bf16[32,16,256]{2,1,0:T(8,128)(2,1)S(1)}, u32[]{:S(2)}, u32[]{:S(2)}) collective-permute-start(bf16[32,16,256]{2,1,0:T(8,128)(2,1)S(1)} %get-tuple-element.124), channel_id=1, source_target_pairs={{0,192},{64,0},{128,64},{192,128},{1,193},{65,1},{129,65},{193,129... | collective-permute-start | bytes 786440 | tf_op jit(solution)/shard_map/ppermute | solution.py:32
  67.9 9.7 %collective-permute-start.15 = (bf16[32,16,256]{2,1,0:T(8,128)(2,1)S(1)}, bf16[32,16,256]{2,1,0:T(8,128)(2,1)S(1)}, u32[]{:S(2)}, u32[]{:S(2)}) collective-permute-start(bf16[32,16,256]{2,1,0:T(8,128)(2,1)S(1)} %get-tuple-element.125), channel_id=1, source_target_pairs={{0,64},{64,128},{128,192},{192,0},{1,65},{65,129},{129,193},{193,1... | collective-permute-start | bytes 786440 | tf_op jit(solution)/shard_map/ppermute | solution.py:32
  71.9 11.2 %collective-permute-start.13 = (bf16[32,16,256]{2,1,0:T(8,128)(2,1)S(1)}, bf16[32,16,256]{2,1,0:T(8,128)(2,1)S(1)}, u32[]{:S(2)}, u32[]{:S(2)}) collective-permute-start(bf16[32,16,256]{2,1,0:T(8,128)(2,1)S(1)} %collective-permute-done.12), channel_id=1, source_target_pairs={{0,64},{64,128},{128,192},{192,0},{1,65},{65,129},{129,193},{193,1... | collective-permute-start | bytes 786440 | tf_op jit(solution)/shard_map/ppermute | solution.py:32
  72.0 11.2 %collective-permute-start.14 = (bf16[32,16,256]{2,1,0:T(8,128)(2,1)S(1)}, bf16[32,16,256]{2,1,0:T(8,128)(2,1)S(1)}, u32[]{:S(2)}, u32[]{:S(2)}) collective-permute-start(bf16[32,16,256]{2,1,0:T(8,128)(2,1)S(1)} %collective-permute-done.11), channel_id=1, source_target_pairs={{0,192},{64,0},{128,64},{192,128},{1,193},{65,1},{129,65},{193,129... | collective-permute-start | bytes 786440 | tf_op jit(solution)/shard_map/ppermute | solution.py:32
  86.0 3.5 %collective-permute-start.18 = (f32[8,128]{1,0:T(8,128)S(1)}, f32[8,128]{1,0:T(8,128)S(1)}, u32[]{:S(2)}, u32[]{:S(2)}) collective-permute-start(f32[8,128]{1,0:T(8,128)S(1)} %get-tuple-element.120.first), channel_id=1, source_target_pairs={{0,192},{64,0},{128,64},{192,128},{1,193},{65,1},{129,65},{193,129... | collective-permute-start | bytes 12296 | tf_op jit(solution)/shard_map/ppermute | solution.py:32
  88.7 4.0 %collective-permute-start.17 = (f32[8,128]{1,0:T(8,128)S(1)}, f32[8,128]{1,0:T(8,128)S(1)}, u32[]{:S(2)}, u32[]{:S(2)}) collective-permute-start(f32[8,128]{1,0:T(8,128)S(1)} %get-tuple-element.120.first), channel_id=1, source_target_pairs={{0,128},{64,192},{128,0},{192,64},{1,129},{65,193},{129,1},{193,65... | collective-permute-start | bytes 12296 | tf_op jit(solution)/shard_map/ppermute | solution.py:32
  88.7 4.0 %collective-permute-start.16 = (f32[8,128]{1,0:T(8,128)S(1)}, f32[8,128]{1,0:T(8,128)S(1)}, u32[]{:S(2)}, u32[]{:S(2)}) collective-permute-start(f32[8,128]{1,0:T(8,128)S(1)} %get-tuple-element.120.first), channel_id=1, source_target_pairs={{0,64},{64,128},{128,192},{192,0},{1,65},{65,129},{129,193},{193,1... | collective-permute-start | bytes 12296 | tf_op jit(solution)/shard_map/ppermute | solution.py:32
  93.5 25.9 %all-to-all-start.1 = ((bf16[64,16,256]{2,1,0:T(8,128)(2,1)}), bf16[64,16,256]{2,1,0:T(8,128)(2,1)S(1)}, u32[]{:S(2)}, u32[]{:S(2)}) async-start(bf16[64,16,256]{2,1,0:T(8,128)(2,1)} %shard_map.144), calls=%async_computation.1 | async-start | bytes 1048576 | tf_op jit(solution)/shard_map/all_to_all | solution.py:401
  106.3 13.1 %copy-start.3 = (s32[64]{0:T(128)S(1)}, s32[64]{0:T(128)}, u32[]{:S(2)}) copy-start(s32[64]{0:T(128)} %copy-done.2) | copy-start | bytes 772
  106.3 13.1 %copy-start.5 = (s32[64]{0:T(128)S(1)}, s32[64]{0:T(128)}, u32[]{:S(2)}) copy-start(s32[64]{0:T(128)} %copy-done.4) | copy-start | bytes 772
  (6 other events, 13.4 us)
